TPU v7x, 128 devices: a whole 4x4x4 slice. The times are simulated.
128 devices in a mesh: dp: 4 (over y), ep: 32 (over x, z, core).
Axes of the slice: x: 4, y: 4, z: 4, core: 2. Of those that a mesh axis runs over, the one named last changes fastest.
Arguments:
- tokens: bfloat16 [8192, 2048], P(('dp', 'ep')), may hold values from -6 to 6
- row_counts: int32 [128], P(('dp', 'ep')), may hold values from 1 to 64, 5120 in all
- expert_ids: int32 [8192, 6], P(('dp', 'ep')), may hold values from 0 to 63, all different within a row; in each aligned block of 64 rows (0 to 63, 64 to 127, ...) at most 8 rows name the same one
- gate_weights: float32 [8192, 6], P(('dp', 'ep')), may hold values from 0.1 to 1
- expert_gate: bfloat16 [64, 2048, 1408], P('ep', None, 'dp'), may hold values from -0.125 to 0.125
- expert_up: bfloat16 [64, 2048, 1408], P('ep', None, 'dp'), may hold values from -0.125 to 0.125
- expert_down: bfloat16 [64, 1408, 2048], P('ep', 'dp'), may hold values from -0.15625 to 0.15625
- shared_gate: bfloat16 [2048, 2816], P(None, 'dp'), may hold values from -0.125 to 0.125
- shared_up: bfloat16 [2048, 2816], P(None, 'dp'), may hold values from -0.125 to 0.125
- shared_down: bfloat16 [2816, 2048], P('dp'), may hold values from -0.109375 to 0.109375
Outputs:
- mixed: bfloat16 [8192, 2048], P(('dp', 'ep'))
Inputs may be any that keep to these rules, and one draw needn't show every extreme that they name: `expert_ids`: in each device's block of 64 rows no expert is named by more than 8 rows, a bound that some block reaches; a row names 6 different experts. `row_counts`: some device's slots are all live.
All inputs are finite; a program needn't handle non-finite values.
Results may differ from a plain program's by a relative error of at most 0.012.
Values may be sent and summed in bfloat16 or wider, within the bound.
No kernel may reach another device: no remote copies, remote signals or barrier semaphores. Data moves between devices by JAX's collectives and lax.ppermute only.
A program may use at most 128 MiB of HBM per device.

v0:
```python
import jax
import jax.numpy as jnp
from jax import lax
from jax.sharding import PartitionSpec as P


def project_rows(rows_in, gate_w, up_w, down_w):
    gate_act = jnp.dot(rows_in, gate_w, preferred_element_type=jnp.float32)
    up_act = jnp.dot(rows_in, up_w, preferred_element_type=jnp.float32)
    hidden = (jax.nn.silu(gate_act) * up_act).astype(jnp.bfloat16)
    return jnp.dot(hidden, down_w, preferred_element_type=jnp.float32)


def on_device(
    tokens,
    row_counts,
    expert_ids,
    gate_weights,
    expert_gate,
    expert_up,
    expert_down,
    shared_gate,
    shared_up,
    shared_down,
):
    tok_rows, feature = tokens.shape
    per_token = expert_ids.shape[1]
    local_experts = expert_gate.shape[0]
    n_ep = lax.axis_size("ep")
    n_experts = local_experts * n_ep
    capacity = tok_rows * per_token * 4 // (3 * n_experts)
    live_rows = jnp.arange(tok_rows, dtype=jnp.int32) < row_counts[0]
    flat_ids = expert_ids.reshape(-1)
    live_pairs = jnp.repeat(live_rows, per_token)
    onehot = (
        (flat_ids[:, None] == jnp.arange(n_experts, dtype=jnp.int32)[None, :]) & live_pairs[:, None]
    ).astype(jnp.int32)
    before = jnp.cumsum(onehot, axis=0) - onehot
    slot_rank = jnp.sum(before * onehot, axis=1)
    slot_index = flat_ids * capacity + slot_rank
    slot_drop = jnp.where(live_pairs, slot_index, n_experts * capacity)
    owners = jnp.arange(tok_rows * per_token, dtype=jnp.int32) // per_token
    source_row = (
        jnp.full((n_experts * capacity,), tok_rows, jnp.int32)
        .at[slot_drop]
        .set(owners, mode="drop")
    )
    padded = jnp.concatenate([tokens, jnp.zeros((1, feature), tokens.dtype)], axis=0)
    outgoing = padded[source_row].reshape(n_ep, local_experts * capacity, feature)
    shared_terms = project_rows(
        lax.all_gather(tokens, "dp", axis=0, tiled=True), shared_gate, shared_up, shared_down
    )
    shared = lax.psum_scatter(
        shared_terms.astype(jnp.bfloat16), "dp", scatter_dimension=0, tiled=True
    ).astype(jnp.float32)
    n_dp = lax.axis_size("dp")
    copies = jnp.broadcast_to(outgoing[None], (n_dp,) + outgoing.shape).reshape(
        n_dp * n_ep, local_experts * capacity, feature
    )
    arrived = lax.all_to_all(copies, ("dp", "ep"), split_axis=0, concat_axis=0, tiled=True)
    sources = arrived.shape[0]
    results = []
    for member in range(local_experts):
        expert_rows = arrived[:, member * capacity : (member + 1) * capacity].reshape(-1, feature)
        produced = project_rows(
            expert_rows, expert_gate[member], expert_up[member], expert_down[member]
        )
        results.append(produced.reshape(sources, capacity, feature))
    partial_value = jnp.concatenate(results, axis=1).astype(jnp.bfloat16)
    returned = lax.all_to_all(partial_value, ("dp", "ep"), split_axis=0, concat_axis=0, tiled=True)
    combined = jnp.sum(
        returned.reshape(n_dp, n_ep, local_experts * capacity, feature).astype(jnp.float32), axis=0
    )
    flat_out = combined.reshape(n_experts * capacity, feature)
    picked = flat_out[jnp.where(live_pairs, slot_index, 0)]
    pair_weights = jnp.where(live_pairs, gate_weights.reshape(-1), 0.0)
    routed = jnp.sum((picked * pair_weights[:, None]).reshape(tok_rows, per_token, feature), axis=1)
    return jnp.where(live_rows[:, None], shared + routed, 0.0).astype(jnp.bfloat16)


def solution(mesh):
    in_specs = (
        P(("dp", "ep"), None),
        P(("dp", "ep")),
        P(("dp", "ep"), None),
        P(("dp", "ep"), None),
        P("ep", None, "dp"),
        P("ep", None, "dp"),
        P("ep", "dp", None),
        P(None, "dp"),
        P(None, "dp"),
        P("dp", None),
    )
    out_specs = P(("dp", "ep"), None)
    return jax.shard_map(
        on_device, mesh=mesh, in_specs=in_specs, out_specs=out_specs, check_vma=False
    )
```

profile of v0, /device:TPU:1, one launch (start us, length us, event | category | flops | bytes accessed | tf_op | source)
XLA Modules:
  0.0 333.1 jit_solution(1387655756324666291)
XLA Ops:
  11.2 2.9 scatter_custom_fusion
  15.2 3.3 %gather_fusion = bf16[512,2048]{1,0:T(8,128)(2,1)} fusion(bf16[65,2048]{1,0:T(8,128)(2,1)S(1)} %concatenate.7, s32[1024]{0:T(1024)S(1)} %pad_clamp_fusion.1), kind=kCustom, calls=%fused_computation | custom fusion | bytes 4196352 | tf_op jit(solution)/shard_map/gather | solution.py:49
  18.5 2.6 broadcast_in_dim.49
  21.2 109.9 %all_to_all.10 = bf16[128,16,2048]{2,1,0:T(8,128)(2,1)S(1)} all-to-all(bf16[128,16,2048]{2,1,0:T(8,128)(2,1)S(1)} %bitcast.75), channel_id=1, replica_groups=mesh['dp'=4,'ep'=32] {'dp','ep'}, dimensions={0} | all-to-all | bytes 16777216 | tf_op jit(solution)/shard_map/all_to_all | solution.py:60
  132.7 2.1 copy-done.1
  135.0 2.7 fusion.18
  137.7 2.3 copy.33
  140.0 4.5 %fusion.3 = f32[1024,352]{0,1:T(8,128)S(1)} fusion(bf16[128,16,2048]{2,1,0:T(8,128)(2,1)} %copy-done.1, bf16[2,2048,352]{1,2,0:T(8,128)(2,1)} %param.14), kind=kOutput, calls=%fused_computation.13 | convolution fusion | flops 1476395008 | bytes 7077888 | tf_op jit(solution)/shard_map/dot_general | solution.py:8
  145.9 2.7 fusion.21
  148.5 2.3 copy.35
  150.8 6.1 %convolution_convert_fusion.1 = bf16[128,8,2048]{2,0,1:T(8,128)(2,1)} fusion(bf16[2,352,2048]{2,1,0:T(8,128)(2,1)} %param.16, bf16[128,8,352]{2,1,0:T(8,128)(2,1)} %bitcast.77), kind=kOutput, calls=%fused_computation.9 | convolution fusion | flops 1478492160 | bytes 6422528 | tf_op jit(solution)/shard_map/dot_general | solution.py:11
  156.9 4.3 %convolution_convert_fusion = bf16[128,8,2048]{2,0,1:T(8,128)(2,1)} fusion(bf16[2,352,2048]{2,1,0:T(8,128)(2,1)S(1)} %copy-done.8, bf16[128,8,352]{2,1,0:T(8,128)(2,1)S(1)} %bitcast.78), kind=kOutput, calls=%fused_computation.8 | convolution fusion | flops 1478492160 | bytes 6422528 | tf_op jit(solution)/shard_map/dot_general | solution.py:11
  161.2 7.4 %pad_maximum_fusion = bf16[128,16,2048]{2,0,1:T(8,128)(2,1)} fusion(bf16[128,8,2048]{2,0,1:T(8,128)(2,1)} %convolution_convert_fusion, bf16[128,8,2048]{2,0,1:T(8,128)(2,1)} %convolution_convert_fusion.1), kind=kLoop, calls=%fused_computation.4 | loop fusion | flops 4194304 | bytes 16777216 | tf_op jit(solution)/shard_map/concatenate | solution.py:69
  168.6 11.4 %copy.37 = bf16[128,16,2048]{2,1,0:T(8,128)(2,1)} copy(bf16[128,16,2048]{2,0,1:T(8,128)(2,1)} %pad_maximum_fusion) | data formatting | bytes 16777216 | tf_op jit(solution)/shard_map/concatenate | solution.py:69
  180.0 6.2 %all-to-all-start.1 = ((bf16[128,16,2048]{2,1,0:T(8,128)(2,1)}), bf16[128,16,2048]{2,1,0:T(8,128)(2,1)}, u32[]{:S(2)}, u32[]{:S(2)}) async-start(bf16[128,16,2048]{2,1,0:T(8,128)(2,1)} %copy.37), calls=%async_computation.2 | async-start | bytes 16777216 | tf_op jit(solution)/shard_map/all_to_all | solution.py:70
  187.0 96.8 %all-gather.2.cloned.1.call-done = bf16[256,2048]{1,0:T(8,128)(2,1)} async-done(((bf16[64,2048]{1,0:T(8,128)(2,1)}), bf16[256,2048]{1,0:T(8,128)(2,1)}) %all-gather.2.cloned.1.call-update) | async-done | bytes 1048592 | tf_op jit(solution)/shard_map/all_gather | solution.py:51
  283.8 4.0 %fusion.42 = f32[256,704]{0,1:T(8,128)} fusion(bf16[256,2048]{1,0:T(8,128)(2,1)} %all-gather.2.cloned.1.call-done, bf16[2048,704]{0,1:T(8,128)(2,1)} %param.17), kind=kOutput, calls=%fused_computation.69 | convolution fusion | flops 738197504 | bytes 4653056 | tf_op jit(solution)/shard_map/dot_general | solution.py:8
  287.8 6.6 %convolution_convert_fusion.2 = bf16[256,2048]{1,0:T(8,128)(2,1)} fusion(bf16[704,2048]{1,0:T(8,128)(2,1)S(1)} %copy-done, bf16[256,2048]{1,0:T(8,128)(2,1)} %all-gather.2.cloned.1.call-done, bf16[2048,704]{0,1:T(8,128)(2,1)} %param.18, f32[256,704]{0,1:T(8,128)} %fusion.42), kind=kOutput, calls=%fused_computation.14 | convolution fusion | flops 1478000640 | bytes 8585216 | tf_op jit(solution)/shard_map/dot_general | solution.py:11
  294.6 7.6 %convert_reduce_fusion = f32[32,16,2048]{2,1,0:T(8,128)} fusion(bf16[4,32,16,2048]{3,2,1,0:T(8,128)(2,1)} %bitcast.18), kind=kLoop, calls=%fused_computation.3 | loop fusion | flops 7340032 | bytes 12582912 | tf_op jit(solution)/shard_map/reduce_sum | solution.py:71
  302.2 7.3 %gather_fusion.1 = f32[384,2048]{1,0:T(8,128)} fusion(f32[512,2048]{1,0:T(8,128)} %bitcast.74, s32[1024]{0:T(1024)S(1)} %pad_clamp_fusion), kind=kCustom, calls=%fused_computation.1 | custom fusion | bytes 6292992 | tf_op jit(solution)/shard_map/gather | solution.py:75
  309.5 4.6 %gather.10 = f32[64,6,2048]{2,1,0:T(8,128)} reshape(f32[384,2048]{1,0:T(8,128)} %gather_fusion.1) | data formatting | bytes 6291456 | tf_op jit(solution)/shard_map/gather | solution.py:75
  314.1 3.8 %multiply_reduce_fusion = f32[64,2048]{1,0:T(8,128)S(1)} fusion(f32[64,6,2048]{2,1,0:T(8,128)} %gather.10, f32[64,6]{1,0:T(8,128)S(1)} %copy.40), kind=kLoop, calls=%fused_computation.7 | loop fusion | flops 1441792 | bytes 3671552 | tf_op jit(solution)/shard_map/reduce_sum | solution.py:77
  317.9 6.6 %reduce-scatter.2.cloned.1.call-done = bf16[64,2048]{1,0:T(8,128)(2,1)} async-done(((bf16[256,2048]{1,0:T(8,128)(2,1)}), bf16[64,2048]{1,0:T(8,128)(2,1)}) %reduce-scatter.2.cloned.1.call-update) | async-done | bytes 262160 | tf_op jit(solution)/shard_map/reduce_scatter | solution.py:53
  324.5 1.7 select_convert_fusion
  (47 shorter events, 9.0 us)
Async XLA Ops:
  6.5 281.3 %copy-start = (bf16[704,2048]{1,0:T(8,128)(2,1)S(1)}, bf16[704,2048]{1,0:T(8,128)(2,1)}, u32[]{:S(2)}) copy-start(bf16[704,2048]{1,0:T(8,128)(2,1)} %param.19) | copy-start | bytes 8650756
  21.1 109.9 %copy-start.5 = (bf16[2,2048,352]{1,2,0:T(8,128)(2,1)S(1)}, bf16[2,2048,352]{1,2,0:T(8,128)(2,1)}, u32[]{:S(2)}) copy-start(bf16[2,2048,352]{1,2,0:T(8,128)(2,1)} %param.14) | copy-start | bytes 8650756
  131.0 3.8 %copy-start.1 = (bf16[128,16,2048]{2,1,0:T(8,128)(2,1)}, bf16[128,16,2048]{2,1,0:T(8,128)(2,1)S(1)}, u32[]{:S(2)}) copy-start(bf16[128,16,2048]{2,1,0:T(8,128)(2,1)S(1)} %all_to_all.10) | copy-start | bytes 25165828
  131.0 3.9 %copy-start.6 = (bf16[2,2048,352]{1,2,0:T(8,128)(2,1)S(1)}, bf16[2,2048,352]{1,2,0:T(8,128)(2,1)}, u32[]{:S(2)}) copy-start(bf16[2,2048,352]{1,2,0:T(8,128)(2,1)} %param.15) | copy-start | bytes 8650756
  140.0 5.1 %copy-start.2 = (bf16[128,16,2048]{2,1,0:T(8,128)(2,1)S(1)}, bf16[128,16,2048]{2,1,0:T(8,128)(2,1)}, u32[]{:S(2)}) copy-start(bf16[128,16,2048]{2,1,0:T(8,128)(2,1)} %copy-done.1) | copy-start | bytes 25165828
  140.0 5.9 %copy-start.7 = (bf16[2,2048,352]{1,2,0:T(8,128)(2,1)S(1)}, bf16[2,2048,352]{1,2,0:T(8,128)(2,1)}, u32[]{:S(2)}) copy-start(bf16[2,2048,352]{1,2,0:T(8,128)(2,1)} %param.15) | copy-start | bytes 8650756
  150.8 6.1 %copy-start.3 = (bf16[1024,352]{1,0:T(8,128)(2,1)S(1)}, bf16[1024,352]{1,0:T(8,128)(2,1)}, u32[]{:S(2)}) copy-start(bf16[1024,352]{1,0:T(8,128)(2,1)} %copy.35) | copy-start | bytes 2162692
  150.8 6.1 %copy-start.8 = (bf16[2,352,2048]{2,1,0:T(8,128)(2,1)S(1)}, bf16[2,352,2048]{2,1,0:T(8,128)(2,1)}, u32[]{:S(2)}) copy-start(bf16[2,352,2048]{2,1,0:T(8,128)(2,1)} %param.16) | copy-start | bytes 8650756
  180.0 114.6 %all-to-all-start.1 = ((bf16[128,16,2048]{2,1,0:T(8,128)(2,1)}), bf16[128,16,2048]{2,1,0:T(8,128)(2,1)}, u32[]{:S(2)}, u32[]{:S(2)}) async-start(bf16[128,16,2048]{2,1,0:T(8,128)(2,1)} %copy.37), calls=%async_computation.2 | async-start | bytes 16777216 | tf_op jit(solution)/shard_map/all_to_all | solution.py:70
  186.3 97.6 %all-gather.2.cloned.1.call-start = ((), (), s32[]{:S(2)}) async-start(), calls=%async_computation.3 | async-start | bytes 1310720 | tf_op jit(solution)/shard_map/all_gather | solution.py:51
  187.0 137.5 %reduce-scatter.2.cloned.1.call-start = ((), (), s32[]{:S(2)}) async-start(), calls=%async_computation.4 | async-start | bytes 1310720 | tf_op jit(solution)/shard_map/reduce_scatter | solution.py:53
  287.8 6.6 %copy-start.4 = (f32[64,6]{0,1:T(8,128)S(1)}, f32[64,6]{0,1:T(8,128)}, u32[]{:S(2)}) copy-start(f32[64,6]{0,1:T(8,128)} %param.13) | copy-start | bytes 4612
Sparse Core Ops, SparseCore 0:
  188.8 95.0 all-gather.1
  294.6 29.9 reduce-scatter.1
where the time goes:
time: 335 us; the launch traced here: 333 us
  blocking collectives  110 us (33%)
  waiting for transfers between devices  104 us (31%)
  local copies, waits for them, and re-layouts  43.6 us (13%)
  matrix products  32.4 us (10%)
  other arithmetic  22.4 us (7%)
  between operations  14.4 us (4%)
  starting transfers between devices  6.32 us (2%)
    all_to_all x1, blocking collectives, on_device(): lax.all_to_all(copies, ('dp', 'ep'), split_axis=0, concat_axis=0, tiled=T...  110 us
    all_gather x1, waiting for transfers between devices, on_device(): lax.all_gather(tokens, 'dp', axis=0, tiled=True)  96.8 us
    dot_general x3, matrix products, project_rows(): return jnp.dot(hidden, down_w, preferred_element_type=jnp.float32)  17 us
    gather x2, local copies, waits for them, and re-layouts, on_device(): picked = flat_out[jnp.where(live_pairs, slot_index, 0)]  11.9 us
    concatenate x1, local copies, waits for them, and re-layouts, on_device(): partial_value = jnp.concatenate(results, axis=1).astype(jnp.bfloat16)  11.4 us
    dot_general x3, matrix products, project_rows(): gate_act = jnp.dot(rows_in, gate_w, preferred_element_type=jnp.float32)  10.1 us
    reduce_sum x1, other arithmetic, on_device(): jnp.sum(returned.reshape(n_dp, n_ep, local_experts * capacity, feature).a...  7.65 us
    concatenate x1, other arithmetic, on_device(): partial_value = jnp.concatenate(results, axis=1).astype(jnp.bfloat16)  7.41 us
  transfers between devices with their start and end apart: 3, of which 2 were waited for; matrix products, arithmetic and copies ran while one was open for 10% of the time, Pallas kernels for 0%

commit v1 on v0

v1 whole, which is shorter than its diff:
```python
import functools

import jax
import jax.numpy as jnp
from jax import lax
from jax.experimental import pallas as pl
from jax.experimental.pallas import tpu as pltpu
from jax.sharding import PartitionSpec as P

CAP = 8
SEND_COLS = 1280
BACK_COLS = 1280


def shifted(x, shift, n_dp):
    return lax.ppermute(x, "dp", [(i, (i + shift) % n_dp) for i in range(n_dp)])


def dot_f32(a, b):
    return jnp.dot(a, b, preferred_element_type=jnp.float32)


def split_hi_lo(x):
    hi = x.astype(jnp.bfloat16)
    lo = (x - hi.astype(jnp.float32)).astype(jnp.bfloat16)
    return hi, lo


def expert_kernel(x0, x1, x2, x3, xb, wg, wu, wd, o0, o1, o2, o3, ob):
    dims = (((1,), (1,)), ((), ()))
    for j, (x, o) in enumerate(((x0, o0), (x1, o1), (x2, o2), (x3, o3))):
        cols = x.shape[-1]
        rows_d = x[0]
        rows_b = xb[0, j]

        def project(w):
            return lax.dot_general(
                rows_d, w[0, :, :cols], dims, preferred_element_type=jnp.float32
            ) + lax.dot_general(rows_b, w[0, :, cols:], dims, preferred_element_type=jnp.float32)

        gate = project(wg)
        up = project(wu)
        hidden = (gate / (1.0 + jnp.exp(-gate)) * up).astype(jnp.bfloat16)
        out = jnp.dot(hidden, wd[0], preferred_element_type=jnp.float32).astype(jnp.bfloat16)
        back = o.shape[-1]
        o[0] = out[:, :back]
        ob[0, j] = out[:, back:]


def run_experts(planes, xb, wg, wu, wd, back):
    members, rows, cols = planes[0].shape
    ffe, feature = wg.shape[1:]
    n = len(planes)
    one = lambda shape: pl.BlockSpec((1,) + shape, lambda m: (m,) + (0,) * len(shape))
    return pl.pallas_call(
        expert_kernel,
        grid=(members,),
        in_specs=[one((rows, cols))] * n
        + [one((n, rows, feature - cols))]
        + [one((ffe, feature))] * 3,
        out_specs=[one((rows, back))] * n + [one((n, rows, feature - back))],
        out_shape=[jax.ShapeDtypeStruct((members, rows, back), jnp.bfloat16)] * n
        + [jax.ShapeDtypeStruct((members, n, rows, feature - back), jnp.bfloat16)],
        compiler_params=pltpu.CompilerParams(vmem_limit_bytes=48 * 1024 * 1024),
        cost_estimate=pl.CostEstimate(
            flops=members * n * rows * ffe * feature * 6,
            bytes_accessed=members * (n * rows * feature * 4 + 3 * ffe * feature * 2),
            transcendentals=members * n * rows * ffe,
        ),
    )(*planes, xb, wg, wu, wd)


def on_device(
    tokens,
    row_counts,
    expert_ids,
    gate_weights,
    expert_gate,
    expert_up,
    expert_down,
    shared_gate,
    shared_up,
    shared_down,
):
    tok, feature = tokens.shape
    members = expert_gate.shape[0]
    n_ep = lax.axis_size("ep")
    n_dp = lax.axis_size("dp")
    n_experts = members * n_ep
    sc, bc = SEND_COLS, BACK_COLS

    live = jnp.arange(tok, dtype=jnp.int32) < row_counts[0]
    named = expert_ids[:, :, None] == jnp.arange(n_experts, dtype=jnp.int32)[None, None, :]
    gates = jnp.sum(
        jnp.where(named & live[:, None, None], gate_weights[:, :, None], 0.0), axis=1
    )
    hi, lo = split_hi_lo(gates)
    extended = jnp.concatenate([tokens, hi, lo], axis=1)

    around = [extended] + [shifted(extended, s, n_dp) for s in (1, -1, 2)]
    gathered = jnp.concatenate(around, axis=0)

    def slots_of(hi_cols, blocks):
        rows = blocks * tok
        used = hi_cols > 0
        at = jnp.arange(rows, dtype=jnp.int32)
        earlier = (at[:, None] > at[None, :]) & (at[:, None] // tok == at[None, :] // tok)
        rank = dot_f32(earlier.astype(jnp.bfloat16), used.astype(jnp.bfloat16))
        code = jnp.where(used, rank, -1.0).T.astype(jnp.int32)
        want = jnp.arange(CAP, dtype=jnp.int32)
        block = at // tok
        hit = (code[:, None, None, :] == want[None, None, :, None]) & (
            block[None, None, None, :] == jnp.arange(blocks, dtype=jnp.int32)[None, :, None, None]
        )
        return hit.reshape(n_experts * blocks * CAP, rows)

    hit_d = slots_of(hi, 1)
    send_d = dot_f32(hit_d.astype(jnp.bfloat16), tokens[:, :sc]).astype(jnp.bfloat16)
    came_d = lax.all_to_all(
        send_d.reshape(n_ep, members * CAP, sc), "ep", split_axis=0, concat_axis=0, tiled=True
    )
    own = (
        came_d.reshape(n_ep, members, CAP, sc)
        .transpose(1, 0, 2, 3)
        .reshape(members, n_ep * CAP, sc)
    )
    planes = [own] + [shifted(own, s, n_dp) for s in (1, -1, 2)]

    hit_b = slots_of(gathered[:, feature : feature + n_experts], n_dp)
    send_b = dot_f32(hit_b.astype(jnp.bfloat16), gathered[:, sc:feature]).astype(jnp.bfloat16)
    came_b = lax.all_to_all(
        send_b.reshape(n_ep, members * n_dp * CAP, feature - sc),
        "ep",
        split_axis=0,
        concat_axis=0,
        tiled=True,
    )
    xb = (
        came_b.reshape(n_ep, members, n_dp, CAP, feature - sc)
        .transpose(1, 2, 0, 3, 4)
        .reshape(members, n_dp, n_ep * CAP, feature - sc)
    )

    rows_in = gathered[:, :feature]
    gate_act = dot_f32(rows_in, shared_gate)
    up_act = dot_f32(rows_in, shared_up)
    hidden = (jax.nn.silu(gate_act) * up_act).astype(jnp.bfloat16)
    shared = dot_f32(hidden, shared_down)

    *out_d, out_b = run_experts(
        planes,
        xb,
        expert_gate.swapaxes(1, 2),
        expert_up.swapaxes(1, 2),
        expert_down,
        bc,
    )
    total_d = out_d[0].astype(jnp.float32)
    for j, s in ((1, -1), (2, 1), (3, 2)):
        total_d = total_d + shifted(out_d[j], s, n_dp).astype(jnp.float32)

    back_b = (
        out_b.reshape(members, n_dp, n_ep, CAP, feature - bc)
        .transpose(2, 0, 1, 3, 4)
        .reshape(n_ep, members * n_dp * CAP, feature - bc)
    )
    ret_b = lax.all_to_all(back_b, "ep", split_axis=0, concat_axis=0, tiled=True).reshape(
        n_experts * n_dp * CAP, feature - bc
    )

    def weigh(hit, hi_cols, lo_cols, blocks, values):
        rows = hit.shape[1]
        spread = lambda g: jnp.broadcast_to(
            g.T[:, None, :], (n_experts, blocks * CAP, rows)
        ).reshape(hit.shape)
        contract = (((0,), (0,)), ((), ()))
        zero = jnp.zeros((), jnp.bfloat16)
        parts = [
            lax.dot_general(
                jnp.where(hit, spread(g), zero), values, contract, preferred_element_type=jnp.float32
            )
            for g in (hi_cols, lo_cols)
        ]
        return parts[0] + parts[1]

    routed_b = weigh(
        hit_b,
        gathered[:, feature : feature + n_experts],
        gathered[:, feature + n_experts :],
        n_dp,
        ret_b,
    )
    partial_sum = jnp.concatenate(
        [shared[:, :bc], shared[:, bc:] + routed_b], axis=1
    ).astype(jnp.bfloat16)
    total = partial_sum[:tok].astype(jnp.float32)
    for j, s in ((1, -1), (2, 1), (3, 2)):
        total = total + shifted(partial_sum[j * tok : (j + 1) * tok], s, n_dp).astype(jnp.float32)

    back_d = (
        total_d.astype(jnp.bfloat16)
        .reshape(members, n_ep, CAP, bc)
        .transpose(1, 0, 2, 3)
        .reshape(n_ep, members * CAP, bc)
    )
    ret_d = lax.all_to_all(back_d, "ep", split_axis=0, concat_axis=0, tiled=True).reshape(
        n_experts * CAP, bc
    )
    routed_d = weigh(hit_d, hi, lo, 1, ret_d)
    result = total + jnp.concatenate(
        [routed_d, jnp.zeros((tok, feature - bc), jnp.float32)], axis=1
    )
    return jnp.where(live[:, None], result, 0.0).astype(jnp.bfloat16)


def solution(mesh):
    in_specs = (
        P(("dp", "ep"), None),
        P(("dp", "ep")),
        P(("dp", "ep"), None),
        P(("dp", "ep"), None),
        P("ep", None, "dp"),
        P("ep", None, "dp"),
        P("ep", "dp", None),
        P(None, "dp"),
        P(None, "dp"),
        P("dp", None),
    )
    out_specs = P(("dp", "ep"), None)
    return jax.shard_map(
        on_device, mesh=mesh, in_specs=in_specs, out_specs=out_specs, check_vma=False
    )
```

time: 335 us -> 289 us (0.86)
  blocking collectives: 110 us -> 0 us
  waiting for transfers between devices: 104 us -> 164 us
  starting transfers between devices: 6.32 us -> 43.3 us
  local copies, waits for them, and re-layouts: 43.6 us -> 24.4 us
  Pallas kernels: 0 us -> 18.7 us
  between operations: 14.4 us -> 1.15 us
  other arithmetic: 22.4 us -> 9.33 us
  matrix products: 32.4 us -> 27.2 us
    all_to_all x1 -> x0, blocking collectives: 110 us -> none  [on_device(): lax.all_to_all(copies, ('dp', 'ep'), split_axis=0, concat_axis=0, tiled=T...]
    all_gather x1 -> x0, waiting for transfers between devices: 96.8 us -> none  [on_device(): lax.all_gather(tokens, 'dp', axis=0, tiled=True)]
    ppermute x0 -> x12, waiting for transfers between devices: none -> 84.5 us  [shifted(): return lax.ppermute(x, 'dp', [(i, (i + shift) % n_dp) for i in range(n_dp)])]
    all_to_all x1 -> x4, waiting for transfers between devices: 0.01 us -> 79.1 us  [the longest x1 34.6 us: on_device(): lax.all_to_all(send_b.reshape(n_ep, members * n_dp * CAP, feature - sc),...]
    all_to_all x1 -> x4, starting transfers between devices: 6.24 us -> 27.9 us  [the longest x1 9.49 us: on_device(): lax.all_to_all(send_d.reshape(n_ep, members * CAP, sc), 'ep', split_axis=...]
    pallas_call x0 -> x1, Pallas kernels: none -> 18.7 us  [run_experts(): pl.pallas_call(expert_kernel, grid=(members,), in_specs=[one((rows, cols)...]
    ppermute x0 -> x12, starting transfers between devices: none -> 15.4 us  [shifted(): return lax.ppermute(x, 'dp', [(i, (i + shift) % n_dp) for i in range(n_dp)])]
    gather x3 -> x0, local copies, waits for them, and re-layouts: 15.2 us -> none  [the longest x2 11.9 us: on_device(): picked = flat_out[jnp.where(live_pairs, slot_index, 0)]]
  transfers between devices with their start and end apart: 3 -> 16, of which waited for: 2 -> 10; matrix products, arithmetic and copies ran while one was open for 10% -> 16% of each run, Pallas kernels for 0% -> 0%
where the time goes in v1:
time: 289 us; the launch traced here: 288 us
  waiting for transfers between devices  164 us (57%)
  starting transfers between devices  43.3 us (15%)
  matrix products  27.2 us (9%)
  local copies, waits for them, and re-layouts  24.4 us (8%)
  Pallas kernels  18.7 us (6%)
  other arithmetic  9.33 us (3%)
    ppermute x12, waiting for transfers between devices, shifted(): return lax.ppermute(x, 'dp', [(i, (i + shift) % n_dp) for i in range(n_dp)])  84.5 us
    all_to_all x1, waiting for transfers between devices, on_device(): lax.all_to_all(send_b.reshape(n_ep, members * n_dp * CAP, feature - sc),...  34.6 us
    all_to_all x1, waiting for transfers between devices, on_device(): lax.all_to_all(back_b, 'ep', split_axis=0, concat_axis=0, tiled=True)  21.7 us
    pallas_call x1, Pallas kernels, run_experts(): pl.pallas_call(expert_kernel, grid=(members,), in_specs=[one((rows, cols)...  18.7 us
    dot_general x6, matrix products, dot_f32(): return jnp.dot(a, b, preferred_element_type=jnp.float32)  16.6 us
    all_to_all x1, waiting for transfers between devices, on_device(): lax.all_to_all(back_d, 'ep', split_axis=0, concat_axis=0, tiled=True)  15.8 us
    ppermute x12, starting transfers between devices, shifted(): return lax.ppermute(x, 'dp', [(i, (i + shift) % n_dp) for i in range(n_dp)])  15.4 us
    dot_general x4, matrix products, weigh(): lax.dot_general(jnp.where(hit, spread(g), zero), values, contract, prefer...  10.6 us
  transfers between devices with their start and end apart: 16, of which 10 were waited for; matrix products, arithmetic and copies ran while one was open for 16% of the time, Pallas kernels for 0%

profile of v1, /device:TPU:1, one launch (start us, length us, event | category | flops | bytes accessed | tf_op | source)
XLA Modules:
  0.0 287.6 jit_solution(11000280512724096101)
XLA Ops:
  12.1 2.6 convolution_convert_fusion.1
  14.7 9.5 %all-to-all-start = ((bf16[32,16,1280]{2,1,0:T(8,128)(2,1)}), bf16[32,16,1280]{2,1,0:T(8,128)(2,1)}, u32[]{:S(2)}, u32[]{:S(2)}) async-start(bf16[32,16,1280]{2,1,0:T(8,128)(2,1)} %bitcast.79), calls=%async_computation | async-start | bytes 2621440 | tf_op jit(solution)/shard_map/all_to_all | solution.py:119
  34.4 2.7 convolution_convert_fusion
  37.2 6.9 %all-to-all-done = bf16[32,16,1280]{2,1,0:T(8,128)(2,1)} async-done(((bf16[32,16,1280]{2,1,0:T(8,128)(2,1)}), bf16[32,16,1280]{2,1,0:T(8,128)(2,1)}, u32[]{:S(2)}, u32[]{:S(2)}) %all-to-all-start) | async-done | bytes 1310752 | tf_op jit(solution)/shard_map/all_to_all | solution.py:119
  44.1 4.8 %all-to-all-start.1 = ((bf16[32,64,768]{2,1,0:T(8,128)(2,1)}), bf16[32,64,768]{2,1,0:T(8,128)(2,1)}, u32[]{:S(2)}, u32[]{:S(2)}) async-start(bf16[32,64,768]{2,1,0:T(8,128)(2,1)} %bitcast.78), calls=%async_computation.1 | async-start | bytes 6291456 | tf_op jit(solution)/shard_map/all_to_all | solution.py:131
  48.9 2.6 copy_bitcast_fusion.2.x0
  54.2 34.6 %all-to-all-done.1 = bf16[32,64,768]{2,1,0:T(8,128)(2,1)} async-done(((bf16[32,64,768]{2,1,0:T(8,128)(2,1)}), bf16[32,64,768]{2,1,0:T(8,128)(2,1)}, u32[]{:S(2)}, u32[]{:S(2)}) %all-to-all-start.1) | async-done | bytes 3145760 | tf_op jit(solution)/shard_map/all_to_all | solution.py:131
  88.8 3.8 %copy.77 = bf16[2,4,32,8,768]{4,3,2,1,0:T(8,128)(2,1)} copy(bf16[2,4,32,8,768]{4,3,1,0,2:T(8,128)(2,1)} %bitcast.15) | data formatting | bytes 6291456 | tf_op jit(solution)/shard_map/transpose | solution.py:140
  92.6 17.7 %collective-permute-done.5.x3 = bf16[2,256,1280]{2,1,0:T(8,128)(2,1)} collective-permute-done((bf16[2,256,1280]{2,1,0:T(8,128)(2,1)}, bf16[2,256,1280]{2,1,0:T(8,128)(2,1)}, u32[]{:S(2)}, u32[]{:S(2)}) %collective-permute-start.5) | collective-permute-done | bytes 1310752 | tf_op jit(solution)/shard_map/ppermute | solution.py:16
  110.3 18.7 %shard_map.100 = (bf16[2,256,1280]{2,1,0:T(8,128)(2,1)S(1)}, bf16[2,256,1280]{2,1,0:T(8,128)(2,1)S(1)}, bf16[2,256,1280]{2,1,0:T(8,128)(2,1)S(1)}, bf16[2,256,12...) custom-call(bf16[2,256,1280]{2,1,0:T(8,128)(2,1)} %copy_bitcast_fusion.2.x0, ...), custom_call_target="tpu_custom_call" | custom-call | flops 8858370048 | bytes 25427968 | tf_op jit(solution)/shard_map/pallas_call | solution.py:55
  132.7 26.0 %collective-permute-done.10 = bf16[2,256,1280]{2,1,0:T(8,128)(2,1)S(1)} collective-permute-done((bf16[2,256,1280]{2,1,0:T(8,128)(2,1)S(1)}, bf16[2,256,1280]{2,1,0:T(8,128)(2,1)S(1)}, u32[]{:S(2)}, u32[]{:S(2)}) %collective-permute-start.10) | collective-permute-done | bytes 1310752 | tf_op jit(solution)/shard_map/ppermute | solution.py:16
  158.7 27.7 %collective-permute-done.11 = bf16[2,256,1280]{2,1,0:T(8,128)(2,1)S(1)} collective-permute-done((bf16[2,256,1280]{2,1,0:T(8,128)(2,1)S(1)}, bf16[2,256,1280]{2,1,0:T(8,128)(2,1)S(1)}, u32[]{:S(2)}, u32[]{:S(2)}) %collective-permute-start.11) | collective-permute-done | bytes 1310752 | tf_op jit(solution)/shard_map/ppermute | solution.py:16
  190.3 8.8 %all-to-all-start.3 = ((bf16[32,16,1280]{2,1,0:T(8,128)(2,1)}), bf16[32,16,1280]{2,1,0:T(8,128)(2,1)}, u32[]{:S(2)}, u32[]{:S(2)}) async-start(bf16[32,16,1280]{2,1,0:T(8,128)(2,1)} %copy_bitcast_fusion.1), calls=%async_computation.3 | async-start | bytes 2621440 | tf_op jit(solution)/shard_map/all_to_all | solution.py:206
  199.1 4.0 %copy.68 = bf16[2,4,32,8,768]{4,3,1,0,2:T(8,128)(2,1)} copy(bf16[2,4,32,8,768]{4,3,2,1,0:T(8,128)(2,1)} %bitcast.80) | data formatting | bytes 6291456 | tf_op jit(solution)/shard_map/reshape | solution.py:163
  203.1 15.8 %all-to-all-done.3 = bf16[32,16,1280]{2,1,0:T(8,128)(2,1)} async-done(((bf16[32,16,1280]{2,1,0:T(8,128)(2,1)}), bf16[32,16,1280]{2,1,0:T(8,128)(2,1)}, u32[]{:S(2)}, u32[]{:S(2)}) %all-to-all-start.3) | async-done | bytes 1310752 | tf_op jit(solution)/shard_map/all_to_all | solution.py:206
  219.0 4.8 %all-to-all-start.2 = ((bf16[32,64,768]{2,1,0:T(8,128)(2,1)}), bf16[32,64,768]{2,1,0:T(8,128)(2,1)}, u32[]{:S(2)}, u32[]{:S(2)}) async-start(bf16[32,64,768]{2,1,0:T(8,128)(2,1)} %bitcast.77), calls=%async_computation.2 | async-start | bytes 6291456 | tf_op jit(solution)/shard_map/all_to_all | solution.py:167
  225.2 3.9 %fusion.9 = f32[256,704]{0,1:T(8,128)} fusion(bf16[2048,704]{0,1:T(8,128)(2,1)} %param.17, bf16[256,2176]{0,1:T(8,128)(2,1)} %copy-done.4), kind=kOutput, calls=%fused_computation.30 | convolution fusion | flops 738197504 | bytes 4653056 | tf_op jit(solution)/shard_map/dot_general | solution.py:20
  229.1 7.0 %fusion.13 = f32[256,2048]{1,0:T(8,128)} fusion(bf16[704,2048]{1,0:T(8,128)(2,1)S(1)} %copy-done, bf16[2048,704]{0,1:T(8,128)(2,1)} %param.18, bf16[256,2176]{0,1:T(8,128)(2,1)} %copy-done.4, f32[256,704]{0,1:T(8,128)} %fusion.9), kind=kOutput, calls=%fused_computation.33 | convolution fusion | flops 1477476352 | bytes 9633792 | tf_op jit(solution)/shard_map/dot_general | solution.py:20
  239.6 2.4 fusion.36
  242.0 21.7 %all-to-all-done.2 = bf16[32,64,768]{2,1,0:T(8,128)(2,1)} async-done(((bf16[32,64,768]{2,1,0:T(8,128)(2,1)}), bf16[32,64,768]{2,1,0:T(8,128)(2,1)}, u32[]{:S(2)}, u32[]{:S(2)}) %all-to-all-start.2) | async-done | bytes 3145760 | tf_op jit(solution)/shard_map/all_to_all | solution.py:167
  263.7 3.3 %fusion.68 = f32[256,768]{1,0:T(8,128)S(1)} fusion(bf16[2048,256]{1,0:T(8,128)(2,1)} %bitcast.84, bf16[2048,768]{1,0:T(8,128)(2,1)} %bitcast.22), kind=kOutput, calls=%fused_computation.109 | convolution fusion | flops 805306368 | bytes 4980736 | tf_op jit(solution)/shard_map/dot_general | solution.py:179
  267.0 3.1 %fusion.4 = bf16[256,768]{1,0:T(8,128)(2,1)S(1)} fusion(f32[256,768]{1,0:T(8,128)S(1)} %fusion.68, bf16[2048,256]{1,0:T(8,128)(2,1)S(1)} %bitcast.83, bf16[2048,768]{1,0:T(8,128)(2,1)} %bitcast.22, f32[256,2048]{1,0:T(8,128)} %fusion.13), kind=kOutput, calls=%fused_computation.18 | convolution fusion | flops 805896192 | bytes 6160384 | tf_op jit(solution)/shard_map/dot_general | solution.py:179
  275.7 2.9 %collective-permute-done.6 = bf16[64,2048]{1,0:T(8,128)(2,1)S(1)} collective-permute-done((bf16[64,2048]{1,0:T(8,128)(2,1)S(1)}, bf16[64,2048]{1,0:T(8,128)(2,1)S(1)}, u32[]{:S(2)}, u32[]{:S(2)}) %collective-permute-start.6) | collective-permute-done | bytes 262176 | tf_op jit(solution)/shard_map/ppermute | solution.py:16
  278.6 8.0 %collective-permute-done.7 = bf16[64,2048]{1,0:T(8,128)(2,1)S(1)} collective-permute-done((bf16[64,2048]{1,0:T(8,128)(2,1)S(1)}, bf16[64,2048]{1,0:T(8,128)(2,1)S(1)}, u32[]{:S(2)}, u32[]{:S(2)}) %collective-permute-start.7) | collective-permute-done | bytes 262176 | tf_op jit(solution)/shard_map/ppermute | solution.py:16
  (95 shorter events, 43.0 us)
Async XLA Ops:
  0.0 229.1 %copy-start = (bf16[704,2048]{1,0:T(8,128)(2,1)S(1)}, bf16[704,2048]{1,0:T(8,128)(2,1)}, u32[]{:S(2)}) copy-start(bf16[704,2048]{1,0:T(8,128)(2,1)} %param.19) | copy-start | bytes 8650756
  6.5 17.7 %collective-permute-start = (bf16[64,2176]{1,0:T(8,128)(2,1)}, bf16[64,2176]{1,0:T(8,128)(2,1)}, u32[]{:S(2)}, u32[]{:S(2)}) collective-permute-start(bf16[64,2176]{1,0:T(8,128)(2,1)} %copy.58), channel_id=1, source_target_pairs={{0,32},{32,64},{64,96},{96,0},{1,33},{33,65},{65,97},{97,1},{2,34}... | collective-permute-start | bytes 835592 | tf_op jit(solution)/shard_map/ppermute | solution.py:16
  8.7 17.6 %collective-permute-start.1 = (bf16[64,2176]{1,0:T(8,128)(2,1)}, bf16[64,2176]{1,0:T(8,128)(2,1)}, u32[]{:S(2)}, u32[]{:S(2)}) collective-permute-start(bf16[64,2176]{1,0:T(8,128)(2,1)} %copy.58), channel_id=1, source_target_pairs={{0,96},{32,0},{64,32},{96,64},{1,97},{33,1},{65,33},{97,65},{2,98}... | collective-permute-start | bytes 835592 | tf_op jit(solution)/shard_map/ppermute | solution.py:16
  10.1 18.2 %collective-permute-start.2 = (bf16[64,2176]{1,0:T(8,128)(2,1)}, bf16[64,2176]{1,0:T(8,128)(2,1)}, u32[]{:S(2)}, u32[]{:S(2)}) collective-permute-start(bf16[64,2176]{1,0:T(8,128)(2,1)} %copy.58), channel_id=1, source_target_pairs={{0,64},{32,96},{64,0},{96,32},{1,65},{33,97},{65,1},{97,33},{2,66}... | collective-permute-start | bytes 835592 | tf_op jit(solution)/shard_map/ppermute | solution.py:16
  11.8 3.0 %copy-start.17 = (pred[64]{0:T(512)(128)(4,1)}, pred[64]{0:T(512)(128)(4,1)S(1)}, u32[]{:S(2)}) copy-start(pred[64]{0:T(512)(128)(4,1)S(1)} %broadcast_compare_fusion) | copy-start | bytes 196
  12.0 2.7 copy-start.9
  14.7 29.4 %all-to-all-start = ((bf16[32,16,1280]{2,1,0:T(8,128)(2,1)}), bf16[32,16,1280]{2,1,0:T(8,128)(2,1)}, u32[]{:S(2)}, u32[]{:S(2)}) async-start(bf16[32,16,1280]{2,1,0:T(8,128)(2,1)} %bitcast.79), calls=%async_computation | async-start | bytes 2621440 | tf_op jit(solution)/shard_map/all_to_all | solution.py:119
  44.1 44.7 %all-to-all-start.1 = ((bf16[32,64,768]{2,1,0:T(8,128)(2,1)}), bf16[32,64,768]{2,1,0:T(8,128)(2,1)}, u32[]{:S(2)}, u32[]{:S(2)}) async-start(bf16[32,64,768]{2,1,0:T(8,128)(2,1)} %bitcast.78), calls=%async_computation.1 | async-start | bytes 6291456 | tf_op jit(solution)/shard_map/all_to_all | solution.py:131
  51.4 41.2 %collective-permute-start.3 = (bf16[2,256,1280]{2,1,0:T(8,128)(2,1)}, bf16[2,256,1280]{2,1,0:T(8,128)(2,1)}, u32[]{:S(2)}, u32[]{:S(2)}) collective-permute-start(bf16[2,256,1280]{2,1,0:T(8,128)(2,1)} %copy_bitcast_fusion.2.x0), channel_id=1, source_target_pairs={{0,32},{32,64},{64,96},{96,0},{1,33},{33,65},{65,97},{97,1},{2,34}... | collective-permute-start | bytes 3932168 | tf_op jit(solution)/shard_map/ppermute | solution.py:16
  51.8 40.8 %collective-permute-start.4 = (bf16[2,256,1280]{2,1,0:T(8,128)(2,1)}, bf16[2,256,1280]{2,1,0:T(8,128)(2,1)}, u32[]{:S(2)}, u32[]{:S(2)}) collective-permute-start(bf16[2,256,1280]{2,1,0:T(8,128)(2,1)} %copy_bitcast_fusion.2.x0), channel_id=1, source_target_pairs={{0,96},{32,0},{64,32},{96,64},{1,97},{33,1},{65,33},{97,65},{2,98}... | collective-permute-start | bytes 3932168 | tf_op jit(solution)/shard_map/ppermute | solution.py:16
  54.1 56.2 %collective-permute-start.5 = (bf16[2,256,1280]{2,1,0:T(8,128)(2,1)}, bf16[2,256,1280]{2,1,0:T(8,128)(2,1)}, u32[]{:S(2)}, u32[]{:S(2)}) collective-permute-start(bf16[2,256,1280]{2,1,0:T(8,128)(2,1)} %copy_bitcast_fusion.2.x0), channel_id=1, source_target_pairs={{0,64},{32,96},{64,0},{96,32},{1,65},{33,97},{65,1},{97,33},{2,66}... | collective-permute-start | bytes 3932168 | tf_op jit(solution)/shard_map/ppermute | solution.py:16
  129.0 29.7 %collective-permute-start.10 = (bf16[2,256,1280]{2,1,0:T(8,128)(2,1)S(1)}, bf16[2,256,1280]{2,1,0:T(8,128)(2,1)S(1)}, u32[]{:S(2)}, u32[]{:S(2)}) collective-permute-start(bf16[2,256,1280]{2,1,0:T(8,128)(2,1)S(1)} %get-tuple-element.13), channel_id=1, source_target_pairs={{0,32},{32,64},{64,96},{96,0},{1,33},{33,65},{65,97},{97,1},{2,34}... | collective-permute-start | bytes 3932168 | tf_op jit(solution)/shard_map/ppermute | solution.py:16
  130.3 56.1 %collective-permute-start.11 = (bf16[2,256,1280]{2,1,0:T(8,128)(2,1)S(1)}, bf16[2,256,1280]{2,1,0:T(8,128)(2,1)S(1)}, u32[]{:S(2)}, u32[]{:S(2)}) collective-permute-start(bf16[2,256,1280]{2,1,0:T(8,128)(2,1)S(1)} %get-tuple-element.14), channel_id=1, source_target_pairs={{0,64},{32,96},{64,0},{96,32},{1,65},{33,97},{65,1},{97,33},{2,66}... | collective-permute-start | bytes 3932168 | tf_op jit(solution)/shard_map/ppermute | solution.py:16
  132.1 56.4 %collective-permute-start.9 = (bf16[2,256,1280]{2,1,0:T(8,128)(2,1)S(1)}, bf16[2,256,1280]{2,1,0:T(8,128)(2,1)S(1)}, u32[]{:S(2)}, u32[]{:S(2)}) collective-permute-start(bf16[2,256,1280]{2,1,0:T(8,128)(2,1)S(1)} %get-tuple-element.12), channel_id=1, source_target_pairs={{0,96},{32,0},{64,32},{96,64},{1,97},{33,1},{65,33},{97,65},{2,98}... | collective-permute-start | bytes 3932168 | tf_op jit(solution)/shard_map/ppermute | solution.py:16
  190.3 28.7 %all-to-all-start.3 = ((bf16[32,16,1280]{2,1,0:T(8,128)(2,1)}), bf16[32,16,1280]{2,1,0:T(8,128)(2,1)}, u32[]{:S(2)}, u32[]{:S(2)}) async-start(bf16[32,16,1280]{2,1,0:T(8,128)(2,1)} %copy_bitcast_fusion.1), calls=%async_computation.3 | async-start | bytes 2621440 | tf_op jit(solution)/shard_map/all_to_all | solution.py:206
  219.0 44.7 %all-to-all-start.2 = ((bf16[32,64,768]{2,1,0:T(8,128)(2,1)}), bf16[32,64,768]{2,1,0:T(8,128)(2,1)}, u32[]{:S(2)}, u32[]{:S(2)}) async-start(bf16[32,64,768]{2,1,0:T(8,128)(2,1)} %bitcast.77), calls=%async_computation.2 | async-start | bytes 6291456 | tf_op jit(solution)/shard_map/all_to_all | solution.py:167
  263.7 3.3 %copy-start.8 = (bf16[64,32,256]{2,1,0:T(8,128)(2,1)S(1)}, bf16[64,32,256]{2,1,0:T(8,128)(2,1)}, u32[]{:S(2)}) copy-start(bf16[64,32,256]{2,1,0:T(8,128)(2,1)} %get-tuple-element.24) | copy-start | bytes 3145732
  270.2 3.8 %copy-start.5 = (f32[64,1280]{1,0:T(8,128)S(1)}, f32[64,1280]{1,0:T(8,128)}, u32[]{:S(2)}) copy-start(f32[64,1280]{1,0:T(8,128)} %fusion.36) | copy-start | bytes 983044
  270.2 3.8 %copy-start.11 = (s32[64,64]{1,0:T(8,128)S(1)}, s32[64,64]{1,0:T(8,128)}, u32[]{:S(2)}) copy-start(s32[64,64]{1,0:T(8,128)} %copy-done.9) | copy-start | bytes 49156
  270.2 3.8 %copy-start.19 = (pred[64]{0:T(512)(128)(4,1)S(1)}, pred[64]{0:T(512)(128)(4,1)}, u32[]{:S(2)}) copy-start(pred[64]{0:T(512)(128)(4,1)} %copy-done.17) | copy-start | bytes 196
  270.3 16.4 %copy-start.21 = (pred[64]{0:T(512)(128)(4,1)S(1)}, pred[64]{0:T(512)(128)(4,1)}, u32[]{:S(2)}) copy-start(pred[64]{0:T(512)(128)(4,1)} %copy-done.20) | copy-start | bytes 196
  270.3 8.3 %collective-permute-start.6 = (bf16[64,2048]{1,0:T(8,128)(2,1)S(1)}, bf16[64,2048]{1,0:T(8,128)(2,1)S(1)}, u32[]{:S(2)}, u32[]{:S(2)}) collective-permute-start(bf16[64,2048]{1,0:T(8,128)(2,1)S(1)} %get-tuple-element.21), channel_id=1, source_target_pairs={{0,96},{32,0},{64,32},{96,64},{1,97},{33,1},{65,33},{97,65},{2,98}... | collective-permute-start | bytes 786440 | tf_op jit(solution)/shard_map/ppermute | solution.py:16
  272.7 13.9 %collective-permute-start.7 = (bf16[64,2048]{1,0:T(8,128)(2,1)S(1)}, bf16[64,2048]{1,0:T(8,128)(2,1)S(1)}, u32[]{:S(2)}, u32[]{:S(2)}) collective-permute-start(bf16[64,2048]{1,0:T(8,128)(2,1)S(1)} %get-tuple-element.23), channel_id=1, source_target_pairs={{0,32},{32,64},{64,96},{96,0},{1,33},{33,65},{65,97},{97,1},{2,34}... | collective-permute-start | bytes 786440 | tf_op jit(solution)/shard_map/ppermute | solution.py:16
  272.7 13.9 %collective-permute-start.8 = (bf16[64,2048]{1,0:T(8,128)(2,1)S(1)}, bf16[64,2048]{1,0:T(8,128)(2,1)S(1)}, u32[]{:S(2)}, u32[]{:S(2)}) collective-permute-start(bf16[64,2048]{1,0:T(8,128)(2,1)S(1)} %get-tuple-element.22), channel_id=1, source_target_pairs={{0,64},{32,96},{64,0},{96,32},{1,65},{33,97},{65,1},{97,33},{2,66}... | collective-permute-start | bytes 786440 | tf_op jit(solution)/shard_map/ppermute | solution.py:16
  (14 other events, 23.1 us)

commit v2 on v1

v2 whole, which is shorter than its diff:
```python
import jax
import jax.numpy as jnp
from jax import lax
from jax.experimental import pallas as pl
from jax.experimental.pallas import tpu as pltpu
from jax.sharding import PartitionSpec as P

CAP = 8
SEND_COLS = 1152
BACK_COLS = 1152
AROUND = (1, -1, 2)
VMEM_LIMIT = 48 * 1024 * 1024


def shifted(x, shift):
    n = lax.axis_size("dp")
    return lax.ppermute(x, "dp", [(i, (i + shift) % n) for i in range(n)])


def dot_f32(a, b):
    return jnp.dot(a, b, preferred_element_type=jnp.float32)


def split_hi_lo(x):
    hi = x.astype(jnp.bfloat16)
    lo = (x - hi.astype(jnp.float32)).astype(jnp.bfloat16)
    return hi, lo


def slot_codes(used):
    tok = used.shape[1]
    before = lax.broadcasted_iota(jnp.int32, (tok, tok), 0) < lax.broadcasted_iota(
        jnp.int32, (tok, tok), 1
    )
    ones = jnp.where(used, 1.0, 0.0)
    rank = dot_f32(
        ones.astype(jnp.bfloat16), jnp.where(before, 1.0, 0.0).astype(jnp.bfloat16)
    )
    return jnp.where(used, rank, -1.0)


def prepare_own(count, ids, weights, tokens, extended, send, hi_out, lo_out):
    top, tok = ids.shape
    feature = tokens.shape[1]
    n_experts = hi_out.shape[0] // CAP
    expert = lax.broadcasted_iota(jnp.int32, (n_experts, tok), 0)
    gates = jnp.zeros((n_experts, tok), jnp.float32)
    for k in range(top):
        gates = gates + jnp.where(expert == ids[k : k + 1, :], weights[k : k + 1, :], 0.0)
    live = lax.broadcasted_iota(jnp.int32, (n_experts, tok), 1) < count[0]
    gates = jnp.where(live, gates, 0.0)
    hi, lo = split_hi_lo(gates)
    code = slot_codes(gates > 0)
    want = lax.broadcasted_iota(jnp.int32, (n_experts, CAP, tok), 1).astype(jnp.float32)
    hit = code[:, None, :] == want
    shape = (n_experts * CAP, tok)
    one_hot = jnp.where(hit, 1.0, 0.0).reshape(shape).astype(jnp.bfloat16)
    spread = lambda g: jnp.where(hit, g.astype(jnp.float32)[:, None, :], 0.0).reshape(shape)
    hi_out[...] = spread(hi).astype(jnp.bfloat16)
    lo_out[...] = spread(lo).astype(jnp.bfloat16)
    extended[:, :feature] = tokens[...]
    extended[:, feature:] = jnp.concatenate(
        [hi.astype(jnp.float32), lo.astype(jnp.float32)], axis=1
    ).astype(jnp.bfloat16)
    step = 128
    for c in range(0, send.shape[1], step):
        send[:, c : c + step] = dot_f32(one_hot, tokens[:, c : c + step]).astype(jnp.bfloat16)


def prepare_ring(e0, e1, e2, e3, send, hi_out, lo_out, rows_out):
    tok, width = e0.shape
    feature = rows_out.shape[1]
    blocks = 4
    n_experts = hi_out.shape[0] // (blocks * CAP)
    first = feature - send.shape[1]
    parts = []
    his = []
    los = []
    for j, e in enumerate((e0, e1, e2, e3)):
        rows_out[j * tok : (j + 1) * tok, :] = e[:, :feature]
        meta = e[:, feature:].astype(jnp.float32)
        hi = meta[:, :tok]
        his.append(hi)
        los.append(meta[:, tok:])
        parts.append(slot_codes(hi > 0))
    code = jnp.concatenate(parts, axis=1)
    hi = jnp.concatenate(his, axis=1)
    lo = jnp.concatenate(los, axis=1)
    rows = blocks * tok
    chunk = 16
    shape = (chunk, blocks * CAP, rows)
    slot = lax.broadcasted_iota(jnp.int32, shape, 1)
    at = lax.broadcasted_iota(jnp.int32, shape, 2)
    want = jnp.where(at // tok == slot // CAP, slot % CAP, -2).astype(jnp.float32)
    flat = chunk * blocks * CAP
    for c in range(0, n_experts, chunk):
        hit = code[c : c + chunk, None, :] == want
        out = slice(c * blocks * CAP, c * blocks * CAP + flat)
        one_hot = jnp.where(hit, 1.0, 0.0).reshape(flat, rows).astype(jnp.bfloat16)
        spread = lambda g: (
            jnp.where(hit, g[c : c + chunk, None, :], 0.0).reshape(flat, rows).astype(jnp.bfloat16)
        )
        hi_out[out, :] = spread(hi)
        lo_out[out, :] = spread(lo)
        send[out, :] = dot_f32(one_hot, rows_out[:, first:]).astype(jnp.bfloat16)


def in_vmem(n):
    return [pl.BlockSpec(memory_space=pltpu.VMEM)] * n


def call_prepare_own(count, ids, weights, tokens, n_experts, cols):
    tok, feature = tokens.shape
    slots = n_experts * CAP
    return pl.pallas_call(
        prepare_own,
        in_specs=[pl.BlockSpec(memory_space=pltpu.SMEM)] + in_vmem(3),
        out_specs=in_vmem(4),
        out_shape=[
            jax.ShapeDtypeStruct((tok, feature + 2 * tok), jnp.bfloat16),
            jax.ShapeDtypeStruct((slots, cols), jnp.bfloat16),
            jax.ShapeDtypeStruct((slots, tok), jnp.bfloat16),
            jax.ShapeDtypeStruct((slots, tok), jnp.bfloat16),
        ],
        compiler_params=pltpu.CompilerParams(vmem_limit_bytes=VMEM_LIMIT),
        name="prepare_own",
    )(count, ids, weights, tokens)


def call_prepare_ring(around, n_experts, feature, cols):
    tok = around[0].shape[0]
    rows = len(around) * tok
    slots = n_experts * CAP * len(around)
    return pl.pallas_call(
        prepare_ring,
        in_specs=in_vmem(4),
        out_specs=in_vmem(4),
        out_shape=[
            jax.ShapeDtypeStruct((slots, cols), jnp.bfloat16),
            jax.ShapeDtypeStruct((slots, rows), jnp.bfloat16),
            jax.ShapeDtypeStruct((slots, rows), jnp.bfloat16),
            jax.ShapeDtypeStruct((rows, feature), jnp.bfloat16),
        ],
        compiler_params=pltpu.CompilerParams(vmem_limit_bytes=VMEM_LIMIT),
        name="prepare_ring",
    )(*around)


def expert_kernel(x0, x1, x2, x3, xb, wg, wu, wd, o0, o1, o2, o3, ob):
    dims = (((1,), (1,)), ((), ()))
    for j, (x, o) in enumerate(((x0, o0), (x1, o1), (x2, o2), (x3, o3))):
        cols = x.shape[-1]
        rows_d = x[0]
        rows_b = xb[0, j]

        def project(w):
            return lax.dot_general(
                rows_d, w[0, :, :cols], dims, preferred_element_type=jnp.float32
            ) + lax.dot_general(rows_b, w[0, :, cols:], dims, preferred_element_type=jnp.float32)

        gate = project(wg)
        up = project(wu)
        hidden = (gate / (1.0 + jnp.exp(-gate)) * up).astype(jnp.bfloat16)
        out = jnp.dot(hidden, wd[0], preferred_element_type=jnp.float32).astype(jnp.bfloat16)
        back = o.shape[-1]
        o[0] = out[:, :back]
        ob[0, j] = out[:, back:]


def run_experts(planes, xb, wg, wu, wd, back):
    members, rows, cols = planes[0].shape
    ffe, feature = wg.shape[1:]
    n = len(planes)
    one = lambda shape: pl.BlockSpec((1,) + shape, lambda m: (m,) + (0,) * len(shape))
    return pl.pallas_call(
        expert_kernel,
        grid=(members,),
        in_specs=[one((rows, cols))] * n
        + [one((n, rows, feature - cols))]
        + [one((ffe, feature))] * 3,
        out_specs=[one((rows, back))] * n + [one((n, rows, feature - back))],
        out_shape=[jax.ShapeDtypeStruct((members, rows, back), jnp.bfloat16)] * n
        + [jax.ShapeDtypeStruct((members, n, rows, feature - back), jnp.bfloat16)],
        compiler_params=pltpu.CompilerParams(vmem_limit_bytes=VMEM_LIMIT),
        cost_estimate=pl.CostEstimate(
            flops=members * n * rows * ffe * feature * 6,
            bytes_accessed=members * (n * rows * feature * 4 + 3 * ffe * feature * 2),
            transcendentals=members * n * rows * ffe,
        ),
        name="experts",
    )(*planes, xb, wg, wu, wd)


def weigh(hi, lo, values):
    contract = (((0,), (0,)), ((), ()))
    return lax.dot_general(
        hi, values, contract, preferred_element_type=jnp.float32
    ) + lax.dot_general(lo, values, contract, preferred_element_type=jnp.float32)


def on_device(
    tokens,
    row_counts,
    expert_ids,
    gate_weights,
    expert_gate,
    expert_up,
    expert_down,
    shared_gate,
    shared_up,
    shared_down,
):
    tok, feature = tokens.shape
    members = expert_gate.shape[0]
    n_ep = lax.axis_size("ep")
    n_dp = lax.axis_size("dp")
    n_experts = members * n_ep
    sc, bc = SEND_COLS, BACK_COLS

    def over_ep(x, rows, cols):
        return lax.all_to_all(
            x.reshape(n_ep, rows, cols), "ep", split_axis=0, concat_axis=0, tiled=True
        )

    extended, send_d, hi_d, lo_d = call_prepare_own(
        row_counts, expert_ids.T, gate_weights.T, tokens, n_experts, sc
    )
    came_d = over_ep(send_d, members * CAP, sc)

    around = [extended] + [shifted(extended, s) for s in AROUND]
    send_b, hi_b, lo_b, gathered = call_prepare_ring(around, n_experts, feature, feature - sc)

    own = (
        came_d.reshape(n_ep, members, CAP, sc)
        .transpose(1, 0, 2, 3)
        .reshape(members, n_ep * CAP, sc)
    )
    planes = [own] + [shifted(own, s) for s in AROUND]
    came_b = over_ep(send_b, members * n_dp * CAP, feature - sc)
    xb = (
        came_b.reshape(n_ep, members, n_dp, CAP, feature - sc)
        .transpose(1, 2, 0, 3, 4)
        .reshape(members, n_dp, n_ep * CAP, feature - sc)
    )

    gate_act = dot_f32(gathered, shared_gate)
    up_act = dot_f32(gathered, shared_up)
    hidden = (jax.nn.silu(gate_act) * up_act).astype(jnp.bfloat16)
    shared = dot_f32(hidden, shared_down)
    planes[0], shared = lax.optimization_barrier((planes[0], shared))

    *out_d, out_b = run_experts(
        planes,
        xb,
        expert_gate.swapaxes(1, 2),
        expert_up.swapaxes(1, 2),
        expert_down,
        bc,
    )
    back_b = out_b.reshape(members, n_dp, n_ep, CAP, feature - bc).transpose(2, 0, 1, 3, 4)
    ret_b = over_ep(back_b, members * n_dp * CAP, feature - bc)

    total_d = out_d[0].astype(jnp.float32)
    for j, s in enumerate(AROUND):
        total_d = total_d + shifted(out_d[j + 1], -s).astype(jnp.float32)
    back_d = (
        total_d.astype(jnp.bfloat16).reshape(members, n_ep, CAP, bc).transpose(1, 0, 2, 3)
    )
    back_d, ret_b = lax.optimization_barrier((back_d, ret_b))
    ret_d = over_ep(back_d, members * CAP, bc)

    routed_b = weigh(hi_b, lo_b, ret_b.reshape(-1, feature - bc))
    partial_sum = jnp.concatenate(
        [shared[:, :bc], shared[:, bc:] + routed_b], axis=1
    ).astype(jnp.bfloat16)
    total = partial_sum[:tok].astype(jnp.float32)
    for j, s in enumerate(AROUND):
        part = partial_sum[(j + 1) * tok : (j + 2) * tok]
        total = total + shifted(part, -s).astype(jnp.float32)

    routed_d = weigh(hi_d, lo_d, ret_d.reshape(-1, bc))
    result = total + jnp.concatenate(
        [routed_d, jnp.zeros((tok, feature - bc), jnp.float32)], axis=1
    )
    live = jnp.arange(tok, dtype=jnp.int32) < row_counts[0]
    return jnp.where(live[:, None], result, 0.0).astype(jnp.bfloat16)


def solution(mesh):
    in_specs = (
        P(("dp", "ep"), None),
        P(("dp", "ep")),
        P(("dp", "ep"), None),
        P(("dp", "ep"), None),
        P("ep", None, "dp"),
        P("ep", None, "dp"),
        P("ep", "dp", None),
        P(None, "dp"),
        P(None, "dp"),
        P("dp", None),
    )
    out_specs = P(("dp", "ep"), None)
    return jax.shard_map(
        on_device, mesh=mesh, in_specs=in_specs, out_specs=out_specs, check_vma=False
    )
```

time: 289 us -> 230 us (0.80)
  waiting for transfers between devices: 164 us -> 109 us
  matrix products: 27.2 us -> 21.4 us
  starting transfers between devices: 43.3 us -> 48.6 us
  Pallas kernels: 18.7 us -> 23.9 us
  other arithmetic: 9.33 us -> 4.64 us
  local copies, waits for them, and re-layouts: 24.4 us -> 20.3 us
    all_to_all x4, waiting for transfers between devices: 79.1 us -> 36.2 us  [over_ep(): lax.all_to_all(x.reshape(n_ep, rows, cols), 'ep', split_axis=0, concat_ax...]
    ppermute x12, waiting for transfers between devices: 84.5 us -> 73 us  [shifted(): return lax.ppermute(x, 'dp', [(i, (i + shift) % n) for i in range(n)])]
    all_to_all x4, starting transfers between devices: 27.9 us -> 34.7 us  [over_ep(): lax.all_to_all(x.reshape(n_ep, rows, cols), 'ep', split_axis=0, concat_ax...]
    ppermute x3 -> x0, local copies, waits for them, and re-layouts: 6.02 us -> none  [shifted(): return lax.ppermute(x, 'dp', [(i, (i + shift) % n_dp) for i in range(n_dp)])]
    dot_general x6 -> x2, matrix products: 16.6 us -> 10.8 us  [dot_f32(): return jnp.dot(a, b, preferred_element_type=jnp.float32)]
    pallas_call x0 -> x2, Pallas kernels: none -> 4.12 us  [the longest x1 3.48 us: call_prepare_ring(): pl.pallas_call(prepare_ring, in_specs=in_vmem(4), out_specs=in_vmem(4), o...]
    unnamed x45 -> x40, local copies, waits for them, and re-layouts: 2.93 us -> 6.38 us
  transfers between devices with their start and end apart: 16 -> 16, of which waited for: 10 -> 11; matrix products, arithmetic and copies ran while one was open for 16% -> 14% of each run, Pallas kernels for 0% -> 2%
where the time goes in v2:
time: 230 us; the launch traced here: 229 us
  waiting for transfers between devices  109 us (47%)
  starting transfers between devices  48.6 us (21%)
  Pallas kernels  23.9 us (10%)
  matrix products  21.4 us (9%)
  local copies, waits for them, and re-layouts  20.3 us (9%)
  other arithmetic  4.64 us (2%)
    ppermute x12, waiting for transfers between devices, shifted(): return lax.ppermute(x, 'dp', [(i, (i + shift) % n) for i in range(n)])  73 us
    all_to_all x4, waiting for transfers between devices, over_ep(): lax.all_to_all(x.reshape(n_ep, rows, cols), 'ep', split_axis=0, concat_ax...  36.2 us
    all_to_all x4, starting transfers between devices, over_ep(): lax.all_to_all(x.reshape(n_ep, rows, cols), 'ep', split_axis=0, concat_ax...  34.7 us
    pallas_call x1, Pallas kernels, run_experts(): pl.pallas_call(expert_kernel, grid=(members,), in_specs=[one((rows, cols)...  19.8 us
    ppermute x12, starting transfers between devices, shifted(): return lax.ppermute(x, 'dp', [(i, (i + shift) % n) for i in range(n)])  14 us
    dot_general x2, matrix products, dot_f32(): return jnp.dot(a, b, preferred_element_type=jnp.float32)  10.8 us
    unnamed x40, local copies, waits for them, and re-layouts  6.38 us
    reshape x1, local copies, waits for them, and re-layouts, on_device(): out_b.reshape(members, n_dp, n_ep, CAP, feature - bc)  5.67 us
  transfers between devices with their start and end apart: 16, of which 11 were waited for; matrix products, arithmetic and copies ran while one was open for 14% of the time, Pallas kernels for 2%

profile of v2, /device:TPU:1, one launch (start us, length us, event | category | flops | bytes accessed | tf_op | source)
XLA Modules:
  0.0 229.2 jit_solution(9681850015843586021)
XLA Ops:
  4.9 9.5 %all-to-all-start = ((bf16[32,16,1152]{2,1,0:T(8,128)(2,1)}), bf16[32,16,1152]{2,1,0:T(8,128)(2,1)}, u32[]{:S(2)}, u32[]{:S(2)}) async-start(bf16[32,16,1152]{2,1,0:T(8,128)(2,1)} %bitcast.46), calls=%async_computation | async-start | bytes 2359296 | tf_op jit(solution)/shard_map/all_to_all | solution.py:221
  14.3 3.0 %collective-permute-start.2 = (bf16[64,2176]{1,0:T(8,128)(2,1)S(1)}, bf16[64,2176]{1,0:T(8,128)(2,1)S(1)}, u32[]{:S(2)}, u32[]{:S(2)}) collective-permute-start(bf16[64,2176]{1,0:T(8,128)(2,1)S(1)} %get-tuple-element.23.e0), channel_id=1, source_target_pairs={{0,64},{32,96},{64,0},{96,32},{1,65},{33,97},{65,1},{97,33},{2,66}... | collective-permute-start | bytes 835592 | tf_op jit(solution)/shard_map/ppermute | solution.py:17
  18.8 5.2 %collective-permute-done.2.e3 = bf16[64,2176]{1,0:T(8,128)(2,1)S(1)} collective-permute-done((bf16[64,2176]{1,0:T(8,128)(2,1)S(1)}, bf16[64,2176]{1,0:T(8,128)(2,1)S(1)}, u32[]{:S(2)}, u32[]{:S(2)}) %collective-permute-start.2) | collective-permute-done | bytes 278560 | tf_op jit(solution)/shard_map/ppermute | solution.py:17
  24.0 6.3 %collective-permute-done.1.e2 = bf16[64,2176]{1,0:T(8,128)(2,1)S(1)} collective-permute-done((bf16[64,2176]{1,0:T(8,128)(2,1)S(1)}, bf16[64,2176]{1,0:T(8,128)(2,1)S(1)}, u32[]{:S(2)}, u32[]{:S(2)}) %collective-permute-start.1) | collective-permute-done | bytes 278560 | tf_op jit(solution)/shard_map/ppermute | solution.py:17
  30.6 3.5 %prepare_ring.1 = (bf16[2048,896]{1,0:T(8,128)(2,1)}, bf16[2048,256]{1,0:T(8,128)(2,1)S(1)}, bf16[2048,256]{1,0:T(8,128)(2,1)S(1)}, bf16[256,2048]{1,0:T(8,128)(2,1)S(1)}) custom-call(bf16[64,2176]{1,0:T(8,128)(2,1)S(1)} %get-tuple-element.23.e0, bf16[64,2176]{1,0:T(8,128)(2,1)S(1)} %collective-permute-done.e1, ...), custom_call_target="tpu_custom_call" | custom-call | tf_op jit(solution)/shard_map/prepare_ring/pallas_call | solution.py:134
  37.0 7.8 %all-to-all-start.1 = ((bf16[32,64,896]{2,1,0:T(8,128)(2,1)}), bf16[32,64,896]{2,1,0:T(8,128)(2,1)}, u32[]{:S(2)}, u32[]{:S(2)}) async-start(bf16[32,64,896]{2,1,0:T(8,128)(2,1)} %bitcast.50), calls=%async_computation.1 | async-start | bytes 7340032 | tf_op jit(solution)/shard_map/all_to_all | solution.py:221
  44.9 2.4 %copy_bitcast_fusion.2.x0 = bf16[2,256,1152]{2,1,0:T(8,128)(2,1)} fusion(bf16[32,16,1152]{2,1,0:T(8,128)(2,1)} %all-to-all-done), kind=kLoop, calls=%fused_computation.15 | loop fusion | bytes 2359296 | tf_op jit(solution)/shard_map/reshape | solution.py:236
  47.3 2.5 %collective-permute-start.5 = (bf16[2,256,1152]{2,1,0:T(8,128)(2,1)}, bf16[2,256,1152]{2,1,0:T(8,128)(2,1)}, u32[]{:S(2)}, u32[]{:S(2)}) collective-permute-start(bf16[2,256,1152]{2,1,0:T(8,128)(2,1)} %copy_bitcast_fusion.2.x0), channel_id=1, source_target_pairs={{0,64},{32,96},{64,0},{96,32},{1,65},{33,97},{65,1},{97,33},{2,66}... | collective-permute-start | bytes 3538952 | tf_op jit(solution)/shard_map/ppermute | solution.py:17
  51.3 3.8 %fusion.11 = f32[256,704]{0,1:T(8,128)} fusion(bf16[256,2048]{1,0:T(8,128)(2,1)S(1)} %copy-done.15, bf16[2048,704]{0,1:T(8,128)(2,1)} %param.17), kind=kOutput, calls=%fused_computation.27 | convolution fusion | flops 738197504 | bytes 4653056 | tf_op jit(solution)/shard_map/dot_general | solution.py:21
  55.1 7.0 %fusion.3 = f32[256,2048]{1,0:T(8,128)} fusion(bf16[704,2048]{1,0:T(8,128)(2,1)S(1)} %copy-done, f32[256,704]{0,1:T(8,128)} %fusion.11, bf16[256,2048]{1,0:T(8,128)(2,1)} %copy-done.14, bf16[2048,704]{0,1:T(8,128)(2,1)} %param.18), kind=kOutput, calls=%fused_computation.18 | convolution fusion | flops 1477476352 | bytes 9633792 | tf_op jit(solution)/shard_map/dot_general | solution.py:21
  62.1 28.8 %all-to-all-done.1 = bf16[32,64,896]{2,1,0:T(8,128)(2,1)} async-done(((bf16[32,64,896]{2,1,0:T(8,128)(2,1)}), bf16[32,64,896]{2,1,0:T(8,128)(2,1)}, u32[]{:S(2)}, u32[]{:S(2)}) %all-to-all-start.1) | async-done | bytes 3670048 | tf_op jit(solution)/shard_map/all_to_all | solution.py:221
  90.9 4.4 %copy.18 = bf16[2,4,32,8,896]{4,3,2,1,0:T(8,128)(2,1)} copy(bf16[2,4,32,8,896]{4,3,1,0,2:T(8,128)(2,1)} %bitcast.9) | data formatting | bytes 7340032 | tf_op jit(solution)/shard_map/transpose | solution.py:242
  95.3 6.4 %collective-permute-done.4.x2 = bf16[2,256,1152]{2,1,0:T(8,128)(2,1)} collective-permute-done((bf16[2,256,1152]{2,1,0:T(8,128)(2,1)}, bf16[2,256,1152]{2,1,0:T(8,128)(2,1)}, u32[]{:S(2)}, u32[]{:S(2)}) %collective-permute-start.4) | collective-permute-done | bytes 1179680 | tf_op jit(solution)/shard_map/ppermute | solution.py:17
  102.3 19.8 %experts.1 = (bf16[2,256,1152]{2,1,0:T(8,128)(2,1)S(1)}, bf16[2,256,1152]{2,1,0:T(8,128)(2,1)S(1)}, bf16[2,256,1152]{2,1,0:T(8,128)(2,1)S(1)}, bf16[2,256,1152]{2,1,0:T(8,128)(2,1)S(1)}, bf16[2,4,256,896]{3,2,1,0:T(8,128)(2,1)}) custom-call(bf16[2,256,1152]{2,1,0:T(8,128)(2,1)} %copy_bitcast_fusion.2.x0, bf16[2,256,1152]{2,1,0:T(8,128)(2,1)} %collective-permute-done.3.x1, ...), custom_call_target="tpu_custom_call" | custom-call | flops 8858370048 | bytes 25427968 | tf_op jit(solution)/shard_map/experts/pallas_call | solution.py:175
  122.2 5.7 %copy.14 = bf16[2,4,32,8,896]{4,3,1,0,2:T(8,128)(2,1)} copy(bf16[2,4,32,8,896]{4,3,2,1,0:T(8,128)(2,1)} %bitcast.52) | data formatting | bytes 7340032 | tf_op jit(solution)/shard_map/reshape | solution.py:260
  127.8 7.7 %all-to-all-start.2 = ((bf16[32,64,896]{2,1,0:T(8,128)(2,1)}), bf16[32,64,896]{2,1,0:T(8,128)(2,1)}, u32[]{:S(2)}, u32[]{:S(2)}) async-start(bf16[32,64,896]{2,1,0:T(8,128)(2,1)} %bitcast.49), calls=%async_computation.2 | async-start | bytes 7340032 | tf_op jit(solution)/shard_map/all_to_all | solution.py:221
  139.6 24.3 %collective-permute-done.6 = bf16[2,256,1152]{2,1,0:T(8,128)(2,1)S(1)} collective-permute-done((bf16[2,256,1152]{2,1,0:T(8,128)(2,1)}, bf16[2,256,1152]{2,1,0:T(8,128)(2,1)S(1)}, u32[]{:S(2)}, u32[]{:S(2)}) %collective-permute-start.6) | collective-permute-done | bytes 1179680 | tf_op jit(solution)/shard_map/ppermute | solution.py:17
  163.9 3.5 %collective-permute-done.7 = bf16[2,256,1152]{2,1,0:T(8,128)(2,1)S(1)} collective-permute-done((bf16[2,256,1152]{2,1,0:T(8,128)(2,1)}, bf16[2,256,1152]{2,1,0:T(8,128)(2,1)S(1)}, u32[]{:S(2)}, u32[]{:S(2)}) %collective-permute-start.7) | collective-permute-done | bytes 1179680 | tf_op jit(solution)/shard_map/ppermute | solution.py:17
  167.5 23.2 %collective-permute-done.8 = bf16[2,256,1152]{2,1,0:T(8,128)(2,1)S(1)} collective-permute-done((bf16[2,256,1152]{2,1,0:T(8,128)(2,1)S(1)}, bf16[2,256,1152]{2,1,0:T(8,128)(2,1)S(1)}, u32[]{:S(2)}, u32[]{:S(2)}) %collective-permute-start.8) | collective-permute-done | bytes 1179680 | tf_op jit(solution)/shard_map/ppermute | solution.py:17
  192.4 9.6 %all-to-all-start.3 = ((bf16[32,16,1152]{2,1,0:T(8,128)(2,1)}), bf16[32,16,1152]{2,1,0:T(8,128)(2,1)}, u32[]{:S(2)}, u32[]{:S(2)}) async-start(bf16[32,16,1152]{2,1,0:T(8,128)(2,1)} %bitcast.19), calls=%async_computation.3 | async-start | bytes 2359296 | tf_op jit(solution)/shard_map/all_to_all | solution.py:221
  203.4 3.5 %fusion.12 = f32[256,896]{1,0:T(8,128)S(1)} fusion(bf16[2048,256]{1,0:T(8,128)(2,1)S(1)} %copy-done.13, bf16[2048,896]{1,0:T(8,128)(2,1)} %bitcast.18), kind=kOutput, calls=%fused_computation.28 | convolution fusion | flops 939524096 | bytes 5636096 | tf_op jit(solution)/shard_map/dot_general | solution.py:198
  207.0 3.6 %fusion.1 = bf16[256,896]{1,0:T(8,128)(2,1)S(1)} fusion(f32[256,896]{1,0:T(8,128)S(1)} %fusion.12, bf16[2048,256]{1,0:T(8,128)(2,1)S(1)} %copy-done.11, bf16[2048,896]{1,0:T(8,128)(2,1)} %bitcast.18, f32[256,2048]{1,0:T(8,128)} %fusion.3), kind=kOutput, calls=%fused_computation.8 | convolution fusion | flops 940212224 | bytes 7012352 | tf_op jit(solution)/shard_map/dot_general | solution.py:196
  213.0 7.5 %all-to-all-done.3 = bf16[32,16,1152]{2,1,0:T(8,128)(2,1)} async-done(((bf16[32,16,1152]{2,1,0:T(8,128)(2,1)}), bf16[32,16,1152]{2,1,0:T(8,128)(2,1)}, u32[]{:S(2)}, u32[]{:S(2)}) %all-to-all-start.3) | async-done | bytes 1179680 | tf_op jit(solution)/shard_map/all_to_all | solution.py:221
  223.9 3.3 %collective-permute-done.10 = bf16[64,2048]{1,0:T(8,128)(2,1)} collective-permute-done((bf16[64,2048]{1,0:T(8,128)(2,1)S(1)}, bf16[64,2048]{1,0:T(8,128)(2,1)}, u32[]{:S(2)}, u32[]{:S(2)}) %collective-permute-start.10) | collective-permute-done | bytes 262176 | tf_op jit(solution)/shard_map/ppermute | solution.py:17
  (65 shorter events, 25.8 us)
Async XLA Ops:
  0.0 55.1 %copy-start = (bf16[704,2048]{1,0:T(8,128)(2,1)S(1)}, bf16[704,2048]{1,0:T(8,128)(2,1)}, u32[]{:S(2)}) copy-start(bf16[704,2048]{1,0:T(8,128)(2,1)} %param.19) | copy-start | bytes 8650756
  4.9 32.1 %all-to-all-start = ((bf16[32,16,1152]{2,1,0:T(8,128)(2,1)}), bf16[32,16,1152]{2,1,0:T(8,128)(2,1)}, u32[]{:S(2)}, u32[]{:S(2)}) async-start(bf16[32,16,1152]{2,1,0:T(8,128)(2,1)} %bitcast.46), calls=%async_computation | async-start | bytes 2359296 | tf_op jit(solution)/shard_map/all_to_all | solution.py:221
  14.3 9.7 %collective-permute-start.2 = (bf16[64,2176]{1,0:T(8,128)(2,1)S(1)}, bf16[64,2176]{1,0:T(8,128)(2,1)S(1)}, u32[]{:S(2)}, u32[]{:S(2)}) collective-permute-start(bf16[64,2176]{1,0:T(8,128)(2,1)S(1)} %get-tuple-element.23.e0), channel_id=1, source_target_pairs={{0,64},{32,96},{64,0},{96,32},{1,65},{33,97},{65,1},{97,33},{2,66}... | collective-permute-start | bytes 835592 | tf_op jit(solution)/shard_map/ppermute | solution.py:17
  17.3 13.0 %collective-permute-start.1 = (bf16[64,2176]{1,0:T(8,128)(2,1)S(1)}, bf16[64,2176]{1,0:T(8,128)(2,1)S(1)}, u32[]{:S(2)}, u32[]{:S(2)}) collective-permute-start(bf16[64,2176]{1,0:T(8,128)(2,1)S(1)} %get-tuple-element.23.e0), channel_id=1, source_target_pairs={{0,96},{32,0},{64,32},{96,64},{1,97},{33,1},{65,33},{97,65},{2,98}... | collective-permute-start | bytes 835592 | tf_op jit(solution)/shard_map/ppermute | solution.py:17
  18.1 12.5 %collective-permute-start = (bf16[64,2176]{1,0:T(8,128)(2,1)S(1)}, bf16[64,2176]{1,0:T(8,128)(2,1)S(1)}, u32[]{:S(2)}, u32[]{:S(2)}) collective-permute-start(bf16[64,2176]{1,0:T(8,128)(2,1)S(1)} %get-tuple-element.23.e0), channel_id=1, source_target_pairs={{0,32},{32,64},{64,96},{96,0},{1,33},{33,65},{65,97},{97,1},{2,34}... | collective-permute-start | bytes 835592 | tf_op jit(solution)/shard_map/ppermute | solution.py:17
  37.0 53.9 %all-to-all-start.1 = ((bf16[32,64,896]{2,1,0:T(8,128)(2,1)}), bf16[32,64,896]{2,1,0:T(8,128)(2,1)}, u32[]{:S(2)}, u32[]{:S(2)}) async-start(bf16[32,64,896]{2,1,0:T(8,128)(2,1)} %bitcast.50), calls=%async_computation.1 | async-start | bytes 7340032 | tf_op jit(solution)/shard_map/all_to_all | solution.py:221
  44.9 6.5 %copy-start.15 = (bf16[256,2048]{1,0:T(8,128)(2,1)S(1)}, bf16[256,2048]{1,0:T(8,128)(2,1)}, u32[]{:S(2)}) copy-start(bf16[256,2048]{1,0:T(8,128)(2,1)} %copy-done.14) | copy-start | bytes 3145732
  47.3 48.0 %collective-permute-start.5 = (bf16[2,256,1152]{2,1,0:T(8,128)(2,1)}, bf16[2,256,1152]{2,1,0:T(8,128)(2,1)}, u32[]{:S(2)}, u32[]{:S(2)}) collective-permute-start(bf16[2,256,1152]{2,1,0:T(8,128)(2,1)} %copy_bitcast_fusion.2.x0), channel_id=1, source_target_pairs={{0,64},{32,96},{64,0},{96,32},{1,65},{33,97},{65,1},{97,33},{2,66}... | collective-permute-start | bytes 3538952 | tf_op jit(solution)/shard_map/ppermute | solution.py:17
  49.9 51.8 %collective-permute-start.4 = (bf16[2,256,1152]{2,1,0:T(8,128)(2,1)}, bf16[2,256,1152]{2,1,0:T(8,128)(2,1)}, u32[]{:S(2)}, u32[]{:S(2)}) collective-permute-start(bf16[2,256,1152]{2,1,0:T(8,128)(2,1)} %copy_bitcast_fusion.2.x0), channel_id=1, source_target_pairs={{0,96},{32,0},{64,32},{96,64},{1,97},{33,1},{65,33},{97,65},{2,98}... | collective-permute-start | bytes 3538952 | tf_op jit(solution)/shard_map/ppermute | solution.py:17
  50.8 51.5 %collective-permute-start.3 = (bf16[2,256,1152]{2,1,0:T(8,128)(2,1)}, bf16[2,256,1152]{2,1,0:T(8,128)(2,1)}, u32[]{:S(2)}, u32[]{:S(2)}) collective-permute-start(bf16[2,256,1152]{2,1,0:T(8,128)(2,1)} %copy_bitcast_fusion.2.x0), channel_id=1, source_target_pairs={{0,32},{32,64},{64,96},{96,0},{1,33},{33,65},{65,97},{97,1},{2,34}... | collective-permute-start | bytes 3538952 | tf_op jit(solution)/shard_map/ppermute | solution.py:17
  127.8 10.1 %copy-start.7 = (bf16[2,256,1152]{2,1,0:T(8,128)(2,1)S(1)}, bf16[2,256,1152]{2,1,0:T(8,128)(2,1)}, u32[]{:S(2)}) copy-start(bf16[2,256,1152]{2,1,0:T(8,128)(2,1)} %copy-done.6) | copy-start | bytes 3538948
  127.8 64.5 %all-to-all-start.2 = ((bf16[32,64,896]{2,1,0:T(8,128)(2,1)}), bf16[32,64,896]{2,1,0:T(8,128)(2,1)}, u32[]{:S(2)}, u32[]{:S(2)}) async-start(bf16[32,64,896]{2,1,0:T(8,128)(2,1)} %bitcast.49), calls=%async_computation.2 | async-start | bytes 7340032 | tf_op jit(solution)/shard_map/all_to_all | solution.py:221
  135.6 28.4 %collective-permute-start.6 = (bf16[2,256,1152]{2,1,0:T(8,128)(2,1)}, bf16[2,256,1152]{2,1,0:T(8,128)(2,1)S(1)}, u32[]{:S(2)}, u32[]{:S(2)}) collective-permute-start(bf16[2,256,1152]{2,1,0:T(8,128)(2,1)} %copy-done.9), channel_id=1, source_target_pairs={{0,96},{32,0},{64,32},{96,64},{1,97},{33,1},{65,33},{97,65},{2,98}... | collective-permute-start | bytes 3538952 | tf_op jit(solution)/shard_map/ppermute | solution.py:17
  138.0 29.5 %collective-permute-start.7 = (bf16[2,256,1152]{2,1,0:T(8,128)(2,1)}, bf16[2,256,1152]{2,1,0:T(8,128)(2,1)S(1)}, u32[]{:S(2)}, u32[]{:S(2)}) collective-permute-start(bf16[2,256,1152]{2,1,0:T(8,128)(2,1)} %copy-done.8), channel_id=1, source_target_pairs={{0,32},{32,64},{64,96},{96,0},{1,33},{33,65},{65,97},{97,1},{2,34}... | collective-permute-start | bytes 3538952 | tf_op jit(solution)/shard_map/ppermute | solution.py:17
  138.0 52.7 %collective-permute-start.8 = (bf16[2,256,1152]{2,1,0:T(8,128)(2,1)S(1)}, bf16[2,256,1152]{2,1,0:T(8,128)(2,1)S(1)}, u32[]{:S(2)}, u32[]{:S(2)}) collective-permute-start(bf16[2,256,1152]{2,1,0:T(8,128)(2,1)S(1)} %copy-done.7), channel_id=1, source_target_pairs={{0,64},{32,96},{64,0},{96,32},{1,65},{33,97},{65,1},{97,33},{2,66}... | collective-permute-start | bytes 3538952 | tf_op jit(solution)/shard_map/ppermute | solution.py:17
  192.4 11.0 %copy-start.13 = (bf16[2048,256]{1,0:T(8,128)(2,1)S(1)}, bf16[2048,256]{1,0:T(8,128)(2,1)}, u32[]{:S(2)}) copy-start(bf16[2048,256]{1,0:T(8,128)(2,1)} %copy-done.12) | copy-start | bytes 3145732
  192.4 28.1 %all-to-all-start.3 = ((bf16[32,16,1152]{2,1,0:T(8,128)(2,1)}), bf16[32,16,1152]{2,1,0:T(8,128)(2,1)}, u32[]{:S(2)}, u32[]{:S(2)}) async-start(bf16[32,16,1152]{2,1,0:T(8,128)(2,1)} %bitcast.19), calls=%async_computation.3 | async-start | bytes 2359296 | tf_op jit(solution)/shard_map/all_to_all | solution.py:221
  203.4 7.2 %copy-start.16 = (bf16[256,1152]{1,0:T(8,128)(2,1)}, bf16[256,1152]{1,0:T(8,128)(2,1)S(1)}, u32[]{:S(2)}) copy-start(bf16[256,1152]{1,0:T(8,128)(2,1)S(1)} %slice.54) | copy-start | bytes 1769476
  211.5 12.4 %collective-permute-start.9 = (bf16[64,2048]{1,0:T(8,128)(2,1)}, bf16[64,2048]{1,0:T(8,128)(2,1)}, u32[]{:S(2)}, u32[]{:S(2)}) collective-permute-start(bf16[64,2048]{1,0:T(8,128)(2,1)} %get-tuple-element.39), channel_id=1, source_target_pairs={{0,96},{32,0},{64,32},{96,64},{1,97},{33,1},{65,33},{97,65},{2,98}... | collective-permute-start | bytes 786440 | tf_op jit(solution)/shard_map/ppermute | solution.py:17
  211.5 12.4 %collective-permute-start.11 = (bf16[64,2048]{1,0:T(8,128)(2,1)}, bf16[64,2048]{1,0:T(8,128)(2,1)}, u32[]{:S(2)}, u32[]{:S(2)}) collective-permute-start(bf16[64,2048]{1,0:T(8,128)(2,1)} %get-tuple-element.40), channel_id=1, source_target_pairs={{0,64},{32,96},{64,0},{96,32},{1,65},{33,97},{65,1},{97,33},{2,66}... | collective-permute-start | bytes 786440 | tf_op jit(solution)/shard_map/ppermute | solution.py:17
  211.8 15.4 %collective-permute-start.10 = (bf16[64,2048]{1,0:T(8,128)(2,1)S(1)}, bf16[64,2048]{1,0:T(8,128)(2,1)}, u32[]{:S(2)}, u32[]{:S(2)}) collective-permute-start(bf16[64,2048]{1,0:T(8,128)(2,1)S(1)} %get-tuple-element.41), channel_id=1, source_target_pairs={{0,32},{32,64},{64,96},{96,0},{1,33},{33,65},{65,97},{97,1},{2,34}... | collective-permute-start | bytes 786440 | tf_op jit(solution)/shard_map/ppermute | solution.py:17
  220.4 6.7 %copy-start.17 = (bf16[256,1152]{1,0:T(8,128)(2,1)S(1)}, bf16[256,1152]{1,0:T(8,128)(2,1)}, u32[]{:S(2)}) copy-start(bf16[256,1152]{1,0:T(8,128)(2,1)} %copy-done.16) | copy-start | bytes 1769476
  220.4 6.7 %copy-start.19 = (bf16[256,896]{1,0:T(8,128)(2,1)S(1)}, bf16[256,896]{1,0:T(8,128)(2,1)}, u32[]{:S(2)}) copy-start(bf16[256,896]{1,0:T(8,128)(2,1)} %copy-done.18) | copy-start | bytes 1376260
  222.1 7.0 %copy-start.1 = (bf16[704,2048]{1,0:T(8,128)(2,1)S(1)}, bf16[704,2048]{1,0:T(8,128)(2,1)}, u32[]{:S(2)}) copy-start(bf16[704,2048]{1,0:T(8,128)(2,1)} %param.19) | copy-start | bytes 8650756
  (12 other events, 29.4 us)

commit v3 on v2

--- a/solution.py
+++ b/solution.py
@@ -1,3 +1,5 @@
+import functools
+
 import jax
 import jax.numpy as jnp
 from jax import lax
@@ -6,9 +8,12 @@
 from jax.sharding import PartitionSpec as P
 
 CAP = 8
-SEND_COLS = 1152
-BACK_COLS = 1152
-AROUND = (1, -1, 2)
+SEND_COLS = 1280
+BACK_COLS = 1280
+COLS = 128
+NT = (((1,), (1,)), ((), ()))
+TN = (((0,), (0,)), ((), ()))
+AROUND = (2, 1, -1)
 VMEM_LIMIT = 48 * 1024 * 1024
 
 
@@ -146,56 +151,107 @@
     )(*around)
 
 
-def expert_kernel(x0, x1, x2, x3, xb, wg, wu, wd, o0, o1, o2, o3, ob):
-    dims = (((1,), (1,)), ((), ()))
-    for j, (x, o) in enumerate(((x0, o0), (x1, o1), (x2, o2), (x3, o3))):
-        cols = x.shape[-1]
-        rows_d = x[0]
-        rows_b = xb[0, j]
-
-        def project(w):
-            return lax.dot_general(
-                rows_d, w[0, :, :cols], dims, preferred_element_type=jnp.float32
-            ) + lax.dot_general(rows_b, w[0, :, cols:], dims, preferred_element_type=jnp.float32)
-
-        gate = project(wg)
-        up = project(wu)
-        hidden = (gate / (1.0 + jnp.exp(-gate)) * up).astype(jnp.bfloat16)
-        out = jnp.dot(hidden, wd[0], preferred_element_type=jnp.float32).astype(jnp.bfloat16)
-        back = o.shape[-1]
-        o[0] = out[:, :back]
-        ob[0, j] = out[:, back:]
-
-
-def run_experts(planes, xb, wg, wu, wd, back):
-    members, rows, cols = planes[0].shape
-    ffe, feature = wg.shape[1:]
-    n = len(planes)
+def expert_kernel(splits, *refs):
+    n_x = sum(len(s) for s in splits)
+    xin, (xb, wg, wu, wd) = refs[:n_x], refs[n_x : n_x + 4]
+    rest = refs[n_x + 4 :]
+    rest = rest[len(rest) - (n_x + 3) :]
+    outs, (ob, xs, keep) = rest[:n_x], rest[n_x:]
+    member = pl.program_id(0)
+    sc, bc = xin[0].shape[-1], outs[0].shape[-1]
+    feature = wg.shape[2]
+    n_ep, slots = xb.shape[:2]
+    rows = n_ep * CAP
+    planes = len(splits)
+    at = 0
+    place = []
+    for p, split in enumerate(splits):
+        row = p * rows
+        for n in split:
+            place.append((xin[at], outs[at], row, n))
+            row += n * CAP
+            at += 1
+    for x, _, row, n in place:
+        for c in range(0, sc, COLS):
+            part = x[:, :, c : c + COLS].astype(jnp.float32).reshape(n, 2, CAP, COLS)
+            part = jnp.where(member == 0, part[:, 0], part[:, 1])
+            xs[row : row + n * CAP, c : c + COLS] = part.reshape(n * CAP, COLS).astype(jnp.bfloat16)
+    for c in range(0, feature - sc, COLS):
+        part = xb[:, :, c : c + COLS].astype(jnp.float32).reshape(n_ep, planes, CAP, COLS)
+        for p in range(planes):
+            xs[p * rows : (p + 1) * rows, sc + c : sc + c + COLS] = (
+                part[:, p].reshape(rows, COLS).astype(jnp.bfloat16)
+            )
+    gate = lax.dot_general(wg[0], xs[...], NT, preferred_element_type=jnp.float32)
+    up = lax.dot_general(wu[0], xs[...], NT, preferred_element_type=jnp.float32)
+    hidden = (gate / (1.0 + jnp.exp(-gate)) * up).astype(jnp.bfloat16)
+    out = lax.dot_general(hidden, wd[0], TN, preferred_element_type=jnp.float32)
+    for c in range(0, feature - bc, COLS):
+        part = out[:, bc + c : bc + c + COLS].reshape(planes, n_ep, CAP, COLS)
+        part = jnp.stack([part[p] for p in range(planes)], axis=1)
+        ob[:, :, c : c + COLS] = part.reshape(n_ep, slots, COLS).astype(jnp.bfloat16)
+
+    @pl.when(member == 0)
+    def _():
+        keep[...] = out[:, :bc]
+
+    @pl.when(member == 1)
+    def _():
+        for _, o, row, n in place:
+            for c in range(0, bc, COLS):
+                parts = [
+                    keep[row : row + n * CAP, c : c + COLS].reshape(n, CAP, COLS),
+                    out[row : row + n * CAP, c : c + COLS].reshape(n, CAP, COLS),
+                ]
+                o[:, :, c : c + COLS] = (
+                    jnp.stack(parts, axis=1).reshape(n, 2 * CAP, COLS).astype(jnp.bfloat16)
+                )
+
+
+def run_experts(planes, pair, xb, sofar, wg, wu, wd, back):
+    members, ffe, feature = wg.shape
+    xin = [x for plane in planes for x in plane]
+    splits = tuple(tuple(x.shape[0] for x in plane) for plane in planes)
+    n_ep, slots, cols_b = xb.shape
+    step = len(planes) * CAP
+    pairs = slots // (members * step)
+    rows = len(planes) * n_ep * CAP
+    whole = lambda shape: pl.BlockSpec(shape, lambda m: (0,) * len(shape))
     one = lambda shape: pl.BlockSpec((1,) + shape, lambda m: (m,) + (0,) * len(shape))
+    slot = lambda cols: pl.BlockSpec((n_ep, step, cols), lambda m: (0, m * pairs + pair, 0))
+    out_x = [jax.ShapeDtypeStruct(x.shape[:2] + (back,), jnp.bfloat16) for x in xin]
+    operands = [*xin, xb, wg, wu, wd]
+    in_specs = [whole(x.shape) for x in xin] + [slot(cols_b)] + [one((ffe, feature))] * 3
+    aliases = {}
+    if sofar is not None:
+        aliases = {len(operands): len(xin)}
+        operands.append(sofar)
+        in_specs.append(pl.BlockSpec(memory_space=pl.ANY))
     return pl.pallas_call(
-        expert_kernel,
+        functools.partial(expert_kernel, splits),
         grid=(members,),
-        in_specs=[one((rows, cols))] * n
-        + [one((n, rows, feature - cols))]
-        + [one((ffe, feature))] * 3,
-        out_specs=[one((rows, back))] * n + [one((n, rows, feature - back))],
-        out_shape=[jax.ShapeDtypeStruct((members, rows, back), jnp.bfloat16)] * n
-        + [jax.ShapeDtypeStruct((members, n, rows, feature - back), jnp.bfloat16)],
+        in_specs=in_specs,
+        out_specs=[whole(x.shape) for x in out_x] + [slot(feature - back)],
+        out_shape=out_x + [jax.ShapeDtypeStruct((n_ep, slots, feature - back), jnp.bfloat16)],
+        scratch_shapes=[
+            pltpu.VMEM((rows, feature), jnp.bfloat16),
+            pltpu.VMEM((rows, back), jnp.float32),
+        ],
+        input_output_aliases=aliases,
         compiler_params=pltpu.CompilerParams(vmem_limit_bytes=VMEM_LIMIT),
         cost_estimate=pl.CostEstimate(
-            flops=members * n * rows * ffe * feature * 6,
-            bytes_accessed=members * (n * rows * feature * 4 + 3 * ffe * feature * 2),
-            transcendentals=members * n * rows * ffe,
+            flops=members * rows * ffe * feature * 6,
+            bytes_accessed=members * (rows * feature * 4 + 3 * ffe * feature * 2),
+            transcendentals=members * rows * ffe,
         ),
         name="experts",
-    )(*planes, xb, wg, wu, wd)
+    )(*operands)
 
 
 def weigh(hi, lo, values):
-    contract = (((0,), (0,)), ((), ()))
-    return lax.dot_general(
-        hi, values, contract, preferred_element_type=jnp.float32
-    ) + lax.dot_general(lo, values, contract, preferred_element_type=jnp.float32)
+    return lax.dot_general(hi, values, TN, preferred_element_type=jnp.float32) + lax.dot_general(
+        lo, values, TN, preferred_element_type=jnp.float32
+    )
 
 
 def on_device(
@@ -225,47 +281,38 @@
     extended, send_d, hi_d, lo_d = call_prepare_own(
         row_counts, expert_ids.T, gate_weights.T, tokens, n_experts, sc
     )
-    came_d = over_ep(send_d, members * CAP, sc)
-
-    around = [extended] + [shifted(extended, s) for s in AROUND]
+    own = over_ep(send_d, members * CAP, sc)
+
+    around = [shifted(extended, s) for s in AROUND] + [extended]
     send_b, hi_b, lo_b, gathered = call_prepare_ring(around, n_experts, feature, feature - sc)
 
-    own = (
-        came_d.reshape(n_ep, members, CAP, sc)
-        .transpose(1, 0, 2, 3)
-        .reshape(members, n_ep * CAP, sc)
-    )
-    planes = [own] + [shifted(own, s) for s in AROUND]
+    half = n_ep // 2
+    below, above = shifted(own, 1), shifted(own, -1)
+    far = [shifted(below[:half], 1), shifted(above[half:], -1)]
     came_b = over_ep(send_b, members * n_dp * CAP, feature - sc)
-    xb = (
-        came_b.reshape(n_ep, members, n_dp, CAP, feature - sc)
-        .transpose(1, 2, 0, 3, 4)
-        .reshape(members, n_dp, n_ep * CAP, feature - sc)
-    )
 
     gate_act = dot_f32(gathered, shared_gate)
     up_act = dot_f32(gathered, shared_up)
     hidden = (jax.nn.silu(gate_act) * up_act).astype(jnp.bfloat16)
     shared = dot_f32(hidden, shared_down)
-    planes[0], shared = lax.optimization_barrier((planes[0], shared))
-
-    *out_d, out_b = run_experts(
-        planes,
-        xb,
-        expert_gate.swapaxes(1, 2),
-        expert_up.swapaxes(1, 2),
-        expert_down,
-        bc,
-    )
-    back_b = out_b.reshape(members, n_dp, n_ep, CAP, feature - bc).transpose(2, 0, 1, 3, 4)
-    ret_b = over_ep(back_b, members * n_dp * CAP, feature - bc)
-
-    total_d = out_d[0].astype(jnp.float32)
-    for j, s in enumerate(AROUND):
-        total_d = total_d + shifted(out_d[j + 1], -s).astype(jnp.float32)
+    came_b, shared = lax.optimization_barrier((came_b, shared))
+
+    weights = (expert_gate.swapaxes(1, 2), expert_up.swapaxes(1, 2), expert_down)
+    far_0, far_1, to_below, out_b = run_experts([far, [below]], 0, came_b, None, *weights, bc)
+    to_above, total_d, out_b = run_experts([[above], [own]], 1, came_b, out_b, *weights, bc)
+    ret_b = over_ep(out_b, members * n_dp * CAP, feature - bc)
+
+    f32 = lambda x: x.astype(jnp.float32)
+    from_below, from_above = shifted(far_0, 1), shifted(far_1, -1)
+    to_above = jnp.concatenate(
+        [(f32(to_above[:half]) + f32(from_below)).astype(jnp.bfloat16), to_above[half:]]
+    )
+    to_below = jnp.concatenate(
+        [to_below[:half], (f32(to_below[half:]) + f32(from_above)).astype(jnp.bfloat16)]
+    )
     back_d = (
-        total_d.astype(jnp.bfloat16).reshape(members, n_ep, CAP, bc).transpose(1, 0, 2, 3)
-    )
+        f32(total_d) + f32(shifted(to_above, 1)) + f32(shifted(to_below, -1))
+    ).astype(jnp.bfloat16)
     back_d, ret_b = lax.optimization_barrier((back_d, ret_b))
     ret_d = over_ep(back_d, members * CAP, bc)
 
@@ -273,9 +320,9 @@
     partial_sum = jnp.concatenate(
         [shared[:, :bc], shared[:, bc:] + routed_b], axis=1
     ).astype(jnp.bfloat16)
-    total = partial_sum[:tok].astype(jnp.float32)
+    total = partial_sum[len(AROUND) * tok :].astype(jnp.float32)
     for j, s in enumerate(AROUND):
-        part = partial_sum[(j + 1) * tok : (j + 2) * tok]
+        part = partial_sum[j * tok : (j + 1) * tok]
         total = total + shifted(part, -s).astype(jnp.float32)
 
     routed_d = weigh(hi_d, lo_d, ret_d.reshape(-1, bc))

time: 230 us -> 209 us (0.909)
  waiting for transfers between devices: 109 us -> 82.4 us
  starting transfers between devices: 48.6 us -> 55.6 us
  local copies, waits for them, and re-layouts: 20.3 us -> 16.2 us
  other arithmetic: 4.64 us -> 7.38 us
    all_to_all x4, waiting for transfers between devices: 36.2 us -> 11 us  [over_ep(): lax.all_to_all(x.reshape(n_ep, rows, cols), 'ep', split_axis=0, concat_ax...]
    reshape x2 -> x0, local copies, waits for them, and re-layouts: 8.12 us -> none  [the longest x1 5.67 us: on_device(): out_b.reshape(members, n_dp, n_ep, CAP, feature - bc)]
    ppermute x12 -> x14, starting transfers between devices: 14 us -> 20.6 us  [shifted(): return lax.ppermute(x, 'dp', [(i, (i + shift) % n) for i in range(n)])]
    unnamed x40 -> x48, local copies, waits for them, and re-layouts: 6.38 us -> 11.1 us
    transpose x1 -> x0, local copies, waits for them, and re-layouts: 4.44 us -> none  [on_device(): xb = came_b.reshape(n_ep, members, n_dp, CAP, feature - sc).transpose(1,...]
    convert_element_type x0 -> x3, other arithmetic: none -> 4.28 us  [the longest x1 1.53 us: on_device(): back_d = (f32(total_d) + f32(shifted(to_above, 1)) + f32(shifted(to_below...]
    slice x0 -> x4, local copies, waits for them, and re-layouts: none -> 3.67 us  [the longest x2 1.86 us: on_device(): far = [shifted(below[:half], 1), shifted(above[half:], -1)]]
    ppermute x12 -> x14, waiting for transfers between devices: 73 us -> 71.4 us  [shifted(): return lax.ppermute(x, 'dp', [(i, (i + shift) % n) for i in range(n)])]
  transfers between devices with their start and end apart: 16 -> 18, of which waited for: 11 -> 11; matrix products, arithmetic and copies ran while one was open for 14% -> 15% of each run, Pallas kernels for 2% -> 7%
where the time goes in v3:
time: 209 us; the launch traced here: 208 us
  waiting for transfers between devices  82.4 us (39%)
  starting transfers between devices  55.6 us (27%)
  Pallas kernels  25.3 us (12%)
  matrix products  20.3 us (10%)
  local copies, waits for them, and re-layouts  16.2 us (8%)
  other arithmetic  7.38 us (4%)
    ppermute x14, waiting for transfers between devices, shifted(): return lax.ppermute(x, 'dp', [(i, (i + shift) % n) for i in range(n)])  71.4 us
    all_to_all x4, starting transfers between devices, over_ep(): lax.all_to_all(x.reshape(n_ep, rows, cols), 'ep', split_axis=0, concat_ax...  35 us
    pallas_call x2, Pallas kernels, run_experts(): pl.pallas_call(functools.partial(expert_kernel, splits), grid=(members,),...  21.5 us
    ppermute x14, starting transfers between devices, shifted(): return lax.ppermute(x, 'dp', [(i, (i + shift) % n) for i in range(n)])  20.6 us
    unnamed x48, local copies, waits for them, and re-layouts  11.1 us
    all_to_all x4, waiting for transfers between devices, over_ep(): lax.all_to_all(x.reshape(n_ep, rows, cols), 'ep', split_axis=0, concat_ax...  11 us
    dot_general x2, matrix products, dot_f32(): return jnp.dot(a, b, preferred_element_type=jnp.float32)  10.7 us
    dot_general x2, matrix products, weigh(): lax.dot_general(hi, values, TN, preferred_element_type=jnp.float32)  4.82 us
  transfers between devices with their start and end apart: 18, of which 11 were waited for; matrix products, arithmetic and copies ran while one was open for 15% of the time, Pallas kernels for 7%

profile of v3, /device:TPU:1, one launch (start us, length us, event | category | flops | bytes accessed | tf_op | source)
XLA Modules:
  0.0 208.2 jit_solution(1649144742694409871)
XLA Ops:
  5.0 9.5 %all-to-all-start.1 = ((bf16[32,16,1280]{2,1,0:T(8,128)(2,1)}), bf16[32,16,1280]{2,1,0:T(8,128)(2,1)}, u32[]{:S(2)}, u32[]{:S(2)}) async-start(bf16[32,16,1280]{2,1,0:T(8,128)(2,1)} %bitcast.23), calls=%async_computation.1 | async-start | bytes 2621440 | tf_op jit(solution)/shard_map/all_to_all | solution.py:277
  14.4 3.0 %collective-permute-start = (bf16[64,2176]{1,0:T(8,128)(2,1)S(1)}, bf16[64,2176]{1,0:T(8,128)(2,1)S(1)}, u32[]{:S(2)}, u32[]{:S(2)}) collective-permute-start(bf16[64,2176]{1,0:T(8,128)(2,1)S(1)} %get-tuple-element.24.e3), channel_id=1, source_target_pairs={{0,64},{32,96},{64,0},{96,32},{1,65},{33,97},{65,1},{97,33},{2,66}... | collective-permute-start | bytes 835592 | tf_op jit(solution)/shard_map/ppermute | solution.py:22
  17.8 2.3 %collective-permute-start.2 = (bf16[64,2176]{1,0:T(8,128)(2,1)S(1)}, bf16[64,2176]{1,0:T(8,128)(2,1)S(1)}, u32[]{:S(2)}, u32[]{:S(2)}) collective-permute-start(bf16[64,2176]{1,0:T(8,128)(2,1)S(1)} %get-tuple-element.24.e3), channel_id=1, source_target_pairs={{0,96},{32,0},{64,32},{96,64},{1,97},{33,1},{65,33},{97,65},{2,98}... | collective-permute-start | bytes 835592 | tf_op jit(solution)/shard_map/ppermute | solution.py:22
  20.1 4.0 %collective-permute-done.e0 = bf16[64,2176]{1,0:T(8,128)(2,1)S(1)} collective-permute-done((bf16[64,2176]{1,0:T(8,128)(2,1)S(1)}, bf16[64,2176]{1,0:T(8,128)(2,1)S(1)}, u32[]{:S(2)}, u32[]{:S(2)}) %collective-permute-start) | collective-permute-done | bytes 278560 | tf_op jit(solution)/shard_map/ppermute | solution.py:22
  24.1 6.6 %collective-permute-done.1.e1 = bf16[64,2176]{1,0:T(8,128)(2,1)S(1)} collective-permute-done((bf16[64,2176]{1,0:T(8,128)(2,1)S(1)}, bf16[64,2176]{1,0:T(8,128)(2,1)S(1)}, u32[]{:S(2)}, u32[]{:S(2)}) %collective-permute-start.1) | collective-permute-done | bytes 278560 | tf_op jit(solution)/shard_map/ppermute | solution.py:22
  30.7 3.1 %prepare_ring.1 = (bf16[2048,768]{1,0:T(8,128)(2,1)}, bf16[2048,256]{1,0:T(8,128)(2,1)S(1)}, bf16[2048,256]{1,0:T(8,128)(2,1)S(1)}, bf16[256,2048]{1,0:T(8,128)(2,1)S(1)}) custom-call(bf16[64,2176]{1,0:T(8,128)(2,1)S(1)} %collective-permute-done.e0, bf16[64,2176]{1,0:T(8,128)(2,1)S(1)} %collective-permute-done.1.e1, ...), custom_call_target="tpu_custom_call" | custom-call | tf_op jit(solution)/shard_map/prepare_ring/pallas_call | solution.py:139
  36.7 7.8 %all-to-all-start = ((bf16[32,64,768]{2,1,0:T(8,128)(2,1)}), bf16[32,64,768]{2,1,0:T(8,128)(2,1)}, u32[]{:S(2)}, u32[]{:S(2)}) async-start(bf16[32,64,768]{2,1,0:T(8,128)(2,1)} %bitcast.26), calls=%async_computation | async-start | bytes 6291456 | tf_op jit(solution)/shard_map/all_to_all | solution.py:277
  47.4 28.9 %collective-permute-done.4.refs_2_ = bf16[32,16,1280]{2,1,0:T(8,128)(2,1)S(1)} collective-permute-done((bf16[32,16,1280]{2,1,0:T(8,128)(2,1)}, bf16[32,16,1280]{2,1,0:T(8,128)(2,1)S(1)}, u32[]{:S(2)}, u32[]{:S(2)}) %collective-permute-start.4) | collective-permute-done | bytes 1310752 | tf_op jit(solution)/shard_map/ppermute | solution.py:22
  79.2 2.7 %collective-permute-start.6 = (bf16[16,16,1280]{2,1,0:T(8,128)(2,1)}, bf16[16,16,1280]{2,1,0:T(8,128)(2,1)}, u32[]{:S(2)}, u32[]{:S(2)}) collective-permute-start(bf16[16,16,1280]{2,1,0:T(8,128)(2,1)} %slice.51), channel_id=1, source_target_pairs={{0,96},{32,0},{64,32},{96,64},{1,97},{33,1},{65,33},{97,65},{2,98}... | collective-permute-start | bytes 1966088 | tf_op jit(solution)/shard_map/ppermute | solution.py:22
  81.9 3.7 %fusion.10 = f32[256,704]{0,1:T(8,128)} fusion(bf16[256,2048]{1,0:T(8,128)(2,1)S(1)} %copy-done.19, bf16[2048,704]{0,1:T(8,128)(2,1)} %param.17), kind=kOutput, calls=%fused_computation.27 | convolution fusion | flops 738197504 | bytes 4653056 | tf_op jit(solution)/shard_map/dot_general | solution.py:26
  85.6 7.0 %fusion.2 = f32[256,2048]{1,0:T(8,128)} fusion(bf16[704,2048]{1,0:T(8,128)(2,1)S(1)} %copy-done, f32[256,704]{0,1:T(8,128)} %fusion.10, bf16[256,2048]{1,0:T(8,128)(2,1)} %copy-done.18, bf16[2048,704]{0,1:T(8,128)(2,1)} %param.18), kind=kOutput, calls=%fused_computation.18 | convolution fusion | flops 1477476352 | bytes 9633792 | tf_op jit(solution)/shard_map/dot_general | solution.py:26
  96.3 10.9 %experts.2 = (bf16[16,16,1280]{2,1,0:T(8,128)(2,1)}, bf16[16,16,1280]{2,1,0:T(8,128)(2,1)}, bf16[32,16,1280]{2,1,0:T(8,128)(2,1)S(1)}, bf16[32,64,768]{2,1,0:T(8,128)(2,1)}) custom-call(bf16[16,16,1280]{2,1,0:T(8,128)(2,1)} %collective-permute-done.5.refs_0_, bf16[16,16,1280]{2,1,0:T(8,128)(2,1)} %collective-permute-done.6.refs_1_, ...), custom_call_target="tpu_custom_call" | custom-call | flops 4429185024 | bytes 17039360 | tf_op jit(solution)/shard_map/experts/pallas_call | solution.py:230
  107.2 3.5 %collective-permute-start.9 = (bf16[16,16,1280]{2,1,0:T(8,128)(2,1)}, bf16[16,16,1280]{2,1,0:T(8,128)(2,1)}, u32[]{:S(2)}, u32[]{:S(2)}) collective-permute-start(bf16[16,16,1280]{2,1,0:T(8,128)(2,1)} %get-tuple-element.36), channel_id=1, source_target_pairs={{0,96},{32,0},{64,32},{96,64},{1,97},{33,1},{65,33},{97,65},{2,98}... | collective-permute-start | bytes 1966088 | tf_op jit(solution)/shard_map/ppermute | solution.py:22
  111.6 10.6 %experts.3 = (bf16[32,16,1280]{2,1,0:T(8,128)(2,1)S(1)}, bf16[32,16,1280]{2,1,0:T(8,128)(2,1)S(1)}, bf16[32,64,768]{2,1,0:T(8,128)(2,1)}) custom-call(bf16[32,16,1280]{2,1,0:T(8,128)(2,1)S(1)} %copy-done.2, bf16[32,16,1280]{2,1,0:T(8,128)(2,1)} %all-to-all-done.1.refs_1_, ...), custom_call_target="tpu_custom_call", output_to_operand_aliasing={{2}: (6, {})} | custom-call | flops 4429185024 | bytes 17039360 | tf_op jit(solution)/shard_map/experts/pallas_call | solution.py:230
  125.2 9.4 %all-to-all-start.2 = ((bf16[32,64,768]{2,1,0:T(8,128)(2,1)}), bf16[32,64,768]{2,1,0:T(8,128)(2,1)}, u32[]{:S(2)}, u32[]{:S(2)}) async-start(bf16[32,64,768]{2,1,0:T(8,128)(2,1)} %get-tuple-element.37), calls=%async_computation.2 | async-start | bytes 6291456 | tf_op jit(solution)/shard_map/all_to_all | solution.py:277
  136.3 3.0 %collective-permute-start.10 = (bf16[32,16,1280]{2,1,0:T(8,128)(2,1)S(1)}, bf16[32,16,1280]{2,1,0:T(8,128)(2,1)S(1)}, u32[]{:S(2)}, u32[]{:S(2)}) collective-permute-start(bf16[32,16,1280]{2,1,0:T(8,128)(2,1)S(1)} %pad_maximum_fusion.1), channel_id=1, source_target_pairs={{0,96},{32,0},{64,32},{96,64},{1,97},{33,1},{65,33},{97,65},{2,98}... | collective-permute-start | bytes 3932168 | tf_op jit(solution)/shard_map/ppermute | solution.py:22
  142.2 25.0 %collective-permute-done.10 = bf16[32,16,1280]{2,1,0:T(8,128)(2,1)S(1)} collective-permute-done((bf16[32,16,1280]{2,1,0:T(8,128)(2,1)S(1)}, bf16[32,16,1280]{2,1,0:T(8,128)(2,1)S(1)}, u32[]{:S(2)}, u32[]{:S(2)}) %collective-permute-start.10) | collective-permute-done | bytes 1310752 | tf_op jit(solution)/shard_map/ppermute | solution.py:22
  167.2 3.1 %collective-permute-done.8 = bf16[32,16,1280]{2,1,0:T(8,128)(2,1)S(1)} collective-permute-done((bf16[32,16,1280]{2,1,0:T(8,128)(2,1)S(1)}, bf16[32,16,1280]{2,1,0:T(8,128)(2,1)S(1)}, u32[]{:S(2)}, u32[]{:S(2)}) %collective-permute-start.8) | collective-permute-done | bytes 1310752 | tf_op jit(solution)/shard_map/ppermute | solution.py:22
  171.8 2.6 %all-to-all-done.2 = bf16[32,64,768]{2,1,0:T(8,128)(2,1)} async-done(((bf16[32,64,768]{2,1,0:T(8,128)(2,1)}), bf16[32,64,768]{2,1,0:T(8,128)(2,1)}, u32[]{:S(2)}, u32[]{:S(2)}) %all-to-all-start.2) | async-done | bytes 3145760 | tf_op jit(solution)/shard_map/all_to_all | solution.py:277
  174.4 8.3 %all-to-all-start.3 = ((bf16[32,16,1280]{2,1,0:T(8,128)(2,1)}), bf16[32,16,1280]{2,1,0:T(8,128)(2,1)}, u32[]{:S(2)}, u32[]{:S(2)}) async-start(bf16[32,16,1280]{2,1,0:T(8,128)(2,1)} %add_convert_fusion), calls=%async_computation.3 | async-start | bytes 2621440 | tf_op jit(solution)/shard_map/all_to_all | solution.py:277
  184.3 3.0 %fusion.11 = f32[256,768]{1,0:T(8,128)S(1)} fusion(bf16[2048,256]{1,0:T(8,128)(2,1)S(1)} %copy-done.17, bf16[2048,768]{1,0:T(8,128)(2,1)} %bitcast.7), kind=kOutput, calls=%fused_computation.28 | convolution fusion | flops 805306368 | bytes 4980736 | tf_op jit(solution)/shard_map/dot_general | solution.py:252
  187.4 3.1 %fusion.1 = bf16[256,768]{1,0:T(8,128)(2,1)S(1)} fusion(f32[256,768]{1,0:T(8,128)S(1)} %fusion.11, bf16[2048,256]{1,0:T(8,128)(2,1)S(1)} %copy-done.15, bf16[2048,768]{1,0:T(8,128)(2,1)} %bitcast.7, f32[256,2048]{1,0:T(8,128)} %fusion.2), kind=kOutput, calls=%fused_computation.12 | convolution fusion | flops 805896192 | bytes 6160384 | tf_op jit(solution)/shard_map/dot_general | solution.py:252
  191.4 2.7 %collective-permute-start.12 = (bf16[64,2048]{1,0:T(8,128)(2,1)}, bf16[64,2048]{1,0:T(8,128)(2,1)}, u32[]{:S(2)}, u32[]{:S(2)}) collective-permute-start(bf16[64,2048]{1,0:T(8,128)(2,1)} %get-tuple-element.45), channel_id=1, source_target_pairs={{0,96},{32,0},{64,32},{96,64},{1,97},{33,1},{65,33},{97,65},{2,98}... | collective-permute-start | bytes 786440 | tf_op jit(solution)/shard_map/ppermute | solution.py:22
  194.1 8.4 %all-to-all-done.3 = bf16[32,16,1280]{2,1,0:T(8,128)(2,1)} async-done(((bf16[32,16,1280]{2,1,0:T(8,128)(2,1)}), bf16[32,16,1280]{2,1,0:T(8,128)(2,1)}, u32[]{:S(2)}, u32[]{:S(2)}) %all-to-all-start.3) | async-done | bytes 1310752 | tf_op jit(solution)/shard_map/all_to_all | solution.py:277
  (83 shorter events, 34.9 us)
Async XLA Ops:
  0.0 85.6 %copy-start = (bf16[704,2048]{1,0:T(8,128)(2,1)S(1)}, bf16[704,2048]{1,0:T(8,128)(2,1)}, u32[]{:S(2)}) copy-start(bf16[704,2048]{1,0:T(8,128)(2,1)} %param.19) | copy-start | bytes 8650756
  5.0 31.8 %all-to-all-start.1 = ((bf16[32,16,1280]{2,1,0:T(8,128)(2,1)}), bf16[32,16,1280]{2,1,0:T(8,128)(2,1)}, u32[]{:S(2)}, u32[]{:S(2)}) async-start(bf16[32,16,1280]{2,1,0:T(8,128)(2,1)} %bitcast.23), calls=%async_computation.1 | async-start | bytes 2621440 | tf_op jit(solution)/shard_map/all_to_all | solution.py:277
  14.4 9.7 %collective-permute-start = (bf16[64,2176]{1,0:T(8,128)(2,1)S(1)}, bf16[64,2176]{1,0:T(8,128)(2,1)S(1)}, u32[]{:S(2)}, u32[]{:S(2)}) collective-permute-start(bf16[64,2176]{1,0:T(8,128)(2,1)S(1)} %get-tuple-element.24.e3), channel_id=1, source_target_pairs={{0,64},{32,96},{64,0},{96,32},{1,65},{33,97},{65,1},{97,33},{2,66}... | collective-permute-start | bytes 835592 | tf_op jit(solution)/shard_map/ppermute | solution.py:22
  17.4 13.2 %collective-permute-start.1 = (bf16[64,2176]{1,0:T(8,128)(2,1)S(1)}, bf16[64,2176]{1,0:T(8,128)(2,1)S(1)}, u32[]{:S(2)}, u32[]{:S(2)}) collective-permute-start(bf16[64,2176]{1,0:T(8,128)(2,1)S(1)} %get-tuple-element.24.e3), channel_id=1, source_target_pairs={{0,32},{32,64},{64,96},{96,0},{1,33},{33,65},{65,97},{97,1},{2,34}... | collective-permute-start | bytes 835592 | tf_op jit(solution)/shard_map/ppermute | solution.py:22
  17.8 12.8 %collective-permute-start.2 = (bf16[64,2176]{1,0:T(8,128)(2,1)S(1)}, bf16[64,2176]{1,0:T(8,128)(2,1)S(1)}, u32[]{:S(2)}, u32[]{:S(2)}) collective-permute-start(bf16[64,2176]{1,0:T(8,128)(2,1)S(1)} %get-tuple-element.24.e3), channel_id=1, source_target_pairs={{0,96},{32,0},{64,32},{96,64},{1,97},{33,1},{65,33},{97,65},{2,98}... | collective-permute-start | bytes 835592 | tf_op jit(solution)/shard_map/ppermute | solution.py:22
  36.7 55.8 %all-to-all-start = ((bf16[32,64,768]{2,1,0:T(8,128)(2,1)}), bf16[32,64,768]{2,1,0:T(8,128)(2,1)}, u32[]{:S(2)}, u32[]{:S(2)}) async-start(bf16[32,64,768]{2,1,0:T(8,128)(2,1)} %bitcast.26), calls=%async_computation | async-start | bytes 6291456 | tf_op jit(solution)/shard_map/all_to_all | solution.py:277
  44.6 37.3 %copy-start.19 = (bf16[256,2048]{1,0:T(8,128)(2,1)S(1)}, bf16[256,2048]{1,0:T(8,128)(2,1)}, u32[]{:S(2)}) copy-start(bf16[256,2048]{1,0:T(8,128)(2,1)} %copy-done.18) | copy-start | bytes 3145732
  44.6 31.7 %collective-permute-start.4 = (bf16[32,16,1280]{2,1,0:T(8,128)(2,1)}, bf16[32,16,1280]{2,1,0:T(8,128)(2,1)S(1)}, u32[]{:S(2)}, u32[]{:S(2)}) collective-permute-start(bf16[32,16,1280]{2,1,0:T(8,128)(2,1)} %all-to-all-done.1.refs_1_), channel_id=1, source_target_pairs={{0,32},{32,64},{64,96},{96,0},{1,33},{33,65},{65,97},{97,1},{2,34}... | collective-permute-start | bytes 3932168 | tf_op jit(solution)/shard_map/ppermute | solution.py:22
  45.7 31.5 %collective-permute-start.3 = (bf16[32,16,1280]{2,1,0:T(8,128)(2,1)}, bf16[32,16,1280]{2,1,0:T(8,128)(2,1)S(1)}, u32[]{:S(2)}, u32[]{:S(2)}) collective-permute-start(bf16[32,16,1280]{2,1,0:T(8,128)(2,1)} %all-to-all-done.1.refs_1_), channel_id=1, source_target_pairs={{0,96},{32,0},{64,32},{96,64},{1,97},{33,1},{65,33},{97,65},{2,98}... | collective-permute-start | bytes 3932168 | tf_op jit(solution)/shard_map/ppermute | solution.py:22
  77.2 16.7 %collective-permute-start.5 = (bf16[16,16,1280]{2,1,0:T(8,128)(2,1)}, bf16[16,16,1280]{2,1,0:T(8,128)(2,1)}, u32[]{:S(2)}, u32[]{:S(2)}) collective-permute-start(bf16[16,16,1280]{2,1,0:T(8,128)(2,1)} %slice.50), channel_id=1, source_target_pairs={{0,32},{32,64},{64,96},{96,0},{1,33},{33,65},{65,97},{97,1},{2,34}... | collective-permute-start | bytes 1966088 | tf_op jit(solution)/shard_map/ppermute | solution.py:22
  79.2 15.7 %collective-permute-start.6 = (bf16[16,16,1280]{2,1,0:T(8,128)(2,1)}, bf16[16,16,1280]{2,1,0:T(8,128)(2,1)}, u32[]{:S(2)}, u32[]{:S(2)}) collective-permute-start(bf16[16,16,1280]{2,1,0:T(8,128)(2,1)} %slice.51), channel_id=1, source_target_pairs={{0,96},{32,0},{64,32},{96,64},{1,97},{33,1},{65,33},{97,65},{2,98}... | collective-permute-start | bytes 1966088 | tf_op jit(solution)/shard_map/ppermute | solution.py:22
  107.2 4.4 %copy-start.2 = (bf16[32,16,1280]{2,1,0:T(8,128)(2,1)S(1)}, bf16[32,16,1280]{2,1,0:T(8,128)(2,1)}, u32[]{:S(2)}) copy-start(bf16[32,16,1280]{2,1,0:T(8,128)(2,1)} %copy-done.1) | copy-start | bytes 3932164
  107.2 27.4 %collective-permute-start.9 = (bf16[16,16,1280]{2,1,0:T(8,128)(2,1)}, bf16[16,16,1280]{2,1,0:T(8,128)(2,1)}, u32[]{:S(2)}, u32[]{:S(2)}) collective-permute-start(bf16[16,16,1280]{2,1,0:T(8,128)(2,1)} %get-tuple-element.36), channel_id=1, source_target_pairs={{0,96},{32,0},{64,32},{96,64},{1,97},{33,1},{65,33},{97,65},{2,98}... | collective-permute-start | bytes 1966088 | tf_op jit(solution)/shard_map/ppermute | solution.py:22
  125.2 15.3 %collective-permute-start.7 = (bf16[16,16,1280]{2,1,0:T(8,128)(2,1)}, bf16[16,16,1280]{2,1,0:T(8,128)(2,1)}, u32[]{:S(2)}, u32[]{:S(2)}) collective-permute-start(bf16[16,16,1280]{2,1,0:T(8,128)(2,1)} %get-tuple-element.34), channel_id=1, source_target_pairs={{0,32},{32,64},{64,96},{96,0},{1,33},{33,65},{65,97},{97,1},{2,34}... | collective-permute-start | bytes 1966088 | tf_op jit(solution)/shard_map/ppermute | solution.py:22
  125.2 49.2 %all-to-all-start.2 = ((bf16[32,64,768]{2,1,0:T(8,128)(2,1)}), bf16[32,64,768]{2,1,0:T(8,128)(2,1)}, u32[]{:S(2)}, u32[]{:S(2)}) async-start(bf16[32,64,768]{2,1,0:T(8,128)(2,1)} %get-tuple-element.37), calls=%async_computation.2 | async-start | bytes 6291456 | tf_op jit(solution)/shard_map/all_to_all | solution.py:277
  136.3 5.4 %copy-start.22 = (bf16[16,16,1280]{2,1,0:T(8,128)(2,1)S(1)}, bf16[16,16,1280]{2,1,0:T(8,128)(2,1)}, u32[]{:S(2)}) copy-start(bf16[16,16,1280]{2,1,0:T(8,128)(2,1)} %slice.42) | copy-start | bytes 1966084
  136.3 30.9 %collective-permute-start.10 = (bf16[32,16,1280]{2,1,0:T(8,128)(2,1)S(1)}, bf16[32,16,1280]{2,1,0:T(8,128)(2,1)S(1)}, u32[]{:S(2)}, u32[]{:S(2)}) collective-permute-start(bf16[32,16,1280]{2,1,0:T(8,128)(2,1)S(1)} %pad_maximum_fusion.1), channel_id=1, source_target_pairs={{0,96},{32,0},{64,32},{96,64},{1,97},{33,1},{65,33},{97,65},{2,98}... | collective-permute-start | bytes 3932168 | tf_op jit(solution)/shard_map/ppermute | solution.py:22
  141.7 28.6 %copy-start.4 = (bf16[32,16,1280]{2,1,0:T(8,128)(2,1)S(1)}, bf16[32,16,1280]{2,1,0:T(8,128)(2,1)}, u32[]{:S(2)}) copy-start(bf16[32,16,1280]{2,1,0:T(8,128)(2,1)} %copy-done.3) | copy-start | bytes 3932164
  141.9 28.5 %collective-permute-start.8 = (bf16[32,16,1280]{2,1,0:T(8,128)(2,1)S(1)}, bf16[32,16,1280]{2,1,0:T(8,128)(2,1)S(1)}, u32[]{:S(2)}, u32[]{:S(2)}) collective-permute-start(bf16[32,16,1280]{2,1,0:T(8,128)(2,1)S(1)} %pad_maximum_fusion), channel_id=1, source_target_pairs={{0,32},{32,64},{64,96},{96,0},{1,33},{33,65},{65,97},{97,1},{2,34}... | collective-permute-start | bytes 3932168 | tf_op jit(solution)/shard_map/ppermute | solution.py:22
  174.4 28.1 %all-to-all-start.3 = ((bf16[32,16,1280]{2,1,0:T(8,128)(2,1)}), bf16[32,16,1280]{2,1,0:T(8,128)(2,1)}, u32[]{:S(2)}, u32[]{:S(2)}) async-start(bf16[32,16,1280]{2,1,0:T(8,128)(2,1)} %add_convert_fusion), calls=%async_computation.3 | async-start | bytes 2621440 | tf_op jit(solution)/shard_map/all_to_all | solution.py:277
  184.2 6.3 %copy-start.20 = (bf16[256,1280]{1,0:T(8,128)(2,1)}, bf16[256,1280]{1,0:T(8,128)(2,1)S(1)}, u32[]{:S(2)}) copy-start(bf16[256,1280]{1,0:T(8,128)(2,1)S(1)} %slice.82) | copy-start | bytes 1966084
  191.4 14.7 %collective-permute-start.13 = (bf16[64,2048]{1,0:T(8,128)(2,1)}, bf16[64,2048]{1,0:T(8,128)(2,1)}, u32[]{:S(2)}, u32[]{:S(2)}) collective-permute-start(bf16[64,2048]{1,0:T(8,128)(2,1)} %get-tuple-element.44), channel_id=1, source_target_pairs={{0,32},{32,64},{64,96},{96,0},{1,33},{33,65},{65,97},{97,1},{2,34}... | collective-permute-start | bytes 786440 | tf_op jit(solution)/shard_map/ppermute | solution.py:22
  191.4 14.7 %collective-permute-start.12 = (bf16[64,2048]{1,0:T(8,128)(2,1)}, bf16[64,2048]{1,0:T(8,128)(2,1)}, u32[]{:S(2)}, u32[]{:S(2)}) collective-permute-start(bf16[64,2048]{1,0:T(8,128)(2,1)} %get-tuple-element.45), channel_id=1, source_target_pairs={{0,96},{32,0},{64,32},{96,64},{1,97},{33,1},{65,33},{97,65},{2,98}... | collective-permute-start | bytes 786440 | tf_op jit(solution)/shard_map/ppermute | solution.py:22
  194.1 12.1 %collective-permute-start.11 = (bf16[64,2048]{1,0:T(8,128)(2,1)}, bf16[64,2048]{1,0:T(8,128)(2,1)}, u32[]{:S(2)}, u32[]{:S(2)}) collective-permute-start(bf16[64,2048]{1,0:T(8,128)(2,1)} %get-tuple-element.43), channel_id=1, source_target_pairs={{0,64},{32,96},{64,0},{96,32},{1,65},{33,97},{65,1},{97,33},{2,66}... | collective-permute-start | bytes 786440 | tf_op jit(solution)/shard_map/ppermute | solution.py:22
  (18 other events, 29.7 us)

commit v4 on v3

--- a/solution.py
+++ b/solution.py
@@ -14,12 +14,22 @@
 NT = (((1,), (1,)), ((), ()))
 TN = (((0,), (0,)), ((), ()))
 AROUND = (2, 1, -1)
-VMEM_LIMIT = 48 * 1024 * 1024
+VMEM_LIMIT = 40 * 1024 * 1024
 
 
 def shifted(x, shift):
     n = lax.axis_size("dp")
     return lax.ppermute(x, "dp", [(i, (i + shift) % n) for i in range(n)])
+
+
+def toward(x):
+    n, m = lax.axis_size("dp"), lax.axis_size("ep")
+    pairs = []
+    for i in range(n):
+        for e in range(m):
+            step = 1 if e % 2 == 0 else -1
+            pairs.append((i * m + e, (i + step) % n * m + e))
+    return lax.ppermute(x, ("dp", "ep"), pairs)
 
 
 def dot_f32(a, b):
@@ -72,7 +82,7 @@
         send[:, c : c + step] = dot_f32(one_hot, tokens[:, c : c + step]).astype(jnp.bfloat16)
 
 
-def prepare_ring(e0, e1, e2, e3, send, hi_out, lo_out, rows_out):
+def prepare_ring(members, e0, e1, e2, e3, send, hi_out, lo_out, rows_out):
     tok, width = e0.shape
     feature = rows_out.shape[1]
     blocks = 4
@@ -96,7 +106,10 @@
     shape = (chunk, blocks * CAP, rows)
     slot = lax.broadcasted_iota(jnp.int32, shape, 1)
     at = lax.broadcasted_iota(jnp.int32, shape, 2)
-    want = jnp.where(at // tok == slot // CAP, slot % CAP, -2).astype(jnp.float32)
+    block = slot // CAP
+    odd = lax.broadcasted_iota(jnp.int32, shape, 0) // members % 2 == 1
+    block = jnp.where(odd & (block == 1), 2, jnp.where(odd & (block == 2), 1, block))
+    want = jnp.where(at // tok == block, slot % CAP, -2).astype(jnp.float32)
     flat = chunk * blocks * CAP
     for c in range(0, n_experts, chunk):
         hit = code[c : c + chunk, None, :] == want
@@ -110,43 +123,36 @@
         send[out, :] = dot_f32(one_hot, rows_out[:, first:]).astype(jnp.bfloat16)
 
 
-def in_vmem(n):
-    return [pl.BlockSpec(memory_space=pltpu.VMEM)] * n
-
-
 def call_prepare_own(count, ids, weights, tokens, n_experts, cols):
     tok, feature = tokens.shape
     slots = n_experts * CAP
     return pl.pallas_call(
         prepare_own,
-        in_specs=[pl.BlockSpec(memory_space=pltpu.SMEM)] + in_vmem(3),
-        out_specs=in_vmem(4),
+        in_specs=[pl.BlockSpec(memory_space=pltpu.SMEM)] + [pl.BlockSpec()] * 3,
         out_shape=[
             jax.ShapeDtypeStruct((tok, feature + 2 * tok), jnp.bfloat16),
             jax.ShapeDtypeStruct((slots, cols), jnp.bfloat16),
             jax.ShapeDtypeStruct((slots, tok), jnp.bfloat16),
             jax.ShapeDtypeStruct((slots, tok), jnp.bfloat16),
         ],
-        compiler_params=pltpu.CompilerParams(vmem_limit_bytes=VMEM_LIMIT),
+        compiler_params=pltpu.CompilerParams(vmem_limit_bytes=24 * 1024 * 1024),
         name="prepare_own",
     )(count, ids, weights, tokens)
 
 
-def call_prepare_ring(around, n_experts, feature, cols):
+def call_prepare_ring(around, members, n_experts, feature, cols):
     tok = around[0].shape[0]
     rows = len(around) * tok
     slots = n_experts * CAP * len(around)
     return pl.pallas_call(
-        prepare_ring,
-        in_specs=in_vmem(4),
-        out_specs=in_vmem(4),
+        functools.partial(prepare_ring, members),
         out_shape=[
             jax.ShapeDtypeStruct((slots, cols), jnp.bfloat16),
             jax.ShapeDtypeStruct((slots, rows), jnp.bfloat16),
             jax.ShapeDtypeStruct((slots, rows), jnp.bfloat16),
             jax.ShapeDtypeStruct((rows, feature), jnp.bfloat16),
         ],
-        compiler_params=pltpu.CompilerParams(vmem_limit_bytes=VMEM_LIMIT),
+        compiler_params=pltpu.CompilerParams(vmem_limit_bytes=24 * 1024 * 1024),
         name="prepare_ring",
     )(*around)
 
@@ -254,6 +260,47 @@
     )
 
 
+def combine(hi, lo, values, shared, *outs):
+    tok, feature = outs[0].shape
+    bc = feature - values.shape[1]
+    for c in range(0, feature, 2 * COLS):
+        cols = slice(c, c + 2 * COLS)
+        total = shared[:, cols]
+        if c >= bc:
+            total = total + weigh(hi[...], lo[...], values[:, c - bc : c - bc + 2 * COLS])
+        for j, o in enumerate(outs):
+            o[:, cols] = total[j * tok : (j + 1) * tok].astype(jnp.bfloat16)
+
+
+def call_combine(hi, lo, values, shared, tok):
+    rows, feature = shared.shape
+    return pl.pallas_call(
+        combine,
+        out_shape=[jax.ShapeDtypeStruct((tok, feature), jnp.bfloat16)] * (rows // tok),
+        compiler_params=pltpu.CompilerParams(vmem_limit_bytes=24 * 1024 * 1024),
+        name="combine",
+    )(hi, lo, values, shared)
+
+
+def finish(hi, lo, values, total, out):
+    bc = values.shape[1]
+    out[:, bc:] = total[:, bc:].astype(jnp.bfloat16)
+    for c in range(0, bc, 2 * COLS):
+        cols = slice(c, c + 2 * COLS)
+        out[:, cols] = (total[:, cols] + weigh(hi[...], lo[...], values[:, cols])).astype(
+            jnp.bfloat16
+        )
+
+
+def call_finish(hi, lo, values, total):
+    return pl.pallas_call(
+        finish,
+        out_shape=jax.ShapeDtypeStruct(total.shape, jnp.bfloat16),
+        compiler_params=pltpu.CompilerParams(vmem_limit_bytes=16 * 1024 * 1024),
+        name="finish",
+    )(hi, lo, values, total)
+
+
 def on_device(
     tokens,
     row_counts,
@@ -284,11 +331,15 @@
     own = over_ep(send_d, members * CAP, sc)
 
     around = [shifted(extended, s) for s in AROUND] + [extended]
-    send_b, hi_b, lo_b, gathered = call_prepare_ring(around, n_experts, feature, feature - sc)
+    send_b, hi_b, lo_b, gathered = call_prepare_ring(
+        around, members, n_experts, feature, feature - sc
+    )
 
     half = n_ep // 2
-    below, above = shifted(own, 1), shifted(own, -1)
-    far = [shifted(below[:half], 1), shifted(above[half:], -1)]
+    own_parts = [own[:half], own[half:]]
+    behind = [toward(x) for x in own_parts]
+    far = [toward(x) for x in behind]
+    ahead = [toward(x) for x in far]
     came_b = over_ep(send_b, members * n_dp * CAP, feature - sc)
 
     gate_act = dot_f32(gathered, shared_gate)
@@ -298,39 +349,28 @@
     came_b, shared = lax.optimization_barrier((came_b, shared))
 
     weights = (expert_gate.swapaxes(1, 2), expert_up.swapaxes(1, 2), expert_down)
-    far_0, far_1, to_below, out_b = run_experts([far, [below]], 0, came_b, None, *weights, bc)
-    to_above, total_d, out_b = run_experts([[above], [own]], 1, came_b, out_b, *weights, bc)
+    f0, f1, b0, b1, out_b = run_experts([far, behind], 0, came_b, None, *weights, bc)
+    a0, a1, o0, o1, out_b = run_experts([ahead, own_parts], 1, came_b, out_b, *weights, bc)
     ret_b = over_ep(out_b, members * n_dp * CAP, feature - bc)
 
     f32 = lambda x: x.astype(jnp.float32)
-    from_below, from_above = shifted(far_0, 1), shifted(far_1, -1)
-    to_above = jnp.concatenate(
-        [(f32(to_above[:half]) + f32(from_below)).astype(jnp.bfloat16), to_above[half:]]
-    )
-    to_below = jnp.concatenate(
-        [to_below[:half], (f32(to_below[half:]) + f32(from_above)).astype(jnp.bfloat16)]
-    )
-    back_d = (
-        f32(total_d) + f32(shifted(to_above, 1)) + f32(shifted(to_below, -1))
-    ).astype(jnp.bfloat16)
+    ends = []
+    for first, second, third, last in ((b0, f0, a0, o0), (b1, f1, a1, o1)):
+        passing = first
+        for mine in (second, third):
+            passing = (f32(mine) + f32(toward(passing))).astype(jnp.bfloat16)
+        ends.append((f32(last) + f32(toward(passing))).astype(jnp.bfloat16))
+    back_d = jnp.concatenate(ends)
     back_d, ret_b = lax.optimization_barrier((back_d, ret_b))
     ret_d = over_ep(back_d, members * CAP, bc)
 
-    routed_b = weigh(hi_b, lo_b, ret_b.reshape(-1, feature - bc))
-    partial_sum = jnp.concatenate(
-        [shared[:, :bc], shared[:, bc:] + routed_b], axis=1
-    ).astype(jnp.bfloat16)
-    total = partial_sum[len(AROUND) * tok :].astype(jnp.float32)
-    for j, s in enumerate(AROUND):
-        part = partial_sum[j * tok : (j + 1) * tok]
-        total = total + shifted(part, -s).astype(jnp.float32)
-
-    routed_d = weigh(hi_d, lo_d, ret_d.reshape(-1, bc))
-    result = total + jnp.concatenate(
-        [routed_d, jnp.zeros((tok, feature - bc), jnp.float32)], axis=1
-    )
+    *parts, kept = call_combine(hi_b, lo_b, ret_b.reshape(-1, feature - bc), shared, tok)
     live = jnp.arange(tok, dtype=jnp.int32) < row_counts[0]
-    return jnp.where(live[:, None], result, 0.0).astype(jnp.bfloat16)
+    total = f32(kept)
+    for part, s in zip(parts, AROUND):
+        total = total + f32(shifted(part, -s))
+    total = jnp.where(live[:, None], total, 0.0)
+    return call_finish(hi_d, lo_d, ret_d.reshape(-1, bc), total)
 
 
 def solution(mesh):

time: 209 us -> 195 us (0.933)
  waiting for transfers between devices: 82.4 us -> 61.6 us
  local copies, waits for them, and re-layouts: 16.2 us -> 27.3 us
  matrix products: 20.3 us -> 10.6 us
  starting transfers between devices: 55.6 us -> 61.4 us
  other arithmetic: 7.38 us -> 4.54 us
  Pallas kernels: 25.3 us -> 27.8 us
    ppermute x14 -> x6, waiting for transfers between devices: 71.4 us -> 21.7 us  [shifted(): return lax.ppermute(x, 'dp', [(i, (i + shift) % n) for i in range(n)])]
    ppermute x0 -> x12, waiting for transfers between devices: none -> 30.3 us  [toward(): return lax.ppermute(x, ('dp', 'ep'), pairs)]
    ppermute x0 -> x12, starting transfers between devices: none -> 24.6 us  [toward(): return lax.ppermute(x, ('dp', 'ep'), pairs)]
    unnamed x48 -> x68, local copies, waits for them, and re-layouts: 11.1 us -> 25.8 us
    ppermute x14 -> x6, starting transfers between devices: 20.6 us -> 9.64 us  [shifted(): return lax.ppermute(x, 'dp', [(i, (i + shift) % n) for i in range(n)])]
    dot_general x4 -> x0, matrix products: 9.63 us -> none  [the longest x2 4.82 us: weigh(): lax.dot_general(hi, values, TN, preferred_element_type=jnp.float32)]
    all_to_all x4, starting transfers between devices: 35 us -> 27.1 us  [over_ep(): lax.all_to_all(x.reshape(n_ep, rows, cols), 'ep', split_axis=0, concat_ax...]
    pallas_call x1 -> x3, Pallas kernels: 3.08 us -> 7.86 us  [the longest x1 3.81 us: call_combine(): pl.pallas_call(combine, out_shape=[jax.ShapeDtypeStruct((tok, feature), j...]
  transfers between devices with their start and end apart: 18 -> 22, of which waited for: 11 -> 13; matrix products, arithmetic and copies ran while one was open for 15% -> 9% of each run, Pallas kernels for 7% -> 13%
where the time goes in v4:
time: 195 us; the launch traced here: 194 us
  waiting for transfers between devices  61.6 us (32%)
  starting transfers between devices  61.4 us (31%)
  Pallas kernels  27.8 us (14%)
  local copies, waits for them, and re-layouts  27.3 us (14%)
  matrix products  10.6 us (5%)
  other arithmetic  4.54 us (2%)
    ppermute x12, waiting for transfers between devices, toward(): return lax.ppermute(x, ('dp', 'ep'), pairs)  30.3 us
    all_to_all x4, starting transfers between devices, over_ep(): lax.all_to_all(x.reshape(n_ep, rows, cols), 'ep', split_axis=0, concat_ax...  27.1 us
    unnamed x68, local copies, waits for them, and re-layouts  25.8 us
    ppermute x12, starting transfers between devices, toward(): return lax.ppermute(x, ('dp', 'ep'), pairs)  24.6 us
    ppermute x6, waiting for transfers between devices, shifted(): return lax.ppermute(x, 'dp', [(i, (i + shift) % n) for i in range(n)])  21.7 us
    pallas_call x2, Pallas kernels, run_experts(): pl.pallas_call(functools.partial(expert_kernel, splits), grid=(members,),...  19.3 us
    dot_general x2, matrix products, dot_f32(): return jnp.dot(a, b, preferred_element_type=jnp.float32)  10.6 us
    ppermute x6, starting transfers between devices, shifted(): return lax.ppermute(x, 'dp', [(i, (i + shift) % n) for i in range(n)])  9.64 us
  transfers between devices with their start and end apart: 22, of which 13 were waited for; matrix products, arithmetic and copies ran while one was open for 9% of the time, Pallas kernels for 13%

profile of v4, /device:TPU:1, one launch (start us, length us, event | category | flops | bytes accessed | tf_op | source)
XLA Modules:
  0.0 194.4 jit_solution(3664798788533079223)
XLA Ops:
  6.4 9.5 %all-to-all-start = ((bf16[32,16,1280]{2,1,0:T(8,128)(2,1)}), bf16[32,16,1280]{2,1,0:T(8,128)(2,1)}, u32[]{:S(2)}, u32[]{:S(2)}) async-start(bf16[32,16,1280]{2,1,0:T(8,128)(2,1)} %bitcast.20), calls=%async_computation | async-start | bytes 2621440 | tf_op jit(solution)/shard_map/all_to_all | solution.py:324
  21.5 4.0 %collective-permute-done.6.e0 = bf16[64,2176]{1,0:T(8,128)(2,1)S(1)} collective-permute-done((bf16[64,2176]{1,0:T(8,128)(2,1)S(1)}, bf16[64,2176]{1,0:T(8,128)(2,1)S(1)}, u32[]{:S(2)}, u32[]{:S(2)}) %collective-permute-start.6) | collective-permute-done | bytes 278560 | tf_op jit(solution)/shard_map/ppermute | solution.py:22
  25.5 6.6 %collective-permute-done.7.e1 = bf16[64,2176]{1,0:T(8,128)(2,1)S(1)} collective-permute-done((bf16[64,2176]{1,0:T(8,128)(2,1)S(1)}, bf16[64,2176]{1,0:T(8,128)(2,1)S(1)}, u32[]{:S(2)}, u32[]{:S(2)}) %collective-permute-start.7) | collective-permute-done | bytes 278560 | tf_op jit(solution)/shard_map/ppermute | solution.py:22
  38.2 7.8 %all-to-all-start.1 = ((bf16[32,64,768]{2,1,0:T(8,128)(2,1)}), bf16[32,64,768]{2,1,0:T(8,128)(2,1)}, u32[]{:S(2)}, u32[]{:S(2)}) async-start(bf16[32,64,768]{2,1,0:T(8,128)(2,1)} %bitcast.15), calls=%async_computation.1 | async-start | bytes 6291456 | tf_op jit(solution)/shard_map/all_to_all | solution.py:324
  50.8 6.7 %collective-permute-done.refs_2_ = bf16[16,16,1280]{2,1,0:T(8,128)(2,1)} collective-permute-done((bf16[16,16,1280]{2,1,0:T(8,128)(2,1)S(1)}, bf16[16,16,1280]{2,1,0:T(8,128)(2,1)}, u32[]{:S(2)}, u32[]{:S(2)}) %collective-permute-start) | collective-permute-done | bytes 655392 | tf_op jit(solution)/shard_map/ppermute | solution.py:32
  57.4 3.5 %collective-permute-start.1 = (bf16[16,16,1280]{2,1,0:T(8,128)(2,1)}, bf16[16,16,1280]{2,1,0:T(8,128)(2,1)}, u32[]{:S(2)}, u32[]{:S(2)}) collective-permute-start(bf16[16,16,1280]{2,1,0:T(8,128)(2,1)} %collective-permute-done.refs_2_), channel_id=1, source_target_pairs={{0,32},{1,97},{2,34},{3,99},{4,36},{5,101},{6,38},{7,103},{8,40},{... | collective-permute-start | bytes 1966088 | tf_op jit(solution)/shard_map/ppermute | solution.py:32
  60.9 3.5 %collective-permute-done.3.refs_3_ = bf16[16,16,1280]{2,1,0:T(8,128)(2,1)} collective-permute-done((bf16[16,16,1280]{2,1,0:T(8,128)(2,1)S(1)}, bf16[16,16,1280]{2,1,0:T(8,128)(2,1)}, u32[]{:S(2)}, u32[]{:S(2)}) %collective-permute-start.3) | collective-permute-done | bytes 655392 | tf_op jit(solution)/shard_map/ppermute | solution.py:32
  64.4 3.5 %collective-permute-start.4 = (bf16[16,16,1280]{2,1,0:T(8,128)(2,1)}, bf16[16,16,1280]{2,1,0:T(8,128)(2,1)}, u32[]{:S(2)}, u32[]{:S(2)}) collective-permute-start(bf16[16,16,1280]{2,1,0:T(8,128)(2,1)} %collective-permute-done.3.refs_3_), channel_id=1, source_target_pairs={{0,32},{1,97},{2,34},{3,99},{4,36},{5,101},{6,38},{7,103},{8,40},{... | collective-permute-start | bytes 1966088 | tf_op jit(solution)/shard_map/ppermute | solution.py:32
  68.0 3.7 %fusion.6 = f32[256,704]{0,1:T(8,128)} fusion(bf16[256,2048]{1,0:T(8,128)(2,1)S(1)} %copy-done.33, bf16[2048,704]{0,1:T(8,128)(2,1)} %param.17), kind=kOutput, calls=%fused_computation.15 | convolution fusion | flops 738197504 | bytes 4653056 | tf_op jit(solution)/shard_map/dot_general | solution.py:36
  71.7 6.9 %fusion.shared = f32[256,2048]{1,0:T(8,128)} fusion(bf16[704,2048]{1,0:T(8,128)(2,1)S(1)} %copy-done, f32[256,704]{0,1:T(8,128)} %fusion.6, bf16[256,2048]{1,0:T(8,128)(2,1)} %copy-done.32, bf16[2048,704]{0,1:T(8,128)(2,1)} %param.18), kind=kOutput, calls=%fused_computation.9 | convolution fusion | flops 1477476352 | bytes 9633792 | tf_op jit(solution)/shard_map/dot_general | solution.py:36
  78.6 3.4 %collective-permute-start.5 = (bf16[16,16,1280]{2,1,0:T(8,128)(2,1)}, bf16[16,16,1280]{2,1,0:T(8,128)(2,1)}, u32[]{:S(2)}, u32[]{:S(2)}) collective-permute-start(bf16[16,16,1280]{2,1,0:T(8,128)(2,1)} %collective-permute-done.4.refs_1_), channel_id=1, source_target_pairs={{0,32},{1,97},{2,34},{3,99},{4,36},{5,101},{6,38},{7,103},{8,40},{... | collective-permute-start | bytes 1966088 | tf_op jit(solution)/shard_map/ppermute | solution.py:32
  82.0 3.8 %all-to-all-done.1.refs_4_ = bf16[32,64,768]{2,1,0:T(8,128)(2,1)} async-done(((bf16[32,64,768]{2,1,0:T(8,128)(2,1)}), bf16[32,64,768]{2,1,0:T(8,128)(2,1)}, u32[]{:S(2)}, u32[]{:S(2)}) %all-to-all-start.1) | async-done | bytes 3145760 | tf_op jit(solution)/shard_map/all_to_all | solution.py:324
  91.3 10.1 %experts.2 = (bf16[16,16,1280]{2,1,0:T(8,128)(2,1)S(1)}, bf16[16,16,1280]{2,1,0:T(8,128)(2,1)S(1)}, bf16[16,16,1280]{2,1,0:T(8,128)(2,1)}, bf16[16,16,1280]{2,1,0:T(8,128)(2,1)}, bf16[32,64,768]{2,1,0:T(8,128)(2,1)}) custom-call(bf16[16,16,1280]{2,1,0:T(8,128)(2,1)} %collective-permute-done.1.refs_0_, bf16[16,16,1280]{2,1,0:T(8,128)(2,1)} %collective-permute-done.4.refs_1_, ...), custom_call_target="tpu_custom_call" | custom-call | flops 4429185024 | bytes 17039360 | tf_op jit(solution)/shard_map/experts/pallas_call | solution.py:236
  105.5 9.2 %experts.3 = (bf16[16,16,1280]{2,1,0:T(8,128)(2,1)S(1)}, bf16[16,16,1280]{2,1,0:T(8,128)(2,1)S(1)}, bf16[16,16,1280]{2,1,0:T(8,128)(2,1)S(1)}, bf16[16,16,1280]{2,1,0:T(8,128)(2,1)S(1)}, bf16[32,64,768]{2,1,0:T(8,128)(2,1)}) custom-call(bf16[16,16,1280]{2,1,0:T(8,128)(2,1)} %collective-permute-done.2.refs_0_, ...), custom_call_target="tpu_custom_call", output_to_operand_aliasing={{4}: (8, {})} | custom-call | flops 4429185024 | bytes 17039360 | tf_op jit(solution)/shard_map/experts/pallas_call | solution.py:236
  118.1 4.8 %all-to-all-start.2 = ((bf16[32,64,768]{2,1,0:T(8,128)(2,1)}), bf16[32,64,768]{2,1,0:T(8,128)(2,1)}, u32[]{:S(2)}, u32[]{:S(2)}) async-start(bf16[32,64,768]{2,1,0:T(8,128)(2,1)} %get-tuple-element.47), calls=%async_computation.2 | async-start | bytes 6291456 | tf_op jit(solution)/shard_map/all_to_all | solution.py:324
  128.3 6.1 %collective-permute-done.13 = bf16[16,16,1280]{2,1,0:T(8,128)(2,1)S(1)} collective-permute-done((bf16[16,16,1280]{2,1,0:T(8,128)(2,1)S(1)}, bf16[16,16,1280]{2,1,0:T(8,128)(2,1)S(1)}, u32[]{:S(2)}, u32[]{:S(2)}) %collective-permute-start.13) | collective-permute-done | bytes 655392 | tf_op jit(solution)/shard_map/ppermute | solution.py:32
  137.9 3.6 %collective-permute-done.10 = bf16[16,16,1280]{2,1,0:T(8,128)(2,1)S(1)} collective-permute-done((bf16[16,16,1280]{2,1,0:T(8,128)(2,1)S(1)}, bf16[16,16,1280]{2,1,0:T(8,128)(2,1)S(1)}, u32[]{:S(2)}, u32[]{:S(2)}) %collective-permute-start.10) | collective-permute-done | bytes 655392 | tf_op jit(solution)/shard_map/ppermute | solution.py:32
  144.9 3.6 %collective-permute-done.14 = bf16[16,16,1280]{2,1,0:T(8,128)(2,1)S(1)} collective-permute-done((bf16[16,16,1280]{2,1,0:T(8,128)(2,1)S(1)}, bf16[16,16,1280]{2,1,0:T(8,128)(2,1)S(1)}, u32[]{:S(2)}, u32[]{:S(2)}) %collective-permute-start.14) | collective-permute-done | bytes 655392 | tf_op jit(solution)/shard_map/ppermute | solution.py:32
  148.6 6.9 %collective-permute-done.11 = bf16[16,16,1280]{2,1,0:T(8,128)(2,1)S(1)} collective-permute-done((bf16[16,16,1280]{2,1,0:T(8,128)(2,1)S(1)}, bf16[16,16,1280]{2,1,0:T(8,128)(2,1)S(1)}, u32[]{:S(2)}, u32[]{:S(2)}) %collective-permute-start.11) | collective-permute-done | bytes 655392 | tf_op jit(solution)/shard_map/ppermute | solution.py:32
  156.9 5.8 %all-to-all-done.2 = bf16[32,64,768]{2,1,0:T(8,128)(2,1)} async-done(((bf16[32,64,768]{2,1,0:T(8,128)(2,1)}), bf16[32,64,768]{2,1,0:T(8,128)(2,1)}, u32[]{:S(2)}, u32[]{:S(2)}) %all-to-all-start.2) | async-done | bytes 3145760 | tf_op jit(solution)/shard_map/all_to_all | solution.py:324
  162.7 5.0 %all-to-all-start.3 = ((bf16[32,16,1280]{2,1,0:T(8,128)(2,1)}), bf16[32,16,1280]{2,1,0:T(8,128)(2,1)}, u32[]{:S(2)}, u32[]{:S(2)}) async-start(bf16[32,16,1280]{2,1,0:T(8,128)(2,1)} %pad_maximum_fusion), calls=%async_computation.3 | async-start | bytes 2621440 | tf_op jit(solution)/shard_map/all_to_all | solution.py:324
  171.8 3.8 %combine.1 = (bf16[64,2048]{1,0:T(8,128)(2,1)S(1)}, bf16[64,2048]{1,0:T(8,128)(2,1)S(1)}, bf16[64,2048]{1,0:T(8,128)(2,1)S(1)}, bf16[64,2048]{1,0:T(8,128)(2,1)S(1)}) custom-call(bf16[2048,256]{1,0:T(8,128)(2,1)S(1)} %copy-done.10, bf16[2048,256]{1,0:T(8,128)(2,1)S(1)} %copy-done.12, bf16[2048,768]{1,0:T(8,128)(2,1)} %bitcast.8.values, f32[256,2048]{1,0:T(8,128)S(1)} %copy-done.7), custom_call_target="tpu_custom_call" | custom-call | tf_op jit(solution)/shard_map/combine/pallas_call | solution.py:277
  179.6 4.8 %collective-permute-done.17 = bf16[64,2048]{1,0:T(8,128)(2,1)S(1)} collective-permute-done((bf16[64,2048]{1,0:T(8,128)(2,1)S(1)}, bf16[64,2048]{1,0:T(8,128)(2,1)S(1)}, u32[]{:S(2)}, u32[]{:S(2)}) %collective-permute-start.17) | collective-permute-done | bytes 262176 | tf_op jit(solution)/shard_map/ppermute | solution.py:22
  184.6 6.1 %collective-permute-done.15 = bf16[64,2048]{1,0:T(8,128)(2,1)S(1)} collective-permute-done((bf16[64,2048]{1,0:T(8,128)(2,1)S(1)}, bf16[64,2048]{1,0:T(8,128)(2,1)S(1)}, u32[]{:S(2)}, u32[]{:S(2)}) %collective-permute-start.15) | collective-permute-done | bytes 262176 | tf_op jit(solution)/shard_map/ppermute | solution.py:22
  (106 shorter events, 60.7 us)
Async XLA Ops:
  0.0 71.7 %copy-start = (bf16[704,2048]{1,0:T(8,128)(2,1)S(1)}, bf16[704,2048]{1,0:T(8,128)(2,1)}, u32[]{:S(2)}) copy-start(bf16[704,2048]{1,0:T(8,128)(2,1)} %param.19) | copy-start | bytes 8650756
  6.4 31.8 %all-to-all-start = ((bf16[32,16,1280]{2,1,0:T(8,128)(2,1)}), bf16[32,16,1280]{2,1,0:T(8,128)(2,1)}, u32[]{:S(2)}, u32[]{:S(2)}) async-start(bf16[32,16,1280]{2,1,0:T(8,128)(2,1)} %bitcast.20), calls=%async_computation | async-start | bytes 2621440 | tf_op jit(solution)/shard_map/all_to_all | solution.py:324
  15.8 9.7 %collective-permute-start.6 = (bf16[64,2176]{1,0:T(8,128)(2,1)S(1)}, bf16[64,2176]{1,0:T(8,128)(2,1)S(1)}, u32[]{:S(2)}, u32[]{:S(2)}) collective-permute-start(bf16[64,2176]{1,0:T(8,128)(2,1)S(1)} %get-tuple-element.34.e3), channel_id=1, source_target_pairs={{0,64},{32,96},{64,0},{96,32},{1,65},{33,97},{65,1},{97,33},{2,66}... | collective-permute-start | bytes 835592 | tf_op jit(solution)/shard_map/ppermute | solution.py:22
  18.8 13.2 %collective-permute-start.7 = (bf16[64,2176]{1,0:T(8,128)(2,1)S(1)}, bf16[64,2176]{1,0:T(8,128)(2,1)S(1)}, u32[]{:S(2)}, u32[]{:S(2)}) collective-permute-start(bf16[64,2176]{1,0:T(8,128)(2,1)S(1)} %get-tuple-element.34.e3), channel_id=1, source_target_pairs={{0,32},{32,64},{64,96},{96,0},{1,33},{33,65},{65,97},{97,1},{2,34}... | collective-permute-start | bytes 835592 | tf_op jit(solution)/shard_map/ppermute | solution.py:22
  19.2 12.8 %collective-permute-start.8 = (bf16[64,2176]{1,0:T(8,128)(2,1)S(1)}, bf16[64,2176]{1,0:T(8,128)(2,1)S(1)}, u32[]{:S(2)}, u32[]{:S(2)}) collective-permute-start(bf16[64,2176]{1,0:T(8,128)(2,1)S(1)} %get-tuple-element.34.e3), channel_id=1, source_target_pairs={{0,96},{32,0},{64,32},{96,64},{1,97},{33,1},{65,33},{97,65},{2,98}... | collective-permute-start | bytes 835592 | tf_op jit(solution)/shard_map/ppermute | solution.py:22
  38.2 47.7 %all-to-all-start.1 = ((bf16[32,64,768]{2,1,0:T(8,128)(2,1)}), bf16[32,64,768]{2,1,0:T(8,128)(2,1)}, u32[]{:S(2)}, u32[]{:S(2)}) async-start(bf16[32,64,768]{2,1,0:T(8,128)(2,1)} %bitcast.15), calls=%async_computation.1 | async-start | bytes 6291456 | tf_op jit(solution)/shard_map/all_to_all | solution.py:324
  46.0 22.0 %copy-start.33 = (bf16[256,2048]{1,0:T(8,128)(2,1)S(1)}, bf16[256,2048]{1,0:T(8,128)(2,1)}, u32[]{:S(2)}) copy-start(bf16[256,2048]{1,0:T(8,128)(2,1)} %copy-done.32) | copy-start | bytes 3145732
  47.5 9.9 %collective-permute-start = (bf16[16,16,1280]{2,1,0:T(8,128)(2,1)S(1)}, bf16[16,16,1280]{2,1,0:T(8,128)(2,1)}, u32[]{:S(2)}, u32[]{:S(2)}) collective-permute-start(bf16[16,16,1280]{2,1,0:T(8,128)(2,1)S(1)} %get-tuple-element.58.refs_2_), channel_id=1, source_target_pairs={{0,32},{1,97},{2,34},{3,99},{4,36},{5,101},{6,38},{7,103},{8,40},{... | collective-permute-start | bytes 1966088 | tf_op jit(solution)/shard_map/ppermute | solution.py:32
  50.7 13.7 %collective-permute-start.3 = (bf16[16,16,1280]{2,1,0:T(8,128)(2,1)S(1)}, bf16[16,16,1280]{2,1,0:T(8,128)(2,1)}, u32[]{:S(2)}, u32[]{:S(2)}) collective-permute-start(bf16[16,16,1280]{2,1,0:T(8,128)(2,1)S(1)} %get-tuple-element.57.refs_3_), channel_id=1, source_target_pairs={{0,32},{1,97},{2,34},{3,99},{4,36},{5,101},{6,38},{7,103},{8,40},{... | collective-permute-start | bytes 1966088 | tf_op jit(solution)/shard_map/ppermute | solution.py:32
  57.4 21.2 %collective-permute-start.1 = (bf16[16,16,1280]{2,1,0:T(8,128)(2,1)}, bf16[16,16,1280]{2,1,0:T(8,128)(2,1)}, u32[]{:S(2)}, u32[]{:S(2)}) collective-permute-start(bf16[16,16,1280]{2,1,0:T(8,128)(2,1)} %collective-permute-done.refs_2_), channel_id=1, source_target_pairs={{0,32},{1,97},{2,34},{3,99},{4,36},{5,101},{6,38},{7,103},{8,40},{... | collective-permute-start | bytes 1966088 | tf_op jit(solution)/shard_map/ppermute | solution.py:32
  64.4 14.2 %collective-permute-start.4 = (bf16[16,16,1280]{2,1,0:T(8,128)(2,1)}, bf16[16,16,1280]{2,1,0:T(8,128)(2,1)}, u32[]{:S(2)}, u32[]{:S(2)}) collective-permute-start(bf16[16,16,1280]{2,1,0:T(8,128)(2,1)} %collective-permute-done.3.refs_3_), channel_id=1, source_target_pairs={{0,32},{1,97},{2,34},{3,99},{4,36},{5,101},{6,38},{7,103},{8,40},{... | collective-permute-start | bytes 1966088 | tf_op jit(solution)/shard_map/ppermute | solution.py:32
  78.6 26.8 %collective-permute-start.2 = (bf16[16,16,1280]{2,1,0:T(8,128)(2,1)}, bf16[16,16,1280]{2,1,0:T(8,128)(2,1)}, u32[]{:S(2)}, u32[]{:S(2)}) collective-permute-start(bf16[16,16,1280]{2,1,0:T(8,128)(2,1)} %collective-permute-done.1.refs_0_), channel_id=1, source_target_pairs={{0,32},{1,97},{2,34},{3,99},{4,36},{5,101},{6,38},{7,103},{8,40},{... | collective-permute-start | bytes 1966088 | tf_op jit(solution)/shard_map/ppermute | solution.py:32
  78.6 26.8 %collective-permute-start.5 = (bf16[16,16,1280]{2,1,0:T(8,128)(2,1)}, bf16[16,16,1280]{2,1,0:T(8,128)(2,1)}, u32[]{:S(2)}, u32[]{:S(2)}) collective-permute-start(bf16[16,16,1280]{2,1,0:T(8,128)(2,1)} %collective-permute-done.4.refs_1_), channel_id=1, source_target_pairs={{0,32},{1,97},{2,34},{3,99},{4,36},{5,101},{6,38},{7,103},{8,40},{... | collective-permute-start | bytes 1966088 | tf_op jit(solution)/shard_map/ppermute | solution.py:32
  103.1 19.8 %collective-permute-start.12 = (bf16[16,16,1280]{2,1,0:T(8,128)(2,1)}, bf16[16,16,1280]{2,1,0:T(8,128)(2,1)}, u32[]{:S(2)}, u32[]{:S(2)}) collective-permute-start(bf16[16,16,1280]{2,1,0:T(8,128)(2,1)} %get-tuple-element.46), channel_id=1, source_target_pairs={{0,32},{1,97},{2,34},{3,99},{4,36},{5,101},{6,38},{7,103},{8,40},{... | collective-permute-start | bytes 1966088 | tf_op jit(solution)/shard_map/ppermute | solution.py:32
  105.4 21.2 %collective-permute-start.9 = (bf16[16,16,1280]{2,1,0:T(8,128)(2,1)}, bf16[16,16,1280]{2,1,0:T(8,128)(2,1)}, u32[]{:S(2)}, u32[]{:S(2)}) collective-permute-start(bf16[16,16,1280]{2,1,0:T(8,128)(2,1)} %get-tuple-element.42), channel_id=1, source_target_pairs={{0,32},{1,97},{2,34},{3,99},{4,36},{5,101},{6,38},{7,103},{8,40},{... | collective-permute-start | bytes 1966088 | tf_op jit(solution)/shard_map/ppermute | solution.py:32
  118.1 44.6 %all-to-all-start.2 = ((bf16[32,64,768]{2,1,0:T(8,128)(2,1)}), bf16[32,64,768]{2,1,0:T(8,128)(2,1)}, u32[]{:S(2)}, u32[]{:S(2)}) async-start(bf16[32,64,768]{2,1,0:T(8,128)(2,1)} %get-tuple-element.47), calls=%async_computation.2 | async-start | bytes 6291456 | tf_op jit(solution)/shard_map/all_to_all | solution.py:324
  124.2 10.2 %collective-permute-start.13 = (bf16[16,16,1280]{2,1,0:T(8,128)(2,1)S(1)}, bf16[16,16,1280]{2,1,0:T(8,128)(2,1)S(1)}, u32[]{:S(2)}, u32[]{:S(2)}) collective-permute-start(bf16[16,16,1280]{2,1,0:T(8,128)(2,1)S(1)} %add_convert_fusion.2), channel_id=1, source_target_pairs={{0,32},{1,97},{2,34},{3,99},{4,36},{5,101},{6,38},{7,103},{8,40},{... | collective-permute-start | bytes 1966088 | tf_op jit(solution)/shard_map/ppermute | solution.py:32
  127.8 13.6 %collective-permute-start.10 = (bf16[16,16,1280]{2,1,0:T(8,128)(2,1)S(1)}, bf16[16,16,1280]{2,1,0:T(8,128)(2,1)S(1)}, u32[]{:S(2)}, u32[]{:S(2)}) collective-permute-start(bf16[16,16,1280]{2,1,0:T(8,128)(2,1)S(1)} %add_convert_fusion.5), channel_id=1, source_target_pairs={{0,32},{1,97},{2,34},{3,99},{4,36},{5,101},{6,38},{7,103},{8,40},{... | collective-permute-start | bytes 1966088 | tf_op jit(solution)/shard_map/ppermute | solution.py:32
  134.6 13.9 %collective-permute-start.14 = (bf16[16,16,1280]{2,1,0:T(8,128)(2,1)S(1)}, bf16[16,16,1280]{2,1,0:T(8,128)(2,1)S(1)}, u32[]{:S(2)}, u32[]{:S(2)}) collective-permute-start(bf16[16,16,1280]{2,1,0:T(8,128)(2,1)S(1)} %add_convert_fusion.1), channel_id=1, source_target_pairs={{0,32},{1,97},{2,34},{3,99},{4,36},{5,101},{6,38},{7,103},{8,40},{... | collective-permute-start | bytes 1966088 | tf_op jit(solution)/shard_map/ppermute | solution.py:32
  141.6 13.9 %collective-permute-start.11 = (bf16[16,16,1280]{2,1,0:T(8,128)(2,1)S(1)}, bf16[16,16,1280]{2,1,0:T(8,128)(2,1)S(1)}, u32[]{:S(2)}, u32[]{:S(2)}) collective-permute-start(bf16[16,16,1280]{2,1,0:T(8,128)(2,1)S(1)} %add_convert_fusion.4), channel_id=1, source_target_pairs={{0,32},{1,97},{2,34},{3,99},{4,36},{5,101},{6,38},{7,103},{8,40},{... | collective-permute-start | bytes 1966088 | tf_op jit(solution)/shard_map/ppermute | solution.py:32
  162.7 28.2 %all-to-all-start.3 = ((bf16[32,16,1280]{2,1,0:T(8,128)(2,1)}), bf16[32,16,1280]{2,1,0:T(8,128)(2,1)}, u32[]{:S(2)}, u32[]{:S(2)}) async-start(bf16[32,16,1280]{2,1,0:T(8,128)(2,1)} %pad_maximum_fusion), calls=%async_computation.3 | async-start | bytes 2621440 | tf_op jit(solution)/shard_map/all_to_all | solution.py:324
  175.6 8.7 %collective-permute-start.17 = (bf16[64,2048]{1,0:T(8,128)(2,1)S(1)}, bf16[64,2048]{1,0:T(8,128)(2,1)S(1)}, u32[]{:S(2)}, u32[]{:S(2)}) collective-permute-start(bf16[64,2048]{1,0:T(8,128)(2,1)S(1)} %get-tuple-element.56), channel_id=1, source_target_pairs={{0,32},{32,64},{64,96},{96,0},{1,33},{33,65},{65,97},{97,1},{2,34}... | collective-permute-start | bytes 786440 | tf_op jit(solution)/shard_map/ppermute | solution.py:22
  177.4 7.1 %collective-permute-start.16 = (bf16[64,2048]{1,0:T(8,128)(2,1)S(1)}, bf16[64,2048]{1,0:T(8,128)(2,1)S(1)}, u32[]{:S(2)}, u32[]{:S(2)}) collective-permute-start(bf16[64,2048]{1,0:T(8,128)(2,1)S(1)} %get-tuple-element.55), channel_id=1, source_target_pairs={{0,96},{32,0},{64,32},{96,64},{1,97},{33,1},{65,33},{97,65},{2,98}... | collective-permute-start | bytes 786440 | tf_op jit(solution)/shard_map/ppermute | solution.py:22
  178.3 12.3 %collective-permute-start.15 = (bf16[64,2048]{1,0:T(8,128)(2,1)S(1)}, bf16[64,2048]{1,0:T(8,128)(2,1)S(1)}, u32[]{:S(2)}, u32[]{:S(2)}) collective-permute-start(bf16[64,2048]{1,0:T(8,128)(2,1)S(1)} %get-tuple-element.54), channel_id=1, source_target_pairs={{0,64},{32,96},{64,0},{96,32},{1,65},{33,97},{65,1},{97,33},{2,66}... | collective-permute-start | bytes 786440 | tf_op jit(solution)/shard_map/ppermute | solution.py:22
  (32 other events, 115.5 us)

commit v5 on v4

--- a/solution.py
+++ b/solution.py
@@ -30,6 +30,14 @@
             step = 1 if e % 2 == 0 else -1
             pairs.append((i * m + e, (i + step) % n * m + e))
     return lax.ppermute(x, ("dp", "ep"), pairs)
+
+
+def hbm(shape):
+    return pltpu.HBM(shape, jnp.bfloat16)
+
+
+def from_hbm(*arrays):
+    return [pltpu.with_memory_space_constraint(x, pltpu.HBM) for x in arrays]
 
 
 def dot_f32(a, b):
@@ -131,13 +139,13 @@
         in_specs=[pl.BlockSpec(memory_space=pltpu.SMEM)] + [pl.BlockSpec()] * 3,
         out_shape=[
             jax.ShapeDtypeStruct((tok, feature + 2 * tok), jnp.bfloat16),
-            jax.ShapeDtypeStruct((slots, cols), jnp.bfloat16),
-            jax.ShapeDtypeStruct((slots, tok), jnp.bfloat16),
-            jax.ShapeDtypeStruct((slots, tok), jnp.bfloat16),
+            hbm((slots, cols)),
+            hbm((slots, tok)),
+            hbm((slots, tok)),
         ],
         compiler_params=pltpu.CompilerParams(vmem_limit_bytes=24 * 1024 * 1024),
         name="prepare_own",
-    )(count, ids, weights, tokens)
+    )(count, *from_hbm(ids, weights, tokens))
 
 
 def call_prepare_ring(around, members, n_experts, feature, cols):
@@ -147,10 +155,10 @@
     return pl.pallas_call(
         functools.partial(prepare_ring, members),
         out_shape=[
-            jax.ShapeDtypeStruct((slots, cols), jnp.bfloat16),
-            jax.ShapeDtypeStruct((slots, rows), jnp.bfloat16),
-            jax.ShapeDtypeStruct((slots, rows), jnp.bfloat16),
-            jax.ShapeDtypeStruct((rows, feature), jnp.bfloat16),
+            hbm((slots, cols)),
+            hbm((slots, rows)),
+            hbm((slots, rows)),
+            hbm((rows, feature)),
         ],
         compiler_params=pltpu.CompilerParams(vmem_limit_bytes=24 * 1024 * 1024),
         name="prepare_ring",
@@ -225,8 +233,8 @@
     whole = lambda shape: pl.BlockSpec(shape, lambda m: (0,) * len(shape))
     one = lambda shape: pl.BlockSpec((1,) + shape, lambda m: (m,) + (0,) * len(shape))
     slot = lambda cols: pl.BlockSpec((n_ep, step, cols), lambda m: (0, m * pairs + pair, 0))
-    out_x = [jax.ShapeDtypeStruct(x.shape[:2] + (back,), jnp.bfloat16) for x in xin]
-    operands = [*xin, xb, wg, wu, wd]
+    out_x = [hbm(x.shape[:2] + (back,)) for x in xin]
+    operands = from_hbm(*xin, xb, wg, wu, wd)
     in_specs = [whole(x.shape) for x in xin] + [slot(cols_b)] + [one((ffe, feature))] * 3
     aliases = {}
     if sofar is not None:
@@ -238,7 +246,7 @@
         grid=(members,),
         in_specs=in_specs,
         out_specs=[whole(x.shape) for x in out_x] + [slot(feature - back)],
-        out_shape=out_x + [jax.ShapeDtypeStruct((n_ep, slots, feature - back), jnp.bfloat16)],
+        out_shape=out_x + [hbm((n_ep, slots, feature - back))],
         scratch_shapes=[
             pltpu.VMEM((rows, feature), jnp.bfloat16),
             pltpu.VMEM((rows, back), jnp.float32),
@@ -263,11 +271,11 @@
 def combine(hi, lo, values, shared, *outs):
     tok, feature = outs[0].shape
     bc = feature - values.shape[1]
-    for c in range(0, feature, 2 * COLS):
-        cols = slice(c, c + 2 * COLS)
+    for c in range(0, feature, COLS):
+        cols = slice(c, c + COLS)
         total = shared[:, cols]
         if c >= bc:
-            total = total + weigh(hi[...], lo[...], values[:, c - bc : c - bc + 2 * COLS])
+            total = total + weigh(hi[...], lo[...], values[:, c - bc : c - bc + COLS])
         for j, o in enumerate(outs):
             o[:, cols] = total[j * tok : (j + 1) * tok].astype(jnp.bfloat16)
 
@@ -279,14 +287,14 @@
         out_shape=[jax.ShapeDtypeStruct((tok, feature), jnp.bfloat16)] * (rows // tok),
         compiler_params=pltpu.CompilerParams(vmem_limit_bytes=24 * 1024 * 1024),
         name="combine",
-    )(hi, lo, values, shared)
+    )(*from_hbm(hi, lo, values, shared))
 
 
 def finish(hi, lo, values, total, out):
     bc = values.shape[1]
     out[:, bc:] = total[:, bc:].astype(jnp.bfloat16)
-    for c in range(0, bc, 2 * COLS):
-        cols = slice(c, c + 2 * COLS)
+    for c in range(0, bc, COLS):
+        cols = slice(c, c + COLS)
         out[:, cols] = (total[:, cols] + weigh(hi[...], lo[...], values[:, cols])).astype(
             jnp.bfloat16
         )
@@ -298,7 +306,7 @@
         out_shape=jax.ShapeDtypeStruct(total.shape, jnp.bfloat16),
         compiler_params=pltpu.CompilerParams(vmem_limit_bytes=16 * 1024 * 1024),
         name="finish",
-    )(hi, lo, values, total)
+    )(*from_hbm(hi, lo, values), total)
 
 
 def on_device(

time: 195 us -> 183 us (0.938)
  local copies, waits for them, and re-layouts: 27.3 us -> 2.34 us
  Pallas kernels: 27.8 us -> 39.7 us
    unnamed x68 -> x22, local copies, waits for them, and re-layouts: 25.8 us -> 0.88 us
    pallas_call x2, Pallas kernels: 19.3 us -> 23.6 us  [run_experts(): pl.pallas_call(functools.partial(expert_kernel, splits), grid=(members,),...]
    pallas_call x1, Pallas kernels: 3.81 us -> 6.77 us  [call_combine(): pl.pallas_call(combine, out_shape=[jax.ShapeDtypeStruct((tok, feature), j...]
    pallas_call x1, Pallas kernels: 0.68 us -> 2.83 us  [call_prepare_own(): pl.pallas_call(prepare_own, in_specs=[pl.BlockSpec(memory_space=pltpu.SME...]
    pallas_call x1, Pallas kernels: 1.41 us -> 3.46 us  [call_prepare_ring(): pl.pallas_call(functools.partial(prepare_ring, members), out_shape=[hbm((...]
  transfers between devices with their start and end apart: 22 -> 22, of which waited for: 13 -> 14; matrix products, arithmetic and copies ran while one was open for 9% -> 9% of each run, Pallas kernels for 13% -> 19%
where the time goes in v5:
time: 183 us; the launch traced here: 182 us
  waiting for transfers between devices  62.5 us (34%)
  starting transfers between devices  61.3 us (33%)
  Pallas kernels  39.7 us (22%)
  matrix products  10.7 us (6%)
  other arithmetic  4.52 us (2%)
  local copies, waits for them, and re-layouts  2.34 us (1%)
    ppermute x12, waiting for transfers between devices, toward(): return lax.ppermute(x, ('dp', 'ep'), pairs)  31.1 us
    all_to_all x4, starting transfers between devices, over_ep(): lax.all_to_all(x.reshape(n_ep, rows, cols), 'ep', split_axis=0, concat_ax...  27 us
    ppermute x12, starting transfers between devices, toward(): return lax.ppermute(x, ('dp', 'ep'), pairs)  24.7 us
    pallas_call x2, Pallas kernels, run_experts(): pl.pallas_call(functools.partial(expert_kernel, splits), grid=(members,),...  23.6 us
    ppermute x6, waiting for transfers between devices, shifted(): return lax.ppermute(x, 'dp', [(i, (i + shift) % n) for i in range(n)])  21.7 us
    dot_general x2, matrix products, dot_f32(): return jnp.dot(a, b, preferred_element_type=jnp.float32)  10.7 us
    all_to_all x4, waiting for transfers between devices, over_ep(): lax.all_to_all(x.reshape(n_ep, rows, cols), 'ep', split_axis=0, concat_ax...  9.77 us
    ppermute x6, starting transfers between devices, shifted(): return lax.ppermute(x, 'dp', [(i, (i + shift) % n) for i in range(n)])  9.63 us
  transfers between devices with their start and end apart: 22, of which 14 were waited for; matrix products, arithmetic and copies ran while one was open for 9% of the time, Pallas kernels for 19%

profile of v5, /device:TPU:1, one launch (start us, length us, event | category | flops | bytes accessed | tf_op | source)
XLA Modules:
  0.0 182.1 jit_solution(12949740590967268640)
XLA Ops:
  3.6 9.5 %all-to-all-start = ((bf16[32,16,1280]{2,1,0:T(8,128)(2,1)}), bf16[32,16,1280]{2,1,0:T(8,128)(2,1)}, u32[]{:S(2)}, u32[]{:S(2)}) async-start(bf16[32,16,1280]{2,1,0:T(8,128)(2,1)} %bitcast.20), calls=%async_computation | async-start | bytes 2621440 | tf_op jit(solution)/shard_map/all_to_all | solution.py:332
  18.8 4.0 %collective-permute-done.6.e0 = bf16[64,2176]{1,0:T(8,128)(2,1)S(1)} collective-permute-done((bf16[64,2176]{1,0:T(8,128)(2,1)S(1)}, bf16[64,2176]{1,0:T(8,128)(2,1)S(1)}, u32[]{:S(2)}, u32[]{:S(2)}) %collective-permute-start.6) | collective-permute-done | bytes 278560 | tf_op jit(solution)/shard_map/ppermute | solution.py:22
  22.8 6.6 %collective-permute-done.7.e1 = bf16[64,2176]{1,0:T(8,128)(2,1)S(1)} collective-permute-done((bf16[64,2176]{1,0:T(8,128)(2,1)S(1)}, bf16[64,2176]{1,0:T(8,128)(2,1)S(1)}, u32[]{:S(2)}, u32[]{:S(2)}) %collective-permute-start.7) | collective-permute-done | bytes 278560 | tf_op jit(solution)/shard_map/ppermute | solution.py:22
  29.4 3.5 %prepare_ring.1 = (bf16[2048,768]{1,0:T(8,128)(2,1)}, bf16[2048,256]{1,0:T(8,128)(2,1)}, bf16[2048,256]{1,0:T(8,128)(2,1)}, bf16[256,2048]{1,0:T(8,128)(2,1)}) custom-call(bf16[64,2176]{1,0:T(8,128)(2,1)S(1)} %collective-permute-done.6.e0, bf16[64,2176]{1,0:T(8,128)(2,1)S(1)} %collective-permute-done.7.e1, bf16[64,2176]{1,0:T(8,128)(2,1)S(1)} %collective-permute-done.8.e2, ...), custom_call_target="tpu_custom_call" | custom-call | tf_op jit(solution)/shard_map/prepare_ring/pallas_call | solution.py:155
  33.0 7.7 %all-to-all-start.1 = ((bf16[32,64,768]{2,1,0:T(8,128)(2,1)}), bf16[32,64,768]{2,1,0:T(8,128)(2,1)}, u32[]{:S(2)}, u32[]{:S(2)}) async-start(bf16[32,64,768]{2,1,0:T(8,128)(2,1)} %bitcast.15), calls=%async_computation.1 | async-start | bytes 6291456 | tf_op jit(solution)/shard_map/all_to_all | solution.py:332
  44.7 7.4 %collective-permute-done.refs_2_ = bf16[16,16,1280]{2,1,0:T(8,128)(2,1)} collective-permute-done((bf16[16,16,1280]{2,1,0:T(8,128)(2,1)S(1)}, bf16[16,16,1280]{2,1,0:T(8,128)(2,1)}, u32[]{:S(2)}, u32[]{:S(2)}) %collective-permute-start) | collective-permute-done | bytes 655392 | tf_op jit(solution)/shard_map/ppermute | solution.py:32
  52.1 3.5 %collective-permute-start.1 = (bf16[16,16,1280]{2,1,0:T(8,128)(2,1)}, bf16[16,16,1280]{2,1,0:T(8,128)(2,1)}, u32[]{:S(2)}, u32[]{:S(2)}) collective-permute-start(bf16[16,16,1280]{2,1,0:T(8,128)(2,1)} %collective-permute-done.refs_2_), channel_id=1, source_target_pairs={{0,32},{1,97},{2,34},{3,99},{4,36},{5,101},{6,38},{7,103},{8,40},{... | collective-permute-start | bytes 1966088 | tf_op jit(solution)/shard_map/ppermute | solution.py:32
  55.6 3.5 %collective-permute-done.3.refs_3_ = bf16[16,16,1280]{2,1,0:T(8,128)(2,1)} collective-permute-done((bf16[16,16,1280]{2,1,0:T(8,128)(2,1)S(1)}, bf16[16,16,1280]{2,1,0:T(8,128)(2,1)}, u32[]{:S(2)}, u32[]{:S(2)}) %collective-permute-start.3) | collective-permute-done | bytes 655392 | tf_op jit(solution)/shard_map/ppermute | solution.py:32
  59.1 3.5 %collective-permute-start.4 = (bf16[16,16,1280]{2,1,0:T(8,128)(2,1)}, bf16[16,16,1280]{2,1,0:T(8,128)(2,1)}, u32[]{:S(2)}, u32[]{:S(2)}) collective-permute-start(bf16[16,16,1280]{2,1,0:T(8,128)(2,1)} %collective-permute-done.3.refs_3_), channel_id=1, source_target_pairs={{0,32},{1,97},{2,34},{3,99},{4,36},{5,101},{6,38},{7,103},{8,40},{... | collective-permute-start | bytes 1966088 | tf_op jit(solution)/shard_map/ppermute | solution.py:32
  62.7 3.7 %fusion.6 = f32[256,704]{0,1:T(8,128)} fusion(bf16[256,2048]{1,0:T(8,128)(2,1)S(1)} %copy-done.10, bf16[2048,704]{0,1:T(8,128)(2,1)} %param.17), kind=kOutput, calls=%fused_computation.15 | convolution fusion | flops 738197504 | bytes 4653056 | tf_op jit(solution)/shard_map/dot_general | solution.py:44
  66.4 6.9 %fusion.shared = f32[256,2048]{1,0:T(8,128)} fusion(bf16[704,2048]{1,0:T(8,128)(2,1)S(1)} %copy-done, f32[256,704]{0,1:T(8,128)} %fusion.6, bf16[256,2048]{1,0:T(8,128)(2,1)} %get-tuple-element.36, bf16[2048,704]{0,1:T(8,128)(2,1)} %param.18), kind=kOutput, calls=%fused_computation.9 | convolution fusion | flops 1477476352 | bytes 9633792 | tf_op jit(solution)/shard_map/dot_general | solution.py:44
  76.7 3.8 %all-to-all-done.1.refs_4_ = bf16[32,64,768]{2,1,0:T(8,128)(2,1)} async-done(((bf16[32,64,768]{2,1,0:T(8,128)(2,1)}), bf16[32,64,768]{2,1,0:T(8,128)(2,1)}, u32[]{:S(2)}, u32[]{:S(2)}) %all-to-all-start.1) | async-done | bytes 3145760 | tf_op jit(solution)/shard_map/all_to_all | solution.py:332
  80.5 11.8 %experts.2 = (bf16[16,16,1280]{2,1,0:T(8,128)(2,1)}, bf16[16,16,1280]{2,1,0:T(8,128)(2,1)}, bf16[16,16,1280]{2,1,0:T(8,128)(2,1)}, bf16[16,16,1280]{2,1,0:T(8,128)(2,1)}, bf16[32,64,768]{2,1,0:T(8,128)(2,1)}) custom-call(bf16[16,16,1280]{2,1,0:T(8,128)(2,1)} %collective-permute-done.1.refs_0_, bf16[16,16,1280]{2,1,0:T(8,128)(2,1)} %collective-permute-done.4.refs_1_, ...), custom_call_target="tpu_custom_call" | custom-call | flops 4429185024 | bytes 17039360 | tf_op jit(solution)/shard_map/experts/pallas_call | solution.py:244
  95.6 11.8 %experts.3 = (bf16[16,16,1280]{2,1,0:T(8,128)(2,1)}, bf16[16,16,1280]{2,1,0:T(8,128)(2,1)}, bf16[16,16,1280]{2,1,0:T(8,128)(2,1)}, bf16[16,16,1280]{2,1,0:T(8,128)(2,1)}, bf16[32,64,768]{2,1,0:T(8,128)(2,1)}) custom-call(bf16[16,16,1280]{2,1,0:T(8,128)(2,1)} %copy-done.3, ...), custom_call_target="tpu_custom_call", output_to_operand_aliasing={{4}: (8, {})} | custom-call | flops 4429185024 | bytes 17039360 | tf_op jit(solution)/shard_map/experts/pallas_call | solution.py:244
  107.3 4.8 %all-to-all-start.2 = ((bf16[32,64,768]{2,1,0:T(8,128)(2,1)}), bf16[32,64,768]{2,1,0:T(8,128)(2,1)}, u32[]{:S(2)}, u32[]{:S(2)}) async-start(bf16[32,64,768]{2,1,0:T(8,128)(2,1)} %get-tuple-element.47), calls=%async_computation.2 | async-start | bytes 6291456 | tf_op jit(solution)/shard_map/all_to_all | solution.py:332
  117.5 6.1 %collective-permute-done.13 = bf16[16,16,1280]{2,1,0:T(8,128)(2,1)S(1)} collective-permute-done((bf16[16,16,1280]{2,1,0:T(8,128)(2,1)S(1)}, bf16[16,16,1280]{2,1,0:T(8,128)(2,1)S(1)}, u32[]{:S(2)}, u32[]{:S(2)}) %collective-permute-start.13) | collective-permute-done | bytes 655392 | tf_op jit(solution)/shard_map/ppermute | solution.py:32
  127.1 3.6 %collective-permute-done.10 = bf16[16,16,1280]{2,1,0:T(8,128)(2,1)S(1)} collective-permute-done((bf16[16,16,1280]{2,1,0:T(8,128)(2,1)S(1)}, bf16[16,16,1280]{2,1,0:T(8,128)(2,1)S(1)}, u32[]{:S(2)}, u32[]{:S(2)}) %collective-permute-start.10) | collective-permute-done | bytes 655392 | tf_op jit(solution)/shard_map/ppermute | solution.py:32
  134.1 3.6 %collective-permute-done.14 = bf16[16,16,1280]{2,1,0:T(8,128)(2,1)S(1)} collective-permute-done((bf16[16,16,1280]{2,1,0:T(8,128)(2,1)S(1)}, bf16[16,16,1280]{2,1,0:T(8,128)(2,1)S(1)}, u32[]{:S(2)}, u32[]{:S(2)}) %collective-permute-start.14) | collective-permute-done | bytes 655392 | tf_op jit(solution)/shard_map/ppermute | solution.py:32
  137.9 6.9 %collective-permute-done.11 = bf16[16,16,1280]{2,1,0:T(8,128)(2,1)S(1)} collective-permute-done((bf16[16,16,1280]{2,1,0:T(8,128)(2,1)S(1)}, bf16[16,16,1280]{2,1,0:T(8,128)(2,1)S(1)}, u32[]{:S(2)}, u32[]{:S(2)}) %collective-permute-start.11) | collective-permute-done | bytes 655392 | tf_op jit(solution)/shard_map/ppermute | solution.py:32
  146.1 5.8 %all-to-all-done.2 = bf16[32,64,768]{2,1,0:T(8,128)(2,1)} async-done(((bf16[32,64,768]{2,1,0:T(8,128)(2,1)}), bf16[32,64,768]{2,1,0:T(8,128)(2,1)}, u32[]{:S(2)}, u32[]{:S(2)}) %all-to-all-start.2) | async-done | bytes 3145760 | tf_op jit(solution)/shard_map/all_to_all | solution.py:332
  151.9 5.0 %all-to-all-start.3 = ((bf16[32,16,1280]{2,1,0:T(8,128)(2,1)}), bf16[32,16,1280]{2,1,0:T(8,128)(2,1)}, u32[]{:S(2)}, u32[]{:S(2)}) async-start(bf16[32,16,1280]{2,1,0:T(8,128)(2,1)} %pad_maximum_fusion), calls=%async_computation.3 | async-start | bytes 2621440 | tf_op jit(solution)/shard_map/all_to_all | solution.py:332
  157.0 6.8 %combine.1 = (bf16[64,2048]{1,0:T(8,128)(2,1)S(1)}, bf16[64,2048]{1,0:T(8,128)(2,1)S(1)}, bf16[64,2048]{1,0:T(8,128)(2,1)S(1)}, bf16[64,2048]{1,0:T(8,128)(2,1)S(1)}) custom-call(bf16[2048,256]{1,0:T(8,128)(2,1)} %get-tuple-element.49.hi, bf16[2048,256]{1,0:T(8,128)(2,1)} %get-tuple-element.50.lo, bf16[2048,768]{1,0:T(8,128)(2,1)} %bitcast.8.values, ...), custom_call_target="tpu_custom_call" | custom-call | tf_op jit(solution)/shard_map/combine/pallas_call | solution.py:285
  167.7 4.8 %collective-permute-done.17 = bf16[64,2048]{1,0:T(8,128)(2,1)S(1)} collective-permute-done((bf16[64,2048]{1,0:T(8,128)(2,1)S(1)}, bf16[64,2048]{1,0:T(8,128)(2,1)S(1)}, u32[]{:S(2)}, u32[]{:S(2)}) %collective-permute-start.17) | collective-permute-done | bytes 262176 | tf_op jit(solution)/shard_map/ppermute | solution.py:22
  172.7 6.1 %collective-permute-done.15 = bf16[64,2048]{1,0:T(8,128)(2,1)S(1)} collective-permute-done((bf16[64,2048]{1,0:T(8,128)(2,1)S(1)}, bf16[64,2048]{1,0:T(8,128)(2,1)S(1)}, u32[]{:S(2)}, u32[]{:S(2)}) %collective-permute-start.15) | collective-permute-done | bytes 262176 | tf_op jit(solution)/shard_map/ppermute | solution.py:22
  (60 shorter events, 40.6 us)
Async XLA Ops:
  0.0 66.4 %copy-start = (bf16[704,2048]{1,0:T(8,128)(2,1)S(1)}, bf16[704,2048]{1,0:T(8,128)(2,1)}, u32[]{:S(2)}) copy-start(bf16[704,2048]{1,0:T(8,128)(2,1)} %param.19) | copy-start | bytes 8650756
  3.6 29.3 %all-to-all-start = ((bf16[32,16,1280]{2,1,0:T(8,128)(2,1)}), bf16[32,16,1280]{2,1,0:T(8,128)(2,1)}, u32[]{:S(2)}, u32[]{:S(2)}) async-start(bf16[32,16,1280]{2,1,0:T(8,128)(2,1)} %bitcast.20), calls=%async_computation | async-start | bytes 2621440 | tf_op jit(solution)/shard_map/all_to_all | solution.py:332
  13.1 9.7 %collective-permute-start.6 = (bf16[64,2176]{1,0:T(8,128)(2,1)S(1)}, bf16[64,2176]{1,0:T(8,128)(2,1)S(1)}, u32[]{:S(2)}, u32[]{:S(2)}) collective-permute-start(bf16[64,2176]{1,0:T(8,128)(2,1)S(1)} %get-tuple-element.34.e3), channel_id=1, source_target_pairs={{0,64},{32,96},{64,0},{96,32},{1,65},{33,97},{65,1},{97,33},{2,66}... | collective-permute-start | bytes 835592 | tf_op jit(solution)/shard_map/ppermute | solution.py:22
  16.1 13.2 %collective-permute-start.7 = (bf16[64,2176]{1,0:T(8,128)(2,1)S(1)}, bf16[64,2176]{1,0:T(8,128)(2,1)S(1)}, u32[]{:S(2)}, u32[]{:S(2)}) collective-permute-start(bf16[64,2176]{1,0:T(8,128)(2,1)S(1)} %get-tuple-element.34.e3), channel_id=1, source_target_pairs={{0,32},{32,64},{64,96},{96,0},{1,33},{33,65},{65,97},{97,1},{2,34}... | collective-permute-start | bytes 835592 | tf_op jit(solution)/shard_map/ppermute | solution.py:22
  16.5 12.8 %collective-permute-start.8 = (bf16[64,2176]{1,0:T(8,128)(2,1)S(1)}, bf16[64,2176]{1,0:T(8,128)(2,1)S(1)}, u32[]{:S(2)}, u32[]{:S(2)}) collective-permute-start(bf16[64,2176]{1,0:T(8,128)(2,1)S(1)} %get-tuple-element.34.e3), channel_id=1, source_target_pairs={{0,96},{32,0},{64,32},{96,64},{1,97},{33,1},{65,33},{97,65},{2,98}... | collective-permute-start | bytes 835592 | tf_op jit(solution)/shard_map/ppermute | solution.py:22
  33.0 47.5 %all-to-all-start.1 = ((bf16[32,64,768]{2,1,0:T(8,128)(2,1)}), bf16[32,64,768]{2,1,0:T(8,128)(2,1)}, u32[]{:S(2)}, u32[]{:S(2)}) async-start(bf16[32,64,768]{2,1,0:T(8,128)(2,1)} %bitcast.15), calls=%async_computation.1 | async-start | bytes 6291456 | tf_op jit(solution)/shard_map/all_to_all | solution.py:332
  42.2 24.2 %copy-start.1 = (bf16[16,16,1280]{2,1,0:T(8,128)(2,1)}, bf16[16,16,1280]{2,1,0:T(8,128)(2,1)S(1)}, u32[]{:S(2)}) copy-start(bf16[16,16,1280]{2,1,0:T(8,128)(2,1)S(1)} %get-tuple-element.57.refs_3_) | copy-start | bytes 1966084
  42.2 9.9 %collective-permute-start = (bf16[16,16,1280]{2,1,0:T(8,128)(2,1)S(1)}, bf16[16,16,1280]{2,1,0:T(8,128)(2,1)}, u32[]{:S(2)}, u32[]{:S(2)}) collective-permute-start(bf16[16,16,1280]{2,1,0:T(8,128)(2,1)S(1)} %get-tuple-element.58.refs_2_), channel_id=1, source_target_pairs={{0,32},{1,97},{2,34},{3,99},{4,36},{5,101},{6,38},{7,103},{8,40},{... | collective-permute-start | bytes 1966088 | tf_op jit(solution)/shard_map/ppermute | solution.py:32
  44.6 14.6 %collective-permute-start.3 = (bf16[16,16,1280]{2,1,0:T(8,128)(2,1)S(1)}, bf16[16,16,1280]{2,1,0:T(8,128)(2,1)}, u32[]{:S(2)}, u32[]{:S(2)}) collective-permute-start(bf16[16,16,1280]{2,1,0:T(8,128)(2,1)S(1)} %get-tuple-element.57.refs_3_), channel_id=1, source_target_pairs={{0,32},{1,97},{2,34},{3,99},{4,36},{5,101},{6,38},{7,103},{8,40},{... | collective-permute-start | bytes 1966088 | tf_op jit(solution)/shard_map/ppermute | solution.py:32
  52.1 21.2 %collective-permute-start.1 = (bf16[16,16,1280]{2,1,0:T(8,128)(2,1)}, bf16[16,16,1280]{2,1,0:T(8,128)(2,1)}, u32[]{:S(2)}, u32[]{:S(2)}) collective-permute-start(bf16[16,16,1280]{2,1,0:T(8,128)(2,1)} %collective-permute-done.refs_2_), channel_id=1, source_target_pairs={{0,32},{1,97},{2,34},{3,99},{4,36},{5,101},{6,38},{7,103},{8,40},{... | collective-permute-start | bytes 1966088 | tf_op jit(solution)/shard_map/ppermute | solution.py:32
  59.1 14.2 %collective-permute-start.4 = (bf16[16,16,1280]{2,1,0:T(8,128)(2,1)}, bf16[16,16,1280]{2,1,0:T(8,128)(2,1)}, u32[]{:S(2)}, u32[]{:S(2)}) collective-permute-start(bf16[16,16,1280]{2,1,0:T(8,128)(2,1)} %collective-permute-done.3.refs_3_), channel_id=1, source_target_pairs={{0,32},{1,97},{2,34},{3,99},{4,36},{5,101},{6,38},{7,103},{8,40},{... | collective-permute-start | bytes 1966088 | tf_op jit(solution)/shard_map/ppermute | solution.py:32
  73.3 21.4 %collective-permute-start.2 = (bf16[16,16,1280]{2,1,0:T(8,128)(2,1)}, bf16[16,16,1280]{2,1,0:T(8,128)(2,1)S(1)}, u32[]{:S(2)}, u32[]{:S(2)}) collective-permute-start(bf16[16,16,1280]{2,1,0:T(8,128)(2,1)} %collective-permute-done.1.refs_0_), channel_id=1, source_target_pairs={{0,32},{1,97},{2,34},{3,99},{4,36},{5,101},{6,38},{7,103},{8,40},{... | collective-permute-start | bytes 1966088 | tf_op jit(solution)/shard_map/ppermute | solution.py:32
  73.3 21.4 %collective-permute-start.5 = (bf16[16,16,1280]{2,1,0:T(8,128)(2,1)}, bf16[16,16,1280]{2,1,0:T(8,128)(2,1)}, u32[]{:S(2)}, u32[]{:S(2)}) collective-permute-start(bf16[16,16,1280]{2,1,0:T(8,128)(2,1)} %collective-permute-done.4.refs_1_), channel_id=1, source_target_pairs={{0,32},{1,97},{2,34},{3,99},{4,36},{5,101},{6,38},{7,103},{8,40},{... | collective-permute-start | bytes 1966088 | tf_op jit(solution)/shard_map/ppermute | solution.py:32
  92.3 19.8 %collective-permute-start.12 = (bf16[16,16,1280]{2,1,0:T(8,128)(2,1)}, bf16[16,16,1280]{2,1,0:T(8,128)(2,1)}, u32[]{:S(2)}, u32[]{:S(2)}) collective-permute-start(bf16[16,16,1280]{2,1,0:T(8,128)(2,1)} %get-tuple-element.46), channel_id=1, source_target_pairs={{0,32},{1,97},{2,34},{3,99},{4,36},{5,101},{6,38},{7,103},{8,40},{... | collective-permute-start | bytes 1966088 | tf_op jit(solution)/shard_map/ppermute | solution.py:32
  94.6 21.2 %collective-permute-start.9 = (bf16[16,16,1280]{2,1,0:T(8,128)(2,1)}, bf16[16,16,1280]{2,1,0:T(8,128)(2,1)}, u32[]{:S(2)}, u32[]{:S(2)}) collective-permute-start(bf16[16,16,1280]{2,1,0:T(8,128)(2,1)} %get-tuple-element.42), channel_id=1, source_target_pairs={{0,32},{1,97},{2,34},{3,99},{4,36},{5,101},{6,38},{7,103},{8,40},{... | collective-permute-start | bytes 1966088 | tf_op jit(solution)/shard_map/ppermute | solution.py:32
  107.3 44.6 %all-to-all-start.2 = ((bf16[32,64,768]{2,1,0:T(8,128)(2,1)}), bf16[32,64,768]{2,1,0:T(8,128)(2,1)}, u32[]{:S(2)}, u32[]{:S(2)}) async-start(bf16[32,64,768]{2,1,0:T(8,128)(2,1)} %get-tuple-element.47), calls=%async_computation.2 | async-start | bytes 6291456 | tf_op jit(solution)/shard_map/all_to_all | solution.py:332
  113.5 10.2 %collective-permute-start.13 = (bf16[16,16,1280]{2,1,0:T(8,128)(2,1)S(1)}, bf16[16,16,1280]{2,1,0:T(8,128)(2,1)S(1)}, u32[]{:S(2)}, u32[]{:S(2)}) collective-permute-start(bf16[16,16,1280]{2,1,0:T(8,128)(2,1)S(1)} %add_convert_fusion.2), channel_id=1, source_target_pairs={{0,32},{1,97},{2,34},{3,99},{4,36},{5,101},{6,38},{7,103},{8,40},{... | collective-permute-start | bytes 1966088 | tf_op jit(solution)/shard_map/ppermute | solution.py:32
  117.1 13.6 %collective-permute-start.10 = (bf16[16,16,1280]{2,1,0:T(8,128)(2,1)S(1)}, bf16[16,16,1280]{2,1,0:T(8,128)(2,1)S(1)}, u32[]{:S(2)}, u32[]{:S(2)}) collective-permute-start(bf16[16,16,1280]{2,1,0:T(8,128)(2,1)S(1)} %add_convert_fusion.5), channel_id=1, source_target_pairs={{0,32},{1,97},{2,34},{3,99},{4,36},{5,101},{6,38},{7,103},{8,40},{... | collective-permute-start | bytes 1966088 | tf_op jit(solution)/shard_map/ppermute | solution.py:32
  123.8 13.9 %collective-permute-start.14 = (bf16[16,16,1280]{2,1,0:T(8,128)(2,1)S(1)}, bf16[16,16,1280]{2,1,0:T(8,128)(2,1)S(1)}, u32[]{:S(2)}, u32[]{:S(2)}) collective-permute-start(bf16[16,16,1280]{2,1,0:T(8,128)(2,1)S(1)} %add_convert_fusion.1), channel_id=1, source_target_pairs={{0,32},{1,97},{2,34},{3,99},{4,36},{5,101},{6,38},{7,103},{8,40},{... | collective-permute-start | bytes 1966088 | tf_op jit(solution)/shard_map/ppermute | solution.py:32
  130.9 13.9 %collective-permute-start.11 = (bf16[16,16,1280]{2,1,0:T(8,128)(2,1)S(1)}, bf16[16,16,1280]{2,1,0:T(8,128)(2,1)S(1)}, u32[]{:S(2)}, u32[]{:S(2)}) collective-permute-start(bf16[16,16,1280]{2,1,0:T(8,128)(2,1)S(1)} %add_convert_fusion.4), channel_id=1, source_target_pairs={{0,32},{1,97},{2,34},{3,99},{4,36},{5,101},{6,38},{7,103},{8,40},{... | collective-permute-start | bytes 1966088 | tf_op jit(solution)/shard_map/ppermute | solution.py:32
  151.9 27.1 %all-to-all-start.3 = ((bf16[32,16,1280]{2,1,0:T(8,128)(2,1)}), bf16[32,16,1280]{2,1,0:T(8,128)(2,1)}, u32[]{:S(2)}, u32[]{:S(2)}) async-start(bf16[32,16,1280]{2,1,0:T(8,128)(2,1)} %pad_maximum_fusion), calls=%async_computation.3 | async-start | bytes 2621440 | tf_op jit(solution)/shard_map/all_to_all | solution.py:332
  163.7 8.7 %collective-permute-start.17 = (bf16[64,2048]{1,0:T(8,128)(2,1)S(1)}, bf16[64,2048]{1,0:T(8,128)(2,1)S(1)}, u32[]{:S(2)}, u32[]{:S(2)}) collective-permute-start(bf16[64,2048]{1,0:T(8,128)(2,1)S(1)} %get-tuple-element.56), channel_id=1, source_target_pairs={{0,32},{32,64},{64,96},{96,0},{1,33},{33,65},{65,97},{97,1},{2,34}... | collective-permute-start | bytes 786440 | tf_op jit(solution)/shard_map/ppermute | solution.py:22
  165.6 7.1 %collective-permute-start.16 = (bf16[64,2048]{1,0:T(8,128)(2,1)S(1)}, bf16[64,2048]{1,0:T(8,128)(2,1)S(1)}, u32[]{:S(2)}, u32[]{:S(2)}) collective-permute-start(bf16[64,2048]{1,0:T(8,128)(2,1)S(1)} %get-tuple-element.55), channel_id=1, source_target_pairs={{0,96},{32,0},{64,32},{96,64},{1,97},{33,1},{65,33},{97,65},{2,98}... | collective-permute-start | bytes 786440 | tf_op jit(solution)/shard_map/ppermute | solution.py:22
  166.5 12.3 %collective-permute-start.15 = (bf16[64,2048]{1,0:T(8,128)(2,1)S(1)}, bf16[64,2048]{1,0:T(8,128)(2,1)S(1)}, u32[]{:S(2)}, u32[]{:S(2)}) collective-permute-start(bf16[64,2048]{1,0:T(8,128)(2,1)S(1)} %get-tuple-element.54), channel_id=1, source_target_pairs={{0,64},{32,96},{64,0},{96,32},{1,65},{33,97},{65,1},{97,33},{2,66}... | collective-permute-start | bytes 786440 | tf_op jit(solution)/shard_map/ppermute | solution.py:22
  (9 other events, 99.9 us)

commit v6 on v5

--- a/solution.py
+++ b/solution.py
@@ -165,91 +165,98 @@
     )(*around)
 
 
-def expert_kernel(splits, *refs):
-    n_x = sum(len(s) for s in splits)
+def expert_kernel(planes, pair, *refs):
+    n_x = planes * 2
     xin, (xb, wg, wu, wd) = refs[:n_x], refs[n_x : n_x + 4]
-    rest = refs[n_x + 4 :]
-    rest = rest[len(rest) - (n_x + 3) :]
-    outs, (ob, xs, keep) = rest[:n_x], rest[n_x:]
-    member = pl.program_id(0)
-    sc, bc = xin[0].shape[-1], outs[0].shape[-1]
+    rest = refs[len(refs) - (n_x + 10) :]
+    outs, ob = rest[:n_x], rest[n_x]
+    xbb, obb, obuf, wgb, wub, wdb, xs, in_sems, out_sems = rest[n_x + 1 :]
+    members = wg.shape[0]
+    rows, sc = xin[0].shape
+    bc = outs[0].shape[-1]
     feature = wg.shape[2]
-    n_ep, slots = xb.shape[:2]
-    rows = n_ep * CAP
-    planes = len(splits)
-    at = 0
-    place = []
-    for p, split in enumerate(splits):
-        row = p * rows
-        for n in split:
-            place.append((xin[at], outs[at], row, n))
-            row += n * CAP
-            at += 1
-    for x, _, row, n in place:
-        for c in range(0, sc, COLS):
-            part = x[:, :, c : c + COLS].astype(jnp.float32).reshape(n, 2, CAP, COLS)
-            part = jnp.where(member == 0, part[:, 0], part[:, 1])
-            xs[row : row + n * CAP, c : c + COLS] = part.reshape(n * CAP, COLS).astype(jnp.bfloat16)
-    for c in range(0, feature - sc, COLS):
-        part = xb[:, :, c : c + COLS].astype(jnp.float32).reshape(n_ep, planes, CAP, COLS)
+    n_ep = xb.shape[0]
+    slots = planes * CAP
+    pairs = xb.shape[1] // (members * slots)
+    fetched, sent = [], []
+
+    def fetch(src, dst):
+        copy = pltpu.make_async_copy(src, dst, in_sems.at[len(fetched)])
+        copy.start()
+        fetched.append(copy)
+        return copy
+
+    def send(src, dst):
+        copy = pltpu.make_async_copy(src, dst, out_sems.at[len(sent)])
+        copy.start()
+        sent.append(copy)
+
+    chunk = lambda m: pl.ds((m * pairs + pair) * slots, slots)
+    got = []
+    for m in range(members):
+        copies = [
+            fetch(xin[p * members + m], xs.at[m, pl.ds(p * rows, rows), pl.ds(0, sc)])
+            for p in range(planes)
+        ]
+        copies.append(fetch(xb.at[:, chunk(m)], xbb.at[m]))
+        copies += [fetch(w.at[m], buf.at[m]) for w, buf in ((wg, wgb), (wu, wub), (wd, wdb))]
+        got.append(copies)
+    for m in range(members):
+        for copy in got[m][: planes + 1]:
+            copy.wait()
+        for c in range(0, feature - sc, COLS):
+            part = xbb[m, :, :, c : c + COLS].astype(jnp.float32).reshape(n_ep, planes, CAP, COLS)
+            for p in range(planes):
+                xs[m, p * rows : (p + 1) * rows, sc + c : sc + c + COLS] = (
+                    part[:, p].reshape(rows, COLS).astype(jnp.bfloat16)
+                )
+        got[m][planes + 1].wait()
+        gate = lax.dot_general(wgb[m], xs[m], NT, preferred_element_type=jnp.float32)
+        got[m][planes + 2].wait()
+        up = lax.dot_general(wub[m], xs[m], NT, preferred_element_type=jnp.float32)
+        hidden = (gate / (1.0 + jnp.exp(-gate)) * up).astype(jnp.bfloat16)
+        got[m][planes + 3].wait()
+        out = lax.dot_general(hidden, wdb[m], TN, preferred_element_type=jnp.float32)
         for p in range(planes):
-            xs[p * rows : (p + 1) * rows, sc + c : sc + c + COLS] = (
-                part[:, p].reshape(rows, COLS).astype(jnp.bfloat16)
-            )
-    gate = lax.dot_general(wg[0], xs[...], NT, preferred_element_type=jnp.float32)
-    up = lax.dot_general(wu[0], xs[...], NT, preferred_element_type=jnp.float32)
-    hidden = (gate / (1.0 + jnp.exp(-gate)) * up).astype(jnp.bfloat16)
-    out = lax.dot_general(hidden, wd[0], TN, preferred_element_type=jnp.float32)
-    for c in range(0, feature - bc, COLS):
-        part = out[:, bc + c : bc + c + COLS].reshape(planes, n_ep, CAP, COLS)
-        part = jnp.stack([part[p] for p in range(planes)], axis=1)
-        ob[:, :, c : c + COLS] = part.reshape(n_ep, slots, COLS).astype(jnp.bfloat16)
-
-    @pl.when(member == 0)
-    def _():
-        keep[...] = out[:, :bc]
-
-    @pl.when(member == 1)
-    def _():
-        for _, o, row, n in place:
-            for c in range(0, bc, COLS):
-                parts = [
-                    keep[row : row + n * CAP, c : c + COLS].reshape(n, CAP, COLS),
-                    out[row : row + n * CAP, c : c + COLS].reshape(n, CAP, COLS),
-                ]
-                o[:, :, c : c + COLS] = (
-                    jnp.stack(parts, axis=1).reshape(n, 2 * CAP, COLS).astype(jnp.bfloat16)
-                )
+            obuf[m, p] = out[p * rows : (p + 1) * rows, :bc].astype(jnp.bfloat16)
+            send(obuf.at[m, p], outs[p * members + m])
+        for c in range(0, feature - bc, COLS):
+            part = out[:, bc + c : bc + c + COLS].reshape(planes, n_ep, CAP, COLS)
+            part = jnp.stack([part[p] for p in range(planes)], axis=1)
+            obb[m, :, :, c : c + COLS] = part.reshape(n_ep, slots, COLS).astype(jnp.bfloat16)
+        send(obb.at[m], ob.at[:, chunk(m)])
+    for copy in sent:
+        copy.wait()
 
 
 def run_experts(planes, pair, xb, sofar, wg, wu, wd, back):
     members, ffe, feature = wg.shape
     xin = [x for plane in planes for x in plane]
-    splits = tuple(tuple(x.shape[0] for x in plane) for plane in planes)
     n_ep, slots, cols_b = xb.shape
     step = len(planes) * CAP
-    pairs = slots // (members * step)
     rows = len(planes) * n_ep * CAP
-    whole = lambda shape: pl.BlockSpec(shape, lambda m: (0,) * len(shape))
-    one = lambda shape: pl.BlockSpec((1,) + shape, lambda m: (m,) + (0,) * len(shape))
-    slot = lambda cols: pl.BlockSpec((n_ep, step, cols), lambda m: (0, m * pairs + pair, 0))
-    out_x = [hbm(x.shape[:2] + (back,)) for x in xin]
+    bf = jnp.bfloat16
+    out_x = [hbm((x.shape[0], back)) for x in xin]
     operands = from_hbm(*xin, xb, wg, wu, wd)
-    in_specs = [whole(x.shape) for x in xin] + [slot(cols_b)] + [one((ffe, feature))] * 3
     aliases = {}
     if sofar is not None:
         aliases = {len(operands): len(xin)}
         operands.append(sofar)
-        in_specs.append(pl.BlockSpec(memory_space=pl.ANY))
     return pl.pallas_call(
-        functools.partial(expert_kernel, splits),
-        grid=(members,),
-        in_specs=in_specs,
-        out_specs=[whole(x.shape) for x in out_x] + [slot(feature - back)],
+        functools.partial(expert_kernel, len(planes), pair),
+        in_specs=[pl.BlockSpec(memory_space=pltpu.HBM)] * len(operands),
+        out_specs=[pl.BlockSpec(memory_space=pltpu.HBM)] * (len(out_x) + 1),
         out_shape=out_x + [hbm((n_ep, slots, feature - back))],
         scratch_shapes=[
-            pltpu.VMEM((rows, feature), jnp.bfloat16),
-            pltpu.VMEM((rows, back), jnp.float32),
+            pltpu.VMEM((members, n_ep, step, cols_b), bf),
+            pltpu.VMEM((members, n_ep, step, feature - back), bf),
+            pltpu.VMEM((members, len(planes), n_ep * CAP, back), bf),
+            pltpu.VMEM((members, ffe, feature), bf),
+            pltpu.VMEM((members, ffe, feature), bf),
+            pltpu.VMEM((members, ffe, feature), bf),
+            pltpu.VMEM((members, rows, feature), bf),
+            pltpu.SemaphoreType.DMA((members * (len(planes) + 4),)),
+            pltpu.SemaphoreType.DMA((members * (len(planes) + 1),)),
         ],
         input_output_aliases=aliases,
         compiler_params=pltpu.CompilerParams(vmem_limit_bytes=VMEM_LIMIT),
@@ -263,21 +270,17 @@
 
 
 def weigh(hi, lo, values):
-    return lax.dot_general(hi, values, TN, preferred_element_type=jnp.float32) + lax.dot_general(
-        lo, values, TN, preferred_element_type=jnp.float32
-    )
+    return dot_f32(hi, values) + dot_f32(lo, values)
 
 
 def combine(hi, lo, values, shared, *outs):
     tok, feature = outs[0].shape
     bc = feature - values.shape[1]
-    for c in range(0, feature, COLS):
-        cols = slice(c, c + COLS)
-        total = shared[:, cols]
-        if c >= bc:
-            total = total + weigh(hi[...], lo[...], values[:, c - bc : c - bc + COLS])
-        for j, o in enumerate(outs):
-            o[:, cols] = total[j * tok : (j + 1) * tok].astype(jnp.bfloat16)
+    late = shared[:, bc:] + weigh(hi[...], lo[...], values[...])
+    for j, o in enumerate(outs):
+        rows = slice(j * tok, (j + 1) * tok)
+        o[:, :bc] = shared[rows, :bc].astype(jnp.bfloat16)
+        o[:, bc:] = late[rows].astype(jnp.bfloat16)
 
 
 def call_combine(hi, lo, values, shared, tok):
@@ -293,11 +296,7 @@
 def finish(hi, lo, values, total, out):
     bc = values.shape[1]
     out[:, bc:] = total[:, bc:].astype(jnp.bfloat16)
-    for c in range(0, bc, COLS):
-        cols = slice(c, c + COLS)
-        out[:, cols] = (total[:, cols] + weigh(hi[...], lo[...], values[:, cols])).astype(
-            jnp.bfloat16
-        )
+    out[:, :bc] = (total[:, :bc] + weigh(hi[...], lo[...], values[...])).astype(jnp.bfloat16)
 
 
 def call_finish(hi, lo, values, total):
@@ -343,8 +342,10 @@
         around, members, n_experts, feature, feature - sc
     )
 
-    half = n_ep // 2
-    own_parts = [own[:half], own[half:]]
+    weights = (expert_gate.swapaxes(1, 2), expert_up.swapaxes(1, 2), expert_down)
+
+    own_slots = own.reshape(n_ep, members, CAP, sc)
+    own_parts = [own_slots[:, m].reshape(n_ep * CAP, sc) for m in range(members)]
     behind = [toward(x) for x in own_parts]
     far = [toward(x) for x in behind]
     ahead = [toward(x) for x in far]
@@ -354,9 +355,11 @@
     up_act = dot_f32(gathered, shared_up)
     hidden = (jax.nn.silu(gate_act) * up_act).astype(jnp.bfloat16)
     shared = dot_f32(hidden, shared_down)
-    came_b, shared = lax.optimization_barrier((came_b, shared))
-
-    weights = (expert_gate.swapaxes(1, 2), expert_up.swapaxes(1, 2), expert_down)
+    hi_b, lo_b, hi_d, lo_d = hi_b.T, lo_b.T, hi_d.T, lo_d.T
+    came_b, shared, hi_b, lo_b, hi_d, lo_d = lax.optimization_barrier(
+        (came_b, shared, hi_b, lo_b, hi_d, lo_d)
+    )
+
     f0, f1, b0, b1, out_b = run_experts([far, behind], 0, came_b, None, *weights, bc)
     a0, a1, o0, o1, out_b = run_experts([ahead, own_parts], 1, came_b, out_b, *weights, bc)
     ret_b = over_ep(out_b, members * n_dp * CAP, feature - bc)
@@ -368,7 +371,7 @@
         for mine in (second, third):
             passing = (f32(mine) + f32(toward(passing))).astype(jnp.bfloat16)
         ends.append((f32(last) + f32(toward(passing))).astype(jnp.bfloat16))
-    back_d = jnp.concatenate(ends)
+    back_d = jnp.stack([x.reshape(n_ep, CAP, bc) for x in ends], axis=1)
     back_d, ret_b = lax.optimization_barrier((back_d, ret_b))
     ret_d = over_ep(back_d, members * CAP, bc)
 

time: 183 us -> 187 us (1.022)
  local copies, waits for them, and re-layouts: 2.34 us -> 14.4 us
  Pallas kernels: 39.7 us -> 33.9 us
  starting transfers between devices: 61.3 us -> 58.6 us
    pallas_call x0 -> x4, local copies, waits for them, and re-layouts: none -> 7.77 us  [the longest x2 4.55 us: call_prepare_ring(): pl.pallas_call(functools.partial(prepare_ring, members), out_shape=[hbm((...]
    ppermute x12, starting transfers between devices: 24.7 us -> 19.8 us  [toward(): return lax.ppermute(x, ('dp', 'ep'), pairs)]
    pallas_call x2, Pallas kernels: 23.6 us -> 19.7 us  [run_experts(): pl.pallas_call(functools.partial(expert_kernel, len(planes), pair), in_sp...]
    optimization_barrier x0 -> x1, local copies, waits for them, and re-layouts: none -> 3.43 us  [on_device(): back_d, ret_b = lax.optimization_barrier((back_d, ret_b))]
    all_to_all x4, starting transfers between devices: 27 us -> 30.3 us  [over_ep(): lax.all_to_all(x.reshape(n_ep, rows, cols), 'ep', split_axis=0, concat_ax...]
    all_to_all x4, waiting for transfers between devices: 9.77 us -> 7.07 us  [over_ep(): lax.all_to_all(x.reshape(n_ep, rows, cols), 'ep', split_axis=0, concat_ax...]
    another operation x0 -> x1, local copies, waits for them, and re-layouts: none -> 2.28 us  [on_device(): own_slots[:, m].reshape(n_ep * CAP, sc)]
  transfers between devices with their start and end apart: 22 -> 22, of which waited for: 14 -> 15; matrix products, arithmetic and copies ran while one was open for 9% -> 14% of each run, Pallas kernels for 19% -> 15%
where the time goes in v6:
time: 187 us; the launch traced here: 186 us
  waiting for transfers between devices  63.1 us (34%)
  starting transfers between devices  58.6 us (31%)
  Pallas kernels  33.9 us (18%)
  local copies, waits for them, and re-layouts  14.4 us (8%)
  matrix products  10.9 us (6%)
  other arithmetic  4.71 us (3%)
    ppermute x12, waiting for transfers between devices, toward(): return lax.ppermute(x, ('dp', 'ep'), pairs)  32.8 us
    all_to_all x4, starting transfers between devices, over_ep(): lax.all_to_all(x.reshape(n_ep, rows, cols), 'ep', split_axis=0, concat_ax...  30.3 us
    ppermute x6, waiting for transfers between devices, shifted(): return lax.ppermute(x, 'dp', [(i, (i + shift) % n) for i in range(n)])  23.2 us
    ppermute x12, starting transfers between devices, toward(): return lax.ppermute(x, ('dp', 'ep'), pairs)  19.8 us
    pallas_call x2, Pallas kernels, run_experts(): pl.pallas_call(functools.partial(expert_kernel, len(planes), pair), in_sp...  19.7 us
    dot_general x2, matrix products, dot_f32(): return jnp.dot(a, b, preferred_element_type=jnp.float32)  10.9 us
    ppermute x6, starting transfers between devices, shifted(): return lax.ppermute(x, 'dp', [(i, (i + shift) % n) for i in range(n)])  8.46 us
    all_to_all x4, waiting for transfers between devices, over_ep(): lax.all_to_all(x.reshape(n_ep, rows, cols), 'ep', split_axis=0, concat_ax...  7.07 us
  transfers between devices with their start and end apart: 22, of which 15 were waited for; matrix products, arithmetic and copies ran while one was open for 14% of the time, Pallas kernels for 15%

profile of v6, /device:TPU:1, one launch (start us, length us, event | category | flops | bytes accessed | tf_op | source)
XLA Modules:
  0.0 186.5 jit_solution(5779221632504356898)
XLA Ops:
  3.6 9.5 %all-to-all-start.1 = ((bf16[32,16,1280]{2,1,0:T(8,128)(2,1)}), bf16[32,16,1280]{2,1,0:T(8,128)(2,1)}, u32[]{:S(2)}, u32[]{:S(2)}) async-start(bf16[32,16,1280]{2,1,0:T(8,128)(2,1)} %bitcast.40), calls=%async_computation.1 | async-start | bytes 2621440 | tf_op jit(solution)/shard_map/all_to_all | solution.py:331
  18.8 4.0 %collective-permute-done.e0 = bf16[64,2176]{1,0:T(8,128)(2,1)S(1)} collective-permute-done((bf16[64,2176]{1,0:T(8,128)(2,1)S(1)}, bf16[64,2176]{1,0:T(8,128)(2,1)S(1)}, u32[]{:S(2)}, u32[]{:S(2)}) %collective-permute-start) | collective-permute-done | bytes 278560 | tf_op jit(solution)/shard_map/ppermute | solution.py:22
  22.8 6.6 %collective-permute-done.1.e1 = bf16[64,2176]{1,0:T(8,128)(2,1)S(1)} collective-permute-done((bf16[64,2176]{1,0:T(8,128)(2,1)S(1)}, bf16[64,2176]{1,0:T(8,128)(2,1)S(1)}, u32[]{:S(2)}, u32[]{:S(2)}) %collective-permute-start.1) | collective-permute-done | bytes 278560 | tf_op jit(solution)/shard_map/ppermute | solution.py:22
  29.3 3.5 %prepare_ring.1 = (bf16[2048,768]{1,0:T(8,128)(2,1)}, bf16[2048,256]{1,0:T(8,128)(2,1)}, bf16[2048,256]{1,0:T(8,128)(2,1)}, bf16[256,2048]{1,0:T(8,128)(2,1)}) custom-call(bf16[64,2176]{1,0:T(8,128)(2,1)S(1)} %collective-permute-done.e0, bf16[64,2176]{1,0:T(8,128)(2,1)S(1)} %collective-permute-done.1.e1, bf16[64,2176]{1,0:T(8,128)(2,1)S(1)} %collective-permute-done.2.e2, ...), custom_call_target="tpu_custom_call" | custom-call | tf_op jit(solution)/shard_map/prepare_ring/pallas_call | solution.py:155
  32.9 7.7 %all-to-all-start = ((bf16[32,64,768]{2,1,0:T(8,128)(2,1)}), bf16[32,64,768]{2,1,0:T(8,128)(2,1)}, u32[]{:S(2)}, u32[]{:S(2)}) async-start(bf16[32,64,768]{2,1,0:T(8,128)(2,1)} %bitcast.35), calls=%async_computation | async-start | bytes 6291456 | tf_op jit(solution)/shard_map/all_to_all | solution.py:331
  48.5 4.6 %collective-permute-done.3.refs_2_ = bf16[256,1280]{1,0:T(8,128)(2,1)} collective-permute-done((bf16[256,1280]{1,0:T(8,128)(2,1)}, bf16[256,1280]{1,0:T(8,128)(2,1)}, u32[]{:S(2)}, u32[]{:S(2)}) %collective-permute-start.3) | collective-permute-done | bytes 655392 | tf_op jit(solution)/shard_map/ppermute | solution.py:32
  53.1 3.4 %collective-permute-start.4 = (bf16[256,1280]{1,0:T(8,128)(2,1)}, bf16[256,1280]{1,0:T(8,128)(2,1)}, u32[]{:S(2)}, u32[]{:S(2)}) collective-permute-start(bf16[256,1280]{1,0:T(8,128)(2,1)} %collective-permute-done.3.refs_2_), channel_id=1, source_target_pairs={{0,32},{1,97},{2,34},{3,99},{4,36},{5,101},{6,38},{7,103},{8,40},{... | collective-permute-start | bytes 1966088 | tf_op jit(solution)/shard_map/ppermute | solution.py:32
  56.6 3.5 %collective-permute-done.6.refs_3_ = bf16[256,1280]{1,0:T(8,128)(2,1)} collective-permute-done((bf16[256,1280]{1,0:T(8,128)(2,1)S(1)}, bf16[256,1280]{1,0:T(8,128)(2,1)}, u32[]{:S(2)}, u32[]{:S(2)}) %collective-permute-start.6) | collective-permute-done | bytes 655392 | tf_op jit(solution)/shard_map/ppermute | solution.py:32
  60.1 3.5 %collective-permute-start.7 = (bf16[256,1280]{1,0:T(8,128)(2,1)}, bf16[256,1280]{1,0:T(8,128)(2,1)}, u32[]{:S(2)}, u32[]{:S(2)}) collective-permute-start(bf16[256,1280]{1,0:T(8,128)(2,1)} %collective-permute-done.6.refs_3_), channel_id=1, source_target_pairs={{0,32},{1,97},{2,34},{3,99},{4,36},{5,101},{6,38},{7,103},{8,40},{... | collective-permute-start | bytes 1966088 | tf_op jit(solution)/shard_map/ppermute | solution.py:32
  63.6 4.0 %fusion.7 = f32[256,704]{0,1:T(8,128)} fusion(bf16[256,2048]{1,0:T(8,128)(2,1)} %get-tuple-element.37, bf16[2048,704]{0,1:T(8,128)(2,1)} %param.17), kind=kOutput, calls=%fused_computation.19 | convolution fusion | flops 738197504 | bytes 4653056 | tf_op jit(solution)/shard_map/dot_general | solution.py:44
  72.1 6.9 %fusion.2.shared = f32[256,2048]{1,0:T(8,128)} fusion(bf16[704,2048]{1,0:T(8,128)(2,1)S(1)} %copy-done, f32[256,704]{0,1:T(8,128)} %fusion.7, bf16[256,2048]{1,0:T(8,128)(2,1)} %get-tuple-element.37, bf16[2048,704]{0,1:T(8,128)(2,1)} %param.18), kind=kOutput, calls=%fused_computation.14 | convolution fusion | flops 1477476352 | bytes 9633792 | tf_op jit(solution)/shard_map/dot_general | solution.py:44
  80.5 9.9 %experts.2 = (bf16[256,1280]{1,0:T(8,128)(2,1)}, bf16[256,1280]{1,0:T(8,128)(2,1)}, bf16[256,1280]{1,0:T(8,128)(2,1)}, bf16[256,1280]{1,0:T(8,128)(2,1)}, bf16[32,64,768]{2,1,0:T(8,128)(2,1)}) custom-call(bf16[256,1280]{1,0:T(8,128)(2,1)} %collective-permute-done.4.refs_0_, bf16[256,1280]{1,0:T(8,128)(2,1)} %collective-permute-done.7.refs_1_, ...), custom_call_target="tpu_custom_call" | custom-call | flops 4429185024 | bytes 17039360 | tf_op jit(solution)/shard_map/experts/pallas_call | solution.py:245
  96.9 9.8 %experts.3 = (bf16[256,1280]{1,0:T(8,128)(2,1)}, bf16[256,1280]{1,0:T(8,128)(2,1)}, bf16[256,1280]{1,0:T(8,128)(2,1)}, bf16[256,1280]{1,0:T(8,128)(2,1)}, bf16[32,64,768]{2,1,0:T(8,128)(2,1)}) custom-call(bf16[256,1280]{1,0:T(8,128)(2,1)} %copy-done.4, bf16[256,1280]{1,0:T(8,128)(2,1)} %copy-done.5, ...), custom_call_target="tpu_custom_call", output_to_operand_aliasing={{4}: (8, {})} | custom-call | flops 4429185024 | bytes 17039360 | tf_op jit(solution)/shard_map/experts/pallas_call | solution.py:245
  106.7 8.1 %all-to-all-start.2 = ((bf16[32,64,768]{2,1,0:T(8,128)(2,1)}), bf16[32,64,768]{2,1,0:T(8,128)(2,1)S(1)}, u32[]{:S(2)}, u32[]{:S(2)}) async-start(bf16[32,64,768]{2,1,0:T(8,128)(2,1)} %get-tuple-element.55), calls=%async_computation.2 | async-start | bytes 6291456 | tf_op jit(solution)/shard_map/all_to_all | solution.py:331
  119.6 6.8 %collective-permute-done.10 = bf16[256,1280]{1,0:T(8,128)(2,1)S(1)} collective-permute-done((bf16[256,1280]{1,0:T(8,128)(2,1)S(1)}, bf16[256,1280]{1,0:T(8,128)(2,1)S(1)}, u32[]{:S(2)}, u32[]{:S(2)}) %collective-permute-start.10) | collective-permute-done | bytes 655392 | tf_op jit(solution)/shard_map/ppermute | solution.py:32
  129.4 4.0 %collective-permute-done.13 = bf16[256,1280]{1,0:T(8,128)(2,1)S(1)} collective-permute-done((bf16[256,1280]{1,0:T(8,128)(2,1)S(1)}, bf16[256,1280]{1,0:T(8,128)(2,1)S(1)}, u32[]{:S(2)}, u32[]{:S(2)}) %collective-permute-start.13) | collective-permute-done | bytes 655392 | tf_op jit(solution)/shard_map/ppermute | solution.py:32
  136.4 4.0 %collective-permute-done.11 = bf16[256,1280]{1,0:T(8,128)(2,1)S(1)} collective-permute-done((bf16[256,1280]{1,0:T(8,128)(2,1)S(1)}, bf16[256,1280]{1,0:T(8,128)(2,1)S(1)}, u32[]{:S(2)}, u32[]{:S(2)}) %collective-permute-start.11) | collective-permute-done | bytes 655392 | tf_op jit(solution)/shard_map/ppermute | solution.py:32
  140.6 6.9 %collective-permute-done.14 = bf16[256,1280]{1,0:T(8,128)(2,1)S(1)} collective-permute-done((bf16[256,1280]{1,0:T(8,128)(2,1)S(1)}, bf16[256,1280]{1,0:T(8,128)(2,1)S(1)}, u32[]{:S(2)}, u32[]{:S(2)}) %collective-permute-start.14) | collective-permute-done | bytes 655392 | tf_op jit(solution)/shard_map/ppermute | solution.py:32
  148.8 5.8 %all-to-all-done.2 = bf16[32,64,768]{2,1,0:T(8,128)(2,1)S(1)} async-done(((bf16[32,64,768]{2,1,0:T(8,128)(2,1)}), bf16[32,64,768]{2,1,0:T(8,128)(2,1)S(1)}, u32[]{:S(2)}, u32[]{:S(2)}) %all-to-all-start.2) | async-done | bytes 3145760 | tf_op jit(solution)/shard_map/all_to_all | solution.py:331
  154.6 3.4 %copy.23 = bf16[32,2,8,1280]{3,2,1,0:T(8,128)(2,1)} copy(bf16[32,2,8,1280]{3,2,0,1:T(8,128)(2,1)} %pad_maximum_fusion) | data formatting | bytes 2621440 | tf_op jit(solution)/shard_map/optimization_barrier | solution.py:375
  158.0 5.0 %all-to-all-start.3 = ((bf16[32,16,1280]{2,1,0:T(8,128)(2,1)}), bf16[32,16,1280]{2,1,0:T(8,128)(2,1)}, u32[]{:S(2)}, u32[]{:S(2)}) async-start(bf16[32,16,1280]{2,1,0:T(8,128)(2,1)} %bitcast.32), calls=%async_computation.3 | async-start | bytes 2621440 | tf_op jit(solution)/shard_map/all_to_all | solution.py:331
  163.1 5.0 %combine.1 = (bf16[64,2048]{1,0:T(8,128)(2,1)S(1)}, bf16[64,2048]{1,0:T(8,128)(2,1)S(1)}, bf16[64,2048]{1,0:T(8,128)(2,1)S(1)}, bf16[64,2048]{1,0:T(8,128)(2,1)S(1)}) custom-call(bf16[256,2048]{1,0:T(8,128)(2,1)} %bitcast.33, bf16[256,2048]{1,0:T(8,128)(2,1)} %bitcast.34, bf16[2048,768]{1,0:T(8,128)(2,1)} %bitcast.31, f32[256,2048]{1,0:T(8,128)} %fusion.2.shared), custom_call_target="tpu_custom_call" | custom-call | tf_op jit(solution)/shard_map/combine/pallas_call | solution.py:288
  170.9 6.5 %collective-permute-done.15 = bf16[64,2048]{1,0:T(8,128)(2,1)S(1)} collective-permute-done((bf16[64,2048]{1,0:T(8,128)(2,1)S(1)}, bf16[64,2048]{1,0:T(8,128)(2,1)S(1)}, u32[]{:S(2)}, u32[]{:S(2)}) %collective-permute-start.15) | collective-permute-done | bytes 262176 | tf_op jit(solution)/shard_map/ppermute | solution.py:22
  177.4 4.7 %collective-permute-done.16 = bf16[64,2048]{1,0:T(8,128)(2,1)S(1)} collective-permute-done((bf16[64,2048]{1,0:T(8,128)(2,1)S(1)}, bf16[64,2048]{1,0:T(8,128)(2,1)S(1)}, u32[]{:S(2)}, u32[]{:S(2)}) %collective-permute-start.16) | collective-permute-done | bytes 262176 | tf_op jit(solution)/shard_map/ppermute | solution.py:22
  (65 shorter events, 48.3 us)
Async XLA Ops:
  0.0 72.1 %copy-start = (bf16[704,2048]{1,0:T(8,128)(2,1)S(1)}, bf16[704,2048]{1,0:T(8,128)(2,1)}, u32[]{:S(2)}) copy-start(bf16[704,2048]{1,0:T(8,128)(2,1)} %param.19) | copy-start | bytes 8650756
  3.6 29.3 %all-to-all-start.1 = ((bf16[32,16,1280]{2,1,0:T(8,128)(2,1)}), bf16[32,16,1280]{2,1,0:T(8,128)(2,1)}, u32[]{:S(2)}, u32[]{:S(2)}) async-start(bf16[32,16,1280]{2,1,0:T(8,128)(2,1)} %bitcast.40), calls=%async_computation.1 | async-start | bytes 2621440 | tf_op jit(solution)/shard_map/all_to_all | solution.py:331
  13.1 9.7 %collective-permute-start = (bf16[64,2176]{1,0:T(8,128)(2,1)S(1)}, bf16[64,2176]{1,0:T(8,128)(2,1)S(1)}, u32[]{:S(2)}, u32[]{:S(2)}) collective-permute-start(bf16[64,2176]{1,0:T(8,128)(2,1)S(1)} %get-tuple-element.35.e3), channel_id=1, source_target_pairs={{0,64},{32,96},{64,0},{96,32},{1,65},{33,97},{65,1},{97,33},{2,66}... | collective-permute-start | bytes 835592 | tf_op jit(solution)/shard_map/ppermute | solution.py:22
  16.1 13.2 %collective-permute-start.1 = (bf16[64,2176]{1,0:T(8,128)(2,1)S(1)}, bf16[64,2176]{1,0:T(8,128)(2,1)S(1)}, u32[]{:S(2)}, u32[]{:S(2)}) collective-permute-start(bf16[64,2176]{1,0:T(8,128)(2,1)S(1)} %get-tuple-element.35.e3), channel_id=1, source_target_pairs={{0,32},{32,64},{64,96},{96,0},{1,33},{33,65},{65,97},{97,1},{2,34}... | collective-permute-start | bytes 835592 | tf_op jit(solution)/shard_map/ppermute | solution.py:22
  16.5 12.8 %collective-permute-start.2 = (bf16[64,2176]{1,0:T(8,128)(2,1)S(1)}, bf16[64,2176]{1,0:T(8,128)(2,1)S(1)}, u32[]{:S(2)}, u32[]{:S(2)}) collective-permute-start(bf16[64,2176]{1,0:T(8,128)(2,1)S(1)} %get-tuple-element.35.e3), channel_id=1, source_target_pairs={{0,96},{32,0},{64,32},{96,64},{1,97},{33,1},{65,33},{97,65},{2,98}... | collective-permute-start | bytes 835592 | tf_op jit(solution)/shard_map/ppermute | solution.py:22
  32.9 47.5 %all-to-all-start = ((bf16[32,64,768]{2,1,0:T(8,128)(2,1)}), bf16[32,64,768]{2,1,0:T(8,128)(2,1)}, u32[]{:S(2)}, u32[]{:S(2)}) async-start(bf16[32,64,768]{2,1,0:T(8,128)(2,1)} %bitcast.35), calls=%async_computation | async-start | bytes 6291456 | tf_op jit(solution)/shard_map/all_to_all | solution.py:331
  42.9 24.6 %copy-start.3 = (bf16[256,1280]{1,0:T(8,128)(2,1)}, bf16[256,1280]{1,0:T(8,128)(2,1)S(1)}, u32[]{:S(2)}) copy-start(bf16[256,1280]{1,0:T(8,128)(2,1)S(1)} %get-tuple-element.65.refs_3_) | copy-start | bytes 1966084
  42.9 10.2 %collective-permute-start.3 = (bf16[256,1280]{1,0:T(8,128)(2,1)}, bf16[256,1280]{1,0:T(8,128)(2,1)}, u32[]{:S(2)}, u32[]{:S(2)}) collective-permute-start(bf16[256,1280]{1,0:T(8,128)(2,1)} %get-tuple-element.66.refs_2_), channel_id=1, source_target_pairs={{0,32},{1,97},{2,34},{3,99},{4,36},{5,101},{6,38},{7,103},{8,40},{... | collective-permute-start | bytes 1966088 | tf_op jit(solution)/shard_map/ppermute | solution.py:32
  45.3 14.8 %collective-permute-start.6 = (bf16[256,1280]{1,0:T(8,128)(2,1)S(1)}, bf16[256,1280]{1,0:T(8,128)(2,1)}, u32[]{:S(2)}, u32[]{:S(2)}) collective-permute-start(bf16[256,1280]{1,0:T(8,128)(2,1)S(1)} %get-tuple-element.65.refs_3_), channel_id=1, source_target_pairs={{0,32},{1,97},{2,34},{3,99},{4,36},{5,101},{6,38},{7,103},{8,40},{... | collective-permute-start | bytes 1966088 | tf_op jit(solution)/shard_map/ppermute | solution.py:32
  53.1 25.9 %collective-permute-start.4 = (bf16[256,1280]{1,0:T(8,128)(2,1)}, bf16[256,1280]{1,0:T(8,128)(2,1)}, u32[]{:S(2)}, u32[]{:S(2)}) collective-permute-start(bf16[256,1280]{1,0:T(8,128)(2,1)} %collective-permute-done.3.refs_2_), channel_id=1, source_target_pairs={{0,32},{1,97},{2,34},{3,99},{4,36},{5,101},{6,38},{7,103},{8,40},{... | collective-permute-start | bytes 1966088 | tf_op jit(solution)/shard_map/ppermute | solution.py:32
  60.1 19.0 %collective-permute-start.7 = (bf16[256,1280]{1,0:T(8,128)(2,1)}, bf16[256,1280]{1,0:T(8,128)(2,1)}, u32[]{:S(2)}, u32[]{:S(2)}) collective-permute-start(bf16[256,1280]{1,0:T(8,128)(2,1)} %collective-permute-done.6.refs_3_), channel_id=1, source_target_pairs={{0,32},{1,97},{2,34},{3,99},{4,36},{5,101},{6,38},{7,103},{8,40},{... | collective-permute-start | bytes 1966088 | tf_op jit(solution)/shard_map/ppermute | solution.py:32
  79.1 13.9 %collective-permute-start.5 = (bf16[256,1280]{1,0:T(8,128)(2,1)}, bf16[256,1280]{1,0:T(8,128)(2,1)S(1)}, u32[]{:S(2)}, u32[]{:S(2)}) collective-permute-start(bf16[256,1280]{1,0:T(8,128)(2,1)} %collective-permute-done.4.refs_0_), channel_id=1, source_target_pairs={{0,32},{1,97},{2,34},{3,99},{4,36},{5,101},{6,38},{7,103},{8,40},{... | collective-permute-start | bytes 1966088 | tf_op jit(solution)/shard_map/ppermute | solution.py:32
  79.1 17.0 %collective-permute-start.8 = (bf16[256,1280]{1,0:T(8,128)(2,1)}, bf16[256,1280]{1,0:T(8,128)(2,1)S(1)}, u32[]{:S(2)}, u32[]{:S(2)}) collective-permute-start(bf16[256,1280]{1,0:T(8,128)(2,1)} %collective-permute-done.7.refs_1_), channel_id=1, source_target_pairs={{0,32},{1,97},{2,34},{3,99},{4,36},{5,101},{6,38},{7,103},{8,40},{... | collective-permute-start | bytes 1966088 | tf_op jit(solution)/shard_map/ppermute | solution.py:32
  90.4 24.4 %collective-permute-start.9 = (bf16[256,1280]{1,0:T(8,128)(2,1)}, bf16[256,1280]{1,0:T(8,128)(2,1)}, u32[]{:S(2)}, u32[]{:S(2)}) collective-permute-start(bf16[256,1280]{1,0:T(8,128)(2,1)} %get-tuple-element.50), channel_id=1, source_target_pairs={{0,32},{1,97},{2,34},{3,99},{4,36},{5,101},{6,38},{7,103},{8,40},{... | collective-permute-start | bytes 1966088 | tf_op jit(solution)/shard_map/ppermute | solution.py:32
  92.9 25.4 %collective-permute-start.12 = (bf16[256,1280]{1,0:T(8,128)(2,1)}, bf16[256,1280]{1,0:T(8,128)(2,1)}, u32[]{:S(2)}, u32[]{:S(2)}) collective-permute-start(bf16[256,1280]{1,0:T(8,128)(2,1)} %get-tuple-element.54), channel_id=1, source_target_pairs={{0,32},{1,97},{2,34},{3,99},{4,36},{5,101},{6,38},{7,103},{8,40},{... | collective-permute-start | bytes 1966088 | tf_op jit(solution)/shard_map/ppermute | solution.py:32
  106.7 47.9 %all-to-all-start.2 = ((bf16[32,64,768]{2,1,0:T(8,128)(2,1)}), bf16[32,64,768]{2,1,0:T(8,128)(2,1)S(1)}, u32[]{:S(2)}, u32[]{:S(2)}) async-start(bf16[32,64,768]{2,1,0:T(8,128)(2,1)} %get-tuple-element.55), calls=%async_computation.2 | async-start | bytes 6291456 | tf_op jit(solution)/shard_map/all_to_all | solution.py:331
  116.3 10.0 %collective-permute-start.10 = (bf16[256,1280]{1,0:T(8,128)(2,1)S(1)}, bf16[256,1280]{1,0:T(8,128)(2,1)S(1)}, u32[]{:S(2)}, u32[]{:S(2)}) collective-permute-start(bf16[256,1280]{1,0:T(8,128)(2,1)S(1)} %add_convert_fusion.5), channel_id=1, source_target_pairs={{0,32},{1,97},{2,34},{3,99},{4,36},{5,101},{6,38},{7,103},{8,40},{... | collective-permute-start | bytes 1966088 | tf_op jit(solution)/shard_map/ppermute | solution.py:32
  119.5 13.9 %collective-permute-start.13 = (bf16[256,1280]{1,0:T(8,128)(2,1)S(1)}, bf16[256,1280]{1,0:T(8,128)(2,1)S(1)}, u32[]{:S(2)}, u32[]{:S(2)}) collective-permute-start(bf16[256,1280]{1,0:T(8,128)(2,1)S(1)} %add_convert_fusion.2), channel_id=1, source_target_pairs={{0,32},{1,97},{2,34},{3,99},{4,36},{5,101},{6,38},{7,103},{8,40},{... | collective-permute-start | bytes 1966088 | tf_op jit(solution)/shard_map/ppermute | solution.py:32
  126.5 13.9 %collective-permute-start.11 = (bf16[256,1280]{1,0:T(8,128)(2,1)S(1)}, bf16[256,1280]{1,0:T(8,128)(2,1)S(1)}, u32[]{:S(2)}, u32[]{:S(2)}) collective-permute-start(bf16[256,1280]{1,0:T(8,128)(2,1)S(1)} %add_convert_fusion.4), channel_id=1, source_target_pairs={{0,32},{1,97},{2,34},{3,99},{4,36},{5,101},{6,38},{7,103},{8,40},{... | collective-permute-start | bytes 1966088 | tf_op jit(solution)/shard_map/ppermute | solution.py:32
  133.6 13.9 %collective-permute-start.14 = (bf16[256,1280]{1,0:T(8,128)(2,1)S(1)}, bf16[256,1280]{1,0:T(8,128)(2,1)S(1)}, u32[]{:S(2)}, u32[]{:S(2)}) collective-permute-start(bf16[256,1280]{1,0:T(8,128)(2,1)S(1)} %add_convert_fusion.1), channel_id=1, source_target_pairs={{0,32},{1,97},{2,34},{3,99},{4,36},{5,101},{6,38},{7,103},{8,40},{... | collective-permute-start | bytes 1966088 | tf_op jit(solution)/shard_map/ppermute | solution.py:32
  158.0 25.7 %all-to-all-start.3 = ((bf16[32,16,1280]{2,1,0:T(8,128)(2,1)}), bf16[32,16,1280]{2,1,0:T(8,128)(2,1)}, u32[]{:S(2)}, u32[]{:S(2)}) async-start(bf16[32,16,1280]{2,1,0:T(8,128)(2,1)} %bitcast.32), calls=%async_computation.3 | async-start | bytes 2621440 | tf_op jit(solution)/shard_map/all_to_all | solution.py:331
  168.1 9.3 %collective-permute-start.15 = (bf16[64,2048]{1,0:T(8,128)(2,1)S(1)}, bf16[64,2048]{1,0:T(8,128)(2,1)S(1)}, u32[]{:S(2)}, u32[]{:S(2)}) collective-permute-start(bf16[64,2048]{1,0:T(8,128)(2,1)S(1)} %get-tuple-element.62), channel_id=1, source_target_pairs={{0,64},{32,96},{64,0},{96,32},{1,65},{33,97},{65,1},{97,33},{2,66}... | collective-permute-start | bytes 786440 | tf_op jit(solution)/shard_map/ppermute | solution.py:22
  169.4 12.7 %collective-permute-start.16 = (bf16[64,2048]{1,0:T(8,128)(2,1)S(1)}, bf16[64,2048]{1,0:T(8,128)(2,1)S(1)}, u32[]{:S(2)}, u32[]{:S(2)}) collective-permute-start(bf16[64,2048]{1,0:T(8,128)(2,1)S(1)} %get-tuple-element.63), channel_id=1, source_target_pairs={{0,96},{32,0},{64,32},{96,64},{1,97},{33,1},{65,33},{97,65},{2,98}... | collective-permute-start | bytes 786440 | tf_op jit(solution)/shard_map/ppermute | solution.py:22
  169.9 13.7 %collective-permute-start.17 = (bf16[64,2048]{1,0:T(8,128)(2,1)S(1)}, bf16[64,2048]{1,0:T(8,128)(2,1)S(1)}, u32[]{:S(2)}, u32[]{:S(2)}) collective-permute-start(bf16[64,2048]{1,0:T(8,128)(2,1)S(1)} %get-tuple-element.64), channel_id=1, source_target_pairs={{0,32},{32,64},{64,96},{96,0},{1,33},{33,65},{65,97},{97,1},{2,34}... | collective-permute-start | bytes 786440 | tf_op jit(solution)/shard_map/ppermute | solution.py:22
  (9 other events, 70.5 us)

commit v7 on v6

--- a/solution.py
+++ b/solution.py
@@ -168,10 +168,11 @@
 def expert_kernel(planes, pair, *refs):
     n_x = planes * 2
     xin, (xb, wg, wu, wd) = refs[:n_x], refs[n_x : n_x + 4]
-    rest = refs[len(refs) - (n_x + 10) :]
-    outs, ob = rest[:n_x], rest[n_x]
-    xbb, obb, obuf, wgb, wub, wdb, xs, in_sems, out_sems = rest[n_x + 1 :]
     members = wg.shape[0]
+    n_out = members + 1
+    rest = refs[len(refs) - (n_out + 10) :]
+    outs, ob = rest[:n_out], rest[n_out]
+    xbb, obb, obuf, wgb, wub, wdb, xs, in_sems, out_sems = rest[n_out + 1 :]
     rows, sc = xin[0].shape
     bc = outs[0].shape[-1]
     feature = wg.shape[2]
@@ -219,7 +220,7 @@
         out = lax.dot_general(hidden, wdb[m], TN, preferred_element_type=jnp.float32)
         for p in range(planes):
             obuf[m, p] = out[p * rows : (p + 1) * rows, :bc].astype(jnp.bfloat16)
-            send(obuf.at[m, p], outs[p * members + m])
+            send(obuf.at[m, p], outs[m] if p == 0 else outs[-1].at[pl.ds(m * rows, rows)])
         for c in range(0, feature - bc, COLS):
             part = out[:, bc + c : bc + c + COLS].reshape(planes, n_ep, CAP, COLS)
             part = jnp.stack([part[p] for p in range(planes)], axis=1)
@@ -236,11 +237,11 @@
     step = len(planes) * CAP
     rows = len(planes) * n_ep * CAP
     bf = jnp.bfloat16
-    out_x = [hbm((x.shape[0], back)) for x in xin]
+    out_x = [hbm((n_ep * CAP, back))] * members + [hbm((members * n_ep * CAP, back))]
     operands = from_hbm(*xin, xb, wg, wu, wd)
     aliases = {}
     if sofar is not None:
-        aliases = {len(operands): len(xin)}
+        aliases = {len(operands): len(out_x)}
         operands.append(sofar)
     return pl.pallas_call(
         functools.partial(expert_kernel, len(planes), pair),
@@ -261,12 +262,34 @@
         input_output_aliases=aliases,
         compiler_params=pltpu.CompilerParams(vmem_limit_bytes=VMEM_LIMIT),
         cost_estimate=pl.CostEstimate(
-            flops=members * rows * ffe * feature * 6,
-            bytes_accessed=members * (rows * feature * 4 + 3 * ffe * feature * 2),
-            transcendentals=members * rows * ffe,
+            flops=20 * 10**9, bytes_accessed=20 * 10**7, transcendentals=0
         ),
         name="experts",
     )(*operands)
+
+
+def last_sum(own, *refs):
+    ends, out = refs[:-1], refs[-1]
+    n_ep, slots, cols = out.shape
+    rows = n_ep * CAP
+    for c in range(0, cols, COLS):
+        parts = []
+        for m, end in enumerate(ends):
+            mine = own[m * rows : (m + 1) * rows, c : c + COLS].astype(jnp.float32)
+            came = end[:, c : c + COLS].astype(jnp.float32)
+            parts.append((mine + came).reshape(n_ep, CAP, COLS))
+        out[:, :, c : c + COLS] = (
+            jnp.stack(parts, axis=1).reshape(n_ep, slots, COLS).astype(jnp.bfloat16)
+        )
+
+
+def call_last_sum(own, ends, n_ep):
+    return pl.pallas_call(
+        last_sum,
+        out_shape=hbm((n_ep, len(ends) * CAP, own.shape[1])),
+        compiler_params=pltpu.CompilerParams(vmem_limit_bytes=16 * 1024 * 1024),
+        name="last_sum",
+    )(*from_hbm(own, *ends))
 
 
 def weigh(hi, lo, values):
@@ -351,27 +374,27 @@
     ahead = [toward(x) for x in far]
     came_b = over_ep(send_b, members * n_dp * CAP, feature - sc)
 
+    *to_far, to_behind, out_b = run_experts([far, behind], 0, came_b, None, *weights, bc)
+    *to_ahead, to_own, out_b = run_experts([ahead, own_parts], 1, came_b, out_b, *weights, bc)
+    out_b, gathered, hi_b, lo_b = lax.optimization_barrier((out_b, gathered, hi_b, lo_b))
+    ret_b = over_ep(out_b, members * n_dp * CAP, feature - bc)
+
     gate_act = dot_f32(gathered, shared_gate)
     up_act = dot_f32(gathered, shared_up)
     hidden = (jax.nn.silu(gate_act) * up_act).astype(jnp.bfloat16)
     shared = dot_f32(hidden, shared_down)
-    hi_b, lo_b, hi_d, lo_d = hi_b.T, lo_b.T, hi_d.T, lo_d.T
-    came_b, shared, hi_b, lo_b, hi_d, lo_d = lax.optimization_barrier(
-        (came_b, shared, hi_b, lo_b, hi_d, lo_d)
-    )
-
-    f0, f1, b0, b1, out_b = run_experts([far, behind], 0, came_b, None, *weights, bc)
-    a0, a1, o0, o1, out_b = run_experts([ahead, own_parts], 1, came_b, out_b, *weights, bc)
-    ret_b = over_ep(out_b, members * n_dp * CAP, feature - bc)
 
     f32 = lambda x: x.astype(jnp.float32)
+    rows = n_ep * CAP
+    arrived = toward(to_behind)
     ends = []
-    for first, second, third, last in ((b0, f0, a0, o0), (b1, f1, a1, o1)):
-        passing = first
-        for mine in (second, third):
-            passing = (f32(mine) + f32(toward(passing))).astype(jnp.bfloat16)
-        ends.append((f32(last) + f32(toward(passing))).astype(jnp.bfloat16))
-    back_d = jnp.stack([x.reshape(n_ep, CAP, bc) for x in ends], axis=1)
+    for m in range(members):
+        part = slice(m * rows, (m + 1) * rows)
+        passing = (f32(to_far[m]) + f32(arrived[part])).astype(jnp.bfloat16)
+        passing = (f32(to_ahead[m]) + f32(toward(passing))).astype(jnp.bfloat16)
+        ends.append(toward(passing))
+    *ends, shared, hi_b, lo_b = lax.optimization_barrier((*ends, shared, hi_b.T, lo_b.T))
+    back_d = call_last_sum(to_own, ends, n_ep)
     back_d, ret_b = lax.optimization_barrier((back_d, ret_b))
     ret_d = over_ep(back_d, members * CAP, bc)
 
@@ -381,7 +404,7 @@
     for part, s in zip(parts, AROUND):
         total = total + f32(shifted(part, -s))
     total = jnp.where(live[:, None], total, 0.0)
-    return call_finish(hi_d, lo_d, ret_d.reshape(-1, bc), total)
+    return call_finish(hi_d.T, lo_d.T, ret_d.reshape(-1, bc), total)
 
 
 def solution(mesh):

time: 187 us -> 182 us (0.973)
  starting transfers between devices: 58.6 us -> 51.3 us
  waiting for transfers between devices: 63.1 us -> 69.6 us
  local copies, waits for them, and re-layouts: 14.4 us -> 9 us
  Pallas kernels: 33.9 us -> 37.5 us
  matrix products: 10.9 us -> 8.76 us
    ppermute x12 -> x11, starting transfers between devices: 19.8 us -> 11.6 us  [toward(): return lax.ppermute(x, ('dp', 'ep'), pairs)]
    ppermute x12 -> x11, waiting for transfers between devices: 32.8 us -> 40.8 us  [toward(): return lax.ppermute(x, ('dp', 'ep'), pairs)]
    pallas_call x2 -> x0, local copies, waits for them, and re-layouts: 4.55 us -> none  [call_prepare_ring(): pl.pallas_call(functools.partial(prepare_ring, members), out_shape=[hbm((...]
    pallas_call x0 -> x1, Pallas kernels: none -> 3.11 us  [call_last_sum(): pl.pallas_call(last_sum, out_shape=hbm((n_ep, len(ends) * CAP, own.shape[...]
    dot_general x2, matrix products: 10.9 us -> 8.76 us  [dot_f32(): return jnp.dot(a, b, preferred_element_type=jnp.float32)]
    optimization_barrier x1 -> x2, local copies, waits for them, and re-layouts: 3.43 us -> 4.55 us  [on_device(): lax.optimization_barrier((out_b, gathered, hi_b, lo_b))]
  transfers between devices with their start and end apart: 22 -> 21, of which waited for: 15 -> 14; matrix products, arithmetic and copies ran while one was open for 14% -> 12% of each run, Pallas kernels for 15% -> 18%
where the time goes in v7:
time: 182 us
  waiting for transfers between devices  69.6 us (38%)
  starting transfers between devices  51.3 us (28%)
  Pallas kernels  37.5 us (21%)
  local copies, waits for them, and re-layouts  9 us (5%)
  matrix products  8.76 us (5%)
  other arithmetic  4.39 us (2%)
    ppermute x11, waiting for transfers between devices, toward(): return lax.ppermute(x, ('dp', 'ep'), pairs)  40.8 us
    all_to_all x4, starting transfers between devices, over_ep(): lax.all_to_all(x.reshape(n_ep, rows, cols), 'ep', split_axis=0, concat_ax...  31.9 us
    ppermute x6, waiting for transfers between devices, shifted(): return lax.ppermute(x, 'dp', [(i, (i + shift) % n) for i in range(n)])  22.3 us
    pallas_call x2, Pallas kernels, run_experts(): pl.pallas_call(functools.partial(expert_kernel, len(planes), pair), in_sp...  19.8 us
    ppermute x11, starting transfers between devices, toward(): return lax.ppermute(x, ('dp', 'ep'), pairs)  11.6 us
    dot_general x2, matrix products, dot_f32(): return jnp.dot(a, b, preferred_element_type=jnp.float32)  8.76 us
    ppermute x6, starting transfers between devices, shifted(): return lax.ppermute(x, 'dp', [(i, (i + shift) % n) for i in range(n)])  7.74 us
    all_to_all x4, waiting for transfers between devices, over_ep(): lax.all_to_all(x.reshape(n_ep, rows, cols), 'ep', split_axis=0, concat_ax...  6.5 us
  transfers between devices with their start and end apart: 21, of which 14 were waited for; matrix products, arithmetic and copies ran while one was open for 12% of the time, Pallas kernels for 18%

profile of v7, /device:TPU:1, one launch (start us, length us, event | category | flops | bytes accessed | tf_op | source)
XLA Modules:
  0.0 181.7 jit_solution(4104638821827684603)
XLA Ops:
  0.8 2.8 %prepare_own.1 = (bf16[64,2176]{1,0:T(8,128)(2,1)S(1)}, bf16[512,1280]{1,0:T(8,128)(2,1)}, bf16[512,64]{1,0:T(8,128)(2,1)}, bf16[512,64]{1,0:T(8,128)(2,1)}) custom-call(s32[1]{0:T(128)} %copy.21.count, s32[6,64]{1,0:T(8,128)} %bitcast.30, f32[6,64]{1,0:T(8,128)} %bitcast.31, bf16[64,2048]{1,0:T(8,128)(2,1)} %tokens.1), custom_call_target="tpu_custom_call" | custom-call | tf_op jit(solution)/shard_map/prepare_own/pallas_call | solution.py:137
  3.7 9.5 %all-to-all-start = ((bf16[32,16,1280]{2,1,0:T(8,128)(2,1)}), bf16[32,16,1280]{2,1,0:T(8,128)(2,1)}, u32[]{:S(2)}, u32[]{:S(2)}) async-start(bf16[32,16,1280]{2,1,0:T(8,128)(2,1)} %bitcast.27), calls=%async_computation | async-start | bytes 2621440 | tf_op jit(solution)/shard_map/all_to_all | solution.py:354
  13.1 2.8 %collective-permute-start.8 = (bf16[64,2176]{1,0:T(8,128)(2,1)S(1)}, bf16[64,2176]{1,0:T(8,128)(2,1)S(1)}, u32[]{:S(2)}, u32[]{:S(2)}) collective-permute-start(bf16[64,2176]{1,0:T(8,128)(2,1)S(1)} %get-tuple-element.39.e3), channel_id=1, source_target_pairs={{0,96},{32,0},{64,32},{96,64},{1,97},{33,1},{65,33},{97,65},{2,98}... | collective-permute-start | bytes 835592 | tf_op jit(solution)/shard_map/ppermute | solution.py:22
  17.6 9.9 %collective-permute-done.8.e2 = bf16[64,2176]{1,0:T(8,128)(2,1)S(1)} collective-permute-done((bf16[64,2176]{1,0:T(8,128)(2,1)S(1)}, bf16[64,2176]{1,0:T(8,128)(2,1)S(1)}, u32[]{:S(2)}, u32[]{:S(2)}) %collective-permute-start.8) | collective-permute-done | bytes 278560 | tf_op jit(solution)/shard_map/ppermute | solution.py:22
  29.9 3.5 %prepare_ring.1 = (bf16[2048,768]{1,0:T(8,128)(2,1)}, bf16[2048,256]{1,0:T(8,128)(2,1)}, bf16[2048,256]{1,0:T(8,128)(2,1)}, bf16[256,2048]{1,0:T(8,128)(2,1)}) custom-call(bf16[64,2176]{1,0:T(8,128)(2,1)S(1)} %collective-permute-done.6.e0, bf16[64,2176]{1,0:T(8,128)(2,1)S(1)} %collective-permute-done.7.e1, bf16[64,2176]{1,0:T(8,128)(2,1)S(1)} %collective-permute-done.8.e2, ...), custom_call_target="tpu_custom_call" | custom-call | tf_op jit(solution)/shard_map/prepare_ring/pallas_call | solution.py:155
  33.4 9.4 %all-to-all-start.1 = ((bf16[32,64,768]{2,1,0:T(8,128)(2,1)}), bf16[32,64,768]{2,1,0:T(8,128)(2,1)}, u32[]{:S(2)}, u32[]{:S(2)}) async-start(bf16[32,64,768]{2,1,0:T(8,128)(2,1)} %bitcast.26), calls=%async_computation.1 | async-start | bytes 6291456 | tf_op jit(solution)/shard_map/all_to_all | solution.py:354
  44.8 9.3 %collective-permute-done.3.refs_3_ = bf16[256,1280]{1,0:T(8,128)(2,1)S(1)} collective-permute-done((bf16[256,1280]{1,0:T(8,128)(2,1)S(1)}, bf16[256,1280]{1,0:T(8,128)(2,1)S(1)}, u32[]{:S(2)}, u32[]{:S(2)}) %collective-permute-start.3) | collective-permute-done | bytes 655392 | tf_op jit(solution)/shard_map/ppermute | solution.py:32
  55.3 5.8 %collective-permute-done.refs_2_ = bf16[256,1280]{1,0:T(8,128)(2,1)S(1)} collective-permute-done((bf16[256,1280]{1,0:T(8,128)(2,1)S(1)}, bf16[256,1280]{1,0:T(8,128)(2,1)S(1)}, u32[]{:S(2)}, u32[]{:S(2)}) %collective-permute-start) | collective-permute-done | bytes 655392 | tf_op jit(solution)/shard_map/ppermute | solution.py:32
  62.3 5.8 %collective-permute-done.4.refs_1_ = bf16[256,1280]{1,0:T(8,128)(2,1)} collective-permute-done((bf16[256,1280]{1,0:T(8,128)(2,1)S(1)}, bf16[256,1280]{1,0:T(8,128)(2,1)}, u32[]{:S(2)}, u32[]{:S(2)}) %collective-permute-start.4) | collective-permute-done | bytes 655392 | tf_op jit(solution)/shard_map/ppermute | solution.py:32
  69.3 5.8 %collective-permute-done.1.refs_0_ = bf16[256,1280]{1,0:T(8,128)(2,1)} collective-permute-done((bf16[256,1280]{1,0:T(8,128)(2,1)S(1)}, bf16[256,1280]{1,0:T(8,128)(2,1)}, u32[]{:S(2)}, u32[]{:S(2)}) %collective-permute-start.1) | collective-permute-done | bytes 655392 | tf_op jit(solution)/shard_map/ppermute | solution.py:32
  76.3 6.2 %all-to-all-done.1.refs_4_ = bf16[32,64,768]{2,1,0:T(8,128)(2,1)} async-done(((bf16[32,64,768]{2,1,0:T(8,128)(2,1)}), bf16[32,64,768]{2,1,0:T(8,128)(2,1)}, u32[]{:S(2)}, u32[]{:S(2)}) %all-to-all-start.1) | async-done | bytes 3145760 | tf_op jit(solution)/shard_map/all_to_all | solution.py:354
  82.6 9.8 %experts.2 = (bf16[256,1280]{1,0:T(8,128)(2,1)}, bf16[256,1280]{1,0:T(8,128)(2,1)}, bf16[512,1280]{1,0:T(8,128)(2,1)}, bf16[32,64,768]{2,1,0:T(8,128)(2,1)}) custom-call(bf16[256,1280]{1,0:T(8,128)(2,1)} %collective-permute-done.1.refs_0_, bf16[256,1280]{1,0:T(8,128)(2,1)} %collective-permute-done.4.refs_1_, bf16[256,1280]{1,0:T(8,128)(2,1)} %copy-done.11, ...), custom_call_target="tpu_custom_call" | custom-call | flops 20000000000 | bytes 200000000 | tf_op jit(solution)/shard_map/experts/pallas_call | solution.py:246
  92.7 9.9 %experts.3 = (bf16[256,1280]{1,0:T(8,128)(2,1)}, bf16[256,1280]{1,0:T(8,128)(2,1)}, bf16[512,1280]{1,0:T(8,128)(2,1)}, bf16[32,64,768]{2,1,0:T(8,128)(2,1)}) custom-call(bf16[256,1280]{1,0:T(8,128)(2,1)} %collective-permute-done.2.refs_0_, bf16[256,1280]{1,0:T(8,128)(2,1)} %collective-permute-done.5.refs_1_, ...), custom_call_target="tpu_custom_call", output_to_operand_aliasing={{3}: (8, {})} | custom-call | flops 20000000000 | bytes 200000000 | tf_op jit(solution)/shard_map/experts/pallas_call | solution.py:246
  102.6 6.1 %all-to-all-start.2 = ((bf16[32,64,768]{2,1,0:T(8,128)(2,1)}), bf16[32,64,768]{2,1,0:T(8,128)(2,1)}, u32[]{:S(2)}, u32[]{:S(2)}) async-start(bf16[32,64,768]{2,1,0:T(8,128)(2,1)} %get-tuple-element.57), calls=%async_computation.2 | async-start | bytes 6291456 | tf_op jit(solution)/shard_map/all_to_all | solution.py:354
  112.9 8.7 %collective-permute-done.12 = bf16[256,1280]{1,0:T(8,128)(2,1)S(1)} collective-permute-done((bf16[256,1280]{1,0:T(8,128)(2,1)S(1)}, bf16[256,1280]{1,0:T(8,128)(2,1)S(1)}, u32[]{:S(2)}, u32[]{:S(2)}) %collective-permute-start.12) | collective-permute-done | bytes 655392 | tf_op jit(solution)/shard_map/ppermute | solution.py:32
  121.7 2.4 %collective-permute-start.13 = (bf16[256,1280]{1,0:T(8,128)(2,1)S(1)}, bf16[256,1280]{1,0:T(8,128)(2,1)}, u32[]{:S(2)}, u32[]{:S(2)}) collective-permute-start(bf16[256,1280]{1,0:T(8,128)(2,1)S(1)} %add_convert_fusion), channel_id=1, source_target_pairs={{0,32},{1,97},{2,34},{3,99},{4,36},{5,101},{6,38},{7,103},{8,40},{... | collective-permute-start | bytes 1966088 | tf_op jit(solution)/shard_map/ppermute | solution.py:32
  124.1 4.5 %collective-permute-done.10 = bf16[256,1280]{1,0:T(8,128)(2,1)S(1)} collective-permute-done((bf16[256,1280]{1,0:T(8,128)(2,1)S(1)}, bf16[256,1280]{1,0:T(8,128)(2,1)S(1)}, u32[]{:S(2)}, u32[]{:S(2)}) %collective-permute-start.10) | collective-permute-done | bytes 655392 | tf_op jit(solution)/shard_map/ppermute | solution.py:32
  138.3 6.9 %fusion.1.shared = f32[256,2048]{1,0:T(8,128)} fusion(bf16[704,2048]{1,0:T(8,128)(2,1)S(1)} %copy-done, bf16[256,2048]{1,0:T(8,128)(2,1)} %get-tuple-element.52, bf16[2048,704]{0,1:T(8,128)(2,1)} %param.18, f32[256,704]{0,1:T(8,128)} %fusion.9), kind=kOutput, calls=%fused_computation.6 | convolution fusion | flops 1477476352 | bytes 9633792 | tf_op jit(solution)/shard_map/dot_general | solution.py:44
  145.2 3.1 %last_sum.1 = bf16[32,16,1280]{2,1,0:T(8,128)(2,1)} custom-call(bf16[512,1280]{1,0:T(8,128)(2,1)} %get-tuple-element.42.own, bf16[256,1280]{1,0:T(8,128)(2,1)} %collective-permute-done.11.refs_0_, bf16[256,1280]{1,0:T(8,128)(2,1)} %collective-permute-done.13.refs_1_), custom_call_target="tpu_custom_call" | custom-call | tf_op jit(solution)/shard_map/last_sum/pallas_call | solution.py:287
  148.5 7.0 %all-to-all-start.3 = ((bf16[32,16,1280]{2,1,0:T(8,128)(2,1)}), bf16[32,16,1280]{2,1,0:T(8,128)(2,1)}, u32[]{:S(2)}, u32[]{:S(2)}) async-start(bf16[32,16,1280]{2,1,0:T(8,128)(2,1)} %last_sum.1), calls=%async_computation.3 | async-start | bytes 2621440 | tf_op jit(solution)/shard_map/all_to_all | solution.py:354
  155.6 5.7 %combine.1 = (bf16[64,2048]{1,0:T(8,128)(2,1)}, bf16[64,2048]{1,0:T(8,128)(2,1)S(1)}, bf16[64,2048]{1,0:T(8,128)(2,1)S(1)}, bf16[64,2048]{1,0:T(8,128)(2,1)S(1)}) custom-call(bf16[256,2048]{1,0:T(8,128)(2,1)} %bitcast.24, bf16[256,2048]{1,0:T(8,128)(2,1)} %bitcast.25, bf16[2048,768]{1,0:T(8,128)(2,1)} %bitcast.15.values, f32[256,2048]{1,0:T(8,128)} %fusion.1.shared), custom_call_target="tpu_custom_call" | custom-call | tf_op jit(solution)/shard_map/combine/pallas_call | solution.py:311
  167.6 3.8 %collective-permute-done.14 = bf16[64,2048]{1,0:T(8,128)(2,1)} collective-permute-done((bf16[64,2048]{1,0:T(8,128)(2,1)}, bf16[64,2048]{1,0:T(8,128)(2,1)}, u32[]{:S(2)}, u32[]{:S(2)}) %collective-permute-start.14) | collective-permute-done | bytes 262176 | tf_op jit(solution)/shard_map/ppermute | solution.py:22
  171.4 5.9 %collective-permute-done.15 = bf16[64,2048]{1,0:T(8,128)(2,1)} collective-permute-done((bf16[64,2048]{1,0:T(8,128)(2,1)S(1)}, bf16[64,2048]{1,0:T(8,128)(2,1)}, u32[]{:S(2)}, u32[]{:S(2)}) %collective-permute-start.15) | collective-permute-done | bytes 262176 | tf_op jit(solution)/shard_map/ppermute | solution.py:22
  179.0 2.7 %finish.1 = bf16[64,2048]{1,0:T(8,128)(2,1)} custom-call(bf16[64,512]{1,0:T(8,128)(2,1)} %bitcast.28, bf16[64,512]{1,0:T(8,128)(2,1)} %bitcast.29, bf16[512,1280]{1,0:T(8,128)(2,1)} %bitcast.13.values, f32[64,2048]{1,0:T(8,128)S(1)} %add_select_fusion.total), custom_call_target="tpu_custom_call" | custom-call | tf_op jit(solution)/shard_map/finish/pallas_call | solution.py:326
  (61 shorter events, 33.4 us)
Async XLA Ops:
  0.0 138.3 %copy-start = (bf16[704,2048]{1,0:T(8,128)(2,1)S(1)}, bf16[704,2048]{1,0:T(8,128)(2,1)}, u32[]{:S(2)}) copy-start(bf16[704,2048]{1,0:T(8,128)(2,1)} %param.19) | copy-start | bytes 8650756
  3.7 29.7 %all-to-all-start = ((bf16[32,16,1280]{2,1,0:T(8,128)(2,1)}), bf16[32,16,1280]{2,1,0:T(8,128)(2,1)}, u32[]{:S(2)}, u32[]{:S(2)}) async-start(bf16[32,16,1280]{2,1,0:T(8,128)(2,1)} %bitcast.27), calls=%async_computation | async-start | bytes 2621440 | tf_op jit(solution)/shard_map/all_to_all | solution.py:354
  13.1 14.4 %collective-permute-start.8 = (bf16[64,2176]{1,0:T(8,128)(2,1)S(1)}, bf16[64,2176]{1,0:T(8,128)(2,1)S(1)}, u32[]{:S(2)}, u32[]{:S(2)}) collective-permute-start(bf16[64,2176]{1,0:T(8,128)(2,1)S(1)} %get-tuple-element.39.e3), channel_id=1, source_target_pairs={{0,96},{32,0},{64,32},{96,64},{1,97},{33,1},{65,33},{97,65},{2,98}... | collective-permute-start | bytes 835592 | tf_op jit(solution)/shard_map/ppermute | solution.py:22
  15.9 11.6 %collective-permute-start.7 = (bf16[64,2176]{1,0:T(8,128)(2,1)S(1)}, bf16[64,2176]{1,0:T(8,128)(2,1)S(1)}, u32[]{:S(2)}, u32[]{:S(2)}) collective-permute-start(bf16[64,2176]{1,0:T(8,128)(2,1)S(1)} %get-tuple-element.39.e3), channel_id=1, source_target_pairs={{0,32},{32,64},{64,96},{96,0},{1,33},{33,65},{65,97},{97,1},{2,34}... | collective-permute-start | bytes 835592 | tf_op jit(solution)/shard_map/ppermute | solution.py:22
  15.9 13.9 %collective-permute-start.6 = (bf16[64,2176]{1,0:T(8,128)(2,1)S(1)}, bf16[64,2176]{1,0:T(8,128)(2,1)S(1)}, u32[]{:S(2)}, u32[]{:S(2)}) collective-permute-start(bf16[64,2176]{1,0:T(8,128)(2,1)S(1)} %get-tuple-element.39.e3), channel_id=1, source_target_pairs={{0,64},{32,96},{64,0},{96,32},{1,65},{33,97},{65,1},{97,33},{2,66}... | collective-permute-start | bytes 835592 | tf_op jit(solution)/shard_map/ppermute | solution.py:22
  33.4 49.2 %all-to-all-start.1 = ((bf16[32,64,768]{2,1,0:T(8,128)(2,1)}), bf16[32,64,768]{2,1,0:T(8,128)(2,1)}, u32[]{:S(2)}, u32[]{:S(2)}) async-start(bf16[32,64,768]{2,1,0:T(8,128)(2,1)} %bitcast.26), calls=%async_computation.1 | async-start | bytes 6291456 | tf_op jit(solution)/shard_map/all_to_all | solution.py:354
  44.1 48.3 %copy-start.2 = (bf16[256,1280]{1,0:T(8,128)(2,1)}, bf16[256,1280]{1,0:T(8,128)(2,1)S(1)}, u32[]{:S(2)}) copy-start(bf16[256,1280]{1,0:T(8,128)(2,1)S(1)} %get-tuple-element.69.refs_3_) | copy-start | bytes 1966084
  44.1 9.9 %collective-permute-start.3 = (bf16[256,1280]{1,0:T(8,128)(2,1)S(1)}, bf16[256,1280]{1,0:T(8,128)(2,1)S(1)}, u32[]{:S(2)}, u32[]{:S(2)}) collective-permute-start(bf16[256,1280]{1,0:T(8,128)(2,1)S(1)} %get-tuple-element.69.refs_3_), channel_id=1, source_target_pairs={{0,32},{1,97},{2,34},{3,99},{4,36},{5,101},{6,38},{7,103},{8,40},{... | collective-permute-start | bytes 1966088 | tf_op jit(solution)/shard_map/ppermute | solution.py:32
  44.2 16.8 %collective-permute-start = (bf16[256,1280]{1,0:T(8,128)(2,1)S(1)}, bf16[256,1280]{1,0:T(8,128)(2,1)S(1)}, u32[]{:S(2)}, u32[]{:S(2)}) collective-permute-start(bf16[256,1280]{1,0:T(8,128)(2,1)S(1)} %get-tuple-element.70.refs_2_), channel_id=1, source_target_pairs={{0,32},{1,97},{2,34},{3,99},{4,36},{5,101},{6,38},{7,103},{8,40},{... | collective-permute-start | bytes 1966088 | tf_op jit(solution)/shard_map/ppermute | solution.py:32
  54.0 14.0 %collective-permute-start.4 = (bf16[256,1280]{1,0:T(8,128)(2,1)S(1)}, bf16[256,1280]{1,0:T(8,128)(2,1)}, u32[]{:S(2)}, u32[]{:S(2)}) collective-permute-start(bf16[256,1280]{1,0:T(8,128)(2,1)S(1)} %collective-permute-done.3.refs_3_), channel_id=1, source_target_pairs={{0,32},{1,97},{2,34},{3,99},{4,36},{5,101},{6,38},{7,103},{8,40},{... | collective-permute-start | bytes 1966088 | tf_op jit(solution)/shard_map/ppermute | solution.py:32
  61.1 14.0 %collective-permute-start.1 = (bf16[256,1280]{1,0:T(8,128)(2,1)S(1)}, bf16[256,1280]{1,0:T(8,128)(2,1)}, u32[]{:S(2)}, u32[]{:S(2)}) collective-permute-start(bf16[256,1280]{1,0:T(8,128)(2,1)S(1)} %collective-permute-done.refs_2_), channel_id=1, source_target_pairs={{0,32},{1,97},{2,34},{3,99},{4,36},{5,101},{6,38},{7,103},{8,40},{... | collective-permute-start | bytes 1966088 | tf_op jit(solution)/shard_map/ppermute | solution.py:32
  68.1 24.6 %collective-permute-start.5 = (bf16[256,1280]{1,0:T(8,128)(2,1)}, bf16[256,1280]{1,0:T(8,128)(2,1)}, u32[]{:S(2)}, u32[]{:S(2)}) collective-permute-start(bf16[256,1280]{1,0:T(8,128)(2,1)} %collective-permute-done.4.refs_1_), channel_id=1, source_target_pairs={{0,32},{1,97},{2,34},{3,99},{4,36},{5,101},{6,38},{7,103},{8,40},{... | collective-permute-start | bytes 1966088 | tf_op jit(solution)/shard_map/ppermute | solution.py:32
  75.1 17.6 %collective-permute-start.2 = (bf16[256,1280]{1,0:T(8,128)(2,1)}, bf16[256,1280]{1,0:T(8,128)(2,1)}, u32[]{:S(2)}, u32[]{:S(2)}) collective-permute-start(bf16[256,1280]{1,0:T(8,128)(2,1)} %collective-permute-done.1.refs_0_), channel_id=1, source_target_pairs={{0,32},{1,97},{2,34},{3,99},{4,36},{5,101},{6,38},{7,103},{8,40},{... | collective-permute-start | bytes 1966088 | tf_op jit(solution)/shard_map/ppermute | solution.py:32
  92.4 17.3 %collective-permute-start.9 = (bf16[512,1280]{1,0:T(8,128)(2,1)}, bf16[512,1280]{1,0:T(8,128)(2,1)}, u32[]{:S(2)}, u32[]{:S(2)}) collective-permute-start(bf16[512,1280]{1,0:T(8,128)(2,1)} %get-tuple-element.45), channel_id=1, source_target_pairs={{0,32},{1,97},{2,34},{3,99},{4,36},{5,101},{6,38},{7,103},{8,40},{... | collective-permute-start | bytes 3932168 | tf_op jit(solution)/shard_map/ppermute | solution.py:32
  102.6 45.9 %all-to-all-start.2 = ((bf16[32,64,768]{2,1,0:T(8,128)(2,1)}), bf16[32,64,768]{2,1,0:T(8,128)(2,1)}, u32[]{:S(2)}, u32[]{:S(2)}) async-start(bf16[32,64,768]{2,1,0:T(8,128)(2,1)} %get-tuple-element.57), calls=%async_computation.2 | async-start | bytes 6291456 | tf_op jit(solution)/shard_map/all_to_all | solution.py:354
  111.6 20.3 %copy-start.8 = (bf16[2048,704]{0,1:T(8,128)(2,1)S(1)}, bf16[2048,704]{0,1:T(8,128)(2,1)}, u32[]{:S(2)}) copy-start(bf16[2048,704]{0,1:T(8,128)(2,1)} %param.17) | copy-start | bytes 8650756
  111.6 9.9 %collective-permute-start.12 = (bf16[256,1280]{1,0:T(8,128)(2,1)S(1)}, bf16[256,1280]{1,0:T(8,128)(2,1)S(1)}, u32[]{:S(2)}, u32[]{:S(2)}) collective-permute-start(bf16[256,1280]{1,0:T(8,128)(2,1)S(1)} %get-tuple-element.67), channel_id=1, source_target_pairs={{0,32},{1,97},{2,34},{3,99},{4,36},{5,101},{6,38},{7,103},{8,40},{... | collective-permute-start | bytes 1966088 | tf_op jit(solution)/shard_map/ppermute | solution.py:32
  112.8 15.8 %collective-permute-start.10 = (bf16[256,1280]{1,0:T(8,128)(2,1)S(1)}, bf16[256,1280]{1,0:T(8,128)(2,1)S(1)}, u32[]{:S(2)}, u32[]{:S(2)}) collective-permute-start(bf16[256,1280]{1,0:T(8,128)(2,1)S(1)} %get-tuple-element.68), channel_id=1, source_target_pairs={{0,32},{1,97},{2,34},{3,99},{4,36},{5,101},{6,38},{7,103},{8,40},{... | collective-permute-start | bytes 1966088 | tf_op jit(solution)/shard_map/ppermute | solution.py:32
  121.7 23.5 %collective-permute-start.13 = (bf16[256,1280]{1,0:T(8,128)(2,1)S(1)}, bf16[256,1280]{1,0:T(8,128)(2,1)}, u32[]{:S(2)}, u32[]{:S(2)}) collective-permute-start(bf16[256,1280]{1,0:T(8,128)(2,1)S(1)} %add_convert_fusion), channel_id=1, source_target_pairs={{0,32},{1,97},{2,34},{3,99},{4,36},{5,101},{6,38},{7,103},{8,40},{... | collective-permute-start | bytes 1966088 | tf_op jit(solution)/shard_map/ppermute | solution.py:32
  129.6 15.6 %collective-permute-start.11 = (bf16[256,1280]{1,0:T(8,128)(2,1)}, bf16[256,1280]{1,0:T(8,128)(2,1)}, u32[]{:S(2)}, u32[]{:S(2)}) collective-permute-start(bf16[256,1280]{1,0:T(8,128)(2,1)} %add_convert_fusion.2), channel_id=1, source_target_pairs={{0,32},{1,97},{2,34},{3,99},{4,36},{5,101},{6,38},{7,103},{8,40},{... | collective-permute-start | bytes 1966088 | tf_op jit(solution)/shard_map/ppermute | solution.py:32
  148.5 30.4 %all-to-all-start.3 = ((bf16[32,16,1280]{2,1,0:T(8,128)(2,1)}), bf16[32,16,1280]{2,1,0:T(8,128)(2,1)}, u32[]{:S(2)}, u32[]{:S(2)}) async-start(bf16[32,16,1280]{2,1,0:T(8,128)(2,1)} %last_sum.1), calls=%async_computation.3 | async-start | bytes 2621440 | tf_op jit(solution)/shard_map/all_to_all | solution.py:354
  162.0 9.5 %collective-permute-start.14 = (bf16[64,2048]{1,0:T(8,128)(2,1)}, bf16[64,2048]{1,0:T(8,128)(2,1)}, u32[]{:S(2)}, u32[]{:S(2)}) collective-permute-start(bf16[64,2048]{1,0:T(8,128)(2,1)} %get-tuple-element.64), channel_id=1, source_target_pairs={{0,64},{32,96},{64,0},{96,32},{1,65},{33,97},{65,1},{97,33},{2,66}... | collective-permute-start | bytes 786440 | tf_op jit(solution)/shard_map/ppermute | solution.py:22
  163.4 14.0 %collective-permute-start.15 = (bf16[64,2048]{1,0:T(8,128)(2,1)S(1)}, bf16[64,2048]{1,0:T(8,128)(2,1)}, u32[]{:S(2)}, u32[]{:S(2)}) collective-permute-start(bf16[64,2048]{1,0:T(8,128)(2,1)S(1)} %get-tuple-element.65), channel_id=1, source_target_pairs={{0,96},{32,0},{64,32},{96,64},{1,97},{33,1},{65,33},{97,65},{2,98}... | collective-permute-start | bytes 786440 | tf_op jit(solution)/shard_map/ppermute | solution.py:22
  164.7 13.0 %collective-permute-start.16 = (bf16[64,2048]{1,0:T(8,128)(2,1)S(1)}, bf16[64,2048]{1,0:T(8,128)(2,1)}, u32[]{:S(2)}, u32[]{:S(2)}) collective-permute-start(bf16[64,2048]{1,0:T(8,128)(2,1)S(1)} %get-tuple-element.66), channel_id=1, source_target_pairs={{0,32},{32,64},{64,96},{96,0},{1,33},{33,65},{65,97},{97,1},{2,34}... | collective-permute-start | bytes 786440 | tf_op jit(solution)/shard_map/ppermute | solution.py:22
  (9 other events, 94.9 us)

commit v8 on v7

--- a/solution.py
+++ b/solution.py
@@ -11,6 +11,7 @@
 SEND_COLS = 1280
 BACK_COLS = 1280
 COLS = 128
+WIDE = 256
 NT = (((1,), (1,)), ((), ()))
 TN = (((0,), (0,)), ((), ()))
 AROUND = (2, 1, -1)
@@ -284,9 +285,15 @@
 
 
 def call_last_sum(own, ends, n_ep):
+    rows, cols = own.shape
+    slots = len(ends) * CAP
+    block = lambda n: pl.BlockSpec((n, WIDE), lambda c: (0, c))
     return pl.pallas_call(
         last_sum,
-        out_shape=hbm((n_ep, len(ends) * CAP, own.shape[1])),
+        grid=(cols // WIDE,),
+        in_specs=[block(rows)] + [block(x.shape[0]) for x in ends],
+        out_specs=pl.BlockSpec((n_ep, slots, WIDE), lambda c: (0, 0, c)),
+        out_shape=hbm((n_ep, slots, cols)),
         compiler_params=pltpu.CompilerParams(vmem_limit_bytes=16 * 1024 * 1024),
         name="last_sum",
     )(*from_hbm(own, *ends))
@@ -297,38 +304,58 @@
 
 
 def combine(hi, lo, values, shared, *outs):
-    tok, feature = outs[0].shape
-    bc = feature - values.shape[1]
-    late = shared[:, bc:] + weigh(hi[...], lo[...], values[...])
+    tok = outs[0].shape[0]
+    total = shared[...] + weigh(hi[...], lo[...], values[...])
     for j, o in enumerate(outs):
-        rows = slice(j * tok, (j + 1) * tok)
-        o[:, :bc] = shared[rows, :bc].astype(jnp.bfloat16)
-        o[:, bc:] = late[rows].astype(jnp.bfloat16)
+        o[...] = total[j * tok : (j + 1) * tok].astype(jnp.bfloat16)
 
 
 def call_combine(hi, lo, values, shared, tok):
-    rows, feature = shared.shape
+    rows, slots = hi.shape
+    cols = values.shape[1]
+    whole = pl.BlockSpec((rows, slots), lambda c: (0, 0))
+    block = lambda n: pl.BlockSpec((n, WIDE), lambda c: (0, c))
     return pl.pallas_call(
         combine,
-        out_shape=[jax.ShapeDtypeStruct((tok, feature), jnp.bfloat16)] * (rows // tok),
+        grid=(cols // WIDE,),
+        in_specs=[whole, whole, block(slots), block(rows)],
+        out_specs=[block(tok)] * (rows // tok),
+        out_shape=[jax.ShapeDtypeStruct((tok, cols), jnp.bfloat16)] * (rows // tok),
         compiler_params=pltpu.CompilerParams(vmem_limit_bytes=24 * 1024 * 1024),
         name="combine",
-    )(*from_hbm(hi, lo, values, shared))
-
-
-def finish(hi, lo, values, total, out):
+    )(*from_hbm(hi, lo, values), shared)
+
+
+def finish(hi, lo, values, early, late, out):
+    here = pl.program_id(0)
+    routed_blocks = pl.num_programs(0) - pl.cdiv(late.shape[1], WIDE)
+
+    @pl.when(here < routed_blocks)
+    def _():
+        out[...] = (early[...] + weigh(hi[...], lo[...], values[...])).astype(jnp.bfloat16)
+
+    @pl.when(here >= routed_blocks)
+    def _():
+        at = pl.multiple_of((here - routed_blocks) * WIDE, WIDE)
+        out[...] = late[:, pl.ds(at, WIDE)]
+
+
+def call_finish(hi, lo, values, early, late):
+    tok, slots = hi.shape
     bc = values.shape[1]
-    out[:, bc:] = total[:, bc:].astype(jnp.bfloat16)
-    out[:, :bc] = (total[:, :bc] + weigh(hi[...], lo[...], values[...])).astype(jnp.bfloat16)
-
-
-def call_finish(hi, lo, values, total):
+    cols = bc + late.shape[1]
+    last = bc // WIDE - 1
+    whole = lambda shape: pl.BlockSpec(shape, lambda c: (0, 0))
+    block = lambda n: pl.BlockSpec((n, WIDE), lambda c: (0, jnp.minimum(c, last)))
     return pl.pallas_call(
         finish,
-        out_shape=jax.ShapeDtypeStruct(total.shape, jnp.bfloat16),
+        grid=(cols // WIDE,),
+        in_specs=[whole((tok, slots))] * 2 + [block(slots), block(tok), whole(late.shape)],
+        out_specs=pl.BlockSpec((tok, WIDE), lambda c: (0, c)),
+        out_shape=jax.ShapeDtypeStruct((tok, cols), jnp.bfloat16),
         compiler_params=pltpu.CompilerParams(vmem_limit_bytes=16 * 1024 * 1024),
         name="finish",
-    )(*from_hbm(hi, lo, values), total)
+    )(hi, lo, *from_hbm(values), early, late)
 
 
 def on_device(
@@ -370,21 +397,23 @@
     own_slots = own.reshape(n_ep, members, CAP, sc)
     own_parts = [own_slots[:, m].reshape(n_ep * CAP, sc) for m in range(members)]
     behind = [toward(x) for x in own_parts]
-    far = [toward(x) for x in behind]
-    ahead = [toward(x) for x in far]
-    came_b = over_ep(send_b, members * n_dp * CAP, feature - sc)
-
-    *to_far, to_behind, out_b = run_experts([far, behind], 0, came_b, None, *weights, bc)
-    *to_ahead, to_own, out_b = run_experts([ahead, own_parts], 1, came_b, out_b, *weights, bc)
-    out_b, gathered, hi_b, lo_b = lax.optimization_barrier((out_b, gathered, hi_b, lo_b))
-    ret_b = over_ep(out_b, members * n_dp * CAP, feature - bc)
 
     gate_act = dot_f32(gathered, shared_gate)
     up_act = dot_f32(gathered, shared_up)
     hidden = (jax.nn.silu(gate_act) * up_act).astype(jnp.bfloat16)
     shared = dot_f32(hidden, shared_down)
-
+    behind[0], shared = lax.optimization_barrier((behind[0], shared))
+    far = [toward(x) for x in behind]
+    ahead = [toward(x) for x in far]
+    came_b = over_ep(send_b, members * n_dp * CAP, feature - sc)
+
+    *to_far, to_behind, out_b = run_experts([far, behind], 0, came_b, None, *weights, bc)
     f32 = lambda x: x.astype(jnp.float32)
+    early = shared[:, :bc].astype(jnp.bfloat16).reshape(n_dp, tok, bc)
+    early = [shifted(early[j], -s) for j, s in enumerate(AROUND)] + [early[n_dp - 1]]
+    *to_ahead, to_own, out_b = run_experts([ahead, own_parts], 1, came_b, out_b, *weights, bc)
+    ret_b = over_ep(out_b, members * n_dp * CAP, feature - bc)
+
     rows = n_ep * CAP
     arrived = toward(to_behind)
     ends = []
@@ -393,18 +422,19 @@
         passing = (f32(to_far[m]) + f32(arrived[part])).astype(jnp.bfloat16)
         passing = (f32(to_ahead[m]) + f32(toward(passing))).astype(jnp.bfloat16)
         ends.append(toward(passing))
-    *ends, shared, hi_b, lo_b = lax.optimization_barrier((*ends, shared, hi_b.T, lo_b.T))
+    *ends, late, hi_b, lo_b, hi_d, lo_d = lax.optimization_barrier(
+        (*ends, shared[:, bc:], hi_b.T, lo_b.T, hi_d.T, lo_d.T)
+    )
     back_d = call_last_sum(to_own, ends, n_ep)
     back_d, ret_b = lax.optimization_barrier((back_d, ret_b))
     ret_d = over_ep(back_d, members * CAP, bc)
 
-    *parts, kept = call_combine(hi_b, lo_b, ret_b.reshape(-1, feature - bc), shared, tok)
     live = jnp.arange(tok, dtype=jnp.int32) < row_counts[0]
-    total = f32(kept)
-    for part, s in zip(parts, AROUND):
-        total = total + f32(shifted(part, -s))
-    total = jnp.where(live[:, None], total, 0.0)
-    return call_finish(hi_d.T, lo_d.T, ret_d.reshape(-1, bc), total)
+    early = jnp.where(live[:, None], sum(f32(x) for x in early), 0.0)
+    *parts, late = call_combine(hi_b, lo_b, ret_b.reshape(-1, feature - bc), late, tok)
+    late = f32(late) + sum(f32(shifted(x, -s)) for x, s in zip(parts, AROUND))
+    late = jnp.where(live[:, None], late, 0.0).astype(jnp.bfloat16)
+    return call_finish(hi_d, lo_d, ret_d.reshape(-1, bc), early, late)
 
 
 def solution(mesh):

time: 182 us -> 181 us (level)
  waiting for transfers between devices: 69.6 us -> 40.1 us
  starting transfers between devices: 51.3 us -> 67.7 us
  other arithmetic: 4.39 us -> 7.8 us
  local copies, waits for them, and re-layouts: 9 us -> 12.3 us
  Pallas kernels: 37.5 us -> 40 us
  matrix products: 8.76 us -> 10.7 us
    ppermute x11, waiting for transfers between devices: 40.8 us -> 20.2 us  [toward(): return lax.ppermute(x, ('dp', 'ep'), pairs)]
    ppermute x11, starting transfers between devices: 11.6 us -> 25.8 us  [toward(): return lax.ppermute(x, ('dp', 'ep'), pairs)]
    ppermute x6 -> x9, waiting for transfers between devices: 22.3 us -> 13.2 us  [shifted(): return lax.ppermute(x, 'dp', [(i, (i + shift) % n) for i in range(n)])]
    ppermute x6 -> x9, starting transfers between devices: 7.74 us -> 12.9 us  [shifted(): return lax.ppermute(x, 'dp', [(i, (i + shift) % n) for i in range(n)])]
    pallas_call x0 -> x2, local copies, waits for them, and re-layouts: none -> 4.56 us  [call_prepare_ring(): pl.pallas_call(functools.partial(prepare_ring, members), out_shape=[hbm((...]
    optimization_barrier x2 -> x0, local copies, waits for them, and re-layouts: 4.55 us -> none  [on_device(): lax.optimization_barrier((out_b, gathered, hi_b, lo_b))]
    slice x0 -> x2, local copies, waits for them, and re-layouts: none -> 3.19 us  [the longest x1 2.08 us: on_device(): shared[:, bc:]]
    all_to_all x4, starting transfers between devices: 31.9 us -> 29 us  [over_ep(): lax.all_to_all(x.reshape(n_ep, rows, cols), 'ep', split_axis=0, concat_ax...]
  transfers between devices with their start and end apart: 21 -> 24, of which waited for: 14 -> 12; matrix products, arithmetic and copies ran while one was open for 12% -> 16% of each run, Pallas kernels for 18% -> 18%
where the time goes in v8:
time: 181 us; the launch traced here: 180 us
  starting transfers between devices  67.7 us (37%)
  waiting for transfers between devices  40.1 us (22%)
  Pallas kernels  40 us (22%)
  local copies, waits for them, and re-layouts  12.3 us (7%)
  matrix products  10.7 us (6%)
  other arithmetic  7.8 us (4%)
    all_to_all x4, starting transfers between devices, over_ep(): lax.all_to_all(x.reshape(n_ep, rows, cols), 'ep', split_axis=0, concat_ax...  29 us
    ppermute x11, starting transfers between devices, toward(): return lax.ppermute(x, ('dp', 'ep'), pairs)  25.8 us
    ppermute x11, waiting for transfers between devices, toward(): return lax.ppermute(x, ('dp', 'ep'), pairs)  20.2 us
    pallas_call x2, Pallas kernels, run_experts(): pl.pallas_call(functools.partial(expert_kernel, len(planes), pair), in_sp...  19.7 us
    ppermute x9, waiting for transfers between devices, shifted(): return lax.ppermute(x, 'dp', [(i, (i + shift) % n) for i in range(n)])  13.2 us
    ppermute x9, starting transfers between devices, shifted(): return lax.ppermute(x, 'dp', [(i, (i + shift) % n) for i in range(n)])  12.9 us
    dot_general x2, matrix products, dot_f32(): return jnp.dot(a, b, preferred_element_type=jnp.float32)  10.7 us
    all_to_all x4, waiting for transfers between devices, over_ep(): lax.all_to_all(x.reshape(n_ep, rows, cols), 'ep', split_axis=0, concat_ax...  6.73 us
  transfers between devices with their start and end apart: 24, of which 12 were waited for; matrix products, arithmetic and copies ran while one was open for 16% of the time, Pallas kernels for 18%

profile of v8, /device:TPU:1, one launch (start us, length us, event | category | flops | bytes accessed | tf_op | source)
XLA Modules:
  0.0 179.6 jit_solution(11215095311253130230)
XLA Ops:
  3.7 9.5 %all-to-all-start = ((bf16[32,16,1280]{2,1,0:T(8,128)(2,1)}), bf16[32,16,1280]{2,1,0:T(8,128)(2,1)}, u32[]{:S(2)}, u32[]{:S(2)}) async-start(bf16[32,16,1280]{2,1,0:T(8,128)(2,1)} %bitcast.29), calls=%async_computation | async-start | bytes 2621440 | tf_op jit(solution)/shard_map/all_to_all | solution.py:381
  13.1 3.0 %collective-permute-start.1 = (bf16[64,2176]{1,0:T(8,128)(2,1)S(1)}, bf16[64,2176]{1,0:T(8,128)(2,1)S(1)}, u32[]{:S(2)}, u32[]{:S(2)}) collective-permute-start(bf16[64,2176]{1,0:T(8,128)(2,1)S(1)} %get-tuple-element.37.e3), channel_id=1, source_target_pairs={{0,64},{32,96},{64,0},{96,32},{1,65},{33,97},{65,1},{97,33},{2,66}... | collective-permute-start | bytes 835592 | tf_op jit(solution)/shard_map/ppermute | solution.py:23
  18.8 4.0 %collective-permute-done.1.e0 = bf16[64,2176]{1,0:T(8,128)(2,1)S(1)} collective-permute-done((bf16[64,2176]{1,0:T(8,128)(2,1)S(1)}, bf16[64,2176]{1,0:T(8,128)(2,1)S(1)}, u32[]{:S(2)}, u32[]{:S(2)}) %collective-permute-start.1) | collective-permute-done | bytes 278560 | tf_op jit(solution)/shard_map/ppermute | solution.py:23
  22.8 6.6 %collective-permute-done.2.e1 = bf16[64,2176]{1,0:T(8,128)(2,1)S(1)} collective-permute-done((bf16[64,2176]{1,0:T(8,128)(2,1)S(1)}, bf16[64,2176]{1,0:T(8,128)(2,1)S(1)}, u32[]{:S(2)}, u32[]{:S(2)}) %collective-permute-start.2) | collective-permute-done | bytes 278560 | tf_op jit(solution)/shard_map/ppermute | solution.py:23
  29.4 3.5 %prepare_ring.1 = (bf16[2048,768]{1,0:T(8,128)(2,1)}, bf16[2048,256]{1,0:T(8,128)(2,1)}, bf16[2048,256]{1,0:T(8,128)(2,1)}, bf16[256,2048]{1,0:T(8,128)(2,1)}) custom-call(bf16[64,2176]{1,0:T(8,128)(2,1)S(1)} %collective-permute-done.1.e0, bf16[64,2176]{1,0:T(8,128)(2,1)S(1)} %collective-permute-done.2.e1, bf16[64,2176]{1,0:T(8,128)(2,1)S(1)} %collective-permute-done.3.e2, ...), custom_call_target="tpu_custom_call" | custom-call | tf_op jit(solution)/shard_map/prepare_ring/pallas_call | solution.py:156
  33.0 7.7 %all-to-all-start.1 = ((bf16[32,64,768]{2,1,0:T(8,128)(2,1)}), bf16[32,64,768]{2,1,0:T(8,128)(2,1)}, u32[]{:S(2)}, u32[]{:S(2)}) async-start(bf16[32,64,768]{2,1,0:T(8,128)(2,1)} %bitcast.28), calls=%async_computation.1 | async-start | bytes 6291456 | tf_op jit(solution)/shard_map/all_to_all | solution.py:381
  45.5 3.7 %fusion.6 = f32[256,704]{0,1:T(8,128)} fusion(bf16[256,2048]{1,0:T(8,128)(2,1)S(1)} %copy-done.8, bf16[2048,704]{0,1:T(8,128)(2,1)} %param.17), kind=kOutput, calls=%fused_computation.15 | convolution fusion | flops 738197504 | bytes 4653056 | tf_op jit(solution)/shard_map/dot_general | solution.py:45
  49.2 7.0 %fusion = f32[256,2048]{1,0:T(8,128)} fusion(bf16[704,2048]{1,0:T(8,128)(2,1)S(1)} %copy-done, f32[256,704]{0,1:T(8,128)} %fusion.6, bf16[256,2048]{1,0:T(8,128)(2,1)} %get-tuple-element.38, bf16[2048,704]{0,1:T(8,128)(2,1)} %param.18), kind=kOutput, calls=%fused_computation.7 | convolution fusion | flops 1477476352 | bytes 9633792 | tf_op jit(solution)/shard_map/dot_general | solution.py:45
  57.0 3.3 %collective-permute-done.6.refs_3_ = bf16[256,1280]{1,0:T(8,128)(2,1)} collective-permute-done((bf16[256,1280]{1,0:T(8,128)(2,1)S(1)}, bf16[256,1280]{1,0:T(8,128)(2,1)}, u32[]{:S(2)}, u32[]{:S(2)}) %collective-permute-start.6) | collective-permute-done | bytes 655392 | tf_op jit(solution)/shard_map/ppermute | solution.py:33
  60.2 3.5 %collective-permute-start.7 = (bf16[256,1280]{1,0:T(8,128)(2,1)}, bf16[256,1280]{1,0:T(8,128)(2,1)}, u32[]{:S(2)}, u32[]{:S(2)}) collective-permute-start(bf16[256,1280]{1,0:T(8,128)(2,1)} %collective-permute-done.6.refs_3_), channel_id=1, source_target_pairs={{0,32},{1,97},{2,34},{3,99},{4,36},{5,101},{6,38},{7,103},{8,40},{... | collective-permute-start | bytes 1966088 | tf_op jit(solution)/shard_map/ppermute | solution.py:33
  63.7 3.6 %collective-permute-done.4.refs_0_ = bf16[256,1280]{1,0:T(8,128)(2,1)} collective-permute-done((bf16[256,1280]{1,0:T(8,128)(2,1)}, bf16[256,1280]{1,0:T(8,128)(2,1)}, u32[]{:S(2)}, u32[]{:S(2)}) %collective-permute-start.4) | collective-permute-done | bytes 655392 | tf_op jit(solution)/shard_map/ppermute | solution.py:33
  67.3 3.4 %collective-permute-start.5 = (bf16[256,1280]{1,0:T(8,128)(2,1)}, bf16[256,1280]{1,0:T(8,128)(2,1)S(1)}, u32[]{:S(2)}, u32[]{:S(2)}) collective-permute-start(bf16[256,1280]{1,0:T(8,128)(2,1)} %collective-permute-done.4.refs_0_), channel_id=1, source_target_pairs={{0,32},{1,97},{2,34},{3,99},{4,36},{5,101},{6,38},{7,103},{8,40},{... | collective-permute-start | bytes 1966088 | tf_op jit(solution)/shard_map/ppermute | solution.py:33
  70.8 3.6 %collective-permute-done.7.refs_1_ = bf16[256,1280]{1,0:T(8,128)(2,1)} collective-permute-done((bf16[256,1280]{1,0:T(8,128)(2,1)}, bf16[256,1280]{1,0:T(8,128)(2,1)}, u32[]{:S(2)}, u32[]{:S(2)}) %collective-permute-start.7) | collective-permute-done | bytes 655392 | tf_op jit(solution)/shard_map/ppermute | solution.py:33
  74.4 3.4 %collective-permute-start.8 = (bf16[256,1280]{1,0:T(8,128)(2,1)}, bf16[256,1280]{1,0:T(8,128)(2,1)}, u32[]{:S(2)}, u32[]{:S(2)}) collective-permute-start(bf16[256,1280]{1,0:T(8,128)(2,1)} %collective-permute-done.7.refs_1_), channel_id=1, source_target_pairs={{0,32},{1,97},{2,34},{3,99},{4,36},{5,101},{6,38},{7,103},{8,40},{... | collective-permute-start | bytes 1966088 | tf_op jit(solution)/shard_map/ppermute | solution.py:33
  80.6 9.9 %experts.2 = (bf16[256,1280]{1,0:T(8,128)(2,1)}, bf16[256,1280]{1,0:T(8,128)(2,1)}, bf16[512,1280]{1,0:T(8,128)(2,1)}, bf16[32,64,768]{2,1,0:T(8,128)(2,1)}) custom-call(bf16[256,1280]{1,0:T(8,128)(2,1)} %collective-permute-done.4.refs_0_, bf16[256,1280]{1,0:T(8,128)(2,1)} %collective-permute-done.7.refs_1_, bf16[256,1280]{1,0:T(8,128)(2,1)} %collective-permute-done.refs_2_, ...), custom_call_target="tpu_custom_call" | custom-call | flops 20000000000 | bytes 200000000 | tf_op jit(solution)/shard_map/experts/pallas_call | solution.py:247
  93.7 9.8 %experts.3 = (bf16[256,1280]{1,0:T(8,128)(2,1)}, bf16[256,1280]{1,0:T(8,128)(2,1)}, bf16[512,1280]{1,0:T(8,128)(2,1)}, bf16[32,64,768]{2,1,0:T(8,128)(2,1)}) custom-call(bf16[256,1280]{1,0:T(8,128)(2,1)} %copy-done.9, bf16[256,1280]{1,0:T(8,128)(2,1)} %collective-permute-done.8.refs_1_, ...), custom_call_target="tpu_custom_call", output_to_operand_aliasing={{3}: (8, {})} | custom-call | flops 20000000000 | bytes 200000000 | tf_op jit(solution)/shard_map/experts/pallas_call | solution.py:247
  103.6 4.7 %all-to-all-start.2 = ((bf16[32,64,768]{2,1,0:T(8,128)(2,1)}), bf16[32,64,768]{2,1,0:T(8,128)(2,1)}, u32[]{:S(2)}, u32[]{:S(2)}) async-start(bf16[32,64,768]{2,1,0:T(8,128)(2,1)} %get-tuple-element.57), calls=%async_computation.2 | async-start | bytes 6291456 | tf_op jit(solution)/shard_map/all_to_all | solution.py:381
  113.1 7.2 %collective-permute-done.10 = bf16[256,1280]{1,0:T(8,128)(2,1)S(1)} collective-permute-done((bf16[256,1280]{1,0:T(8,128)(2,1)S(1)}, bf16[256,1280]{1,0:T(8,128)(2,1)S(1)}, u32[]{:S(2)}, u32[]{:S(2)}) %collective-permute-start.10) | collective-permute-done | bytes 655392 | tf_op jit(solution)/shard_map/ppermute | solution.py:33
  121.4 3.5 %collective-permute-start.11 = (bf16[256,1280]{1,0:T(8,128)(2,1)}, bf16[256,1280]{1,0:T(8,128)(2,1)}, u32[]{:S(2)}, u32[]{:S(2)}) collective-permute-start(bf16[256,1280]{1,0:T(8,128)(2,1)} %add_convert_fusion.2), channel_id=1, source_target_pairs={{0,32},{1,97},{2,34},{3,99},{4,36},{5,101},{6,38},{7,103},{8,40},{... | collective-permute-start | bytes 1966088 | tf_op jit(solution)/shard_map/ppermute | solution.py:33
  128.4 3.5 %collective-permute-start.13 = (bf16[256,1280]{1,0:T(8,128)(2,1)}, bf16[256,1280]{1,0:T(8,128)(2,1)}, u32[]{:S(2)}, u32[]{:S(2)}) collective-permute-start(bf16[256,1280]{1,0:T(8,128)(2,1)} %add_convert_fusion), channel_id=1, source_target_pairs={{0,32},{1,97},{2,34},{3,99},{4,36},{5,101},{6,38},{7,103},{8,40},{... | collective-permute-start | bytes 1966088 | tf_op jit(solution)/shard_map/ppermute | solution.py:33
  141.6 4.5 %last_sum.1 = bf16[32,16,1280]{2,1,0:T(8,128)(2,1)} custom-call(bf16[512,1280]{1,0:T(8,128)(2,1)} %get-tuple-element.54.own, bf16[256,1280]{1,0:T(8,128)(2,1)} %collective-permute-done.11.refs_0_, bf16[256,1280]{1,0:T(8,128)(2,1)} %collective-permute-done.13.refs_1_), custom_call_target="tpu_custom_call" | custom-call | tf_op jit(solution)/shard_map/last_sum/pallas_call | solution.py:291
  147.8 7.0 %all-to-all-start.3 = ((bf16[32,16,1280]{2,1,0:T(8,128)(2,1)}), bf16[32,16,1280]{2,1,0:T(8,128)(2,1)}, u32[]{:S(2)}, u32[]{:S(2)}) async-start(bf16[32,16,1280]{2,1,0:T(8,128)(2,1)} %last_sum.1), calls=%async_computation.3 | async-start | bytes 2621440 | tf_op jit(solution)/shard_map/all_to_all | solution.py:381
  159.9 4.6 %combine.1 = (bf16[64,768]{1,0:T(8,128)(2,1)S(1)}, bf16[64,768]{1,0:T(8,128)(2,1)S(1)}, bf16[64,768]{1,0:T(8,128)(2,1)S(1)}, bf16[64,768]{1,0:T(8,128)(2,1)S(1)}) custom-call(bf16[256,2048]{1,0:T(8,128)(2,1)} %bitcast.26, bf16[256,2048]{1,0:T(8,128)(2,1)} %bitcast.27, bf16[2048,768]{1,0:T(8,128)(2,1)} %bitcast.15.values, f32[256,768]{1,0:T(8,128)S(1)} %copy-done.1), custom_call_target="tpu_custom_call" | custom-call | tf_op jit(solution)/shard_map/combine/pallas_call | solution.py:318
  174.7 4.8 %finish.1 = bf16[64,2048]{1,0:T(8,128)(2,1)} custom-call(bf16[64,512]{1,0:T(8,128)(2,1)S(1)} %bitcast.24, bf16[64,512]{1,0:T(8,128)(2,1)S(1)} %bitcast.25, bf16[512,1280]{1,0:T(8,128)(2,1)} %bitcast.13.values, f32[64,1280]{1,0:T(8,128)S(1)} %add_select_fusion.early, bf16[64,768]{1,0:T(8,128)(2,1)S(1)} %select_convert_fusion.late), custom_call_target="tpu_custom_call" | custom-call | tf_op jit(solution)/shard_map/finish/pallas_call | solution.py:350
  (67 shorter events, 53.1 us)
Async XLA Ops:
  3.7 29.3 %all-to-all-start = ((bf16[32,16,1280]{2,1,0:T(8,128)(2,1)}), bf16[32,16,1280]{2,1,0:T(8,128)(2,1)}, u32[]{:S(2)}, u32[]{:S(2)}) async-start(bf16[32,16,1280]{2,1,0:T(8,128)(2,1)} %bitcast.29), calls=%async_computation | async-start | bytes 2621440 | tf_op jit(solution)/shard_map/all_to_all | solution.py:381
  13.1 9.7 %collective-permute-start.1 = (bf16[64,2176]{1,0:T(8,128)(2,1)S(1)}, bf16[64,2176]{1,0:T(8,128)(2,1)S(1)}, u32[]{:S(2)}, u32[]{:S(2)}) collective-permute-start(bf16[64,2176]{1,0:T(8,128)(2,1)S(1)} %get-tuple-element.37.e3), channel_id=1, source_target_pairs={{0,64},{32,96},{64,0},{96,32},{1,65},{33,97},{65,1},{97,33},{2,66}... | collective-permute-start | bytes 835592 | tf_op jit(solution)/shard_map/ppermute | solution.py:23
  16.1 13.2 %collective-permute-start.2 = (bf16[64,2176]{1,0:T(8,128)(2,1)S(1)}, bf16[64,2176]{1,0:T(8,128)(2,1)S(1)}, u32[]{:S(2)}, u32[]{:S(2)}) collective-permute-start(bf16[64,2176]{1,0:T(8,128)(2,1)S(1)} %get-tuple-element.37.e3), channel_id=1, source_target_pairs={{0,32},{32,64},{64,96},{96,0},{1,33},{33,65},{65,97},{97,1},{2,34}... | collective-permute-start | bytes 835592 | tf_op jit(solution)/shard_map/ppermute | solution.py:23
  16.5 12.8 %collective-permute-start.3 = (bf16[64,2176]{1,0:T(8,128)(2,1)S(1)}, bf16[64,2176]{1,0:T(8,128)(2,1)S(1)}, u32[]{:S(2)}, u32[]{:S(2)}) collective-permute-start(bf16[64,2176]{1,0:T(8,128)(2,1)S(1)} %get-tuple-element.37.e3), channel_id=1, source_target_pairs={{0,96},{32,0},{64,32},{96,64},{1,97},{33,1},{65,33},{97,65},{2,98}... | collective-permute-start | bytes 835592 | tf_op jit(solution)/shard_map/ppermute | solution.py:23
  33.0 47.6 %all-to-all-start.1 = ((bf16[32,64,768]{2,1,0:T(8,128)(2,1)}), bf16[32,64,768]{2,1,0:T(8,128)(2,1)}, u32[]{:S(2)}, u32[]{:S(2)}) async-start(bf16[32,64,768]{2,1,0:T(8,128)(2,1)} %bitcast.28), calls=%async_computation.1 | async-start | bytes 6291456 | tf_op jit(solution)/shard_map/all_to_all | solution.py:381
  43.1 13.1 %collective-permute-start = (bf16[256,1280]{1,0:T(8,128)(2,1)}, bf16[256,1280]{1,0:T(8,128)(2,1)}, u32[]{:S(2)}, u32[]{:S(2)}) collective-permute-start(bf16[256,1280]{1,0:T(8,128)(2,1)} %get-tuple-element.70.refs_2_), channel_id=1, source_target_pairs={{0,32},{1,97},{2,34},{3,99},{4,36},{5,101},{6,38},{7,103},{8,40},{... | collective-permute-start | bytes 1966088 | tf_op jit(solution)/shard_map/ppermute | solution.py:33
  45.4 14.8 %collective-permute-start.6 = (bf16[256,1280]{1,0:T(8,128)(2,1)S(1)}, bf16[256,1280]{1,0:T(8,128)(2,1)}, u32[]{:S(2)}, u32[]{:S(2)}) collective-permute-start(bf16[256,1280]{1,0:T(8,128)(2,1)S(1)} %get-tuple-element.69.refs_3_), channel_id=1, source_target_pairs={{0,32},{1,97},{2,34},{3,99},{4,36},{5,101},{6,38},{7,103},{8,40},{... | collective-permute-start | bytes 1966088 | tf_op jit(solution)/shard_map/ppermute | solution.py:33
  56.2 11.2 %collective-permute-start.4 = (bf16[256,1280]{1,0:T(8,128)(2,1)}, bf16[256,1280]{1,0:T(8,128)(2,1)}, u32[]{:S(2)}, u32[]{:S(2)}) collective-permute-start(bf16[256,1280]{1,0:T(8,128)(2,1)} %collective-permute-done.refs_2_), channel_id=1, source_target_pairs={{0,32},{1,97},{2,34},{3,99},{4,36},{5,101},{6,38},{7,103},{8,40},{... | collective-permute-start | bytes 1966088 | tf_op jit(solution)/shard_map/ppermute | solution.py:33
  60.2 14.1 %collective-permute-start.7 = (bf16[256,1280]{1,0:T(8,128)(2,1)}, bf16[256,1280]{1,0:T(8,128)(2,1)}, u32[]{:S(2)}, u32[]{:S(2)}) collective-permute-start(bf16[256,1280]{1,0:T(8,128)(2,1)} %collective-permute-done.6.refs_3_), channel_id=1, source_target_pairs={{0,32},{1,97},{2,34},{3,99},{4,36},{5,101},{6,38},{7,103},{8,40},{... | collective-permute-start | bytes 1966088 | tf_op jit(solution)/shard_map/ppermute | solution.py:33
  67.3 25.6 %collective-permute-start.5 = (bf16[256,1280]{1,0:T(8,128)(2,1)}, bf16[256,1280]{1,0:T(8,128)(2,1)S(1)}, u32[]{:S(2)}, u32[]{:S(2)}) collective-permute-start(bf16[256,1280]{1,0:T(8,128)(2,1)} %collective-permute-done.4.refs_0_), channel_id=1, source_target_pairs={{0,32},{1,97},{2,34},{3,99},{4,36},{5,101},{6,38},{7,103},{8,40},{... | collective-permute-start | bytes 1966088 | tf_op jit(solution)/shard_map/ppermute | solution.py:33
  74.4 18.5 %collective-permute-start.8 = (bf16[256,1280]{1,0:T(8,128)(2,1)}, bf16[256,1280]{1,0:T(8,128)(2,1)}, u32[]{:S(2)}, u32[]{:S(2)}) collective-permute-start(bf16[256,1280]{1,0:T(8,128)(2,1)} %collective-permute-done.7.refs_1_), channel_id=1, source_target_pairs={{0,32},{1,97},{2,34},{3,99},{4,36},{5,101},{6,38},{7,103},{8,40},{... | collective-permute-start | bytes 1966088 | tf_op jit(solution)/shard_map/ppermute | solution.py:33
  90.5 17.9 %collective-permute-start.9 = (bf16[512,1280]{1,0:T(8,128)(2,1)}, bf16[512,1280]{1,0:T(8,128)(2,1)}, u32[]{:S(2)}, u32[]{:S(2)}) collective-permute-start(bf16[512,1280]{1,0:T(8,128)(2,1)} %get-tuple-element.44), channel_id=1, source_target_pairs={{0,32},{1,97},{2,34},{3,99},{4,36},{5,101},{6,38},{7,103},{8,40},{... | collective-permute-start | bytes 3932168 | tf_op jit(solution)/shard_map/ppermute | solution.py:33
  103.6 44.2 %all-to-all-start.2 = ((bf16[32,64,768]{2,1,0:T(8,128)(2,1)}), bf16[32,64,768]{2,1,0:T(8,128)(2,1)}, u32[]{:S(2)}, u32[]{:S(2)}) async-start(bf16[32,64,768]{2,1,0:T(8,128)(2,1)} %get-tuple-element.57), calls=%async_computation.2 | async-start | bytes 6291456 | tf_op jit(solution)/shard_map/all_to_all | solution.py:381
  110.3 10.1 %collective-permute-start.10 = (bf16[256,1280]{1,0:T(8,128)(2,1)S(1)}, bf16[256,1280]{1,0:T(8,128)(2,1)S(1)}, u32[]{:S(2)}, u32[]{:S(2)}) collective-permute-start(bf16[256,1280]{1,0:T(8,128)(2,1)S(1)} %get-tuple-element.68), channel_id=1, source_target_pairs={{0,32},{1,97},{2,34},{3,99},{4,36},{5,101},{6,38},{7,103},{8,40},{... | collective-permute-start | bytes 1966088 | tf_op jit(solution)/shard_map/ppermute | solution.py:33
  112.8 14.6 %collective-permute-start.12 = (bf16[256,1280]{1,0:T(8,128)(2,1)S(1)}, bf16[256,1280]{1,0:T(8,128)(2,1)S(1)}, u32[]{:S(2)}, u32[]{:S(2)}) collective-permute-start(bf16[256,1280]{1,0:T(8,128)(2,1)S(1)} %get-tuple-element.67), channel_id=1, source_target_pairs={{0,32},{1,97},{2,34},{3,99},{4,36},{5,101},{6,38},{7,103},{8,40},{... | collective-permute-start | bytes 1966088 | tf_op jit(solution)/shard_map/ppermute | solution.py:33
  121.4 20.2 %collective-permute-start.11 = (bf16[256,1280]{1,0:T(8,128)(2,1)}, bf16[256,1280]{1,0:T(8,128)(2,1)}, u32[]{:S(2)}, u32[]{:S(2)}) collective-permute-start(bf16[256,1280]{1,0:T(8,128)(2,1)} %add_convert_fusion.2), channel_id=1, source_target_pairs={{0,32},{1,97},{2,34},{3,99},{4,36},{5,101},{6,38},{7,103},{8,40},{... | collective-permute-start | bytes 1966088 | tf_op jit(solution)/shard_map/ppermute | solution.py:33
  128.4 13.2 %collective-permute-start.13 = (bf16[256,1280]{1,0:T(8,128)(2,1)}, bf16[256,1280]{1,0:T(8,128)(2,1)}, u32[]{:S(2)}, u32[]{:S(2)}) collective-permute-start(bf16[256,1280]{1,0:T(8,128)(2,1)} %add_convert_fusion), channel_id=1, source_target_pairs={{0,32},{1,97},{2,34},{3,99},{4,36},{5,101},{6,38},{7,103},{8,40},{... | collective-permute-start | bytes 1966088 | tf_op jit(solution)/shard_map/ppermute | solution.py:33
  147.8 26.9 %all-to-all-start.3 = ((bf16[32,16,1280]{2,1,0:T(8,128)(2,1)}), bf16[32,16,1280]{2,1,0:T(8,128)(2,1)}, u32[]{:S(2)}, u32[]{:S(2)}) async-start(bf16[32,16,1280]{2,1,0:T(8,128)(2,1)} %last_sum.1), calls=%async_computation.3 | async-start | bytes 2621440 | tf_op jit(solution)/shard_map/all_to_all | solution.py:381
  156.0 11.2 %collective-permute-start.16 = (bf16[64,1280]{1,0:T(8,128)(2,1)S(1)}, bf16[64,1280]{1,0:T(8,128)(2,1)S(1)}, u32[]{:S(2)}, u32[]{:S(2)}) collective-permute-start(bf16[64,1280]{1,0:T(8,128)(2,1)S(1)} %get-tuple-element.72), channel_id=1, source_target_pairs={{0,32},{32,64},{64,96},{96,0},{1,33},{33,65},{65,97},{97,1},{2,34}... | collective-permute-start | bytes 491528 | tf_op jit(solution)/shard_map/ppermute | solution.py:23
  156.1 12.9 %collective-permute-start.15 = (bf16[64,1280]{1,0:T(8,128)(2,1)S(1)}, bf16[64,1280]{1,0:T(8,128)(2,1)S(1)}, u32[]{:S(2)}, u32[]{:S(2)}) collective-permute-start(bf16[64,1280]{1,0:T(8,128)(2,1)S(1)} %get-tuple-element.73), channel_id=1, source_target_pairs={{0,96},{32,0},{64,32},{96,64},{1,97},{33,1},{65,33},{97,65},{2,98}... | collective-permute-start | bytes 491528 | tf_op jit(solution)/shard_map/ppermute | solution.py:23
  158.7 10.3 %collective-permute-start.14 = (bf16[64,1280]{1,0:T(8,128)(2,1)S(1)}, bf16[64,1280]{1,0:T(8,128)(2,1)S(1)}, u32[]{:S(2)}, u32[]{:S(2)}) collective-permute-start(bf16[64,1280]{1,0:T(8,128)(2,1)S(1)} %get-tuple-element.71), channel_id=1, source_target_pairs={{0,64},{32,96},{64,0},{96,32},{1,65},{33,97},{65,1},{97,33},{2,66}... | collective-permute-start | bytes 491528 | tf_op jit(solution)/shard_map/ppermute | solution.py:23
  164.5 5.5 %collective-permute-start.19 = (bf16[64,768]{1,0:T(8,128)(2,1)S(1)}, bf16[64,768]{1,0:T(8,128)(2,1)S(1)}, u32[]{:S(2)}, u32[]{:S(2)}) collective-permute-start(bf16[64,768]{1,0:T(8,128)(2,1)S(1)} %get-tuple-element.66), channel_id=1, source_target_pairs={{0,32},{32,64},{64,96},{96,0},{1,33},{33,65},{65,97},{97,1},{2,34}... | collective-permute-start | bytes 294920 | tf_op jit(solution)/shard_map/ppermute | solution.py:23
  165.1 4.9 %collective-permute-start.18 = (bf16[64,768]{1,0:T(8,128)(2,1)S(1)}, bf16[64,768]{1,0:T(8,128)(2,1)S(1)}, u32[]{:S(2)}, u32[]{:S(2)}) collective-permute-start(bf16[64,768]{1,0:T(8,128)(2,1)S(1)} %get-tuple-element.65), channel_id=1, source_target_pairs={{0,96},{32,0},{64,32},{96,64},{1,97},{33,1},{65,33},{97,65},{2,98}... | collective-permute-start | bytes 294920 | tf_op jit(solution)/shard_map/ppermute | solution.py:23
  167.2 5.4 %collective-permute-start.17 = (bf16[64,768]{1,0:T(8,128)(2,1)S(1)}, bf16[64,768]{1,0:T(8,128)(2,1)S(1)}, u32[]{:S(2)}, u32[]{:S(2)}) collective-permute-start(bf16[64,768]{1,0:T(8,128)(2,1)S(1)} %get-tuple-element.64), channel_id=1, source_target_pairs={{0,64},{32,96},{64,0},{96,32},{1,65},{33,97},{65,1},{97,33},{2,66}... | collective-permute-start | bytes 294920 | tf_op jit(solution)/shard_map/ppermute | solution.py:23
  (10 other events, 141.2 us)

commit v9 on v8

--- a/solution.py
+++ b/solution.py
@@ -11,7 +11,6 @@
 SEND_COLS = 1280
 BACK_COLS = 1280
 COLS = 128
-WIDE = 256
 NT = (((1,), (1,)), ((), ()))
 TN = (((0,), (0,)), ((), ()))
 AROUND = (2, 1, -1)
@@ -271,88 +270,92 @@
 
 def last_sum(own, *refs):
     ends, out = refs[:-1], refs[-1]
-    n_ep, slots, cols = out.shape
-    rows = n_ep * CAP
+    sources, slots, cols = out.shape
     for c in range(0, cols, COLS):
         parts = []
         for m, end in enumerate(ends):
-            mine = own[m * rows : (m + 1) * rows, c : c + COLS].astype(jnp.float32)
+            mine = own[m, :, c : c + COLS].astype(jnp.float32)
             came = end[:, c : c + COLS].astype(jnp.float32)
-            parts.append((mine + came).reshape(n_ep, CAP, COLS))
+            parts.append((mine + came).reshape(sources, CAP, COLS))
         out[:, :, c : c + COLS] = (
-            jnp.stack(parts, axis=1).reshape(n_ep, slots, COLS).astype(jnp.bfloat16)
+            jnp.stack(parts, axis=1).reshape(sources, slots, COLS).astype(jnp.bfloat16)
         )
 
 
 def call_last_sum(own, ends, n_ep):
-    rows, cols = own.shape
-    slots = len(ends) * CAP
-    block = lambda n: pl.BlockSpec((n, WIDE), lambda c: (0, c))
+    members, cols = len(ends), own.shape[1]
+    steps = 4
+    rows = n_ep * CAP // steps
     return pl.pallas_call(
         last_sum,
-        grid=(cols // WIDE,),
-        in_specs=[block(rows)] + [block(x.shape[0]) for x in ends],
-        out_specs=pl.BlockSpec((n_ep, slots, WIDE), lambda c: (0, 0, c)),
-        out_shape=hbm((n_ep, slots, cols)),
+        grid=(steps,),
+        in_specs=[pl.BlockSpec((members, rows, cols), lambda i: (0, i, 0))]
+        + [pl.BlockSpec((rows, cols), lambda i: (i, 0))] * members,
+        out_specs=pl.BlockSpec((n_ep // steps, members * CAP, cols), lambda i: (i, 0, 0)),
+        out_shape=hbm((n_ep, members * CAP, cols)),
         compiler_params=pltpu.CompilerParams(vmem_limit_bytes=16 * 1024 * 1024),
         name="last_sum",
-    )(*from_hbm(own, *ends))
+    )(*from_hbm(own.reshape(members, n_ep * CAP, cols), *ends))
 
 
 def weigh(hi, lo, values):
     return dot_f32(hi, values) + dot_f32(lo, values)
 
 
-def combine(hi, lo, values, shared, *outs):
+def combine(hi, lo, values, shared, *refs):
+    outs, total = refs[:-1], refs[-1]
     tok = outs[0].shape[0]
-    total = shared[...] + weigh(hi[...], lo[...], values[...])
-    for j, o in enumerate(outs):
-        o[...] = total[j * tok : (j + 1) * tok].astype(jnp.bfloat16)
+    here = pl.program_id(0)
+    part = weigh(hi[...], lo[...], values[...])
+
+    @pl.when(here == 0)
+    def _():
+        total[...] = shared[...] + part
+
+    @pl.when(here > 0)
+    def _():
+        total[...] = total[...] + part
+
+    @pl.when(here == pl.num_programs(0) - 1)
+    def _():
+        for j, o in enumerate(outs):
+            o[...] = total[j * tok : (j + 1) * tok].astype(jnp.bfloat16)
 
 
 def call_combine(hi, lo, values, shared, tok):
     rows, slots = hi.shape
     cols = values.shape[1]
-    whole = pl.BlockSpec((rows, slots), lambda c: (0, 0))
-    block = lambda n: pl.BlockSpec((n, WIDE), lambda c: (0, c))
+    steps = 4
+    left = pl.BlockSpec((rows, slots // steps), lambda i: (0, i))
     return pl.pallas_call(
         combine,
-        grid=(cols // WIDE,),
-        in_specs=[whole, whole, block(slots), block(rows)],
-        out_specs=[block(tok)] * (rows // tok),
+        grid=(steps,),
+        in_specs=[
+            left,
+            left,
+            pl.BlockSpec((slots // steps, cols), lambda i: (i, 0)),
+            pl.BlockSpec((rows, cols), lambda i: (0, 0)),
+        ],
+        out_specs=[pl.BlockSpec((tok, cols), lambda i: (0, 0))] * (rows // tok),
         out_shape=[jax.ShapeDtypeStruct((tok, cols), jnp.bfloat16)] * (rows // tok),
+        scratch_shapes=[pltpu.VMEM((rows, cols), jnp.float32)],
         compiler_params=pltpu.CompilerParams(vmem_limit_bytes=24 * 1024 * 1024),
         name="combine",
-    )(*from_hbm(hi, lo, values), shared)
+    )(*from_hbm(hi, lo, values, shared))
 
 
 def finish(hi, lo, values, early, late, out):
-    here = pl.program_id(0)
-    routed_blocks = pl.num_programs(0) - pl.cdiv(late.shape[1], WIDE)
-
-    @pl.when(here < routed_blocks)
-    def _():
-        out[...] = (early[...] + weigh(hi[...], lo[...], values[...])).astype(jnp.bfloat16)
-
-    @pl.when(here >= routed_blocks)
-    def _():
-        at = pl.multiple_of((here - routed_blocks) * WIDE, WIDE)
-        out[...] = late[:, pl.ds(at, WIDE)]
+    bc = values.shape[1]
+    out[:, bc:] = late[...]
+    out[:, :bc] = (early[...] + weigh(hi[...], lo[...], values[...])).astype(jnp.bfloat16)
 
 
 def call_finish(hi, lo, values, early, late):
-    tok, slots = hi.shape
-    bc = values.shape[1]
-    cols = bc + late.shape[1]
-    last = bc // WIDE - 1
-    whole = lambda shape: pl.BlockSpec(shape, lambda c: (0, 0))
-    block = lambda n: pl.BlockSpec((n, WIDE), lambda c: (0, jnp.minimum(c, last)))
     return pl.pallas_call(
         finish,
-        grid=(cols // WIDE,),
-        in_specs=[whole((tok, slots))] * 2 + [block(slots), block(tok), whole(late.shape)],
-        out_specs=pl.BlockSpec((tok, WIDE), lambda c: (0, c)),
-        out_shape=jax.ShapeDtypeStruct((tok, cols), jnp.bfloat16),
+        out_shape=jax.ShapeDtypeStruct(
+            (hi.shape[0], values.shape[1] + late.shape[1]), jnp.bfloat16
+        ),
         compiler_params=pltpu.CompilerParams(vmem_limit_bytes=16 * 1024 * 1024),
         name="finish",
     )(hi, lo, *from_hbm(values), early, late)
@@ -410,7 +413,7 @@
     *to_far, to_behind, out_b = run_experts([far, behind], 0, came_b, None, *weights, bc)
     f32 = lambda x: x.astype(jnp.float32)
     early = shared[:, :bc].astype(jnp.bfloat16).reshape(n_dp, tok, bc)
-    early = [shifted(early[j], -s) for j, s in enumerate(AROUND)] + [early[n_dp - 1]]
+    early = [early[j] for j in range(n_dp)]
     *to_ahead, to_own, out_b = run_experts([ahead, own_parts], 1, came_b, out_b, *weights, bc)
     ret_b = over_ep(out_b, members * n_dp * CAP, feature - bc)
 
@@ -422,14 +425,15 @@
         passing = (f32(to_far[m]) + f32(arrived[part])).astype(jnp.bfloat16)
         passing = (f32(to_ahead[m]) + f32(toward(passing))).astype(jnp.bfloat16)
         ends.append(toward(passing))
-    *ends, late, hi_b, lo_b, hi_d, lo_d = lax.optimization_barrier(
-        (*ends, shared[:, bc:], hi_b.T, lo_b.T, hi_d.T, lo_d.T)
+    ends, early, late, hi_b, lo_b, hi_d, lo_d = lax.optimization_barrier(
+        (ends, early, shared[:, bc:], hi_b.T, lo_b.T, hi_d.T, lo_d.T)
     )
     back_d = call_last_sum(to_own, ends, n_ep)
     back_d, ret_b = lax.optimization_barrier((back_d, ret_b))
     ret_d = over_ep(back_d, members * CAP, bc)
 
     live = jnp.arange(tok, dtype=jnp.int32) < row_counts[0]
+    early = [shifted(x, -s) for x, s in zip(early, AROUND)] + [early[-1]]
     early = jnp.where(live[:, None], sum(f32(x) for x in early), 0.0)
     *parts, late = call_combine(hi_b, lo_b, ret_b.reshape(-1, feature - bc), late, tok)
     late = f32(late) + sum(f32(shifted(x, -s)) for x, s in zip(parts, AROUND))

time: 181 us -> 178 us (0.983)
  waiting for transfers between devices: 40.1 us -> 43.7 us
  Pallas kernels: 40 us -> 37.6 us
  other arithmetic: 7.8 us -> 5.83 us
    all_to_all x4, waiting for transfers between devices: 6.73 us -> 9.15 us  [over_ep(): lax.all_to_all(x.reshape(n_ep, rows, cols), 'ep', split_axis=0, concat_ax...]
    pallas_call x3, Pallas kernels: 13.9 us -> 11.5 us  [the longest x1 5.09 us: call_combine(): pl.pallas_call(combine, grid=(steps,), in_specs=[left, left, pl.BlockSpec...]
  transfers between devices with their start and end apart: 24 -> 24, of which waited for: 12 -> 14; matrix products, arithmetic and copies ran while one was open for 16% -> 15% of each run, Pallas kernels for 18% -> 18%
where the time goes in v9:
time: 178 us; the launch traced here: 177 us
  starting transfers between devices  67.1 us (38%)
  waiting for transfers between devices  43.7 us (25%)
  Pallas kernels  37.6 us (21%)
  local copies, waits for them, and re-layouts  10.8 us (6%)
  matrix products  10.7 us (6%)
  other arithmetic  5.83 us (3%)
    all_to_all x4, starting transfers between devices, over_ep(): lax.all_to_all(x.reshape(n_ep, rows, cols), 'ep', split_axis=0, concat_ax...  28.4 us
    ppermute x11, starting transfers between devices, toward(): return lax.ppermute(x, ('dp', 'ep'), pairs)  25.7 us
    ppermute x11, waiting for transfers between devices, toward(): return lax.ppermute(x, ('dp', 'ep'), pairs)  20.5 us
    pallas_call x2, Pallas kernels, run_experts(): pl.pallas_call(functools.partial(expert_kernel, len(planes), pair), in_sp...  19.7 us
    ppermute x9, waiting for transfers between devices, shifted(): return lax.ppermute(x, 'dp', [(i, (i + shift) % n) for i in range(n)])  14.1 us
    ppermute x9, starting transfers between devices, shifted(): return lax.ppermute(x, 'dp', [(i, (i + shift) % n) for i in range(n)])  12.9 us
    dot_general x2, matrix products, dot_f32(): return jnp.dot(a, b, preferred_element_type=jnp.float32)  10.7 us
    all_to_all x4, waiting for transfers between devices, over_ep(): lax.all_to_all(x.reshape(n_ep, rows, cols), 'ep', split_axis=0, concat_ax...  9.15 us
  transfers between devices with their start and end apart: 24, of which 14 were waited for; matrix products, arithmetic and copies ran while one was open for 15% of the time, Pallas kernels for 18%

profile of v9, /device:TPU:1, one launch (start us, length us, event | category | flops | bytes accessed | tf_op | source)
XLA Modules:
  0.0 176.7 jit_solution(18239627601504925293)
XLA Ops:
  3.6 9.5 %all-to-all-start = ((bf16[32,16,1280]{2,1,0:T(8,128)(2,1)}), bf16[32,16,1280]{2,1,0:T(8,128)(2,1)}, u32[]{:S(2)}, u32[]{:S(2)}) async-start(bf16[32,16,1280]{2,1,0:T(8,128)(2,1)} %bitcast.30), calls=%async_computation | async-start | bytes 2621440 | tf_op jit(solution)/shard_map/all_to_all | solution.py:384
  13.1 3.0 %collective-permute-start.1 = (bf16[64,2176]{1,0:T(8,128)(2,1)S(1)}, bf16[64,2176]{1,0:T(8,128)(2,1)S(1)}, u32[]{:S(2)}, u32[]{:S(2)}) collective-permute-start(bf16[64,2176]{1,0:T(8,128)(2,1)S(1)} %get-tuple-element.41.e3), channel_id=1, source_target_pairs={{0,64},{32,96},{64,0},{96,32},{1,65},{33,97},{65,1},{97,33},{2,66}... | collective-permute-start | bytes 835592 | tf_op jit(solution)/shard_map/ppermute | solution.py:22
  18.8 4.0 %collective-permute-done.1.e0 = bf16[64,2176]{1,0:T(8,128)(2,1)S(1)} collective-permute-done((bf16[64,2176]{1,0:T(8,128)(2,1)S(1)}, bf16[64,2176]{1,0:T(8,128)(2,1)S(1)}, u32[]{:S(2)}, u32[]{:S(2)}) %collective-permute-start.1) | collective-permute-done | bytes 278560 | tf_op jit(solution)/shard_map/ppermute | solution.py:22
  22.8 6.6 %collective-permute-done.2.e1 = bf16[64,2176]{1,0:T(8,128)(2,1)S(1)} collective-permute-done((bf16[64,2176]{1,0:T(8,128)(2,1)S(1)}, bf16[64,2176]{1,0:T(8,128)(2,1)S(1)}, u32[]{:S(2)}, u32[]{:S(2)}) %collective-permute-start.2) | collective-permute-done | bytes 278560 | tf_op jit(solution)/shard_map/ppermute | solution.py:22
  29.4 3.5 %prepare_ring.1 = (bf16[2048,768]{1,0:T(8,128)(2,1)}, bf16[2048,256]{1,0:T(8,128)(2,1)}, bf16[2048,256]{1,0:T(8,128)(2,1)}, bf16[256,2048]{1,0:T(8,128)(2,1)}) custom-call(bf16[64,2176]{1,0:T(8,128)(2,1)S(1)} %collective-permute-done.1.e0, bf16[64,2176]{1,0:T(8,128)(2,1)S(1)} %collective-permute-done.2.e1, bf16[64,2176]{1,0:T(8,128)(2,1)S(1)} %collective-permute-done.3.e2, ...), custom_call_target="tpu_custom_call" | custom-call | tf_op jit(solution)/shard_map/prepare_ring/pallas_call | solution.py:155
  33.0 7.8 %all-to-all-start.1 = ((bf16[32,64,768]{2,1,0:T(8,128)(2,1)}), bf16[32,64,768]{2,1,0:T(8,128)(2,1)}, u32[]{:S(2)}, u32[]{:S(2)}) async-start(bf16[32,64,768]{2,1,0:T(8,128)(2,1)} %bitcast.29), calls=%async_computation.1 | async-start | bytes 6291456 | tf_op jit(solution)/shard_map/all_to_all | solution.py:384
  45.5 3.7 %fusion.6 = f32[256,704]{0,1:T(8,128)} fusion(bf16[256,2048]{1,0:T(8,128)(2,1)S(1)} %copy-done.7, bf16[2048,704]{0,1:T(8,128)(2,1)} %param.17), kind=kOutput, calls=%fused_computation.15 | convolution fusion | flops 738197504 | bytes 4653056 | tf_op jit(solution)/shard_map/dot_general | solution.py:44
  49.2 7.0 %fusion = f32[256,2048]{1,0:T(8,128)} fusion(bf16[704,2048]{1,0:T(8,128)(2,1)S(1)} %copy-done, f32[256,704]{0,1:T(8,128)} %fusion.6, bf16[256,2048]{1,0:T(8,128)(2,1)} %get-tuple-element.42, bf16[2048,704]{0,1:T(8,128)(2,1)} %param.18), kind=kOutput, calls=%fused_computation.7 | convolution fusion | flops 1477476352 | bytes 9633792 | tf_op jit(solution)/shard_map/dot_general | solution.py:44
  56.9 3.3 %collective-permute-done.6.refs_3_ = bf16[256,1280]{1,0:T(8,128)(2,1)} collective-permute-done((bf16[256,1280]{1,0:T(8,128)(2,1)S(1)}, bf16[256,1280]{1,0:T(8,128)(2,1)}, u32[]{:S(2)}, u32[]{:S(2)}) %collective-permute-start.6) | collective-permute-done | bytes 655392 | tf_op jit(solution)/shard_map/ppermute | solution.py:32
  60.2 3.5 %collective-permute-start.7 = (bf16[256,1280]{1,0:T(8,128)(2,1)}, bf16[256,1280]{1,0:T(8,128)(2,1)}, u32[]{:S(2)}, u32[]{:S(2)}) collective-permute-start(bf16[256,1280]{1,0:T(8,128)(2,1)} %collective-permute-done.6.refs_3_), channel_id=1, source_target_pairs={{0,32},{1,97},{2,34},{3,99},{4,36},{5,101},{6,38},{7,103},{8,40},{... | collective-permute-start | bytes 1966088 | tf_op jit(solution)/shard_map/ppermute | solution.py:32
  63.7 3.6 %collective-permute-done.4.refs_0_ = bf16[256,1280]{1,0:T(8,128)(2,1)} collective-permute-done((bf16[256,1280]{1,0:T(8,128)(2,1)}, bf16[256,1280]{1,0:T(8,128)(2,1)}, u32[]{:S(2)}, u32[]{:S(2)}) %collective-permute-start.4) | collective-permute-done | bytes 655392 | tf_op jit(solution)/shard_map/ppermute | solution.py:32
  67.3 3.4 %collective-permute-start.5 = (bf16[256,1280]{1,0:T(8,128)(2,1)}, bf16[256,1280]{1,0:T(8,128)(2,1)S(1)}, u32[]{:S(2)}, u32[]{:S(2)}) collective-permute-start(bf16[256,1280]{1,0:T(8,128)(2,1)} %collective-permute-done.4.refs_0_), channel_id=1, source_target_pairs={{0,32},{1,97},{2,34},{3,99},{4,36},{5,101},{6,38},{7,103},{8,40},{... | collective-permute-start | bytes 1966088 | tf_op jit(solution)/shard_map/ppermute | solution.py:32
  70.7 3.6 %collective-permute-done.7.refs_1_ = bf16[256,1280]{1,0:T(8,128)(2,1)} collective-permute-done((bf16[256,1280]{1,0:T(8,128)(2,1)}, bf16[256,1280]{1,0:T(8,128)(2,1)}, u32[]{:S(2)}, u32[]{:S(2)}) %collective-permute-start.7) | collective-permute-done | bytes 655392 | tf_op jit(solution)/shard_map/ppermute | solution.py:32
  74.3 3.4 %collective-permute-start.8 = (bf16[256,1280]{1,0:T(8,128)(2,1)}, bf16[256,1280]{1,0:T(8,128)(2,1)}, u32[]{:S(2)}, u32[]{:S(2)}) collective-permute-start(bf16[256,1280]{1,0:T(8,128)(2,1)} %collective-permute-done.7.refs_1_), channel_id=1, source_target_pairs={{0,32},{1,97},{2,34},{3,99},{4,36},{5,101},{6,38},{7,103},{8,40},{... | collective-permute-start | bytes 1966088 | tf_op jit(solution)/shard_map/ppermute | solution.py:32
  80.6 9.8 %experts.2 = (bf16[256,1280]{1,0:T(8,128)(2,1)}, bf16[256,1280]{1,0:T(8,128)(2,1)}, bf16[512,1280]{1,0:T(8,128)(2,1)}, bf16[32,64,768]{2,1,0:T(8,128)(2,1)}) custom-call(bf16[256,1280]{1,0:T(8,128)(2,1)} %collective-permute-done.4.refs_0_, bf16[256,1280]{1,0:T(8,128)(2,1)} %collective-permute-done.7.refs_1_, bf16[256,1280]{1,0:T(8,128)(2,1)} %collective-permute-done.refs_2_, ...), custom_call_target="tpu_custom_call" | custom-call | flops 20000000000 | bytes 200000000 | tf_op jit(solution)/shard_map/experts/pallas_call | solution.py:246
  93.7 9.8 %experts.3 = (bf16[256,1280]{1,0:T(8,128)(2,1)}, bf16[256,1280]{1,0:T(8,128)(2,1)}, bf16[512,1280]{1,0:T(8,128)(2,1)}, bf16[32,64,768]{2,1,0:T(8,128)(2,1)}) custom-call(bf16[256,1280]{1,0:T(8,128)(2,1)} %copy-done.8, bf16[256,1280]{1,0:T(8,128)(2,1)} %collective-permute-done.8.refs_1_, ...), custom_call_target="tpu_custom_call", output_to_operand_aliasing={{3}: (8, {})} | custom-call | flops 20000000000 | bytes 200000000 | tf_op jit(solution)/shard_map/experts/pallas_call | solution.py:246
  103.5 4.8 %all-to-all-start.2 = ((bf16[32,64,768]{2,1,0:T(8,128)(2,1)}), bf16[32,64,768]{2,1,0:T(8,128)(2,1)}, u32[]{:S(2)}, u32[]{:S(2)}) async-start(bf16[32,64,768]{2,1,0:T(8,128)(2,1)} %get-tuple-element.61), calls=%async_computation.2 | async-start | bytes 6291456 | tf_op jit(solution)/shard_map/all_to_all | solution.py:384
  113.1 7.2 %collective-permute-done.10 = bf16[256,1280]{1,0:T(8,128)(2,1)S(1)} collective-permute-done((bf16[256,1280]{1,0:T(8,128)(2,1)S(1)}, bf16[256,1280]{1,0:T(8,128)(2,1)S(1)}, u32[]{:S(2)}, u32[]{:S(2)}) %collective-permute-start.10) | collective-permute-done | bytes 655392 | tf_op jit(solution)/shard_map/ppermute | solution.py:32
  121.3 3.5 %collective-permute-start.11 = (bf16[256,1280]{1,0:T(8,128)(2,1)}, bf16[256,1280]{1,0:T(8,128)(2,1)}, u32[]{:S(2)}, u32[]{:S(2)}) collective-permute-start(bf16[256,1280]{1,0:T(8,128)(2,1)} %add_convert_fusion.2), channel_id=1, source_target_pairs={{0,32},{1,97},{2,34},{3,99},{4,36},{5,101},{6,38},{7,103},{8,40},{... | collective-permute-start | bytes 1966088 | tf_op jit(solution)/shard_map/ppermute | solution.py:32
  128.3 3.5 %collective-permute-start.13 = (bf16[256,1280]{1,0:T(8,128)(2,1)}, bf16[256,1280]{1,0:T(8,128)(2,1)}, u32[]{:S(2)}, u32[]{:S(2)}) collective-permute-start(bf16[256,1280]{1,0:T(8,128)(2,1)} %add_convert_fusion), channel_id=1, source_target_pairs={{0,32},{1,97},{2,34},{3,99},{4,36},{5,101},{6,38},{7,103},{8,40},{... | collective-permute-start | bytes 1966088 | tf_op jit(solution)/shard_map/ppermute | solution.py:32
  141.5 3.9 %last_sum.1 = bf16[32,16,1280]{2,1,0:T(8,128)(2,1)} custom-call(bf16[2,256,1280]{2,1,0:T(8,128)(2,1)} %bitcast.31, bf16[256,1280]{1,0:T(8,128)(2,1)} %collective-permute-done.11.refs_0_, bf16[256,1280]{1,0:T(8,128)(2,1)} %collective-permute-done.13.refs_1_), custom_call_target="tpu_custom_call" | custom-call | tf_op jit(solution)/shard_map/last_sum/pallas_call | solution.py:289
  147.8 6.5 %all-to-all-start.3 = ((bf16[32,16,1280]{2,1,0:T(8,128)(2,1)}), bf16[32,16,1280]{2,1,0:T(8,128)(2,1)}, u32[]{:S(2)}, u32[]{:S(2)}) async-start(bf16[32,16,1280]{2,1,0:T(8,128)(2,1)} %last_sum.1), calls=%async_computation.3 | async-start | bytes 2621440 | tf_op jit(solution)/shard_map/all_to_all | solution.py:384
  157.0 5.1 %combine.1 = (bf16[64,768]{1,0:T(8,128)(2,1)S(1)}, bf16[64,768]{1,0:T(8,128)(2,1)S(1)}, bf16[64,768]{1,0:T(8,128)(2,1)S(1)}, bf16[64,768]{1,0:T(8,128)(2,1)S(1)}) custom-call(bf16[256,2048]{1,0:T(8,128)(2,1)} %bitcast.27, bf16[256,2048]{1,0:T(8,128)(2,1)} %bitcast.28, bf16[2048,768]{1,0:T(8,128)(2,1)} %bitcast.16.values, f32[256,768]{1,0:T(8,128)} %slice.45.shared), custom_call_target="tpu_custom_call" | custom-call | tf_op jit(solution)/shard_map/combine/pallas_call | solution.py:330
  170.3 3.8 %all-to-all-done.3 = bf16[32,16,1280]{2,1,0:T(8,128)(2,1)} async-done(((bf16[32,16,1280]{2,1,0:T(8,128)(2,1)}), bf16[32,16,1280]{2,1,0:T(8,128)(2,1)}, u32[]{:S(2)}, u32[]{:S(2)}) %all-to-all-start.3) | async-done | bytes 1310752 | tf_op jit(solution)/shard_map/all_to_all | solution.py:384
  (65 shorter events, 52.0 us)
Async XLA Ops:
  3.6 29.3 %all-to-all-start = ((bf16[32,16,1280]{2,1,0:T(8,128)(2,1)}), bf16[32,16,1280]{2,1,0:T(8,128)(2,1)}, u32[]{:S(2)}, u32[]{:S(2)}) async-start(bf16[32,16,1280]{2,1,0:T(8,128)(2,1)} %bitcast.30), calls=%async_computation | async-start | bytes 2621440 | tf_op jit(solution)/shard_map/all_to_all | solution.py:384
  13.1 9.7 %collective-permute-start.1 = (bf16[64,2176]{1,0:T(8,128)(2,1)S(1)}, bf16[64,2176]{1,0:T(8,128)(2,1)S(1)}, u32[]{:S(2)}, u32[]{:S(2)}) collective-permute-start(bf16[64,2176]{1,0:T(8,128)(2,1)S(1)} %get-tuple-element.41.e3), channel_id=1, source_target_pairs={{0,64},{32,96},{64,0},{96,32},{1,65},{33,97},{65,1},{97,33},{2,66}... | collective-permute-start | bytes 835592 | tf_op jit(solution)/shard_map/ppermute | solution.py:22
  16.1 13.2 %collective-permute-start.2 = (bf16[64,2176]{1,0:T(8,128)(2,1)S(1)}, bf16[64,2176]{1,0:T(8,128)(2,1)S(1)}, u32[]{:S(2)}, u32[]{:S(2)}) collective-permute-start(bf16[64,2176]{1,0:T(8,128)(2,1)S(1)} %get-tuple-element.41.e3), channel_id=1, source_target_pairs={{0,32},{32,64},{64,96},{96,0},{1,33},{33,65},{65,97},{97,1},{2,34}... | collective-permute-start | bytes 835592 | tf_op jit(solution)/shard_map/ppermute | solution.py:22
  16.5 12.8 %collective-permute-start.3 = (bf16[64,2176]{1,0:T(8,128)(2,1)S(1)}, bf16[64,2176]{1,0:T(8,128)(2,1)S(1)}, u32[]{:S(2)}, u32[]{:S(2)}) collective-permute-start(bf16[64,2176]{1,0:T(8,128)(2,1)S(1)} %get-tuple-element.41.e3), channel_id=1, source_target_pairs={{0,96},{32,0},{64,32},{96,64},{1,97},{33,1},{65,33},{97,65},{2,98}... | collective-permute-start | bytes 835592 | tf_op jit(solution)/shard_map/ppermute | solution.py:22
  33.0 47.6 %all-to-all-start.1 = ((bf16[32,64,768]{2,1,0:T(8,128)(2,1)}), bf16[32,64,768]{2,1,0:T(8,128)(2,1)}, u32[]{:S(2)}, u32[]{:S(2)}) async-start(bf16[32,64,768]{2,1,0:T(8,128)(2,1)} %bitcast.29), calls=%async_computation.1 | async-start | bytes 6291456 | tf_op jit(solution)/shard_map/all_to_all | solution.py:384
  43.1 13.1 %collective-permute-start = (bf16[256,1280]{1,0:T(8,128)(2,1)}, bf16[256,1280]{1,0:T(8,128)(2,1)}, u32[]{:S(2)}, u32[]{:S(2)}) collective-permute-start(bf16[256,1280]{1,0:T(8,128)(2,1)} %get-tuple-element.78.refs_2_), channel_id=1, source_target_pairs={{0,32},{1,97},{2,34},{3,99},{4,36},{5,101},{6,38},{7,103},{8,40},{... | collective-permute-start | bytes 1966088 | tf_op jit(solution)/shard_map/ppermute | solution.py:32
  45.4 14.8 %collective-permute-start.6 = (bf16[256,1280]{1,0:T(8,128)(2,1)S(1)}, bf16[256,1280]{1,0:T(8,128)(2,1)}, u32[]{:S(2)}, u32[]{:S(2)}) collective-permute-start(bf16[256,1280]{1,0:T(8,128)(2,1)S(1)} %get-tuple-element.77.refs_3_), channel_id=1, source_target_pairs={{0,32},{1,97},{2,34},{3,99},{4,36},{5,101},{6,38},{7,103},{8,40},{... | collective-permute-start | bytes 1966088 | tf_op jit(solution)/shard_map/ppermute | solution.py:32
  56.2 11.1 %collective-permute-start.4 = (bf16[256,1280]{1,0:T(8,128)(2,1)}, bf16[256,1280]{1,0:T(8,128)(2,1)}, u32[]{:S(2)}, u32[]{:S(2)}) collective-permute-start(bf16[256,1280]{1,0:T(8,128)(2,1)} %collective-permute-done.refs_2_), channel_id=1, source_target_pairs={{0,32},{1,97},{2,34},{3,99},{4,36},{5,101},{6,38},{7,103},{8,40},{... | collective-permute-start | bytes 1966088 | tf_op jit(solution)/shard_map/ppermute | solution.py:32
  60.2 14.1 %collective-permute-start.7 = (bf16[256,1280]{1,0:T(8,128)(2,1)}, bf16[256,1280]{1,0:T(8,128)(2,1)}, u32[]{:S(2)}, u32[]{:S(2)}) collective-permute-start(bf16[256,1280]{1,0:T(8,128)(2,1)} %collective-permute-done.6.refs_3_), channel_id=1, source_target_pairs={{0,32},{1,97},{2,34},{3,99},{4,36},{5,101},{6,38},{7,103},{8,40},{... | collective-permute-start | bytes 1966088 | tf_op jit(solution)/shard_map/ppermute | solution.py:32
  67.3 25.5 %collective-permute-start.5 = (bf16[256,1280]{1,0:T(8,128)(2,1)}, bf16[256,1280]{1,0:T(8,128)(2,1)S(1)}, u32[]{:S(2)}, u32[]{:S(2)}) collective-permute-start(bf16[256,1280]{1,0:T(8,128)(2,1)} %collective-permute-done.4.refs_0_), channel_id=1, source_target_pairs={{0,32},{1,97},{2,34},{3,99},{4,36},{5,101},{6,38},{7,103},{8,40},{... | collective-permute-start | bytes 1966088 | tf_op jit(solution)/shard_map/ppermute | solution.py:32
  74.3 18.5 %collective-permute-start.8 = (bf16[256,1280]{1,0:T(8,128)(2,1)}, bf16[256,1280]{1,0:T(8,128)(2,1)}, u32[]{:S(2)}, u32[]{:S(2)}) collective-permute-start(bf16[256,1280]{1,0:T(8,128)(2,1)} %collective-permute-done.7.refs_1_), channel_id=1, source_target_pairs={{0,32},{1,97},{2,34},{3,99},{4,36},{5,101},{6,38},{7,103},{8,40},{... | collective-permute-start | bytes 1966088 | tf_op jit(solution)/shard_map/ppermute | solution.py:32
  90.4 17.9 %collective-permute-start.9 = (bf16[512,1280]{1,0:T(8,128)(2,1)}, bf16[512,1280]{1,0:T(8,128)(2,1)}, u32[]{:S(2)}, u32[]{:S(2)}) collective-permute-start(bf16[512,1280]{1,0:T(8,128)(2,1)} %get-tuple-element.48), channel_id=1, source_target_pairs={{0,32},{1,97},{2,34},{3,99},{4,36},{5,101},{6,38},{7,103},{8,40},{... | collective-permute-start | bytes 3932168 | tf_op jit(solution)/shard_map/ppermute | solution.py:32
  103.5 44.2 %all-to-all-start.2 = ((bf16[32,64,768]{2,1,0:T(8,128)(2,1)}), bf16[32,64,768]{2,1,0:T(8,128)(2,1)}, u32[]{:S(2)}, u32[]{:S(2)}) async-start(bf16[32,64,768]{2,1,0:T(8,128)(2,1)} %get-tuple-element.61), calls=%async_computation.2 | async-start | bytes 6291456 | tf_op jit(solution)/shard_map/all_to_all | solution.py:384
  110.3 10.0 %collective-permute-start.10 = (bf16[256,1280]{1,0:T(8,128)(2,1)S(1)}, bf16[256,1280]{1,0:T(8,128)(2,1)S(1)}, u32[]{:S(2)}, u32[]{:S(2)}) collective-permute-start(bf16[256,1280]{1,0:T(8,128)(2,1)S(1)} %get-tuple-element.76), channel_id=1, source_target_pairs={{0,32},{1,97},{2,34},{3,99},{4,36},{5,101},{6,38},{7,103},{8,40},{... | collective-permute-start | bytes 1966088 | tf_op jit(solution)/shard_map/ppermute | solution.py:32
  112.8 14.6 %collective-permute-start.12 = (bf16[256,1280]{1,0:T(8,128)(2,1)S(1)}, bf16[256,1280]{1,0:T(8,128)(2,1)S(1)}, u32[]{:S(2)}, u32[]{:S(2)}) collective-permute-start(bf16[256,1280]{1,0:T(8,128)(2,1)S(1)} %get-tuple-element.75), channel_id=1, source_target_pairs={{0,32},{1,97},{2,34},{3,99},{4,36},{5,101},{6,38},{7,103},{8,40},{... | collective-permute-start | bytes 1966088 | tf_op jit(solution)/shard_map/ppermute | solution.py:32
  121.3 19.9 %collective-permute-start.11 = (bf16[256,1280]{1,0:T(8,128)(2,1)}, bf16[256,1280]{1,0:T(8,128)(2,1)}, u32[]{:S(2)}, u32[]{:S(2)}) collective-permute-start(bf16[256,1280]{1,0:T(8,128)(2,1)} %add_convert_fusion.2), channel_id=1, source_target_pairs={{0,32},{1,97},{2,34},{3,99},{4,36},{5,101},{6,38},{7,103},{8,40},{... | collective-permute-start | bytes 1966088 | tf_op jit(solution)/shard_map/ppermute | solution.py:32
  128.3 13.1 %collective-permute-start.13 = (bf16[256,1280]{1,0:T(8,128)(2,1)}, bf16[256,1280]{1,0:T(8,128)(2,1)}, u32[]{:S(2)}, u32[]{:S(2)}) collective-permute-start(bf16[256,1280]{1,0:T(8,128)(2,1)} %add_convert_fusion), channel_id=1, source_target_pairs={{0,32},{1,97},{2,34},{3,99},{4,36},{5,101},{6,38},{7,103},{8,40},{... | collective-permute-start | bytes 1966088 | tf_op jit(solution)/shard_map/ppermute | solution.py:32
  147.8 26.3 %all-to-all-start.3 = ((bf16[32,16,1280]{2,1,0:T(8,128)(2,1)}), bf16[32,16,1280]{2,1,0:T(8,128)(2,1)}, u32[]{:S(2)}, u32[]{:S(2)}) async-start(bf16[32,16,1280]{2,1,0:T(8,128)(2,1)} %last_sum.1), calls=%async_computation.3 | async-start | bytes 2621440 | tf_op jit(solution)/shard_map/all_to_all | solution.py:384
  154.2 10.6 %collective-permute-start.16 = (bf16[64,1280]{1,0:T(8,128)(2,1)}, bf16[64,1280]{1,0:T(8,128)(2,1)S(1)}, u32[]{:S(2)}, u32[]{:S(2)}) collective-permute-start(bf16[64,1280]{1,0:T(8,128)(2,1)} %get-tuple-element.65), channel_id=1, source_target_pairs={{0,32},{32,64},{64,96},{96,0},{1,33},{33,65},{65,97},{97,1},{2,34}... | collective-permute-start | bytes 491528 | tf_op jit(solution)/shard_map/ppermute | solution.py:22
  154.3 12.3 %collective-permute-start.15 = (bf16[64,1280]{1,0:T(8,128)(2,1)S(1)}, bf16[64,1280]{1,0:T(8,128)(2,1)S(1)}, u32[]{:S(2)}, u32[]{:S(2)}) collective-permute-start(bf16[64,1280]{1,0:T(8,128)(2,1)S(1)} %get-tuple-element.64), channel_id=1, source_target_pairs={{0,96},{32,0},{64,32},{96,64},{1,97},{33,1},{65,33},{97,65},{2,98}... | collective-permute-start | bytes 491528 | tf_op jit(solution)/shard_map/ppermute | solution.py:22
  157.0 9.6 %collective-permute-start.14 = (bf16[64,1280]{1,0:T(8,128)(2,1)S(1)}, bf16[64,1280]{1,0:T(8,128)(2,1)S(1)}, u32[]{:S(2)}, u32[]{:S(2)}) collective-permute-start(bf16[64,1280]{1,0:T(8,128)(2,1)S(1)} %get-tuple-element.63), channel_id=1, source_target_pairs={{0,64},{32,96},{64,0},{96,32},{1,65},{33,97},{65,1},{97,33},{2,66}... | collective-permute-start | bytes 491528 | tf_op jit(solution)/shard_map/ppermute | solution.py:22
  162.1 5.1 %collective-permute-start.19 = (bf16[64,768]{1,0:T(8,128)(2,1)S(1)}, bf16[64,768]{1,0:T(8,128)(2,1)S(1)}, u32[]{:S(2)}, u32[]{:S(2)}) collective-permute-start(bf16[64,768]{1,0:T(8,128)(2,1)S(1)} %get-tuple-element.74), channel_id=1, source_target_pairs={{0,32},{32,64},{64,96},{96,0},{1,33},{33,65},{65,97},{97,1},{2,34}... | collective-permute-start | bytes 294920 | tf_op jit(solution)/shard_map/ppermute | solution.py:22
  162.7 4.5 %collective-permute-start.18 = (bf16[64,768]{1,0:T(8,128)(2,1)S(1)}, bf16[64,768]{1,0:T(8,128)(2,1)S(1)}, u32[]{:S(2)}, u32[]{:S(2)}) collective-permute-start(bf16[64,768]{1,0:T(8,128)(2,1)S(1)} %get-tuple-element.73), channel_id=1, source_target_pairs={{0,96},{32,0},{64,32},{96,64},{1,97},{33,1},{65,33},{97,65},{2,98}... | collective-permute-start | bytes 294920 | tf_op jit(solution)/shard_map/ppermute | solution.py:22
  164.8 5.4 %collective-permute-start.17 = (bf16[64,768]{1,0:T(8,128)(2,1)S(1)}, bf16[64,768]{1,0:T(8,128)(2,1)S(1)}, u32[]{:S(2)}, u32[]{:S(2)}) collective-permute-start(bf16[64,768]{1,0:T(8,128)(2,1)S(1)} %get-tuple-element.72), channel_id=1, source_target_pairs={{0,64},{32,96},{64,0},{96,32},{1,65},{33,97},{65,1},{97,33},{2,66}... | collective-permute-start | bytes 294920 | tf_op jit(solution)/shard_map/ppermute | solution.py:22
  (9 other events, 140.0 us)

commit v10 on v9

--- a/solution.py
+++ b/solution.py
@@ -270,32 +270,26 @@
 
 def last_sum(own, *refs):
     ends, out = refs[:-1], refs[-1]
-    sources, slots, cols = out.shape
+    n_ep, slots, cols = out.shape
+    rows = n_ep * CAP
     for c in range(0, cols, COLS):
         parts = []
         for m, end in enumerate(ends):
-            mine = own[m, :, c : c + COLS].astype(jnp.float32)
+            mine = own[m * rows : (m + 1) * rows, c : c + COLS].astype(jnp.float32)
             came = end[:, c : c + COLS].astype(jnp.float32)
-            parts.append((mine + came).reshape(sources, CAP, COLS))
+            parts.append((mine + came).reshape(n_ep, CAP, COLS))
         out[:, :, c : c + COLS] = (
-            jnp.stack(parts, axis=1).reshape(sources, slots, COLS).astype(jnp.bfloat16)
+            jnp.stack(parts, axis=1).reshape(n_ep, slots, COLS).astype(jnp.bfloat16)
         )
 
 
 def call_last_sum(own, ends, n_ep):
-    members, cols = len(ends), own.shape[1]
-    steps = 4
-    rows = n_ep * CAP // steps
     return pl.pallas_call(
         last_sum,
-        grid=(steps,),
-        in_specs=[pl.BlockSpec((members, rows, cols), lambda i: (0, i, 0))]
-        + [pl.BlockSpec((rows, cols), lambda i: (i, 0))] * members,
-        out_specs=pl.BlockSpec((n_ep // steps, members * CAP, cols), lambda i: (i, 0, 0)),
-        out_shape=hbm((n_ep, members * CAP, cols)),
+        out_shape=hbm((n_ep, len(ends) * CAP, own.shape[1])),
         compiler_params=pltpu.CompilerParams(vmem_limit_bytes=16 * 1024 * 1024),
         name="last_sum",
-    )(*from_hbm(own.reshape(members, n_ep * CAP, cols), *ends))
+    )(*from_hbm(own, *ends))
 
 
 def weigh(hi, lo, values):
@@ -397,8 +391,11 @@
 
     weights = (expert_gate.swapaxes(1, 2), expert_up.swapaxes(1, 2), expert_down)
 
-    own_slots = own.reshape(n_ep, members, CAP, sc)
-    own_parts = [own_slots[:, m].reshape(n_ep * CAP, sc) for m in range(members)]
+    own_parts = []
+    for m in range(members):
+        own_slots = own.reshape(n_ep, members, CAP, sc)
+        own_parts.append(own_slots[:, m].reshape(n_ep * CAP, sc))
+        own, own_parts[m] = lax.optimization_barrier((own, own_parts[m]))
     behind = [toward(x) for x in own_parts]
 
     gate_act = dot_f32(gathered, shared_gate)

time: 178 us -> 177 us (level)
  starting transfers between devices: 67.1 us -> 63.8 us
  waiting for transfers between devices: 43.7 us -> 46.1 us
    ppermute x11, starting transfers between devices: 25.7 us -> 23.2 us  [toward(): return lax.ppermute(x, ('dp', 'ep'), pairs)]
  transfers between devices with their start and end apart: 24 -> 24, of which waited for: 14 -> 14; matrix products, arithmetic and copies ran while one was open for 15% -> 16% of each run, Pallas kernels for 18% -> 18%
where the time goes in v10:
time: 177 us; the launch traced here: 176 us
  starting transfers between devices  63.8 us (36%)
  waiting for transfers between devices  46.1 us (26%)
  Pallas kernels  36.8 us (21%)
  local copies, waits for them, and re-layouts  11.6 us (7%)
  matrix products  10.7 us (6%)
  other arithmetic  5.84 us (3%)
    all_to_all x4, starting transfers between devices, over_ep(): lax.all_to_all(x.reshape(n_ep, rows, cols), 'ep', split_axis=0, concat_ax...  27.6 us
    ppermute x11, starting transfers between devices, toward(): return lax.ppermute(x, ('dp', 'ep'), pairs)  23.2 us
    ppermute x11, waiting for transfers between devices, toward(): return lax.ppermute(x, ('dp', 'ep'), pairs)  20.9 us
    pallas_call x2, Pallas kernels, run_experts(): pl.pallas_call(functools.partial(expert_kernel, len(planes), pair), in_sp...  19.7 us
    ppermute x9, waiting for transfers between devices, shifted(): return lax.ppermute(x, 'dp', [(i, (i + shift) % n) for i in range(n)])  14.4 us
    ppermute x9, starting transfers between devices, shifted(): return lax.ppermute(x, 'dp', [(i, (i + shift) % n) for i in range(n)])  12.9 us
    all_to_all x4, waiting for transfers between devices, over_ep(): lax.all_to_all(x.reshape(n_ep, rows, cols), 'ep', split_axis=0, concat_ax...  10.8 us
    dot_general x2, matrix products, dot_f32(): return jnp.dot(a, b, preferred_element_type=jnp.float32)  10.7 us
  transfers between devices with their start and end apart: 24, of which 14 were waited for; matrix products, arithmetic and copies ran while one was open for 16% of the time, Pallas kernels for 18%

profile of v10, /device:TPU:1, one launch (start us, length us, event | category | flops | bytes accessed | tf_op | source)
XLA Modules:
  0.0 175.9 jit_solution(14635731565180788976)
XLA Ops:
  3.6 9.5 %all-to-all-start = ((bf16[32,16,1280]{2,1,0:T(8,128)(2,1)}), bf16[32,16,1280]{2,1,0:T(8,128)(2,1)}, u32[]{:S(2)}, u32[]{:S(2)}) async-start(bf16[32,16,1280]{2,1,0:T(8,128)(2,1)} %bitcast.30), calls=%async_computation | async-start | bytes 2621440 | tf_op jit(solution)/shard_map/all_to_all | solution.py:378
  13.1 3.0 %collective-permute-start.1 = (bf16[64,2176]{1,0:T(8,128)(2,1)S(1)}, bf16[64,2176]{1,0:T(8,128)(2,1)S(1)}, u32[]{:S(2)}, u32[]{:S(2)}) collective-permute-start(bf16[64,2176]{1,0:T(8,128)(2,1)S(1)} %get-tuple-element.45.e3), channel_id=1, source_target_pairs={{0,64},{32,96},{64,0},{96,32},{1,65},{33,97},{65,1},{97,33},{2,66}... | collective-permute-start | bytes 835592 | tf_op jit(solution)/shard_map/ppermute | solution.py:22
  18.8 4.0 %collective-permute-done.1.e0 = bf16[64,2176]{1,0:T(8,128)(2,1)S(1)} collective-permute-done((bf16[64,2176]{1,0:T(8,128)(2,1)S(1)}, bf16[64,2176]{1,0:T(8,128)(2,1)S(1)}, u32[]{:S(2)}, u32[]{:S(2)}) %collective-permute-start.1) | collective-permute-done | bytes 278560 | tf_op jit(solution)/shard_map/ppermute | solution.py:22
  22.8 6.6 %collective-permute-done.2.e1 = bf16[64,2176]{1,0:T(8,128)(2,1)S(1)} collective-permute-done((bf16[64,2176]{1,0:T(8,128)(2,1)S(1)}, bf16[64,2176]{1,0:T(8,128)(2,1)S(1)}, u32[]{:S(2)}, u32[]{:S(2)}) %collective-permute-start.2) | collective-permute-done | bytes 278560 | tf_op jit(solution)/shard_map/ppermute | solution.py:22
  29.4 3.5 %prepare_ring.1 = (bf16[2048,768]{1,0:T(8,128)(2,1)}, bf16[2048,256]{1,0:T(8,128)(2,1)}, bf16[2048,256]{1,0:T(8,128)(2,1)}, bf16[256,2048]{1,0:T(8,128)(2,1)}) custom-call(bf16[64,2176]{1,0:T(8,128)(2,1)S(1)} %collective-permute-done.1.e0, bf16[64,2176]{1,0:T(8,128)(2,1)S(1)} %collective-permute-done.2.e1, bf16[64,2176]{1,0:T(8,128)(2,1)S(1)} %collective-permute-done.3.e2, ...), custom_call_target="tpu_custom_call" | custom-call | tf_op jit(solution)/shard_map/prepare_ring/pallas_call | solution.py:155
  33.0 7.7 %all-to-all-start.1 = ((bf16[32,64,768]{2,1,0:T(8,128)(2,1)}), bf16[32,64,768]{2,1,0:T(8,128)(2,1)}, u32[]{:S(2)}, u32[]{:S(2)}) async-start(bf16[32,64,768]{2,1,0:T(8,128)(2,1)} %bitcast.29), calls=%async_computation.1 | async-start | bytes 6291456 | tf_op jit(solution)/shard_map/all_to_all | solution.py:378
  46.6 3.7 %fusion.6 = f32[256,704]{0,1:T(8,128)} fusion(bf16[256,2048]{1,0:T(8,128)(2,1)S(1)} %copy-done.7, bf16[2048,704]{0,1:T(8,128)(2,1)} %param.17), kind=kOutput, calls=%fused_computation.15 | convolution fusion | flops 738197504 | bytes 4653056 | tf_op jit(solution)/shard_map/dot_general | solution.py:44
  50.3 7.0 %fusion = f32[256,2048]{1,0:T(8,128)} fusion(bf16[704,2048]{1,0:T(8,128)(2,1)S(1)} %copy-done, f32[256,704]{0,1:T(8,128)} %fusion.6, bf16[256,2048]{1,0:T(8,128)(2,1)} %get-tuple-element.46, bf16[2048,704]{0,1:T(8,128)(2,1)} %param.18), kind=kOutput, calls=%fused_computation.7 | convolution fusion | flops 1477476352 | bytes 9633792 | tf_op jit(solution)/shard_map/dot_general | solution.py:44
  59.0 3.4 %collective-permute-start.7 = (bf16[256,1280]{1,0:T(8,128)(2,1)}, bf16[256,1280]{1,0:T(8,128)(2,1)}, u32[]{:S(2)}, u32[]{:S(2)}) collective-permute-start(bf16[256,1280]{1,0:T(8,128)(2,1)} %collective-permute-done.6.refs_3_), channel_id=1, source_target_pairs={{0,32},{1,97},{2,34},{3,99},{4,36},{5,101},{6,38},{7,103},{8,40},{... | collective-permute-start | bytes 1966088 | tf_op jit(solution)/shard_map/ppermute | solution.py:32
  62.5 4.9 %collective-permute-done.4.refs_0_ = bf16[256,1280]{1,0:T(8,128)(2,1)} collective-permute-done((bf16[256,1280]{1,0:T(8,128)(2,1)}, bf16[256,1280]{1,0:T(8,128)(2,1)}, u32[]{:S(2)}, u32[]{:S(2)}) %collective-permute-start.4) | collective-permute-done | bytes 655392 | tf_op jit(solution)/shard_map/ppermute | solution.py:32
  69.5 4.9 %collective-permute-done.7.refs_1_ = bf16[256,1280]{1,0:T(8,128)(2,1)} collective-permute-done((bf16[256,1280]{1,0:T(8,128)(2,1)}, bf16[256,1280]{1,0:T(8,128)(2,1)}, u32[]{:S(2)}, u32[]{:S(2)}) %collective-permute-start.7) | collective-permute-done | bytes 655392 | tf_op jit(solution)/shard_map/ppermute | solution.py:32
  76.5 4.0 %all-to-all-done.1.refs_4_ = bf16[32,64,768]{2,1,0:T(8,128)(2,1)} async-done(((bf16[32,64,768]{2,1,0:T(8,128)(2,1)}), bf16[32,64,768]{2,1,0:T(8,128)(2,1)}, u32[]{:S(2)}, u32[]{:S(2)}) %all-to-all-start.1) | async-done | bytes 3145760 | tf_op jit(solution)/shard_map/all_to_all | solution.py:378
  80.5 9.8 %experts.2 = (bf16[256,1280]{1,0:T(8,128)(2,1)}, bf16[256,1280]{1,0:T(8,128)(2,1)}, bf16[512,1280]{1,0:T(8,128)(2,1)}, bf16[32,64,768]{2,1,0:T(8,128)(2,1)}) custom-call(bf16[256,1280]{1,0:T(8,128)(2,1)} %collective-permute-done.4.refs_0_, bf16[256,1280]{1,0:T(8,128)(2,1)} %collective-permute-done.7.refs_1_, bf16[256,1280]{1,0:T(8,128)(2,1)} %collective-permute-done.refs_2_, ...), custom_call_target="tpu_custom_call" | custom-call | flops 20000000000 | bytes 200000000 | tf_op jit(solution)/shard_map/experts/pallas_call | solution.py:246
  93.7 9.8 %experts.3 = (bf16[256,1280]{1,0:T(8,128)(2,1)}, bf16[256,1280]{1,0:T(8,128)(2,1)}, bf16[512,1280]{1,0:T(8,128)(2,1)}, bf16[32,64,768]{2,1,0:T(8,128)(2,1)}) custom-call(bf16[256,1280]{1,0:T(8,128)(2,1)} %copy-done.8, bf16[256,1280]{1,0:T(8,128)(2,1)} %collective-permute-done.8.refs_1_, ...), custom_call_target="tpu_custom_call", output_to_operand_aliasing={{3}: (8, {})} | custom-call | flops 20000000000 | bytes 200000000 | tf_op jit(solution)/shard_map/experts/pallas_call | solution.py:246
  103.5 4.7 %all-to-all-start.2 = ((bf16[32,64,768]{2,1,0:T(8,128)(2,1)}), bf16[32,64,768]{2,1,0:T(8,128)(2,1)}, u32[]{:S(2)}, u32[]{:S(2)}) async-start(bf16[32,64,768]{2,1,0:T(8,128)(2,1)} %get-tuple-element.67), calls=%async_computation.2 | async-start | bytes 6291456 | tf_op jit(solution)/shard_map/all_to_all | solution.py:378
  113.0 7.2 %collective-permute-done.10 = bf16[256,1280]{1,0:T(8,128)(2,1)S(1)} collective-permute-done((bf16[256,1280]{1,0:T(8,128)(2,1)S(1)}, bf16[256,1280]{1,0:T(8,128)(2,1)S(1)}, u32[]{:S(2)}, u32[]{:S(2)}) %collective-permute-start.10) | collective-permute-done | bytes 655392 | tf_op jit(solution)/shard_map/ppermute | solution.py:32
  121.3 3.5 %collective-permute-start.11 = (bf16[256,1280]{1,0:T(8,128)(2,1)}, bf16[256,1280]{1,0:T(8,128)(2,1)}, u32[]{:S(2)}, u32[]{:S(2)}) collective-permute-start(bf16[256,1280]{1,0:T(8,128)(2,1)} %add_convert_fusion.2), channel_id=1, source_target_pairs={{0,32},{1,97},{2,34},{3,99},{4,36},{5,101},{6,38},{7,103},{8,40},{... | collective-permute-start | bytes 1966088 | tf_op jit(solution)/shard_map/ppermute | solution.py:32
  128.3 3.5 %collective-permute-start.13 = (bf16[256,1280]{1,0:T(8,128)(2,1)}, bf16[256,1280]{1,0:T(8,128)(2,1)}, u32[]{:S(2)}, u32[]{:S(2)}) collective-permute-start(bf16[256,1280]{1,0:T(8,128)(2,1)} %add_convert_fusion), channel_id=1, source_target_pairs={{0,32},{1,97},{2,34},{3,99},{4,36},{5,101},{6,38},{7,103},{8,40},{... | collective-permute-start | bytes 1966088 | tf_op jit(solution)/shard_map/ppermute | solution.py:32
  141.4 3.1 %last_sum.1 = bf16[32,16,1280]{2,1,0:T(8,128)(2,1)} custom-call(bf16[512,1280]{1,0:T(8,128)(2,1)} %get-tuple-element.64.own, bf16[256,1280]{1,0:T(8,128)(2,1)} %collective-permute-done.11.refs_0_, bf16[256,1280]{1,0:T(8,128)(2,1)} %collective-permute-done.13.refs_1_), custom_call_target="tpu_custom_call" | custom-call | tf_op jit(solution)/shard_map/last_sum/pallas_call | solution.py:287
  144.5 3.2 %all-to-all-done.2 = bf16[32,64,768]{2,1,0:T(8,128)(2,1)} async-done(((bf16[32,64,768]{2,1,0:T(8,128)(2,1)}), bf16[32,64,768]{2,1,0:T(8,128)(2,1)}, u32[]{:S(2)}, u32[]{:S(2)}) %all-to-all-start.2) | async-done | bytes 3145760 | tf_op jit(solution)/shard_map/all_to_all | solution.py:378
  147.8 5.7 %all-to-all-start.3 = ((bf16[32,16,1280]{2,1,0:T(8,128)(2,1)}), bf16[32,16,1280]{2,1,0:T(8,128)(2,1)}, u32[]{:S(2)}, u32[]{:S(2)}) async-start(bf16[32,16,1280]{2,1,0:T(8,128)(2,1)} %last_sum.1), calls=%async_computation.3 | async-start | bytes 2621440 | tf_op jit(solution)/shard_map/all_to_all | solution.py:378
  156.6 5.1 %combine.1 = (bf16[64,768]{1,0:T(8,128)(2,1)S(1)}, bf16[64,768]{1,0:T(8,128)(2,1)S(1)}, bf16[64,768]{1,0:T(8,128)(2,1)S(1)}, bf16[64,768]{1,0:T(8,128)(2,1)S(1)}) custom-call(bf16[256,2048]{1,0:T(8,128)(2,1)} %bitcast.27, bf16[256,2048]{1,0:T(8,128)(2,1)} %bitcast.28, bf16[2048,768]{1,0:T(8,128)(2,1)} %bitcast.16.values, f32[256,768]{1,0:T(8,128)} %slice.45.shared), custom_call_target="tpu_custom_call" | custom-call | tf_op jit(solution)/shard_map/combine/pallas_call | solution.py:324
  166.8 3.0 %collective-permute-done.17 = bf16[64,768]{1,0:T(8,128)(2,1)S(1)} collective-permute-done((bf16[64,768]{1,0:T(8,128)(2,1)S(1)}, bf16[64,768]{1,0:T(8,128)(2,1)S(1)}, u32[]{:S(2)}, u32[]{:S(2)}) %collective-permute-start.17) | collective-permute-done | bytes 98336 | tf_op jit(solution)/shard_map/ppermute | solution.py:22
  169.9 3.4 %all-to-all-done.3 = bf16[32,16,1280]{2,1,0:T(8,128)(2,1)} async-done(((bf16[32,16,1280]{2,1,0:T(8,128)(2,1)}), bf16[32,16,1280]{2,1,0:T(8,128)(2,1)}, u32[]{:S(2)}, u32[]{:S(2)}) %all-to-all-start.3) | async-done | bytes 1310752 | tf_op jit(solution)/shard_map/all_to_all | solution.py:378
  (66 shorter events, 50.5 us)
Async XLA Ops:
  3.6 29.3 %all-to-all-start = ((bf16[32,16,1280]{2,1,0:T(8,128)(2,1)}), bf16[32,16,1280]{2,1,0:T(8,128)(2,1)}, u32[]{:S(2)}, u32[]{:S(2)}) async-start(bf16[32,16,1280]{2,1,0:T(8,128)(2,1)} %bitcast.30), calls=%async_computation | async-start | bytes 2621440 | tf_op jit(solution)/shard_map/all_to_all | solution.py:378
  13.1 9.7 %collective-permute-start.1 = (bf16[64,2176]{1,0:T(8,128)(2,1)S(1)}, bf16[64,2176]{1,0:T(8,128)(2,1)S(1)}, u32[]{:S(2)}, u32[]{:S(2)}) collective-permute-start(bf16[64,2176]{1,0:T(8,128)(2,1)S(1)} %get-tuple-element.45.e3), channel_id=1, source_target_pairs={{0,64},{32,96},{64,0},{96,32},{1,65},{33,97},{65,1},{97,33},{2,66}... | collective-permute-start | bytes 835592 | tf_op jit(solution)/shard_map/ppermute | solution.py:22
  16.1 13.2 %collective-permute-start.2 = (bf16[64,2176]{1,0:T(8,128)(2,1)S(1)}, bf16[64,2176]{1,0:T(8,128)(2,1)S(1)}, u32[]{:S(2)}, u32[]{:S(2)}) collective-permute-start(bf16[64,2176]{1,0:T(8,128)(2,1)S(1)} %get-tuple-element.45.e3), channel_id=1, source_target_pairs={{0,32},{32,64},{64,96},{96,0},{1,33},{33,65},{65,97},{97,1},{2,34}... | collective-permute-start | bytes 835592 | tf_op jit(solution)/shard_map/ppermute | solution.py:22
  16.5 12.8 %collective-permute-start.3 = (bf16[64,2176]{1,0:T(8,128)(2,1)S(1)}, bf16[64,2176]{1,0:T(8,128)(2,1)S(1)}, u32[]{:S(2)}, u32[]{:S(2)}) collective-permute-start(bf16[64,2176]{1,0:T(8,128)(2,1)S(1)} %get-tuple-element.45.e3), channel_id=1, source_target_pairs={{0,96},{32,0},{64,32},{96,64},{1,97},{33,1},{65,33},{97,65},{2,98}... | collective-permute-start | bytes 835592 | tf_op jit(solution)/shard_map/ppermute | solution.py:22
  33.0 47.6 %all-to-all-start.1 = ((bf16[32,64,768]{2,1,0:T(8,128)(2,1)}), bf16[32,64,768]{2,1,0:T(8,128)(2,1)}, u32[]{:S(2)}, u32[]{:S(2)}) async-start(bf16[32,64,768]{2,1,0:T(8,128)(2,1)} %bitcast.29), calls=%async_computation.1 | async-start | bytes 6291456 | tf_op jit(solution)/shard_map/all_to_all | solution.py:378
  42.0 15.3 %collective-permute-start = (bf16[256,1280]{1,0:T(8,128)(2,1)S(1)}, bf16[256,1280]{1,0:T(8,128)(2,1)}, u32[]{:S(2)}, u32[]{:S(2)}) collective-permute-start(bf16[256,1280]{1,0:T(8,128)(2,1)S(1)} %slice_bitcast_fusion.1.refs_2_), channel_id=1, source_target_pairs={{0,32},{1,97},{2,34},{3,99},{4,36},{5,101},{6,38},{7,103},{8,40},{... | collective-permute-start | bytes 1966088 | tf_op jit(solution)/shard_map/ppermute | solution.py:32
  46.4 12.7 %collective-permute-start.6 = (bf16[256,1280]{1,0:T(8,128)(2,1)}, bf16[256,1280]{1,0:T(8,128)(2,1)}, u32[]{:S(2)}, u32[]{:S(2)}) collective-permute-start(bf16[256,1280]{1,0:T(8,128)(2,1)} %slice_bitcast_fusion.refs_3_), channel_id=1, source_target_pairs={{0,32},{1,97},{2,34},{3,99},{4,36},{5,101},{6,38},{7,103},{8,40},{... | collective-permute-start | bytes 1966088 | tf_op jit(solution)/shard_map/ppermute | solution.py:32
  57.3 10.0 %collective-permute-start.4 = (bf16[256,1280]{1,0:T(8,128)(2,1)}, bf16[256,1280]{1,0:T(8,128)(2,1)}, u32[]{:S(2)}, u32[]{:S(2)}) collective-permute-start(bf16[256,1280]{1,0:T(8,128)(2,1)} %collective-permute-done.refs_2_), channel_id=1, source_target_pairs={{0,32},{1,97},{2,34},{3,99},{4,36},{5,101},{6,38},{7,103},{8,40},{... | collective-permute-start | bytes 1966088 | tf_op jit(solution)/shard_map/ppermute | solution.py:32
  59.0 15.3 %collective-permute-start.7 = (bf16[256,1280]{1,0:T(8,128)(2,1)}, bf16[256,1280]{1,0:T(8,128)(2,1)}, u32[]{:S(2)}, u32[]{:S(2)}) collective-permute-start(bf16[256,1280]{1,0:T(8,128)(2,1)} %collective-permute-done.6.refs_3_), channel_id=1, source_target_pairs={{0,32},{1,97},{2,34},{3,99},{4,36},{5,101},{6,38},{7,103},{8,40},{... | collective-permute-start | bytes 1966088 | tf_op jit(solution)/shard_map/ppermute | solution.py:32
  67.3 25.5 %collective-permute-start.5 = (bf16[256,1280]{1,0:T(8,128)(2,1)}, bf16[256,1280]{1,0:T(8,128)(2,1)S(1)}, u32[]{:S(2)}, u32[]{:S(2)}) collective-permute-start(bf16[256,1280]{1,0:T(8,128)(2,1)} %collective-permute-done.4.refs_0_), channel_id=1, source_target_pairs={{0,32},{1,97},{2,34},{3,99},{4,36},{5,101},{6,38},{7,103},{8,40},{... | collective-permute-start | bytes 1966088 | tf_op jit(solution)/shard_map/ppermute | solution.py:32
  74.3 18.5 %collective-permute-start.8 = (bf16[256,1280]{1,0:T(8,128)(2,1)}, bf16[256,1280]{1,0:T(8,128)(2,1)}, u32[]{:S(2)}, u32[]{:S(2)}) collective-permute-start(bf16[256,1280]{1,0:T(8,128)(2,1)} %collective-permute-done.7.refs_1_), channel_id=1, source_target_pairs={{0,32},{1,97},{2,34},{3,99},{4,36},{5,101},{6,38},{7,103},{8,40},{... | collective-permute-start | bytes 1966088 | tf_op jit(solution)/shard_map/ppermute | solution.py:32
  90.4 17.9 %collective-permute-start.9 = (bf16[512,1280]{1,0:T(8,128)(2,1)}, bf16[512,1280]{1,0:T(8,128)(2,1)}, u32[]{:S(2)}, u32[]{:S(2)}) collective-permute-start(bf16[512,1280]{1,0:T(8,128)(2,1)} %get-tuple-element.54), channel_id=1, source_target_pairs={{0,32},{1,97},{2,34},{3,99},{4,36},{5,101},{6,38},{7,103},{8,40},{... | collective-permute-start | bytes 3932168 | tf_op jit(solution)/shard_map/ppermute | solution.py:32
  103.5 44.3 %all-to-all-start.2 = ((bf16[32,64,768]{2,1,0:T(8,128)(2,1)}), bf16[32,64,768]{2,1,0:T(8,128)(2,1)}, u32[]{:S(2)}, u32[]{:S(2)}) async-start(bf16[32,64,768]{2,1,0:T(8,128)(2,1)} %get-tuple-element.67), calls=%async_computation.2 | async-start | bytes 6291456 | tf_op jit(solution)/shard_map/all_to_all | solution.py:378
  110.2 10.1 %collective-permute-start.10 = (bf16[256,1280]{1,0:T(8,128)(2,1)S(1)}, bf16[256,1280]{1,0:T(8,128)(2,1)S(1)}, u32[]{:S(2)}, u32[]{:S(2)}) collective-permute-start(bf16[256,1280]{1,0:T(8,128)(2,1)S(1)} %get-tuple-element.82), channel_id=1, source_target_pairs={{0,32},{1,97},{2,34},{3,99},{4,36},{5,101},{6,38},{7,103},{8,40},{... | collective-permute-start | bytes 1966088 | tf_op jit(solution)/shard_map/ppermute | solution.py:32
  112.7 14.6 %collective-permute-start.12 = (bf16[256,1280]{1,0:T(8,128)(2,1)S(1)}, bf16[256,1280]{1,0:T(8,128)(2,1)S(1)}, u32[]{:S(2)}, u32[]{:S(2)}) collective-permute-start(bf16[256,1280]{1,0:T(8,128)(2,1)S(1)} %get-tuple-element.81), channel_id=1, source_target_pairs={{0,32},{1,97},{2,34},{3,99},{4,36},{5,101},{6,38},{7,103},{8,40},{... | collective-permute-start | bytes 1966088 | tf_op jit(solution)/shard_map/ppermute | solution.py:32
  121.3 19.9 %collective-permute-start.11 = (bf16[256,1280]{1,0:T(8,128)(2,1)}, bf16[256,1280]{1,0:T(8,128)(2,1)}, u32[]{:S(2)}, u32[]{:S(2)}) collective-permute-start(bf16[256,1280]{1,0:T(8,128)(2,1)} %add_convert_fusion.2), channel_id=1, source_target_pairs={{0,32},{1,97},{2,34},{3,99},{4,36},{5,101},{6,38},{7,103},{8,40},{... | collective-permute-start | bytes 1966088 | tf_op jit(solution)/shard_map/ppermute | solution.py:32
  128.3 13.1 %collective-permute-start.13 = (bf16[256,1280]{1,0:T(8,128)(2,1)}, bf16[256,1280]{1,0:T(8,128)(2,1)}, u32[]{:S(2)}, u32[]{:S(2)}) collective-permute-start(bf16[256,1280]{1,0:T(8,128)(2,1)} %add_convert_fusion), channel_id=1, source_target_pairs={{0,32},{1,97},{2,34},{3,99},{4,36},{5,101},{6,38},{7,103},{8,40},{... | collective-permute-start | bytes 1966088 | tf_op jit(solution)/shard_map/ppermute | solution.py:32
  147.8 25.5 %all-to-all-start.3 = ((bf16[32,16,1280]{2,1,0:T(8,128)(2,1)}), bf16[32,16,1280]{2,1,0:T(8,128)(2,1)}, u32[]{:S(2)}, u32[]{:S(2)}) async-start(bf16[32,16,1280]{2,1,0:T(8,128)(2,1)} %last_sum.1), calls=%async_computation.3 | async-start | bytes 2621440 | tf_op jit(solution)/shard_map/all_to_all | solution.py:378
  153.4 11.0 %collective-permute-start.16 = (bf16[64,1280]{1,0:T(8,128)(2,1)}, bf16[64,1280]{1,0:T(8,128)(2,1)S(1)}, u32[]{:S(2)}, u32[]{:S(2)}) collective-permute-start(bf16[64,1280]{1,0:T(8,128)(2,1)} %get-tuple-element.71), channel_id=1, source_target_pairs={{0,32},{32,64},{64,96},{96,0},{1,33},{33,65},{65,97},{97,1},{2,34}... | collective-permute-start | bytes 491528 | tf_op jit(solution)/shard_map/ppermute | solution.py:22
  153.5 12.3 %collective-permute-start.15 = (bf16[64,1280]{1,0:T(8,128)(2,1)S(1)}, bf16[64,1280]{1,0:T(8,128)(2,1)S(1)}, u32[]{:S(2)}, u32[]{:S(2)}) collective-permute-start(bf16[64,1280]{1,0:T(8,128)(2,1)S(1)} %get-tuple-element.70), channel_id=1, source_target_pairs={{0,96},{32,0},{64,32},{96,64},{1,97},{33,1},{65,33},{97,65},{2,98}... | collective-permute-start | bytes 491528 | tf_op jit(solution)/shard_map/ppermute | solution.py:22
  156.2 9.6 %collective-permute-start.14 = (bf16[64,1280]{1,0:T(8,128)(2,1)S(1)}, bf16[64,1280]{1,0:T(8,128)(2,1)S(1)}, u32[]{:S(2)}, u32[]{:S(2)}) collective-permute-start(bf16[64,1280]{1,0:T(8,128)(2,1)S(1)} %get-tuple-element.69), channel_id=1, source_target_pairs={{0,64},{32,96},{64,0},{96,32},{1,65},{33,97},{65,1},{97,33},{2,66}... | collective-permute-start | bytes 491528 | tf_op jit(solution)/shard_map/ppermute | solution.py:22
  161.7 5.1 %collective-permute-start.19 = (bf16[64,768]{1,0:T(8,128)(2,1)S(1)}, bf16[64,768]{1,0:T(8,128)(2,1)S(1)}, u32[]{:S(2)}, u32[]{:S(2)}) collective-permute-start(bf16[64,768]{1,0:T(8,128)(2,1)S(1)} %get-tuple-element.80), channel_id=1, source_target_pairs={{0,32},{32,64},{64,96},{96,0},{1,33},{33,65},{65,97},{97,1},{2,34}... | collective-permute-start | bytes 294920 | tf_op jit(solution)/shard_map/ppermute | solution.py:22
  161.9 4.9 %collective-permute-start.18 = (bf16[64,768]{1,0:T(8,128)(2,1)S(1)}, bf16[64,768]{1,0:T(8,128)(2,1)S(1)}, u32[]{:S(2)}, u32[]{:S(2)}) collective-permute-start(bf16[64,768]{1,0:T(8,128)(2,1)S(1)} %get-tuple-element.79), channel_id=1, source_target_pairs={{0,96},{32,0},{64,32},{96,64},{1,97},{33,1},{65,33},{97,65},{2,98}... | collective-permute-start | bytes 294920 | tf_op jit(solution)/shard_map/ppermute | solution.py:22
  164.4 5.4 %collective-permute-start.17 = (bf16[64,768]{1,0:T(8,128)(2,1)S(1)}, bf16[64,768]{1,0:T(8,128)(2,1)S(1)}, u32[]{:S(2)}, u32[]{:S(2)}) collective-permute-start(bf16[64,768]{1,0:T(8,128)(2,1)S(1)} %get-tuple-element.78), channel_id=1, source_target_pairs={{0,64},{32,96},{64,0},{96,32},{1,65},{33,97},{65,1},{97,33},{2,66}... | collective-permute-start | bytes 294920 | tf_op jit(solution)/shard_map/ppermute | solution.py:22
  (9 other events, 144.5 us)

commit v11 on v10

--- a/solution.py
+++ b/solution.py
@@ -293,7 +293,9 @@
 
 
 def weigh(hi, lo, values):
-    return dot_f32(hi, values) + dot_f32(lo, values)
+    rows = hi.shape[0]
+    both = dot_f32(jnp.concatenate([hi, lo], axis=0), values)
+    return both[:rows] + both[rows:]
 
 
 def combine(hi, lo, values, shared, *refs):

time: 177 us -> 176 us (level)
  no operation moved by 1% of the time
where the time goes in v11:
time: 176 us
  starting transfers between devices  63.8 us (36%)
  waiting for transfers between devices  46.1 us (26%)
  Pallas kernels  36.5 us (21%)
  local copies, waits for them, and re-layouts  11.6 us (7%)
  matrix products  10.7 us (6%)
  other arithmetic  5.84 us (3%)
    all_to_all x4, starting transfers between devices, over_ep(): lax.all_to_all(x.reshape(n_ep, rows, cols), 'ep', split_axis=0, concat_ax...  27.6 us
    ppermute x11, starting transfers between devices, toward(): return lax.ppermute(x, ('dp', 'ep'), pairs)  23.2 us
    ppermute x11, waiting for transfers between devices, toward(): return lax.ppermute(x, ('dp', 'ep'), pairs)  20.9 us
    pallas_call x2, Pallas kernels, run_experts(): pl.pallas_call(functools.partial(expert_kernel, len(planes), pair), in_sp...  19.7 us
    ppermute x9, waiting for transfers between devices, shifted(): return lax.ppermute(x, 'dp', [(i, (i + shift) % n) for i in range(n)])  14.4 us
    ppermute x9, starting transfers between devices, shifted(): return lax.ppermute(x, 'dp', [(i, (i + shift) % n) for i in range(n)])  12.9 us
    all_to_all x4, waiting for transfers between devices, over_ep(): lax.all_to_all(x.reshape(n_ep, rows, cols), 'ep', split_axis=0, concat_ax...  10.8 us
    dot_general x2, matrix products, dot_f32(): return jnp.dot(a, b, preferred_element_type=jnp.float32)  10.7 us
  transfers between devices with their start and end apart: 24, of which 14 were waited for; matrix products, arithmetic and copies ran while one was open for 16% of the time, Pallas kernels for 18%

profile of v11, /device:TPU:1, one launch (start us, length us, event | category | flops | bytes accessed | tf_op | source)
XLA Modules:
  0.0 175.7 jit_solution(5057516633101082412)
XLA Ops:
  3.6 9.5 %all-to-all-start = ((bf16[32,16,1280]{2,1,0:T(8,128)(2,1)}), bf16[32,16,1280]{2,1,0:T(8,128)(2,1)}, u32[]{:S(2)}, u32[]{:S(2)}) async-start(bf16[32,16,1280]{2,1,0:T(8,128)(2,1)} %bitcast.30), calls=%async_computation | async-start | bytes 2621440 | tf_op jit(solution)/shard_map/all_to_all | solution.py:380
  13.1 3.0 %collective-permute-start.1 = (bf16[64,2176]{1,0:T(8,128)(2,1)S(1)}, bf16[64,2176]{1,0:T(8,128)(2,1)S(1)}, u32[]{:S(2)}, u32[]{:S(2)}) collective-permute-start(bf16[64,2176]{1,0:T(8,128)(2,1)S(1)} %get-tuple-element.45.e3), channel_id=1, source_target_pairs={{0,64},{32,96},{64,0},{96,32},{1,65},{33,97},{65,1},{97,33},{2,66}... | collective-permute-start | bytes 835592 | tf_op jit(solution)/shard_map/ppermute | solution.py:22
  18.8 4.0 %collective-permute-done.1.e0 = bf16[64,2176]{1,0:T(8,128)(2,1)S(1)} collective-permute-done((bf16[64,2176]{1,0:T(8,128)(2,1)S(1)}, bf16[64,2176]{1,0:T(8,128)(2,1)S(1)}, u32[]{:S(2)}, u32[]{:S(2)}) %collective-permute-start.1) | collective-permute-done | bytes 278560 | tf_op jit(solution)/shard_map/ppermute | solution.py:22
  22.8 6.6 %collective-permute-done.2.e1 = bf16[64,2176]{1,0:T(8,128)(2,1)S(1)} collective-permute-done((bf16[64,2176]{1,0:T(8,128)(2,1)S(1)}, bf16[64,2176]{1,0:T(8,128)(2,1)S(1)}, u32[]{:S(2)}, u32[]{:S(2)}) %collective-permute-start.2) | collective-permute-done | bytes 278560 | tf_op jit(solution)/shard_map/ppermute | solution.py:22
  29.4 3.5 %prepare_ring.1 = (bf16[2048,768]{1,0:T(8,128)(2,1)}, bf16[2048,256]{1,0:T(8,128)(2,1)}, bf16[2048,256]{1,0:T(8,128)(2,1)}, bf16[256,2048]{1,0:T(8,128)(2,1)}) custom-call(bf16[64,2176]{1,0:T(8,128)(2,1)S(1)} %collective-permute-done.1.e0, bf16[64,2176]{1,0:T(8,128)(2,1)S(1)} %collective-permute-done.2.e1, bf16[64,2176]{1,0:T(8,128)(2,1)S(1)} %collective-permute-done.3.e2, ...), custom_call_target="tpu_custom_call" | custom-call | tf_op jit(solution)/shard_map/prepare_ring/pallas_call | solution.py:155
  33.0 7.7 %all-to-all-start.1 = ((bf16[32,64,768]{2,1,0:T(8,128)(2,1)}), bf16[32,64,768]{2,1,0:T(8,128)(2,1)}, u32[]{:S(2)}, u32[]{:S(2)}) async-start(bf16[32,64,768]{2,1,0:T(8,128)(2,1)} %bitcast.29), calls=%async_computation.1 | async-start | bytes 6291456 | tf_op jit(solution)/shard_map/all_to_all | solution.py:380
  46.6 3.7 %fusion.6 = f32[256,704]{0,1:T(8,128)} fusion(bf16[256,2048]{1,0:T(8,128)(2,1)S(1)} %copy-done.7, bf16[2048,704]{0,1:T(8,128)(2,1)} %param.17), kind=kOutput, calls=%fused_computation.15 | convolution fusion | flops 738197504 | bytes 4653056 | tf_op jit(solution)/shard_map/dot_general | solution.py:44
  50.3 7.0 %fusion = f32[256,2048]{1,0:T(8,128)} fusion(bf16[704,2048]{1,0:T(8,128)(2,1)S(1)} %copy-done, f32[256,704]{0,1:T(8,128)} %fusion.6, bf16[256,2048]{1,0:T(8,128)(2,1)} %get-tuple-element.46, bf16[2048,704]{0,1:T(8,128)(2,1)} %param.18), kind=kOutput, calls=%fused_computation.7 | convolution fusion | flops 1477476352 | bytes 9633792 | tf_op jit(solution)/shard_map/dot_general | solution.py:44
  59.0 3.4 %collective-permute-start.7 = (bf16[256,1280]{1,0:T(8,128)(2,1)}, bf16[256,1280]{1,0:T(8,128)(2,1)}, u32[]{:S(2)}, u32[]{:S(2)}) collective-permute-start(bf16[256,1280]{1,0:T(8,128)(2,1)} %collective-permute-done.6.refs_3_), channel_id=1, source_target_pairs={{0,32},{1,97},{2,34},{3,99},{4,36},{5,101},{6,38},{7,103},{8,40},{... | collective-permute-start | bytes 1966088 | tf_op jit(solution)/shard_map/ppermute | solution.py:32
  62.5 4.9 %collective-permute-done.4.refs_0_ = bf16[256,1280]{1,0:T(8,128)(2,1)} collective-permute-done((bf16[256,1280]{1,0:T(8,128)(2,1)}, bf16[256,1280]{1,0:T(8,128)(2,1)}, u32[]{:S(2)}, u32[]{:S(2)}) %collective-permute-start.4) | collective-permute-done | bytes 655392 | tf_op jit(solution)/shard_map/ppermute | solution.py:32
  69.5 4.9 %collective-permute-done.7.refs_1_ = bf16[256,1280]{1,0:T(8,128)(2,1)} collective-permute-done((bf16[256,1280]{1,0:T(8,128)(2,1)}, bf16[256,1280]{1,0:T(8,128)(2,1)}, u32[]{:S(2)}, u32[]{:S(2)}) %collective-permute-start.7) | collective-permute-done | bytes 655392 | tf_op jit(solution)/shard_map/ppermute | solution.py:32
  76.5 4.0 %all-to-all-done.1.refs_4_ = bf16[32,64,768]{2,1,0:T(8,128)(2,1)} async-done(((bf16[32,64,768]{2,1,0:T(8,128)(2,1)}), bf16[32,64,768]{2,1,0:T(8,128)(2,1)}, u32[]{:S(2)}, u32[]{:S(2)}) %all-to-all-start.1) | async-done | bytes 3145760 | tf_op jit(solution)/shard_map/all_to_all | solution.py:380
  80.5 9.8 %experts.2 = (bf16[256,1280]{1,0:T(8,128)(2,1)}, bf16[256,1280]{1,0:T(8,128)(2,1)}, bf16[512,1280]{1,0:T(8,128)(2,1)}, bf16[32,64,768]{2,1,0:T(8,128)(2,1)}) custom-call(bf16[256,1280]{1,0:T(8,128)(2,1)} %collective-permute-done.4.refs_0_, bf16[256,1280]{1,0:T(8,128)(2,1)} %collective-permute-done.7.refs_1_, bf16[256,1280]{1,0:T(8,128)(2,1)} %collective-permute-done.refs_2_, ...), custom_call_target="tpu_custom_call" | custom-call | flops 20000000000 | bytes 200000000 | tf_op jit(solution)/shard_map/experts/pallas_call | solution.py:246
  93.7 9.8 %experts.3 = (bf16[256,1280]{1,0:T(8,128)(2,1)}, bf16[256,1280]{1,0:T(8,128)(2,1)}, bf16[512,1280]{1,0:T(8,128)(2,1)}, bf16[32,64,768]{2,1,0:T(8,128)(2,1)}) custom-call(bf16[256,1280]{1,0:T(8,128)(2,1)} %copy-done.8, bf16[256,1280]{1,0:T(8,128)(2,1)} %collective-permute-done.8.refs_1_, ...), custom_call_target="tpu_custom_call", output_to_operand_aliasing={{3}: (8, {})} | custom-call | flops 20000000000 | bytes 200000000 | tf_op jit(solution)/shard_map/experts/pallas_call | solution.py:246
  103.5 4.7 %all-to-all-start.2 = ((bf16[32,64,768]{2,1,0:T(8,128)(2,1)}), bf16[32,64,768]{2,1,0:T(8,128)(2,1)}, u32[]{:S(2)}, u32[]{:S(2)}) async-start(bf16[32,64,768]{2,1,0:T(8,128)(2,1)} %get-tuple-element.67), calls=%async_computation.2 | async-start | bytes 6291456 | tf_op jit(solution)/shard_map/all_to_all | solution.py:380
  113.0 7.2 %collective-permute-done.10 = bf16[256,1280]{1,0:T(8,128)(2,1)S(1)} collective-permute-done((bf16[256,1280]{1,0:T(8,128)(2,1)S(1)}, bf16[256,1280]{1,0:T(8,128)(2,1)S(1)}, u32[]{:S(2)}, u32[]{:S(2)}) %collective-permute-start.10) | collective-permute-done | bytes 655392 | tf_op jit(solution)/shard_map/ppermute | solution.py:32
  121.3 3.5 %collective-permute-start.11 = (bf16[256,1280]{1,0:T(8,128)(2,1)}, bf16[256,1280]{1,0:T(8,128)(2,1)}, u32[]{:S(2)}, u32[]{:S(2)}) collective-permute-start(bf16[256,1280]{1,0:T(8,128)(2,1)} %add_convert_fusion.2), channel_id=1, source_target_pairs={{0,32},{1,97},{2,34},{3,99},{4,36},{5,101},{6,38},{7,103},{8,40},{... | collective-permute-start | bytes 1966088 | tf_op jit(solution)/shard_map/ppermute | solution.py:32
  128.3 3.5 %collective-permute-start.13 = (bf16[256,1280]{1,0:T(8,128)(2,1)}, bf16[256,1280]{1,0:T(8,128)(2,1)}, u32[]{:S(2)}, u32[]{:S(2)}) collective-permute-start(bf16[256,1280]{1,0:T(8,128)(2,1)} %add_convert_fusion), channel_id=1, source_target_pairs={{0,32},{1,97},{2,34},{3,99},{4,36},{5,101},{6,38},{7,103},{8,40},{... | collective-permute-start | bytes 1966088 | tf_op jit(solution)/shard_map/ppermute | solution.py:32
  141.4 3.1 %last_sum.1 = bf16[32,16,1280]{2,1,0:T(8,128)(2,1)} custom-call(bf16[512,1280]{1,0:T(8,128)(2,1)} %get-tuple-element.64.own, bf16[256,1280]{1,0:T(8,128)(2,1)} %collective-permute-done.11.refs_0_, bf16[256,1280]{1,0:T(8,128)(2,1)} %collective-permute-done.13.refs_1_), custom_call_target="tpu_custom_call" | custom-call | tf_op jit(solution)/shard_map/last_sum/pallas_call | solution.py:287
  144.5 3.2 %all-to-all-done.2 = bf16[32,64,768]{2,1,0:T(8,128)(2,1)} async-done(((bf16[32,64,768]{2,1,0:T(8,128)(2,1)}), bf16[32,64,768]{2,1,0:T(8,128)(2,1)}, u32[]{:S(2)}, u32[]{:S(2)}) %all-to-all-start.2) | async-done | bytes 3145760 | tf_op jit(solution)/shard_map/all_to_all | solution.py:380
  147.8 5.7 %all-to-all-start.3 = ((bf16[32,16,1280]{2,1,0:T(8,128)(2,1)}), bf16[32,16,1280]{2,1,0:T(8,128)(2,1)}, u32[]{:S(2)}, u32[]{:S(2)}) async-start(bf16[32,16,1280]{2,1,0:T(8,128)(2,1)} %last_sum.1), calls=%async_computation.3 | async-start | bytes 2621440 | tf_op jit(solution)/shard_map/all_to_all | solution.py:380
  156.6 5.1 %combine.1 = (bf16[64,768]{1,0:T(8,128)(2,1)S(1)}, bf16[64,768]{1,0:T(8,128)(2,1)S(1)}, bf16[64,768]{1,0:T(8,128)(2,1)S(1)}, bf16[64,768]{1,0:T(8,128)(2,1)S(1)}) custom-call(bf16[256,2048]{1,0:T(8,128)(2,1)} %bitcast.27, bf16[256,2048]{1,0:T(8,128)(2,1)} %bitcast.28, bf16[2048,768]{1,0:T(8,128)(2,1)} %bitcast.16.values, f32[256,768]{1,0:T(8,128)} %slice.45.shared), custom_call_target="tpu_custom_call" | custom-call | tf_op jit(solution)/shard_map/combine/pallas_call | solution.py:326
  166.8 3.0 %collective-permute-done.17 = bf16[64,768]{1,0:T(8,128)(2,1)S(1)} collective-permute-done((bf16[64,768]{1,0:T(8,128)(2,1)S(1)}, bf16[64,768]{1,0:T(8,128)(2,1)S(1)}, u32[]{:S(2)}, u32[]{:S(2)}) %collective-permute-start.17) | collective-permute-done | bytes 98336 | tf_op jit(solution)/shard_map/ppermute | solution.py:22
  169.9 3.4 %all-to-all-done.3 = bf16[32,16,1280]{2,1,0:T(8,128)(2,1)} async-done(((bf16[32,16,1280]{2,1,0:T(8,128)(2,1)}), bf16[32,16,1280]{2,1,0:T(8,128)(2,1)}, u32[]{:S(2)}, u32[]{:S(2)}) %all-to-all-start.3) | async-done | bytes 1310752 | tf_op jit(solution)/shard_map/all_to_all | solution.py:380
  (66 shorter events, 50.3 us)
Async XLA Ops:
  3.6 29.3 %all-to-all-start = ((bf16[32,16,1280]{2,1,0:T(8,128)(2,1)}), bf16[32,16,1280]{2,1,0:T(8,128)(2,1)}, u32[]{:S(2)}, u32[]{:S(2)}) async-start(bf16[32,16,1280]{2,1,0:T(8,128)(2,1)} %bitcast.30), calls=%async_computation | async-start | bytes 2621440 | tf_op jit(solution)/shard_map/all_to_all | solution.py:380
  13.1 9.7 %collective-permute-start.1 = (bf16[64,2176]{1,0:T(8,128)(2,1)S(1)}, bf16[64,2176]{1,0:T(8,128)(2,1)S(1)}, u32[]{:S(2)}, u32[]{:S(2)}) collective-permute-start(bf16[64,2176]{1,0:T(8,128)(2,1)S(1)} %get-tuple-element.45.e3), channel_id=1, source_target_pairs={{0,64},{32,96},{64,0},{96,32},{1,65},{33,97},{65,1},{97,33},{2,66}... | collective-permute-start | bytes 835592 | tf_op jit(solution)/shard_map/ppermute | solution.py:22
  16.1 13.2 %collective-permute-start.2 = (bf16[64,2176]{1,0:T(8,128)(2,1)S(1)}, bf16[64,2176]{1,0:T(8,128)(2,1)S(1)}, u32[]{:S(2)}, u32[]{:S(2)}) collective-permute-start(bf16[64,2176]{1,0:T(8,128)(2,1)S(1)} %get-tuple-element.45.e3), channel_id=1, source_target_pairs={{0,32},{32,64},{64,96},{96,0},{1,33},{33,65},{65,97},{97,1},{2,34}... | collective-permute-start | bytes 835592 | tf_op jit(solution)/shard_map/ppermute | solution.py:22
  16.5 12.8 %collective-permute-start.3 = (bf16[64,2176]{1,0:T(8,128)(2,1)S(1)}, bf16[64,2176]{1,0:T(8,128)(2,1)S(1)}, u32[]{:S(2)}, u32[]{:S(2)}) collective-permute-start(bf16[64,2176]{1,0:T(8,128)(2,1)S(1)} %get-tuple-element.45.e3), channel_id=1, source_target_pairs={{0,96},{32,0},{64,32},{96,64},{1,97},{33,1},{65,33},{97,65},{2,98}... | collective-permute-start | bytes 835592 | tf_op jit(solution)/shard_map/ppermute | solution.py:22
  33.0 47.6 %all-to-all-start.1 = ((bf16[32,64,768]{2,1,0:T(8,128)(2,1)}), bf16[32,64,768]{2,1,0:T(8,128)(2,1)}, u32[]{:S(2)}, u32[]{:S(2)}) async-start(bf16[32,64,768]{2,1,0:T(8,128)(2,1)} %bitcast.29), calls=%async_computation.1 | async-start | bytes 6291456 | tf_op jit(solution)/shard_map/all_to_all | solution.py:380
  42.0 15.3 %collective-permute-start = (bf16[256,1280]{1,0:T(8,128)(2,1)S(1)}, bf16[256,1280]{1,0:T(8,128)(2,1)}, u32[]{:S(2)}, u32[]{:S(2)}) collective-permute-start(bf16[256,1280]{1,0:T(8,128)(2,1)S(1)} %slice_bitcast_fusion.1.refs_2_), channel_id=1, source_target_pairs={{0,32},{1,97},{2,34},{3,99},{4,36},{5,101},{6,38},{7,103},{8,40},{... | collective-permute-start | bytes 1966088 | tf_op jit(solution)/shard_map/ppermute | solution.py:32
  46.4 12.7 %collective-permute-start.6 = (bf16[256,1280]{1,0:T(8,128)(2,1)}, bf16[256,1280]{1,0:T(8,128)(2,1)}, u32[]{:S(2)}, u32[]{:S(2)}) collective-permute-start(bf16[256,1280]{1,0:T(8,128)(2,1)} %slice_bitcast_fusion.refs_3_), channel_id=1, source_target_pairs={{0,32},{1,97},{2,34},{3,99},{4,36},{5,101},{6,38},{7,103},{8,40},{... | collective-permute-start | bytes 1966088 | tf_op jit(solution)/shard_map/ppermute | solution.py:32
  57.3 10.0 %collective-permute-start.4 = (bf16[256,1280]{1,0:T(8,128)(2,1)}, bf16[256,1280]{1,0:T(8,128)(2,1)}, u32[]{:S(2)}, u32[]{:S(2)}) collective-permute-start(bf16[256,1280]{1,0:T(8,128)(2,1)} %collective-permute-done.refs_2_), channel_id=1, source_target_pairs={{0,32},{1,97},{2,34},{3,99},{4,36},{5,101},{6,38},{7,103},{8,40},{... | collective-permute-start | bytes 1966088 | tf_op jit(solution)/shard_map/ppermute | solution.py:32
  59.0 15.3 %collective-permute-start.7 = (bf16[256,1280]{1,0:T(8,128)(2,1)}, bf16[256,1280]{1,0:T(8,128)(2,1)}, u32[]{:S(2)}, u32[]{:S(2)}) collective-permute-start(bf16[256,1280]{1,0:T(8,128)(2,1)} %collective-permute-done.6.refs_3_), channel_id=1, source_target_pairs={{0,32},{1,97},{2,34},{3,99},{4,36},{5,101},{6,38},{7,103},{8,40},{... | collective-permute-start | bytes 1966088 | tf_op jit(solution)/shard_map/ppermute | solution.py:32
  67.3 25.5 %collective-permute-start.5 = (bf16[256,1280]{1,0:T(8,128)(2,1)}, bf16[256,1280]{1,0:T(8,128)(2,1)S(1)}, u32[]{:S(2)}, u32[]{:S(2)}) collective-permute-start(bf16[256,1280]{1,0:T(8,128)(2,1)} %collective-permute-done.4.refs_0_), channel_id=1, source_target_pairs={{0,32},{1,97},{2,34},{3,99},{4,36},{5,101},{6,38},{7,103},{8,40},{... | collective-permute-start | bytes 1966088 | tf_op jit(solution)/shard_map/ppermute | solution.py:32
  74.3 18.5 %collective-permute-start.8 = (bf16[256,1280]{1,0:T(8,128)(2,1)}, bf16[256,1280]{1,0:T(8,128)(2,1)}, u32[]{:S(2)}, u32[]{:S(2)}) collective-permute-start(bf16[256,1280]{1,0:T(8,128)(2,1)} %collective-permute-done.7.refs_1_), channel_id=1, source_target_pairs={{0,32},{1,97},{2,34},{3,99},{4,36},{5,101},{6,38},{7,103},{8,40},{... | collective-permute-start | bytes 1966088 | tf_op jit(solution)/shard_map/ppermute | solution.py:32
  90.4 17.9 %collective-permute-start.9 = (bf16[512,1280]{1,0:T(8,128)(2,1)}, bf16[512,1280]{1,0:T(8,128)(2,1)}, u32[]{:S(2)}, u32[]{:S(2)}) collective-permute-start(bf16[512,1280]{1,0:T(8,128)(2,1)} %get-tuple-element.54), channel_id=1, source_target_pairs={{0,32},{1,97},{2,34},{3,99},{4,36},{5,101},{6,38},{7,103},{8,40},{... | collective-permute-start | bytes 3932168 | tf_op jit(solution)/shard_map/ppermute | solution.py:32
  103.5 44.3 %all-to-all-start.2 = ((bf16[32,64,768]{2,1,0:T(8,128)(2,1)}), bf16[32,64,768]{2,1,0:T(8,128)(2,1)}, u32[]{:S(2)}, u32[]{:S(2)}) async-start(bf16[32,64,768]{2,1,0:T(8,128)(2,1)} %get-tuple-element.67), calls=%async_computation.2 | async-start | bytes 6291456 | tf_op jit(solution)/shard_map/all_to_all | solution.py:380
  110.2 10.1 %collective-permute-start.10 = (bf16[256,1280]{1,0:T(8,128)(2,1)S(1)}, bf16[256,1280]{1,0:T(8,128)(2,1)S(1)}, u32[]{:S(2)}, u32[]{:S(2)}) collective-permute-start(bf16[256,1280]{1,0:T(8,128)(2,1)S(1)} %get-tuple-element.82), channel_id=1, source_target_pairs={{0,32},{1,97},{2,34},{3,99},{4,36},{5,101},{6,38},{7,103},{8,40},{... | collective-permute-start | bytes 1966088 | tf_op jit(solution)/shard_map/ppermute | solution.py:32
  112.7 14.6 %collective-permute-start.12 = (bf16[256,1280]{1,0:T(8,128)(2,1)S(1)}, bf16[256,1280]{1,0:T(8,128)(2,1)S(1)}, u32[]{:S(2)}, u32[]{:S(2)}) collective-permute-start(bf16[256,1280]{1,0:T(8,128)(2,1)S(1)} %get-tuple-element.81), channel_id=1, source_target_pairs={{0,32},{1,97},{2,34},{3,99},{4,36},{5,101},{6,38},{7,103},{8,40},{... | collective-permute-start | bytes 1966088 | tf_op jit(solution)/shard_map/ppermute | solution.py:32
  121.3 19.9 %collective-permute-start.11 = (bf16[256,1280]{1,0:T(8,128)(2,1)}, bf16[256,1280]{1,0:T(8,128)(2,1)}, u32[]{:S(2)}, u32[]{:S(2)}) collective-permute-start(bf16[256,1280]{1,0:T(8,128)(2,1)} %add_convert_fusion.2), channel_id=1, source_target_pairs={{0,32},{1,97},{2,34},{3,99},{4,36},{5,101},{6,38},{7,103},{8,40},{... | collective-permute-start | bytes 1966088 | tf_op jit(solution)/shard_map/ppermute | solution.py:32
  128.3 13.1 %collective-permute-start.13 = (bf16[256,1280]{1,0:T(8,128)(2,1)}, bf16[256,1280]{1,0:T(8,128)(2,1)}, u32[]{:S(2)}, u32[]{:S(2)}) collective-permute-start(bf16[256,1280]{1,0:T(8,128)(2,1)} %add_convert_fusion), channel_id=1, source_target_pairs={{0,32},{1,97},{2,34},{3,99},{4,36},{5,101},{6,38},{7,103},{8,40},{... | collective-permute-start | bytes 1966088 | tf_op jit(solution)/shard_map/ppermute | solution.py:32
  147.8 25.5 %all-to-all-start.3 = ((bf16[32,16,1280]{2,1,0:T(8,128)(2,1)}), bf16[32,16,1280]{2,1,0:T(8,128)(2,1)}, u32[]{:S(2)}, u32[]{:S(2)}) async-start(bf16[32,16,1280]{2,1,0:T(8,128)(2,1)} %last_sum.1), calls=%async_computation.3 | async-start | bytes 2621440 | tf_op jit(solution)/shard_map/all_to_all | solution.py:380
  153.4 11.0 %collective-permute-start.16 = (bf16[64,1280]{1,0:T(8,128)(2,1)}, bf16[64,1280]{1,0:T(8,128)(2,1)S(1)}, u32[]{:S(2)}, u32[]{:S(2)}) collective-permute-start(bf16[64,1280]{1,0:T(8,128)(2,1)} %get-tuple-element.71), channel_id=1, source_target_pairs={{0,32},{32,64},{64,96},{96,0},{1,33},{33,65},{65,97},{97,1},{2,34}... | collective-permute-start | bytes 491528 | tf_op jit(solution)/shard_map/ppermute | solution.py:22
  153.5 12.3 %collective-permute-start.15 = (bf16[64,1280]{1,0:T(8,128)(2,1)S(1)}, bf16[64,1280]{1,0:T(8,128)(2,1)S(1)}, u32[]{:S(2)}, u32[]{:S(2)}) collective-permute-start(bf16[64,1280]{1,0:T(8,128)(2,1)S(1)} %get-tuple-element.70), channel_id=1, source_target_pairs={{0,96},{32,0},{64,32},{96,64},{1,97},{33,1},{65,33},{97,65},{2,98}... | collective-permute-start | bytes 491528 | tf_op jit(solution)/shard_map/ppermute | solution.py:22
  156.2 9.6 %collective-permute-start.14 = (bf16[64,1280]{1,0:T(8,128)(2,1)S(1)}, bf16[64,1280]{1,0:T(8,128)(2,1)S(1)}, u32[]{:S(2)}, u32[]{:S(2)}) collective-permute-start(bf16[64,1280]{1,0:T(8,128)(2,1)S(1)} %get-tuple-element.69), channel_id=1, source_target_pairs={{0,64},{32,96},{64,0},{96,32},{1,65},{33,97},{65,1},{97,33},{2,66}... | collective-permute-start | bytes 491528 | tf_op jit(solution)/shard_map/ppermute | solution.py:22
  161.7 5.1 %collective-permute-start.19 = (bf16[64,768]{1,0:T(8,128)(2,1)S(1)}, bf16[64,768]{1,0:T(8,128)(2,1)S(1)}, u32[]{:S(2)}, u32[]{:S(2)}) collective-permute-start(bf16[64,768]{1,0:T(8,128)(2,1)S(1)} %get-tuple-element.80), channel_id=1, source_target_pairs={{0,32},{32,64},{64,96},{96,0},{1,33},{33,65},{65,97},{97,1},{2,34}... | collective-permute-start | bytes 294920 | tf_op jit(solution)/shard_map/ppermute | solution.py:22
  161.9 4.9 %collective-permute-start.18 = (bf16[64,768]{1,0:T(8,128)(2,1)S(1)}, bf16[64,768]{1,0:T(8,128)(2,1)S(1)}, u32[]{:S(2)}, u32[]{:S(2)}) collective-permute-start(bf16[64,768]{1,0:T(8,128)(2,1)S(1)} %get-tuple-element.79), channel_id=1, source_target_pairs={{0,96},{32,0},{64,32},{96,64},{1,97},{33,1},{65,33},{97,65},{2,98}... | collective-permute-start | bytes 294920 | tf_op jit(solution)/shard_map/ppermute | solution.py:22
  164.4 5.4 %collective-permute-start.17 = (bf16[64,768]{1,0:T(8,128)(2,1)S(1)}, bf16[64,768]{1,0:T(8,128)(2,1)S(1)}, u32[]{:S(2)}, u32[]{:S(2)}) collective-permute-start(bf16[64,768]{1,0:T(8,128)(2,1)S(1)} %get-tuple-element.78), channel_id=1, source_target_pairs={{0,64},{32,96},{64,0},{96,32},{1,65},{33,97},{65,1},{97,33},{2,66}... | collective-permute-start | bytes 294920 | tf_op jit(solution)/shard_map/ppermute | solution.py:22
  (9 other events, 144.5 us)
